TPU v7x, 32 devices: a whole 2x2x4 slice. The times are simulated.
32 devices in a mesh: grp: 2 (over x), rb: 16 (over z, y, core).
Axes of the slice: x: 2, y: 2, z: 4, core: 2. Of those that a mesh axis runs over, the one named last changes fastest.
Arguments:
- tiles: bfloat16 [2816, 256, 256], P(('grp', 'rb')), parts along dimension 0, may hold values from -0.25 to 0.25
- tile_rows: int32 [2816], P(('grp', 'rb')), parts along dimension 0, may hold values from 0 to 7, as said below
- tile_cols: int32 [2816], P(('grp', 'rb')), parts along dimension 0, may hold values from 0 to 191, as said below
- tile_counts: int32 [32], P(('grp', 'rb')), parts along dimension 0, may hold values from 29 to 88, as said below
- dual_step: float32 [65536], P(('grp', 'rb')), parts along dimension 0, may hold values from 0.1 to 1
- primal_step: float32 [98304], P(('grp', 'rb')), parts along dimension 0, may hold values from 0.1 to 1
- primal_mask: int32 [4, 16, 49152], P(None, 'grp', 'rb'), parts along dimension 1, may hold values 0 or 1
- dual_mask: int32 [4, 16, 32768], P(None, 'grp', 'rb'), parts along dimension 1, may hold values 0 or 1
- cot_x: float32 [16, 49152], P('grp', 'rb'), parts along dimension 0, may hold values from -6 to 6
- cot_y: float32 [16, 32768], P('grp', 'rb'), parts along dimension 0, may hold values from -6 to 6
Outputs:
- grad_cost: float32 [16, 49152], P('grp', 'rb'), parts along dimension 0
- grad_rhs: float32 [16, 32768], P('grp', 'rb'), parts along dimension 0
- grad_primal: float32 [16, 49152], P('grp', 'rb'), parts along dimension 0
- grad_dual: float32 [16, 32768], P('grp', 'rb'), parts along dimension 0
There are 2 independent parts, one for each index of `grp`. A program takes and returns all parts, laid end to end along the dimension named above; each array names one. Nothing has to cross between parts.
Inputs may be any that keep to these rules, and one draw needn't show every extreme that they name: `tile_rows`: row block within its device's 8 row blocks. `tile_cols`: the owner of column block j is device j // 12; among the tiles of one device at most 6 have column blocks of one owner, and every device has 6 such tiles for some owner. A device's live tiles are the first tile_counts entries of its lists; some device has all 88 live in every draw.
All inputs are finite; a program needn't handle non-finite values. No bound on the sum of `primal_mask` or of `dual_mask` on one device may be relied on, other than what follows from the above.
Results may differ from a plain program's by a relative error of at most 0.008.
Values may be sent and summed in bfloat16 or wider, within the bound.
No kernel may reach another device: no remote copies, remote signals or barrier semaphores. Data moves between devices by JAX's collectives and lax.ppermute only.
A program may use at most 64 MiB of HBM per device.

v0:
```python
import jax
import jax.numpy as jnp
from jax import lax
from jax.sharding import PartitionSpec as P


def on_device(
    tiles,
    tile_rows,
    tile_cols,
    tile_counts,
    dual_step,
    primal_step,
    primal_mask,
    dual_mask,
    cot_x,
    cot_y,
):
    peers = lax.axis_size("rb")
    position = lax.axis_index("rb")
    tile_slots = tiles.shape[0]
    side = tiles.shape[1]
    row_blocks = dual_step.shape[0] // side
    col_blocks = primal_step.shape[0] // side
    capacity = max(2, (tile_slots + peers - 1) // peers)
    slots = peers * capacity
    everyone_cols, everyone_counts = (
        lax.all_gather(tile_cols, "rb", axis=0, tiled=True),
        lax.all_gather(tile_counts, "rb", axis=0, tiled=True),
    )
    everyone_cols = everyone_cols.reshape(peers, tile_slots)
    tile_order = jnp.arange(tile_slots, dtype=jnp.int32)
    live = tile_order < tile_counts[0]
    own_owner = tile_cols // col_blocks
    same = (own_owner[:, None] == own_owner[None, :]) & (tile_order[None, :] < tile_order[:, None])
    rank = jnp.sum(same.astype(jnp.int32), axis=1)
    slot = own_owner * capacity + rank
    send_map = (
        (slot[:, None] == jnp.arange(slots, dtype=jnp.int32)[None, :]) & live[:, None]
    ).astype(jnp.bfloat16)
    row_hot = (tile_rows[:, None] == jnp.arange(row_blocks, dtype=jnp.int32)[None, :]) & live[
        :, None
    ]
    row_map = row_hot.astype(jnp.bfloat16)
    row_sum = row_hot.astype(jnp.float32)
    everyone_live = tile_order[None, :] < everyone_counts[:, None]
    to_me = (everyone_cols // col_blocks == position) & everyone_live
    mine = to_me.astype(jnp.int32)
    arrival = jnp.cumsum(mine, axis=1) - mine
    local_column = everyone_cols - position * col_blocks
    column_hot = (
        local_column[:, :, None] == jnp.arange(col_blocks, dtype=jnp.int32)[None, None, :]
    ) & to_me[:, :, None]
    rank_hot = arrival[:, :, None] == jnp.arange(capacity, dtype=jnp.int32)[None, None, :]
    receive_map = jnp.einsum(
        "stc,str->csr", column_hot.astype(jnp.float32), rank_hot.astype(jnp.float32)
    )
    receive_map = receive_map.reshape(col_blocks, slots).astype(jnp.bfloat16)
    batch = cot_x.shape[0]
    bounds = [(0, batch)]
    state_x = [cot_x for first, finish in bounds]
    state_y = [cot_y for first, finish in bounds]
    cost_parts = [jnp.zeros_like(state) for state in state_x]
    rhs_parts = [jnp.zeros_like(state) for state in state_y]
    for step in reversed(range(primal_mask.shape[0])):
        for piece, (first, finish) in enumerate(bounds):
            dual_part = dual_mask[step, first:finish].astype(jnp.float32) * state_y[piece]
            scaled = dual_step[None, :] * dual_part
            scaled_bf = scaled.astype(jnp.bfloat16)
            transpose_width = scaled_bf.shape[0]
            transpose_blocks = scaled_bf.reshape(transpose_width, row_blocks, side)
            picked = jnp.einsum(
                "tr,brk->tbk", row_map, transpose_blocks, preferred_element_type=jnp.float32
            ).astype(jnp.bfloat16)
            transpose_outgoing = jnp.einsum(
                "ts,tbj->sbj",
                send_map,
                jnp.einsum(
                    "tbi,tij->tbj", picked, tiles, preferred_element_type=jnp.float32
                ).astype(jnp.bfloat16),
                preferred_element_type=jnp.float32,
            )
            transpose_arrived = lax.all_to_all(
                transpose_outgoing.astype(jnp.bfloat16),
                "rb",
                split_axis=0,
                concat_axis=0,
                tiled=True,
            )
            transpose_total = jnp.einsum(
                "cs,sbj->bcj", receive_map, transpose_arrived, preferred_element_type=jnp.float32
            )
            back = transpose_total.reshape(transpose_width, col_blocks * side)
            primal_part = primal_mask[step, first:finish].astype(jnp.float32) * (
                state_x[piece] + 2.0 * back
            )
            moved = primal_step[None, :] * primal_part
            state_x[piece] = primal_part - back
            moved_bf = moved.astype(jnp.bfloat16)
            width = moved_bf.shape[0]
            blocks = moved_bf.reshape(width, col_blocks, side)
            outgoing = jnp.einsum(
                "cs,bcj->sbj", receive_map, blocks, preferred_element_type=jnp.float32
            ).astype(jnp.bfloat16)
            arrived = lax.all_to_all(outgoing, "rb", split_axis=0, concat_axis=0, tiled=True)
            products_picked = jnp.einsum(
                "ts,sbj->tbj", send_map, arrived, preferred_element_type=jnp.float32
            ).astype(jnp.bfloat16)
            product = jnp.einsum(
                "tbj,tij->tbi", products_picked, tiles, preferred_element_type=jnp.float32
            )
            total = jnp.einsum("tr,tbi->bri", row_sum, product, precision=lax.Precision.HIGHEST)
            state_y[piece] = dual_part - total.reshape(width, row_blocks * side)
            cost_parts[piece] = cost_parts[piece] - moved
            rhs_parts[piece] = rhs_parts[piece] - scaled
    grad_cost = cost_parts[0]
    grad_rhs = rhs_parts[0]
    grad_primal = state_x[0]
    grad_dual = state_y[0]
    return (grad_cost, grad_rhs, grad_primal, grad_dual)


def solution(mesh):
    return jax.shard_map(
        on_device,
        mesh=mesh,
        in_specs=(
            P(("grp", "rb"), None, None),
            P(("grp", "rb")),
            P(("grp", "rb")),
            P(("grp", "rb")),
            P(("grp", "rb")),
            P(("grp", "rb")),
            P(None, "grp", "rb"),
            P(None, "grp", "rb"),
            P("grp", "rb"),
            P("grp", "rb"),
        ),
        out_specs=(P("grp", "rb"), P("grp", "rb"), P("grp", "rb"), P("grp", "rb")),
        check_vma=False,
    )
```

profile of v0, /device:TPU:0, one launch (start us, length us, event | category | flops | bytes accessed | tf_op | source)
XLA Modules:
  0.0 185.2 jit_solution(14350017144080098969)
XLA Ops:
  2.8 0.9 multiply_convert_fusion.7
  3.7 0.9 convolution_convert_fusion.19
  4.7 5.9 %convolution_convert_fusion.18 = bf16[88,8,256]{2,1,0:T(8,128)(2,1)S(1)} fusion(bf16[88,256,256]{2,1,0:T(8,128)(2,1)} %param.10, bf16[88,8,256]{2,0,1:T(8,128)(2,1)S(1)} %convolution_convert_fusion.19), kind=kOutput, calls=%fused_computation.18 | convolution fusion | flops 92454912 | bytes 12255232 | tf_op jit(solution)/shard_map/tbi,tij->tbj/dot_general | solution.py:78
  11.1 1.0 copy.96
  12.1 7.4 %all-to-all-start = ((bf16[96,8,256]{2,1,0:T(8,128)(2,1)}), bf16[96,8,256]{2,1,0:T(8,128)(2,1)S(1)}, u32[]{:S(2)}, u32[]{:S(2)}) async-start(bf16[96,8,256]{2,1,0:T(8,128)(2,1)} %copy.96), calls=%async_computation | async-start | bytes 786432 | tf_op jit(solution)/shard_map/all_to_all | solution.py:83
  20.7 0.8 dynamic-update-slice.1
  21.7 12.8 %all-reduce.2 = (s32[1408]{0:T(1024)S(1)}, s32[16]{0:T(128)S(1)}) all-reduce(s32[1408]{0:T(1024)S(1)} %dynamic-update-slice, s32[16]{0:T(128)S(1)} %dynamic-update-slice.1), channel_id=1, replica_groups=mesh['grp'=2,'rb'=16] {'rb'}, use_global_device_ids=true, to_apply=%add | all-reduce | flops 1424 | bytes 11392
  36.2 14.8 %all_to_all.40 = bf16[96,8,256]{2,1,0:T(8,128)(2,1)S(1)} all-to-all(bf16[96,8,256]{2,1,0:T(8,128)(2,1)S(1)} %copy.100), channel_id=1, replica_groups=mesh['grp'=2,'rb'=16] {'rb'}, dimensions={0} | all-to-all | bytes 786432 | tf_op jit(solution)/shard_map/all_to_all | solution.py:105
  51.3 7.3 %fusion.25 = f32[88,8,256]{2,1,0:T(8,128)S(1)} fusion(bf16[88,256,256]{2,1,0:T(8,128)(2,1)} %param.10, bf16[88,8,256]{2,0,1:T(8,128)(2,1)S(1)} %convolution_convert_fusion.17), kind=kOutput, calls=%fused_computation.54 | convolution fusion | flops 92274688 | bytes 12615680 | tf_op jit(solution)/shard_map/tbj,tij->tbi/dot_general | solution.py:109
  59.6 6.0 %convolution_convert_fusion.15 = bf16[88,8,256]{2,1,0:T(8,128)(2,1)S(1)} fusion(bf16[88,256,256]{2,1,0:T(8,128)(2,1)} %param.10, bf16[88,8,256]{2,0,1:T(8,128)(2,1)S(1)} %convolution_convert_fusion.16), kind=kOutput, calls=%fused_computation.15 | convolution fusion | flops 92454912 | bytes 12255232 | tf_op jit(solution)/shard_map/tbi,tij->tbj/dot_general | solution.py:78
  66.3 15.5 %all_to_all.41 = bf16[96,8,256]{2,1,0:T(8,128)(2,1)S(1)} all-to-all(bf16[96,8,256]{2,1,0:T(8,128)(2,1)S(1)} %copy.107), channel_id=1, replica_groups=mesh['grp'=2,'rb'=16] {'rb'}, dimensions={0} | all-to-all | bytes 786432 | tf_op jit(solution)/shard_map/all_to_all | solution.py:83
  82.6 15.5 %all_to_all.42 = bf16[96,8,256]{2,1,0:T(8,128)(2,1)S(1)} all-to-all(bf16[96,8,256]{2,1,0:T(8,128)(2,1)S(1)} %copy.110), channel_id=1, replica_groups=mesh['grp'=2,'rb'=16] {'rb'}, dimensions={0} | all-to-all | bytes 786432 | tf_op jit(solution)/shard_map/all_to_all | solution.py:105
  98.4 3.1 %fusion.21 = f32[88,8,256]{2,1,0:T(8,128)S(1)} fusion(bf16[88,256,256]{2,1,0:T(8,128)(2,1)S(1)} %bitcast.132, bf16[88,8,256]{2,0,1:T(8,128)(2,1)S(1)} %convolution_convert_fusion.14), kind=kOutput, calls=%fused_computation.50 | convolution fusion | flops 92274688 | bytes 12615680 | tf_op jit(solution)/shard_map/tbj,tij->tbi/dot_general | solution.py:109
  102.4 1.6 convolution_convert_fusion.12
  104.6 15.5 %all_to_all.43 = bf16[96,8,256]{2,1,0:T(8,128)(2,1)S(1)} all-to-all(bf16[96,8,256]{2,1,0:T(8,128)(2,1)S(1)} %copy.117), channel_id=1, replica_groups=mesh['grp'=2,'rb'=16] {'rb'}, dimensions={0} | all-to-all | bytes 786432 | tf_op jit(solution)/shard_map/all_to_all | solution.py:83
  120.9 15.5 %all_to_all.44 = bf16[96,8,256]{2,1,0:T(8,128)(2,1)S(1)} all-to-all(bf16[96,8,256]{2,1,0:T(8,128)(2,1)S(1)} %copy.120), channel_id=1, replica_groups=mesh['grp'=2,'rb'=16] {'rb'}, dimensions={0} | all-to-all | bytes 786432 | tf_op jit(solution)/shard_map/all_to_all | solution.py:105
  136.8 3.1 %fusion.17 = f32[88,8,256]{2,1,0:T(8,128)S(1)} fusion(bf16[88,256,256]{2,1,0:T(8,128)(2,1)S(1)} %bitcast.132, bf16[88,8,256]{2,0,1:T(8,128)(2,1)S(1)} %convolution_convert_fusion.11), kind=kOutput, calls=%fused_computation.46 | convolution fusion | flops 92274688 | bytes 12615680 | tf_op jit(solution)/shard_map/tbj,tij->tbi/dot_general | solution.py:109
  141.4 1.6 convolution_convert_fusion.9
  143.6 15.5 %all_to_all.45 = bf16[96,8,256]{2,1,0:T(8,128)(2,1)S(1)} all-to-all(bf16[96,8,256]{2,1,0:T(8,128)(2,1)S(1)} %copy.127), channel_id=1, replica_groups=mesh['grp'=2,'rb'=16] {'rb'}, dimensions={0} | all-to-all | bytes 786432 | tf_op jit(solution)/shard_map/all_to_all | solution.py:83
  159.7 1.0 copy.130
  160.7 3.6 %all-to-all-start.7 = ((bf16[96,8,256]{2,1,0:T(8,128)(2,1)}), bf16[96,8,256]{2,1,0:T(8,128)(2,1)S(1)}, u32[]{:S(2)}, u32[]{:S(2)}) async-start(bf16[96,8,256]{2,1,0:T(8,128)(2,1)} %copy.130), calls=%async_computation.7 | async-start | bytes 786432 | tf_op jit(solution)/shard_map/all_to_all | solution.py:105
  164.2 0.7 fusion.76
  164.9 11.5 %all-to-all-done.7 = bf16[96,8,256]{2,1,0:T(8,128)(2,1)S(1)} async-done(((bf16[96,8,256]{2,1,0:T(8,128)(2,1)}), bf16[96,8,256]{2,1,0:T(8,128)(2,1)S(1)}, u32[]{:S(2)}, u32[]{:S(2)}) %all-to-all-start.7) | async-done | bytes 393248 | tf_op jit(solution)/shard_map/all_to_all | solution.py:105
  176.7 7.3 %fusion.13 = f32[88,8,256]{2,1,0:T(8,128)S(1)} fusion(bf16[88,256,256]{2,1,0:T(8,128)(2,1)} %param.10, bf16[88,8,256]{2,0,1:T(8,128)(2,1)S(1)} %convolution_convert_fusion.8), kind=kOutput, calls=%fused_computation.42 | convolution fusion | flops 92274688 | bytes 12615680 | tf_op jit(solution)/shard_map/tbj,tij->tbi/dot_general | solution.py:109
  (90 shorter events, 14.1 us)
Async XLA Ops:
  4.7 14.8 %copy-start.8 = (u32[32]{0:T(128)S(1)}, u32[32]{0:T(128)}, u32[]{:S(2)}) copy-start(u32[32]{0:T(128)} %constant.37) | copy-start | bytes 388
  4.7 16.8 %copy-start.7 = (s32[88]{0:T(128)S(1)}, s32[88]{0:T(128)}, u32[]{:S(2)}) copy-start(s32[88]{0:T(128)} %param.12) | copy-start | bytes 1060
  4.7 31.0 %copy-start.2 = (s32[4,8,3072]{2,1,0:T(8,128)S(1)}, s32[4,8,3072]{2,1,0:T(8,128)}, u32[]{:S(2)}) copy-start(s32[4,8,3072]{2,1,0:T(8,128)} %param.16) | copy-start | bytes 1179652
  4.7 31.0 %copy-start.3 = (f32[3072]{0:T(1024)S(1)}, f32[3072]{0:T(1024)}, u32[]{:S(2)}) copy-start(f32[3072]{0:T(1024)} %param.15) | copy-start | bytes 36868
  4.7 31.0 %copy-start.5 = (f32[8,3072]{1,0:T(8,128)S(1)}, f32[8,3072]{1,0:T(8,128)}, u32[]{:S(2)}) copy-start(f32[8,3072]{1,0:T(8,128)} %param.18) | copy-start | bytes 294916
  10.7 48.0 %copy-start.6 = (s32[88]{0:T(128)S(1)}, s32[88]{0:T(128)}, u32[]{:S(2)}) copy-start(s32[88]{0:T(128)} %param.11) | copy-start | bytes 1060
  10.7 48.6 %copy-start = (s32[4,8,2048]{2,1,0:T(8,128)S(1)}, s32[4,8,2048]{2,1,0:T(8,128)}, u32[]{:S(2)}) copy-start(s32[4,8,2048]{2,1,0:T(8,128)} %param.17) | copy-start | bytes 786436
  10.7 48.6 %copy-start.1 = (f32[8,2048]{1,0:T(8,128)S(1)}, f32[8,2048]{1,0:T(8,128)}, u32[]{:S(2)}) copy-start(f32[8,2048]{1,0:T(8,128)} %param.19) | copy-start | bytes 196612
  10.7 48.6 %copy-start.4 = (f32[2048]{0:T(1024)S(1)}, f32[2048]{0:T(1024)}, u32[]{:S(2)}) copy-start(f32[2048]{0:T(1024)} %param.14) | copy-start | bytes 24580
  12.1 23.3 %all-to-all-start = ((bf16[96,8,256]{2,1,0:T(8,128)(2,1)}), bf16[96,8,256]{2,1,0:T(8,128)(2,1)S(1)}, u32[]{:S(2)}, u32[]{:S(2)}) async-start(bf16[96,8,256]{2,1,0:T(8,128)(2,1)} %copy.96), calls=%async_computation | async-start | bytes 786432 | tf_op jit(solution)/shard_map/all_to_all | solution.py:83
  59.3 39.1 %slice-start = ((s8[11534336]{0:T(1024)(128)(4,1)}), s8[4194304]{0:T(1024)(128)(4,1)S(1)}, s32[]{:S(2)}) async-start(s8[11534336]{0:T(1024)(128)(4,1)} %bitcast.131), calls=%async_computation.8 | async-start | bytes 8388608
  59.6 38.8 %slice-start.1 = ((s8[11534336]{0:T(1024)(128)(4,1)}), s8[4194304]{0:T(1024)(128)(4,1)S(1)}, s32[]{:S(2)}) async-start(s8[11534336]{0:T(1024)(128)(4,1)} %bitcast.131), calls=%async_computation.9 | async-start | bytes 8388608
  59.6 38.8 %slice-start.2 = ((s8[11534336]{0:T(1024)(128)(4,1)}), s8[3145728]{0:T(1024)(128)(4,1)S(1)}, s32[]{:S(2)}) async-start(s8[11534336]{0:T(1024)(128)(4,1)} %bitcast.131), calls=%async_computation.10 | async-start | bytes 6291456
  160.7 15.7 %all-to-all-start.7 = ((bf16[96,8,256]{2,1,0:T(8,128)(2,1)}), bf16[96,8,256]{2,1,0:T(8,128)(2,1)S(1)}, u32[]{:S(2)}, u32[]{:S(2)}) async-start(bf16[96,8,256]{2,1,0:T(8,128)(2,1)} %copy.130), calls=%async_computation.7 | async-start | bytes 786432 | tf_op jit(solution)/shard_map/all_to_all | solution.py:105
where the time goes:
time: 186 us; the launch traced here: 185 us
  blocking collectives  105 us (56%)
  matrix products  44.6 us (24%)
  waiting for transfers between devices  11.5 us (6%)
  starting transfers between devices  10.9 us (6%)
  local copies, waits for them, and re-layouts  5.62 us (3%)
  other arithmetic  5.01 us (3%)
  between operations  2.43 us (1%)
    all_to_all x3, blocking collectives, on_device(): lax.all_to_all(transpose_outgoing.astype(jnp.bfloat16), 'rb', split_axis=...  46.5 us
    all_to_all x3, blocking collectives, on_device(): lax.all_to_all(outgoing, 'rb', split_axis=0, concat_axis=0, tiled=True)  45.8 us
    dot_general x4, matrix products, on_device(): jnp.einsum('tbj,tij->tbi', products_picked, tiles, preferred_element_type...  20.8 us
    dot_general x4, matrix products, on_device(): jnp.einsum('tbi,tij->tbj', picked, tiles, preferred_element_type=jnp.floa...  15.2 us
    unnamed x1, blocking collectives  12.8 us
    all_to_all x1, waiting for transfers between devices, on_device(): lax.all_to_all(outgoing, 'rb', split_axis=0, concat_axis=0, tiled=True)  11.5 us
    all_to_all x1, starting transfers between devices, on_device(): lax.all_to_all(transpose_outgoing.astype(jnp.bfloat16), 'rb', split_axis=...  7.38 us
  transfers between devices with their start and end apart: 2, of which 1 were waited for; matrix products, arithmetic and copies ran while one was open for 2% of the time, Pallas kernels for 0%

commit v1 on v0

v1 whole, which is shorter than its diff:
```python
import functools

import jax
import jax.numpy as jnp
from jax import lax
from jax.experimental import pallas as pl
from jax.experimental.pallas import tpu as pltpu
from jax.sharding import PartitionSpec as P

QUAD = 4
CHUNK = 8
VM = pl.BlockSpec(memory_space=pltpu.VMEM)
SM = pl.BlockSpec(memory_space=pltpu.SMEM)
ANY = pl.BlockSpec(memory_space=pl.ANY)
PARAMS = pltpu.CompilerParams(vmem_limit_bytes=20 * 1024 * 1024)


def shape(dims, dtype):
    return jax.ShapeDtypeStruct(dims, dtype)


def dual_update(step, side, dy, dual_mask, dual_step, hb, h_into):
    for r in range(hb.shape[0]):
        at = pl.ds(r * side, side)
        h = dual_step[:, at] * dy[:, at]
        hb[r] = h.astype(jnp.bfloat16)
        h_into(at, h)


def transpose_products(first, count, tiles, rows, slots, hb, staged):
    for j in range(count):
        t = first + j
        term = jnp.dot(hb[rows[t]], tiles[t], preferred_element_type=jnp.float32)
        staged[slots[t]] = term.astype(jnp.bfloat16)


def spread(staged, outs):
    for x, out in enumerate(outs):
        for s in range(out.shape[0]):
            out[s] = staged[x * out.shape[0] + s]


def start_kernel(step, peers, cap, col_blocks, place, rows, cols, count, tiles, dual_step, dual_mask, cot_y,
                 held, dy, rhs, slots, lands, wants, o0, o1, o2, o3, hb, staged, filled, sems):
    side = tiles.shape[1]
    tile_slots = tiles.shape[0]
    group = peers // QUAD
    per = group * cap
    chunks = tile_slots // CHUNK
    copies = [
        pltpu.make_async_copy(tiles.at[pl.ds(c * CHUNK, CHUNK)], held.at[pl.ds(c * CHUNK, CHUNK)], sems.at[c])
        for c in range(chunks)
    ]
    for copy in copies:
        copy.start()
    dy[...] = dual_mask[step].astype(jnp.float32) * cot_y[...]

    def h_into(at, h):
        rhs[:, at] = -h

    dual_update(step, side, dy, dual_mask, dual_step, hb, h_into)
    me = place[0]
    my_high, my_quad = me // QUAD, me % QUAD
    for x in range(QUAD):
        for s in range(per):
            wants[x, s] = group * col_blocks

    def clear(o, _):
        filled[o] = 0
        return 0

    lax.fori_loop(0, peers, clear, 0)

    def place_tile(t, _):
        col = cols[t]
        owner = col // col_blocks
        live = t < count[0]
        rank = filled[owner]
        high, quad = (owner // QUAD) ^ my_high, (owner % QUAD) ^ my_quad
        within = high * cap + rank
        slots[t] = jnp.where(live, quad * per + within, QUAD * per)
        lands[t] = jnp.where(live, rows[t], hb.shape[0])

        @pl.when(live)
        def _():
            filled[owner] = rank + 1
            wants[quad, within] = high * col_blocks + (col - owner * col_blocks)

        return 0

    lax.fori_loop(0, tile_slots, place_tile, 0)

    def one_chunk(c, _):
        pltpu.make_async_copy(tiles.at[pl.ds(c * CHUNK, CHUNK)], held.at[pl.ds(c * CHUNK, CHUNK)], sems.at[c]).wait()
        transpose_products(c * CHUNK, CHUNK, held, rows, slots, hb, staged)
        return 0

    lax.fori_loop(0, chunks, one_chunk, 0)
    spread(staged, (o0, o1, o2, o3))


def sum_kernel(wants, got1, got2, got3, a0, a1, a2, a3, *rest):
    total = rest[-1]
    outs = rest[:-1]
    total[...] = jnp.zeros_like(total)
    for x, (want, part) in enumerate(((None, a0), (got1, a1), (got2, a2), (got3, a3))):
        for s in range(part.shape[0]):
            c = wants[0, s] if x == 0 else want[x, s]
            total[c] = total[c] + part[s].astype(jnp.float32)
    blocks = outs[0].shape[0]
    for high, out in enumerate(outs):
        for c in range(blocks):
            out[c] = total[high * blocks + c].astype(out.dtype)


def primal_kernel(step, first, primal_mask, primal_step, x, cost, *refs):
    parts, (new_x, new_cost, q_out) = refs[:-3], refs[-3:]
    blocks, _, side = q_out.shape
    for c in range(blocks):
        at = pl.ds(c * side, side)
        u = parts[0][c]
        for part in parts[1:]:
            u = u + part[c].astype(jnp.float32)
        dx = primal_mask[step, :, at].astype(jnp.float32) * (x[:, at] + 2.0 * u)
        q = primal_step[:, at] * dx
        new_x[:, at] = dx - u
        new_cost[:, at] = -q if first else cost[:, at] - q
        q_out[c] = q.astype(jnp.bfloat16)


def forward_products(tiles, lands, cols, moved, total):
    total[...] = jnp.zeros_like(total)

    def one_chunk(c, _):
        for j in range(CHUNK):
            t = c * CHUNK + j
            product = lax.dot_general(
                moved[cols[t]], tiles[t], (((1,), (1,)), ((), ())), preferred_element_type=jnp.float32
            )
            r = lands[t]
            total[r] = total[r] + product
        return 0

    lax.fori_loop(0, tiles.shape[0] // CHUNK, one_chunk, 0)


def middle_kernel(step, rows, lands, cols, slots, tiles, dual_step, dual_mask, moved, dy, rhs,
                  new_dy, new_rhs, o0, o1, o2, o3, total, hb, staged):
    side = tiles.shape[1]
    forward_products(tiles, lands, cols, moved, total)
    for r in range(total.shape[0] - 1):
        at = pl.ds(r * side, side)
        new_dy[:, at] = dual_mask[step, :, at].astype(jnp.float32) * (dy[:, at] - total[r])

    def h_into(at, h):
        new_rhs[:, at] = rhs[:, at] - h

    dual_update(step, side, new_dy, dual_mask, dual_step, hb, h_into)

    def one_chunk(c, _):
        transpose_products(c * CHUNK, CHUNK, tiles, rows, slots, hb, staged)
        return 0

    lax.fori_loop(0, tiles.shape[0] // CHUNK, one_chunk, 0)
    spread(staged, (o0, o1, o2, o3))


def last_kernel(lands, cols, tiles, moved, dy, new_y, total):
    side = tiles.shape[1]
    forward_products(tiles, lands, cols, moved, total)
    for r in range(total.shape[0] - 1):
        at = pl.ds(r * side, side)
        new_y[:, at] = dy[:, at] - total[r]


def on_device(tiles, tile_rows, tile_cols, tile_counts, dual_step, primal_step, primal_mask, dual_mask, cot_x, cot_y):
    peers = lax.axis_size("rb")
    me = lax.axis_index("rb").astype(jnp.int32)
    tile_slots, side, _ = tiles.shape
    batch = cot_x.shape[0]
    row_blocks = dual_step.shape[0] // side
    col_blocks = primal_step.shape[0] // side
    cap = max(2, (tile_slots + peers - 1) // peers)
    group = peers // QUAD
    per = group * cap
    steps = primal_mask.shape[0]
    dual_step = dual_step.reshape(1, -1)
    primal_step = primal_step.reshape(1, -1)
    f32, bf16 = jnp.float32, jnp.bfloat16
    y_shape = shape(cot_y.shape, f32)
    x_shape = shape(cot_x.shape, f32)
    out_part = shape((per, batch, side), bf16)
    block_set = shape((col_blocks, batch, side), bf16)
    hb_scratch = pltpu.VMEM((row_blocks, batch, side), bf16)
    staged_scratch = pltpu.VMEM((QUAD * per + 1, batch, side), bf16)
    row_total = pltpu.VMEM((row_blocks + 1, batch, side), f32)

    def near(x):
        return [(p, p ^ x) for p in range(peers)]

    def far(x):
        return [(p, p ^ (x * QUAD)) for p in range(peers)]

    step = steps - 1
    held, dy, rhs, slots, lands, wants, *outs = pl.pallas_call(
        functools.partial(start_kernel, step, peers, cap, col_blocks),
        out_shape=(
            pltpu.VMEM(tiles.shape, bf16), y_shape, y_shape, shape((tile_slots,), jnp.int32), shape((tile_slots,), jnp.int32),
            shape((QUAD, per), jnp.int32), out_part, out_part, out_part, out_part,
        ),
        in_specs=[SM, SM, SM, SM, ANY, VM, VM, VM],
        out_specs=(VM, VM, VM, SM, SM, SM, VM, VM, VM, VM),
        scratch_shapes=[hb_scratch, staged_scratch, pltpu.SMEM((peers,), jnp.int32),
                        pltpu.SemaphoreType.DMA((tile_slots // CHUNK,))],
        compiler_params=PARAMS,
        name="start",
    )(me.reshape(1), tile_rows, tile_cols, tile_counts, tiles, dual_step, dual_mask, cot_y)
    got_wants = [lax.ppermute(wants, "rb", near(x)) for x in range(1, QUAD)]
    x_state, cost = cot_x, cot_x
    while True:
        parts = [outs[0]] + [lax.ppermute(outs[x], "rb", near(x)) for x in range(1, QUAD)]
        sums = pl.pallas_call(
            sum_kernel,
            out_shape=(shape(block_set.shape, f32),) + (block_set,) * (group - 1),
            in_specs=[SM] * 4 + [VM] * 4,
            out_specs=(VM,) * group,
            scratch_shapes=[pltpu.VMEM((group * col_blocks + 1, batch, side), f32)],
            compiler_params=PARAMS,
            name="quad_sum",
        )(wants, *got_wants, *parts)
        parts = [sums[0]] + [lax.ppermute(sums[x], "rb", far(x)) for x in range(1, group)]
        x_state, cost, moved = pl.pallas_call(
            functools.partial(primal_kernel, step, step == steps - 1),
            out_shape=(x_shape, x_shape, block_set),
            in_specs=[VM] * (4 + group),
            out_specs=(VM,) * 3,
            compiler_params=PARAMS,
            name="primal",
        )(primal_mask, primal_step, x_state, cost, *parts)
        moved = lax.all_gather(moved, "rb", axis=0, tiled=True)
        if step == 0:
            break
        step -= 1
        dy, rhs, *outs = pl.pallas_call(
            functools.partial(middle_kernel, step),
            out_shape=(y_shape, y_shape, out_part, out_part, out_part, out_part),
            in_specs=[SM] * 4 + [VM] * 6,
            out_specs=(VM,) * 6,
            scratch_shapes=[row_total, hb_scratch, staged_scratch],
            compiler_params=PARAMS,
            name="middle",
        )(tile_rows, lands, tile_cols, slots, held, dual_step, dual_mask, moved, dy, rhs)
    y_state = pl.pallas_call(
        last_kernel,
        out_shape=y_shape,
        in_specs=[SM] * 2 + [VM] * 3,
        out_specs=VM,
        scratch_shapes=[row_total],
        compiler_params=PARAMS,
        name="last",
    )(lands, tile_cols, held, moved, dy)
    return cost, rhs, x_state, y_state


def solution(mesh):
    rb = ("grp", "rb")
    return jax.shard_map(
        on_device,
        mesh=mesh,
        in_specs=(
            P(rb, None, None), P(rb), P(rb), P(rb), P(rb), P(rb),
            P(None, "grp", "rb"), P(None, "grp", "rb"), P("grp", "rb"), P("grp", "rb"),
        ),
        out_specs=(P("grp", "rb"),) * 4,
        check_vma=False,
    )
```

time: 186 us -> 203 us (1.091)
  matrix products: 44.6 us -> 0 us
  Pallas kernels: 0 us -> 42 us
  waiting for transfers between devices: 11.5 us -> 34.1 us
  starting transfers between devices: 10.9 us -> 28.6 us
  blocking collectives: 105 us -> 88.1 us
  other arithmetic: 5.01 us -> 0 us
  local copies, waits for them, and re-layouts: 5.62 us -> 8.09 us
    all_to_all x6 -> x0, blocking collectives: 92.3 us -> none  [the longest x3 46.5 us: on_device(): lax.all_to_all(transpose_outgoing.astype(jnp.bfloat16), 'rb', split_axis=...]
    all_gather x0 -> x4, blocking collectives: none -> 88.1 us  [on_device(): moved = lax.all_gather(moved, 'rb', axis=0, tiled=True)]
    dot_general x33 -> x0, matrix products: 44.6 us -> none  [the longest x4 20.8 us: on_device(): jnp.einsum('tbj,tij->tbi', products_picked, tiles, preferred_element_type...]
    pallas_call x0 -> x13, Pallas kernels: none -> 42 us  [the longest x3 23.6 us: on_device(): pl.pallas_call(functools.partial(middle_kernel, step), out_shape=(y_shape...]
    ppermute x0 -> x27, waiting for transfers between devices: none -> 34.1 us  [the longest x12 15.6 us: on_device(): lax.ppermute(sums[x], 'rb', far(x))]
    ppermute x0 -> x27, starting transfers between devices: none -> 28.6 us  [the longest x12 17.8 us: on_device(): lax.ppermute(sums[x], 'rb', far(x))]
    unnamed x1 -> x0, blocking collectives: 12.8 us -> none
    all_to_all x2 -> x0, waiting for transfers between devices: 11.5 us -> none  [the longest x1 11.5 us: on_device(): lax.all_to_all(outgoing, 'rb', split_axis=0, concat_axis=0, tiled=True)]
  transfers between devices with their start and end apart: 2 -> 27, of which waited for: 1 -> 14; matrix products, arithmetic and copies ran while one was open for 2% -> 0% of each run, Pallas kernels for 0% -> 0%
where the time goes in v1:
time: 203 us; the launch traced here: 202 us
  blocking collectives  88.1 us (43%)
  Pallas kernels  42 us (21%)
  waiting for transfers between devices  34.1 us (17%)
  starting transfers between devices  28.6 us (14%)
  local copies, waits for them, and re-layouts  8.09 us (4%)
    all_gather x4, blocking collectives, on_device(): moved = lax.all_gather(moved, 'rb', axis=0, tiled=True)  88.1 us
    pallas_call x3, Pallas kernels, on_device(): pl.pallas_call(functools.partial(middle_kernel, step), out_shape=(y_shape...  23.6 us
    ppermute x12, starting transfers between devices, on_device(): lax.ppermute(sums[x], 'rb', far(x))  17.8 us
    ppermute x12, waiting for transfers between devices, on_device(): lax.ppermute(sums[x], 'rb', far(x))  15.6 us
    ppermute x12, waiting for transfers between devices, on_device(): lax.ppermute(outs[x], 'rb', near(x))  14.1 us
    ppermute x12, starting transfers between devices, on_device(): lax.ppermute(outs[x], 'rb', near(x))  8.89 us
    unnamed x24, local copies, waits for them, and re-layouts  8.09 us
    pallas_call x1, Pallas kernels, on_device(): pl.pallas_call(functools.partial(start_kernel, step, peers, cap, col_bloc...  7.52 us
  transfers between devices with their start and end apart: 27, of which 14 were waited for; matrix products, arithmetic and copies ran while one was open for 0% of the time, Pallas kernels for 0%

profile of v1, /device:TPU:0, one launch (start us, length us, event | category | flops | bytes accessed | tf_op | source)
XLA Modules:
  0.0 202.3 jit_solution(17817251454333472881)
XLA Ops:
  1.3 4.3 %copy-done = bf16[88,256,256]{2,1,0:T(8,128)(2,1)S(1)} copy-done((bf16[88,256,256]{2,1,0:T(8,128)(2,1)S(1)}, bf16[88,256,256]{2,1,0:T(8,128)(2,1)}, u32[]{:S(2)}) %copy-start) | copy-done | bytes 11534360
  9.4 7.5 %start.1 = (bf16[88,256,256]{2,1,0:T(8,128)(2,1)S(1)}, f32[8,2048]{1,0:T(8,128)S(1)}, f32[8,2048]{1,0:T(8,128)S(1)}, s32[88]{0:T(128)S(1)}, s32[88]{0:T(128)S(1)...) custom-call(s32[1]{0:T(128)} %bitcast.1.place, ...), custom_call_target="tpu_custom_call" | custom-call | tf_op jit(solution)/shard_map/start/pallas_call | solution.py:205
  17.4 2.6 %collective-permute-start.4 = (bf16[24,8,256]{2,1,0:T(8,128)(2,1)S(1)}, bf16[24,8,256]{2,1,0:T(8,128)(2,1)S(1)}, u32[]{:S(2)}, u32[]{:S(2)}) collective-permute-start(bf16[24,8,256]{2,1,0:T(8,128)(2,1)S(1)} %get-tuple-element.63), channel_id=1, source_target_pairs={{0,2},{1,3},{2,0},{3,1},{4,6},{5,7},{6,4},{7,5},{8,10},{9,11},{10,... | collective-permute-start | bytes 294920 | tf_op jit(solution)/shard_map/ppermute | solution.py:221
  21.9 3.4 %collective-permute-done.2.got3 = s32[4,24]{1,0:T(4,128)S(1)} collective-permute-done((s32[4,24]{1,0:T(4,128)S(1)}, s32[4,24]{1,0:T(4,128)S(1)}, u32[]{:S(2)}, u32[]{:S(2)}) %collective-permute-start.2) | collective-permute-done | bytes 416 | tf_op jit(solution)/shard_map/ppermute | solution.py:218
  29.3 2.6 %collective-permute-start.7 = (bf16[12,8,256]{2,1,0:T(8,128)(2,1)S(1)}, bf16[12,8,256]{2,1,0:T(8,128)(2,1)S(1)}, u32[]{:S(2)}, u32[]{:S(2)}) collective-permute-start(bf16[12,8,256]{2,1,0:T(8,128)(2,1)S(1)} %get-tuple-element.67), channel_id=1, source_target_pairs={{0,8},{1,9},{2,10},{3,11},{4,12},{5,13},{6,14},{7,15},{8,0},{9,1},... | collective-permute-start | bytes 147464 | tf_op jit(solution)/shard_map/ppermute | solution.py:231
  32.0 3.3 %collective-permute-done.7.refs_2_ = bf16[12,8,256]{2,1,0:T(8,128)(2,1)S(1)} collective-permute-done((bf16[12,8,256]{2,1,0:T(8,128)(2,1)S(1)}, bf16[12,8,256]{2,1,0:T(8,128)(2,1)S(1)}, u32[]{:S(2)}, u32[]{:S(2)}) %collective-permute-start.7) | collective-permute-done | bytes 49184 | tf_op jit(solution)/shard_map/ppermute | solution.py:231
  35.3 2.4 %collective-permute-done.8.refs_3_ = bf16[12,8,256]{2,1,0:T(8,128)(2,1)S(1)} collective-permute-done((bf16[12,8,256]{2,1,0:T(8,128)(2,1)S(1)}, bf16[12,8,256]{2,1,0:T(8,128)(2,1)S(1)}, u32[]{:S(2)}, u32[]{:S(2)}) %collective-permute-start.8) | collective-permute-done | bytes 49184 | tf_op jit(solution)/shard_map/ppermute | solution.py:231
  37.9 21.4 %all_gather.12.moved = bf16[192,8,256]{2,1,0:T(8,128)(2,1)S(1)} all-gather(bf16[12,8,256]{2,1,0:T(8,128)(2,1)S(1)} %get-tuple-element.74), channel_id=1, replica_groups=mesh['grp'=2,'rb'=16] {'rb'}, dimensions={0}, use_global_device_ids=true | all-gather | bytes 835584 | tf_op jit(solution)/shard_map/all_gather | solution.py:240
  59.2 7.7 %middle.3 = (f32[8,2048]{1,0:T(8,128)S(1)}, f32[8,2048]{1,0:T(8,128)S(1)}, bf16[24,8,256]{2,1,0:T(8,128)(2,1)S(1)}, bf16[24,8,256]{2,1,0:T(8,128)(2,1)S(1)}, bf1...) custom-call(s32[88]{0:T(128)S(1)} %copy-done.11, s32[88]{0:T(128)S(1)} %get-tuple-element.71.lands, ...), custom_call_target="tpu_custom_call" | custom-call | tf_op jit(solution)/shard_map/middle/pallas_call | solution.py:244
  68.9 4.1 %collective-permute-done.10.a2 = bf16[24,8,256]{2,1,0:T(8,128)(2,1)S(1)} collective-permute-done((bf16[24,8,256]{2,1,0:T(8,128)(2,1)S(1)}, bf16[24,8,256]{2,1,0:T(8,128)(2,1)S(1)}, u32[]{:S(2)}, u32[]{:S(2)}) %collective-permute-start.10) | collective-permute-done | bytes 98336 | tf_op jit(solution)/shard_map/ppermute | solution.py:221
  74.8 4.3 %collective-permute-start.14 = (bf16[12,8,256]{2,1,0:T(8,128)(2,1)S(1)}, bf16[12,8,256]{2,1,0:T(8,128)(2,1)S(1)}, u32[]{:S(2)}, u32[]{:S(2)}) collective-permute-start(bf16[12,8,256]{2,1,0:T(8,128)(2,1)S(1)} %get-tuple-element.84), channel_id=1, source_target_pairs={{0,12},{1,13},{2,14},{3,15},{4,8},{5,9},{6,10},{7,11},{8,4},{9,5},... | collective-permute-start | bytes 147464 | tf_op jit(solution)/shard_map/ppermute | solution.py:231
  79.2 3.3 %collective-permute-done.13.refs_2_ = bf16[12,8,256]{2,1,0:T(8,128)(2,1)S(1)} collective-permute-done((bf16[12,8,256]{2,1,0:T(8,128)(2,1)S(1)}, bf16[12,8,256]{2,1,0:T(8,128)(2,1)S(1)}, u32[]{:S(2)}, u32[]{:S(2)}) %collective-permute-start.13) | collective-permute-done | bytes 49184 | tf_op jit(solution)/shard_map/ppermute | solution.py:231
  82.5 22.2 %all_gather.13.moved = bf16[192,8,256]{2,1,0:T(8,128)(2,1)S(1)} all-gather(bf16[12,8,256]{2,1,0:T(8,128)(2,1)S(1)} %get-tuple-element.87), channel_id=1, replica_groups=mesh['grp'=2,'rb'=16] {'rb'}, dimensions={0}, use_global_device_ids=true | all-gather | bytes 835584 | tf_op jit(solution)/shard_map/all_gather | solution.py:240
  104.8 7.7 %middle.4 = (f32[8,2048]{1,0:T(8,128)S(1)}, f32[8,2048]{1,0:T(8,128)S(1)}, bf16[24,8,256]{2,1,0:T(8,128)(2,1)S(1)}, bf16[24,8,256]{2,1,0:T(8,128)(2,1)S(1)}, bf1...) custom-call(s32[88]{0:T(128)S(1)} %copy-done.11, s32[88]{0:T(128)S(1)} %get-tuple-element.71.lands, ...), custom_call_target="tpu_custom_call" | custom-call | tf_op jit(solution)/shard_map/middle/pallas_call | solution.py:244
  114.4 4.1 %collective-permute-done.16.a2 = bf16[24,8,256]{2,1,0:T(8,128)(2,1)S(1)} collective-permute-done((bf16[24,8,256]{2,1,0:T(8,128)(2,1)S(1)}, bf16[24,8,256]{2,1,0:T(8,128)(2,1)S(1)}, u32[]{:S(2)}, u32[]{:S(2)}) %collective-permute-start.16) | collective-permute-done | bytes 98336 | tf_op jit(solution)/shard_map/ppermute | solution.py:221
  120.4 4.3 %collective-permute-start.20 = (bf16[12,8,256]{2,1,0:T(8,128)(2,1)S(1)}, bf16[12,8,256]{2,1,0:T(8,128)(2,1)S(1)}, u32[]{:S(2)}, u32[]{:S(2)}) collective-permute-start(bf16[12,8,256]{2,1,0:T(8,128)(2,1)S(1)} %get-tuple-element.97), channel_id=1, source_target_pairs={{0,12},{1,13},{2,14},{3,15},{4,8},{5,9},{6,10},{7,11},{8,4},{9,5},... | collective-permute-start | bytes 147464 | tf_op jit(solution)/shard_map/ppermute | solution.py:231
  124.7 3.3 %collective-permute-done.19.refs_2_ = bf16[12,8,256]{2,1,0:T(8,128)(2,1)S(1)} collective-permute-done((bf16[12,8,256]{2,1,0:T(8,128)(2,1)S(1)}, bf16[12,8,256]{2,1,0:T(8,128)(2,1)S(1)}, u32[]{:S(2)}, u32[]{:S(2)}) %collective-permute-start.19) | collective-permute-done | bytes 49184 | tf_op jit(solution)/shard_map/ppermute | solution.py:231
  128.1 22.2 %all_gather.14.moved = bf16[192,8,256]{2,1,0:T(8,128)(2,1)S(1)} all-gather(bf16[12,8,256]{2,1,0:T(8,128)(2,1)S(1)} %get-tuple-element.100), channel_id=1, replica_groups=mesh['grp'=2,'rb'=16] {'rb'}, dimensions={0}, use_global_device_ids=true | all-gather | bytes 835584 | tf_op jit(solution)/shard_map/all_gather | solution.py:240
  150.3 8.1 %middle.5 = (f32[8,2048]{1,0:T(8,128)S(1)}, f32[8,2048]{1,0:T(8,128)}, bf16[24,8,256]{2,1,0:T(8,128)(2,1)S(1)}, bf16[24,8,256]{2,1,0:T(8,128)(2,1)S(1)}, bf16[24...) custom-call(s32[88]{0:T(128)S(1)} %copy-done.11, s32[88]{0:T(128)S(1)} %get-tuple-element.71.lands, ...), custom_call_target="tpu_custom_call" | custom-call | tf_op jit(solution)/shard_map/middle/pallas_call | solution.py:244
  160.3 4.1 %collective-permute-done.22.a2 = bf16[24,8,256]{2,1,0:T(8,128)(2,1)S(1)} collective-permute-done((bf16[24,8,256]{2,1,0:T(8,128)(2,1)S(1)}, bf16[24,8,256]{2,1,0:T(8,128)(2,1)S(1)}, u32[]{:S(2)}, u32[]{:S(2)}) %collective-permute-start.22) | collective-permute-done | bytes 98336 | tf_op jit(solution)/shard_map/ppermute | solution.py:221
  166.2 4.3 %collective-permute-start.26 = (bf16[12,8,256]{2,1,0:T(8,128)(2,1)S(1)}, bf16[12,8,256]{2,1,0:T(8,128)(2,1)S(1)}, u32[]{:S(2)}, u32[]{:S(2)}) collective-permute-start(bf16[12,8,256]{2,1,0:T(8,128)(2,1)S(1)} %get-tuple-element.110), channel_id=1, source_target_pairs={{0,12},{1,13},{2,14},{3,15},{4,8},{5,9},{6,10},{7,11},{8,4},{9,5},... | collective-permute-start | bytes 147464 | tf_op jit(solution)/shard_map/ppermute | solution.py:231
  170.5 3.3 %collective-permute-done.25.refs_2_ = bf16[12,8,256]{2,1,0:T(8,128)(2,1)S(1)} collective-permute-done((bf16[12,8,256]{2,1,0:T(8,128)(2,1)S(1)}, bf16[12,8,256]{2,1,0:T(8,128)(2,1)S(1)}, u32[]{:S(2)}, u32[]{:S(2)}) %collective-permute-start.25) | collective-permute-done | bytes 49184 | tf_op jit(solution)/shard_map/ppermute | solution.py:231
  174.6 22.2 %all_gather.15.moved = bf16[192,8,256]{2,1,0:T(8,128)(2,1)S(1)} all-gather(bf16[12,8,256]{2,1,0:T(8,128)(2,1)S(1)} %get-tuple-element.114), channel_id=1, replica_groups=mesh['grp'=2,'rb'=16] {'rb'}, dimensions={0}, use_global_device_ids=true | all-gather | bytes 835584 | tf_op jit(solution)/shard_map/all_gather | solution.py:240
  196.8 5.5 %last.1 = f32[8,2048]{1,0:T(8,128)} custom-call(s32[88]{0:T(128)S(1)} %get-tuple-element.71.lands, s32[88]{0:T(128)S(1)} %copy-done.9, bf16[88,256,256]{2,1,0:T(8,128)(2,1)S(1)} %get-tuple-element.73.tiles, bf16[192,8,256]{2,1,0:T(8,128)(2,1)S(1)} %all_gather.15.moved, f32[8,2048]{1,0:T(8,128)S(1)} %get-tuple-element.115.dy), custom_call_target="tpu_custom_call" | custom-call | tf_op jit(solution)/shard_map/last/pallas_call | solution.py:253
  (71 shorter events, 22.4 us)
Async XLA Ops:
  16.9 9.5 %collective-permute-start.3 = (bf16[24,8,256]{2,1,0:T(8,128)(2,1)S(1)}, bf16[24,8,256]{2,1,0:T(8,128)(2,1)S(1)}, u32[]{:S(2)}, u32[]{:S(2)}) collective-permute-start(bf16[24,8,256]{2,1,0:T(8,128)(2,1)S(1)} %get-tuple-element.62), channel_id=1, source_target_pairs={{0,1},{1,0},{2,3},{3,2},{4,5},{5,4},{6,7},{7,6},{8,9},{9,8},{10,11... | collective-permute-start | bytes 294920 | tf_op jit(solution)/shard_map/ppermute | solution.py:221
  17.4 9.0 %collective-permute-start.4 = (bf16[24,8,256]{2,1,0:T(8,128)(2,1)S(1)}, bf16[24,8,256]{2,1,0:T(8,128)(2,1)S(1)}, u32[]{:S(2)}, u32[]{:S(2)}) collective-permute-start(bf16[24,8,256]{2,1,0:T(8,128)(2,1)S(1)} %get-tuple-element.63), channel_id=1, source_target_pairs={{0,2},{1,3},{2,0},{3,1},{4,6},{5,7},{6,4},{7,5},{8,10},{9,11},{10,... | collective-permute-start | bytes 294920 | tf_op jit(solution)/shard_map/ppermute | solution.py:221
  20.0 6.4 %collective-permute-start.5 = (bf16[24,8,256]{2,1,0:T(8,128)(2,1)S(1)}, bf16[24,8,256]{2,1,0:T(8,128)(2,1)S(1)}, u32[]{:S(2)}, u32[]{:S(2)}) collective-permute-start(bf16[24,8,256]{2,1,0:T(8,128)(2,1)S(1)} %get-tuple-element.64), channel_id=1, source_target_pairs={{0,3},{1,2},{2,1},{3,0},{4,7},{5,6},{6,5},{7,4},{8,11},{9,10},{10,... | collective-permute-start | bytes 294920 | tf_op jit(solution)/shard_map/ppermute | solution.py:221
  20.1 5.2 %collective-permute-start.2 = (s32[4,24]{1,0:T(4,128)S(1)}, s32[4,24]{1,0:T(4,128)S(1)}, u32[]{:S(2)}, u32[]{:S(2)}) collective-permute-start(s32[4,24]{1,0:T(4,128)S(1)} %get-tuple-element.60.wants), channel_id=1, source_target_pairs={{0,3},{1,2},{2,1},{3,0},{4,7},{5,6},{6,5},{7,4},{8,11},{9,10},{10,... | collective-permute-start | bytes 1160 | tf_op jit(solution)/shard_map/ppermute | solution.py:218
  21.8 3.8 %collective-permute-start.1 = (s32[4,24]{1,0:T(4,128)S(1)}, s32[4,24]{1,0:T(4,128)S(1)}, u32[]{:S(2)}, u32[]{:S(2)}) collective-permute-start(s32[4,24]{1,0:T(4,128)S(1)} %get-tuple-element.60.wants), channel_id=1, source_target_pairs={{0,2},{1,3},{2,0},{3,1},{4,6},{5,7},{6,4},{7,5},{8,10},{9,11},{10,... | collective-permute-start | bytes 1160 | tf_op jit(solution)/shard_map/ppermute | solution.py:218
  27.6 4.5 %collective-permute-start.6 = (bf16[12,8,256]{2,1,0:T(8,128)(2,1)S(1)}, bf16[12,8,256]{2,1,0:T(8,128)(2,1)S(1)}, u32[]{:S(2)}, u32[]{:S(2)}) collective-permute-start(bf16[12,8,256]{2,1,0:T(8,128)(2,1)S(1)} %get-tuple-element.66), channel_id=1, source_target_pairs={{0,4},{1,5},{2,6},{3,7},{4,0},{5,1},{6,2},{7,3},{8,12},{9,13},{10,... | collective-permute-start | bytes 147464 | tf_op jit(solution)/shard_map/ppermute | solution.py:231
  29.3 6.1 %collective-permute-start.7 = (bf16[12,8,256]{2,1,0:T(8,128)(2,1)S(1)}, bf16[12,8,256]{2,1,0:T(8,128)(2,1)S(1)}, u32[]{:S(2)}, u32[]{:S(2)}) collective-permute-start(bf16[12,8,256]{2,1,0:T(8,128)(2,1)S(1)} %get-tuple-element.67), channel_id=1, source_target_pairs={{0,8},{1,9},{2,10},{3,11},{4,12},{5,13},{6,14},{7,15},{8,0},{9,1},... | collective-permute-start | bytes 147464 | tf_op jit(solution)/shard_map/ppermute | solution.py:231
  31.9 5.9 %collective-permute-start.8 = (bf16[12,8,256]{2,1,0:T(8,128)(2,1)S(1)}, bf16[12,8,256]{2,1,0:T(8,128)(2,1)S(1)}, u32[]{:S(2)}, u32[]{:S(2)}) collective-permute-start(bf16[12,8,256]{2,1,0:T(8,128)(2,1)S(1)} %get-tuple-element.68), channel_id=1, source_target_pairs={{0,12},{1,13},{2,14},{3,15},{4,8},{5,9},{6,10},{7,11},{8,4},{9,5},... | collective-permute-start | bytes 147464 | tf_op jit(solution)/shard_map/ppermute | solution.py:231
  67.0 1.9 collective-permute-start.9
  67.4 5.6 %collective-permute-start.10 = (bf16[24,8,256]{2,1,0:T(8,128)(2,1)S(1)}, bf16[24,8,256]{2,1,0:T(8,128)(2,1)S(1)}, u32[]{:S(2)}, u32[]{:S(2)}) collective-permute-start(bf16[24,8,256]{2,1,0:T(8,128)(2,1)S(1)} %get-tuple-element.79), channel_id=1, source_target_pairs={{0,2},{1,3},{2,0},{3,1},{4,6},{5,7},{6,4},{7,5},{8,10},{9,11},{10,... | collective-permute-start | bytes 294920 | tf_op jit(solution)/shard_map/ppermute | solution.py:221
  67.4 6.2 %collective-permute-start.11 = (bf16[24,8,256]{2,1,0:T(8,128)(2,1)S(1)}, bf16[24,8,256]{2,1,0:T(8,128)(2,1)S(1)}, u32[]{:S(2)}, u32[]{:S(2)}) collective-permute-start(bf16[24,8,256]{2,1,0:T(8,128)(2,1)S(1)} %get-tuple-element.80), channel_id=1, source_target_pairs={{0,3},{1,2},{2,1},{3,0},{4,7},{5,6},{6,5},{7,4},{8,11},{9,10},{10,... | collective-permute-start | bytes 294920 | tf_op jit(solution)/shard_map/ppermute | solution.py:221
  74.7 4.5 %collective-permute-start.12 = (bf16[12,8,256]{2,1,0:T(8,128)(2,1)S(1)}, bf16[12,8,256]{2,1,0:T(8,128)(2,1)S(1)}, u32[]{:S(2)}, u32[]{:S(2)}) collective-permute-start(bf16[12,8,256]{2,1,0:T(8,128)(2,1)S(1)} %get-tuple-element.82), channel_id=1, source_target_pairs={{0,4},{1,5},{2,6},{3,7},{4,0},{5,1},{6,2},{7,3},{8,12},{9,13},{10,... | collective-permute-start | bytes 147464 | tf_op jit(solution)/shard_map/ppermute | solution.py:231
  74.8 7.7 %collective-permute-start.13 = (bf16[12,8,256]{2,1,0:T(8,128)(2,1)S(1)}, bf16[12,8,256]{2,1,0:T(8,128)(2,1)S(1)}, u32[]{:S(2)}, u32[]{:S(2)}) collective-permute-start(bf16[12,8,256]{2,1,0:T(8,128)(2,1)S(1)} %get-tuple-element.83), channel_id=1, source_target_pairs={{0,8},{1,9},{2,10},{3,11},{4,12},{5,13},{6,14},{7,15},{8,0},{9,1},... | collective-permute-start | bytes 147464 | tf_op jit(solution)/shard_map/ppermute | solution.py:231
  74.8 7.6 %collective-permute-start.14 = (bf16[12,8,256]{2,1,0:T(8,128)(2,1)S(1)}, bf16[12,8,256]{2,1,0:T(8,128)(2,1)S(1)}, u32[]{:S(2)}, u32[]{:S(2)}) collective-permute-start(bf16[12,8,256]{2,1,0:T(8,128)(2,1)S(1)} %get-tuple-element.84), channel_id=1, source_target_pairs={{0,12},{1,13},{2,14},{3,15},{4,8},{5,9},{6,10},{7,11},{8,4},{9,5},... | collective-permute-start | bytes 147464 | tf_op jit(solution)/shard_map/ppermute | solution.py:231
  112.9 5.6 %collective-permute-start.16 = (bf16[24,8,256]{2,1,0:T(8,128)(2,1)S(1)}, bf16[24,8,256]{2,1,0:T(8,128)(2,1)S(1)}, u32[]{:S(2)}, u32[]{:S(2)}) collective-permute-start(bf16[24,8,256]{2,1,0:T(8,128)(2,1)S(1)} %get-tuple-element.92), channel_id=1, source_target_pairs={{0,2},{1,3},{2,0},{3,1},{4,6},{5,7},{6,4},{7,5},{8,10},{9,11},{10,... | collective-permute-start | bytes 294920 | tf_op jit(solution)/shard_map/ppermute | solution.py:221
  112.9 6.2 %collective-permute-start.17 = (bf16[24,8,256]{2,1,0:T(8,128)(2,1)S(1)}, bf16[24,8,256]{2,1,0:T(8,128)(2,1)S(1)}, u32[]{:S(2)}, u32[]{:S(2)}) collective-permute-start(bf16[24,8,256]{2,1,0:T(8,128)(2,1)S(1)} %get-tuple-element.93), channel_id=1, source_target_pairs={{0,3},{1,2},{2,1},{3,0},{4,7},{5,6},{6,5},{7,4},{8,11},{9,10},{10,... | collective-permute-start | bytes 294920 | tf_op jit(solution)/shard_map/ppermute | solution.py:221
  120.2 4.5 %collective-permute-start.18 = (bf16[12,8,256]{2,1,0:T(8,128)(2,1)S(1)}, bf16[12,8,256]{2,1,0:T(8,128)(2,1)S(1)}, u32[]{:S(2)}, u32[]{:S(2)}) collective-permute-start(bf16[12,8,256]{2,1,0:T(8,128)(2,1)S(1)} %get-tuple-element.95), channel_id=1, source_target_pairs={{0,4},{1,5},{2,6},{3,7},{4,0},{5,1},{6,2},{7,3},{8,12},{9,13},{10,... | collective-permute-start | bytes 147464 | tf_op jit(solution)/shard_map/ppermute | solution.py:231
  120.3 7.7 %collective-permute-start.19 = (bf16[12,8,256]{2,1,0:T(8,128)(2,1)S(1)}, bf16[12,8,256]{2,1,0:T(8,128)(2,1)S(1)}, u32[]{:S(2)}, u32[]{:S(2)}) collective-permute-start(bf16[12,8,256]{2,1,0:T(8,128)(2,1)S(1)} %get-tuple-element.96), channel_id=1, source_target_pairs={{0,8},{1,9},{2,10},{3,11},{4,12},{5,13},{6,14},{7,15},{8,0},{9,1},... | collective-permute-start | bytes 147464 | tf_op jit(solution)/shard_map/ppermute | solution.py:231
  120.4 7.6 %collective-permute-start.20 = (bf16[12,8,256]{2,1,0:T(8,128)(2,1)S(1)}, bf16[12,8,256]{2,1,0:T(8,128)(2,1)S(1)}, u32[]{:S(2)}, u32[]{:S(2)}) collective-permute-start(bf16[12,8,256]{2,1,0:T(8,128)(2,1)S(1)} %get-tuple-element.97), channel_id=1, source_target_pairs={{0,12},{1,13},{2,14},{3,15},{4,8},{5,9},{6,10},{7,11},{8,4},{9,5},... | collective-permute-start | bytes 147464 | tf_op jit(solution)/shard_map/ppermute | solution.py:231
  158.8 5.6 %collective-permute-start.22 = (bf16[24,8,256]{2,1,0:T(8,128)(2,1)S(1)}, bf16[24,8,256]{2,1,0:T(8,128)(2,1)S(1)}, u32[]{:S(2)}, u32[]{:S(2)}) collective-permute-start(bf16[24,8,256]{2,1,0:T(8,128)(2,1)S(1)} %get-tuple-element.105), channel_id=1, source_target_pairs={{0,2},{1,3},{2,0},{3,1},{4,6},{5,7},{6,4},{7,5},{8,10},{9,11},{10,... | collective-permute-start | bytes 294920 | tf_op jit(solution)/shard_map/ppermute | solution.py:221
  158.8 6.2 %collective-permute-start.23 = (bf16[24,8,256]{2,1,0:T(8,128)(2,1)S(1)}, bf16[24,8,256]{2,1,0:T(8,128)(2,1)S(1)}, u32[]{:S(2)}, u32[]{:S(2)}) collective-permute-start(bf16[24,8,256]{2,1,0:T(8,128)(2,1)S(1)} %get-tuple-element.106), channel_id=1, source_target_pairs={{0,3},{1,2},{2,1},{3,0},{4,7},{5,6},{6,5},{7,4},{8,11},{9,10},{10,... | collective-permute-start | bytes 294920 | tf_op jit(solution)/shard_map/ppermute | solution.py:221
  166.1 4.5 %collective-permute-start.24 = (bf16[12,8,256]{2,1,0:T(8,128)(2,1)S(1)}, bf16[12,8,256]{2,1,0:T(8,128)(2,1)S(1)}, u32[]{:S(2)}, u32[]{:S(2)}) collective-permute-start(bf16[12,8,256]{2,1,0:T(8,128)(2,1)S(1)} %get-tuple-element.108), channel_id=1, source_target_pairs={{0,4},{1,5},{2,6},{3,7},{4,0},{5,1},{6,2},{7,3},{8,12},{9,13},{10,... | collective-permute-start | bytes 147464 | tf_op jit(solution)/shard_map/ppermute | solution.py:231
  166.1 7.7 %collective-permute-start.25 = (bf16[12,8,256]{2,1,0:T(8,128)(2,1)S(1)}, bf16[12,8,256]{2,1,0:T(8,128)(2,1)S(1)}, u32[]{:S(2)}, u32[]{:S(2)}) collective-permute-start(bf16[12,8,256]{2,1,0:T(8,128)(2,1)S(1)} %get-tuple-element.109), channel_id=1, source_target_pairs={{0,8},{1,9},{2,10},{3,11},{4,12},{5,13},{6,14},{7,15},{8,0},{9,1},... | collective-permute-start | bytes 147464 | tf_op jit(solution)/shard_map/ppermute | solution.py:231
  166.2 7.6 %collective-permute-start.26 = (bf16[12,8,256]{2,1,0:T(8,128)(2,1)S(1)}, bf16[12,8,256]{2,1,0:T(8,128)(2,1)S(1)}, u32[]{:S(2)}, u32[]{:S(2)}) collective-permute-start(bf16[12,8,256]{2,1,0:T(8,128)(2,1)S(1)} %get-tuple-element.110), channel_id=1, source_target_pairs={{0,12},{1,13},{2,14},{3,15},{4,8},{5,9},{6,10},{7,11},{8,4},{9,5},... | collective-permute-start | bytes 147464 | tf_op jit(solution)/shard_map/ppermute | solution.py:231
  (15 other events, 265.2 us)

commit v2 on v1

v2 whole, which is shorter than its diff:
```python
import functools

import jax
import jax.numpy as jnp
from jax import lax
from jax.experimental import pallas as pl
from jax.experimental.pallas import tpu as pltpu
from jax.sharding import PartitionSpec as P

QUAD = 4
CHUNK = 8
VM = pl.BlockSpec(memory_space=pltpu.VMEM)
SM = pl.BlockSpec(memory_space=pltpu.SMEM)
ANY = pl.BlockSpec(memory_space=pl.ANY)
PARAMS = pltpu.CompilerParams(vmem_limit_bytes=16 * 1024 * 1024)
F32, BF16, I32 = jnp.float32, jnp.bfloat16, jnp.int32


def shape(dims, dtype):
    return jax.ShapeDtypeStruct(dims, dtype)


def scaled_blocks(side, dy, dual_step, hb, h_into):
    for r in range(hb.shape[0]):
        at = pl.ds(r * side, side)
        h = dual_step[:, at] * dy[:, at]
        hb[r] = h.astype(BF16)
        h_into(at, h)


def transpose_products(first, tiles, rows, slots, hb, out):
    for j in range(CHUNK):
        t = first + j
        term = jnp.dot(hb[rows[t]], tiles[t], preferred_element_type=F32)
        out[slots[t]] = term.astype(BF16)


def forward_products(turned, lands, places, moved, total):
    total[...] = jnp.zeros_like(total)

    def one_chunk(c, _):
        for j in range(CHUNK):
            t = c * CHUNK + j
            product = jnp.dot(moved[places[t]], turned[t], preferred_element_type=F32)
            r = lands[t]
            total[r] = total[r] + product
        return 0

    lax.fori_loop(0, turned.shape[0] // CHUNK, one_chunk, 0)


def start_kernel(step, peers, cap, col_blocks, rows_in, cols_in, count_in, tiles, dual_step, dual_mask, cot_y,
                 held, turned, dy, rhs, slots, places, lands, rows, out, cols, count, hb, filled, taken, sems, small):
    tile_slots, side, _ = tiles.shape
    group = peers // QUAD
    per = group * cap
    chunks = tile_slots // CHUNK
    minor = [
        pltpu.make_async_copy(src, dst, small.at[i])
        for i, (src, dst) in enumerate(((rows_in, rows), (cols_in, cols), (count_in, count)))
    ]
    for copy in minor:
        copy.start()

    def tile_copy(c):
        at = pl.ds(c * CHUNK, CHUNK)
        return pltpu.make_async_copy(tiles.at[at], held.at[at], sems.at[c])

    for c in range(chunks):
        tile_copy(c).start()
    dy[...] = dual_mask[step].astype(F32) * cot_y[...]

    def h_into(at, h):
        rhs[:, at] = -h

    scaled_blocks(side, dy, dual_step, hb, h_into)
    for copy in minor:
        copy.wait()

    def clear(o, _):
        filled[o] = 0
        return 0

    lax.fori_loop(0, peers, clear, 0)

    def clear_slot(s, _):
        taken[s] = 0
        return 0

    lax.fori_loop(0, QUAD * per, clear_slot, 0)
    lane = lax.broadcasted_iota(I32, (2 * QUAD, side), 1)
    line = lax.broadcasted_iota(I32, (2 * QUAD, side), 0)

    def place_tile(t, plan):
        col = cols[t]
        owner = col // col_blocks
        live = t < count[0]
        rank = filled[owner]
        high, quad = owner // QUAD, owner % QUAD
        within = high * cap + rank
        slot = quad * per + within
        slots[t] = jnp.where(live, slot, -1)
        lands[t] = jnp.where(live, rows[t], hb.shape[0])

        @pl.when(live)
        def _():
            filled[owner] = rank + 1
            taken[slot] = 1

        here = (lane == within) & live
        plan = jnp.where(here & (line == 2 * quad), high, plan)
        return jnp.where(here & (line == 2 * quad + 1), col - owner * col_blocks, plan)

    plan = lax.fori_loop(0, tile_slots, place_tile, jnp.full((2 * QUAD, side), -1, I32))
    for q in range(QUAD):
        out[q * (per + 1) + per] = plan.astype(BF16)
    spare = lax.fori_loop(0, QUAD * per, lambda s, best: jnp.where(taken[s] == 0, s, best), 0)

    def settle(t, _):
        slot = jnp.where(slots[t] < 0, spare, slots[t])
        slots[t] = slot
        places[t] = slot + slot // per
        return 0

    lax.fori_loop(0, tile_slots, settle, 0)

    def one_chunk(c, _):
        tile_copy(c).wait()
        transpose_products(c * CHUNK, held, rows, places, hb, out)
        for j in range(CHUNK):
            turned[c * CHUNK + j] = held[c * CHUNK + j].T
        return 0

    lax.fori_loop(0, chunks, one_chunk, 0)


def read_plan(col_blocks, group, got, wants, whole, sem):
    per = wants.shape[0] // QUAD
    mine = lax.axis_index("rb") % QUAD
    line = lax.broadcasted_iota(I32, got.shape[1:], 0)
    for q in range(QUAD):
        plan = got[q * (per + 1) + per].astype(F32)
        high = jnp.sum(jnp.where(line == 2 * mine, plan, 0.0), axis=0, keepdims=True)
        within = jnp.sum(jnp.where(line == 2 * mine + 1, plan, 0.0), axis=0, keepdims=True)
        index = jnp.where(high < 0.0, float(group * col_blocks), high * col_blocks + within)
        whole[pl.ds(q, 1)] = index.astype(I32)


def sum_kernel(first, col_blocks, *refs):
    if first:
        got, out, wants, total, whole, wide, sem = refs
    else:
        wants, got, out, total = refs
    group = out.shape[0] // col_blocks
    per = wants.shape[0] // QUAD
    stride = got.shape[0] // QUAD
    if first:
        read_plan(col_blocks, group, got, wants, whole, sem)
        copy = pltpu.make_async_copy(whole, wide, sem)
        copy.start()
    total[...] = jnp.zeros_like(total)
    if first:
        copy.wait()
    for q in range(QUAD):
        for s in range(per):
            if first:
                c = wide[q, s]
                wants[q * per + s] = c
            else:
                c = wants[q * per + s]
            total[c] = total[c] + got[q * stride + s].astype(F32)
    for c in range(out.shape[0]):
        out[c] = total[c].astype(BF16)


def primal_kernel(step, first, primal_mask, primal_step, x, cost, got, new_x, new_cost, out):
    side = out.shape[2]
    blocks = new_x.shape[1] // side
    group = out.shape[0] // blocks
    for c in range(blocks):
        at = pl.ds(c * side, side)
        u = got[c].astype(F32)
        for high in range(1, group):
            u = u + got[high * blocks + c].astype(F32)
        dx = primal_mask[step, :, at].astype(F32) * (x[:, at] + 2.0 * u)
        q = primal_step[:, at] * dx
        new_x[:, at] = dx - u
        new_cost[:, at] = -q if first else cost[:, at] - q
        rounded = q.astype(BF16)
        for high in range(group):
            out[high * blocks + c] = rounded


def pick_kernel(wants, blocks, out):
    last = blocks.shape[0] - 1
    for s in range(out.shape[0]):
        out[s] = blocks[jnp.minimum(wants[s], last)]


def middle_kernel(step, rows, lands, slots, held, turned, dual_step, dual_mask, moved, dy, rhs,
                  new_dy, new_rhs, out, total, hb):
    side = held.shape[1]
    forward_products(turned, lands, slots, moved, total)
    for r in range(total.shape[0] - 1):
        at = pl.ds(r * side, side)
        new_dy[:, at] = dual_mask[step, :, at].astype(F32) * (dy[:, at] - total[r])

    def h_into(at, h):
        new_rhs[:, at] = rhs[:, at] - h

    scaled_blocks(side, new_dy, dual_step, hb, h_into)

    def one_chunk(c, _):
        transpose_products(c * CHUNK, held, rows, slots, hb, out)
        return 0

    lax.fori_loop(0, held.shape[0] // CHUNK, one_chunk, 0)


def last_kernel(lands, slots, turned, moved, dy, new_y, total):
    side = turned.shape[1]
    forward_products(turned, lands, slots, moved, total)
    for r in range(total.shape[0] - 1):
        at = pl.ds(r * side, side)
        new_y[:, at] = dy[:, at] - total[r]


def on_device(tiles, tile_rows, tile_cols, tile_counts, dual_step, primal_step, primal_mask, dual_mask, cot_x, cot_y):
    peers = lax.axis_size("rb")
    tile_slots, side, _ = tiles.shape
    batch = cot_x.shape[0]
    row_blocks = dual_step.shape[0] // side
    col_blocks = primal_step.shape[0] // side
    cap = max(2, (tile_slots + peers - 1) // peers)
    group = peers // QUAD
    per = group * cap
    steps = primal_mask.shape[0]
    dual_step = dual_step.reshape(1, -1)
    primal_step = primal_step.reshape(1, -1)
    y_shape = shape(cot_y.shape, F32)
    x_shape = shape(cot_x.shape, F32)
    slot_set = shape((QUAD * per, batch, side), BF16)
    block_set = shape((group * col_blocks, batch, side), BF16)
    per_tile = shape((tile_slots,), I32)
    hb_scratch = pltpu.VMEM((row_blocks, batch, side), BF16)
    row_total = pltpu.VMEM((row_blocks + 1, batch, side), F32)
    col_total = pltpu.VMEM((group * col_blocks + 1, batch, side), F32)
    near = [[h * QUAD + q for q in range(QUAD)] for h in range(group)]
    far = [[h * QUAD + q for h in range(group)] for q in range(QUAD)]

    def swap(array, groups):
        return lax.all_to_all(array, "rb", 0, 0, axis_index_groups=groups, tiled=True)

    step = steps - 1
    held, turned, dy, rhs, slots, places, lands, rows, sent = pl.pallas_call(
        functools.partial(start_kernel, step, peers, cap, col_blocks),
        out_shape=(
            pltpu.VMEM(tiles.shape, BF16), pltpu.VMEM(tiles.shape, BF16), y_shape, y_shape,
            per_tile, per_tile, per_tile, per_tile, shape((QUAD * (per + 1), batch, side), BF16),
        ),
        in_specs=[ANY, ANY, ANY, ANY, VM, VM, VM],
        out_specs=(VM, VM, VM, VM, SM, SM, SM, SM, VM),
        scratch_shapes=[
            pltpu.SMEM((tile_slots,), I32), pltpu.SMEM((1,), I32), hb_scratch, pltpu.SMEM((peers,), I32),
            pltpu.SMEM((QUAD * per,), I32), pltpu.SemaphoreType.DMA((tile_slots // CHUNK,)),
            pltpu.SemaphoreType.DMA((3,)),
        ],
        compiler_params=PARAMS,
        name="start",
    )(tile_rows, tile_cols, tile_counts, tiles, dual_step, dual_mask, cot_y)
    x_state, cost, wants = cot_x, cot_x, None
    while True:
        got = swap(sent, near)
        if wants is None:
            sums, wants = pl.pallas_call(
                functools.partial(sum_kernel, True, col_blocks),
                out_shape=(block_set, shape((QUAD * per,), I32)),
                in_specs=[VM],
                out_specs=(VM, SM),
                scratch_shapes=[
                    col_total, pltpu.VMEM((8, side), I32), pltpu.SMEM((8, side), I32), pltpu.SemaphoreType.DMA,
                ],
                compiler_params=PARAMS,
                name="quad_sum_plan",
            )(got)
        else:
            sums = pl.pallas_call(
                functools.partial(sum_kernel, False, col_blocks),
                out_shape=block_set,
                in_specs=[SM, VM],
                out_specs=VM,
                scratch_shapes=[col_total],
                compiler_params=PARAMS,
                name="quad_sum",
            )(wants, got)
        x_state, cost, moved = pl.pallas_call(
            functools.partial(primal_kernel, step, step == steps - 1),
            out_shape=(x_shape, x_shape, block_set),
            in_specs=[VM] * 5,
            out_specs=(VM,) * 3,
            compiler_params=PARAMS,
            name="primal",
        )(primal_mask, primal_step, x_state, cost, swap(sums, far))
        picked = pl.pallas_call(
            pick_kernel,
            out_shape=slot_set,
            in_specs=[SM, VM],
            out_specs=VM,
            compiler_params=PARAMS,
            name="pick",
        )(wants, swap(moved, far))
        moved = swap(picked, near)
        if step == 0:
            break
        step -= 1
        dy, rhs, sent = pl.pallas_call(
            functools.partial(middle_kernel, step),
            out_shape=(y_shape, y_shape, slot_set),
            in_specs=[SM] * 3 + [VM] * 7,
            out_specs=(VM,) * 3,
            scratch_shapes=[row_total, hb_scratch],
            compiler_params=PARAMS,
            name="middle",
        )(rows, lands, slots, held, turned, dual_step, dual_mask, moved, dy, rhs)
    y_state = pl.pallas_call(
        last_kernel,
        out_shape=y_shape,
        in_specs=[SM] * 2 + [VM] * 3,
        out_specs=VM,
        scratch_shapes=[row_total],
        compiler_params=PARAMS,
        name="last",
    )(lands, slots, turned, moved, dy)
    return cost, rhs, x_state, y_state


def solution(mesh):
    rb = ("grp", "rb")
    return jax.shard_map(
        on_device,
        mesh=mesh,
        in_specs=(
            P(rb, None, None), P(rb), P(rb), P(rb), P(rb), P(rb),
            P(None, "grp", "rb"), P(None, "grp", "rb"), P("grp", "rb"), P("grp", "rb"),
        ),
        out_specs=(P("grp", "rb"),) * 4,
        check_vma=False,
    )
```

time: 203 us -> 222 us (1.094)
  blocking collectives: 88.1 us -> 162 us
  waiting for transfers between devices: 34.1 us -> 0 us
  starting transfers between devices: 28.6 us -> 0 us
  local copies, waits for them, and re-layouts: 8.09 us -> 16.7 us
    all_to_all x0 -> x16, blocking collectives: none -> 162 us  [swap(): lax.all_to_all(array, 'rb', 0, 0, axis_index_groups=groups, tiled=True)]
    all_gather x4 -> x0, blocking collectives: 88.1 us -> none  [on_device(): moved = lax.all_gather(moved, 'rb', axis=0, tiled=True)]
    ppermute x27 -> x0, waiting for transfers between devices: 34.1 us -> none  [the longest x12 15.6 us: on_device(): lax.ppermute(sums[x], 'rb', far(x))]
    ppermute x27 -> x0, starting transfers between devices: 28.6 us -> none  [the longest x12 17.8 us: on_device(): lax.ppermute(sums[x], 'rb', far(x))]
    unnamed x24 -> x28, local copies, waits for them, and re-layouts: 8.09 us -> 16.7 us
    pallas_call x3, Pallas kernels: 23.6 us -> 18.8 us  [on_device(): pl.pallas_call(functools.partial(middle_kernel, step), out_shape=(y_shape...]
    pallas_call x4 -> x8, Pallas kernels: 4.38 us -> 7.47 us  [the longest x3 3.1 us: on_device(): pl.pallas_call(functools.partial(sum_kernel, False, col_blocks), out_shap...]
    pallas_call x1, Pallas kernels: 7.52 us -> 10.5 us  [on_device(): pl.pallas_call(functools.partial(start_kernel, step, peers, cap, col_bloc...]
  transfers between devices with their start and end apart: 27 -> 0, of which waited for: 14 -> 0; matrix products, arithmetic and copies ran while one was open for 0% -> 0% of each run, Pallas kernels for 0% -> 0%
where the time goes in v2:
time: 222 us; the launch traced here: 221 us
  blocking collectives  162 us (73%)
  Pallas kernels  41.7 us (19%)
  local copies, waits for them, and re-layouts  16.7 us (8%)
    all_to_all x16, blocking collectives, swap(): lax.all_to_all(array, 'rb', 0, 0, axis_index_groups=groups, tiled=True)  162 us
    pallas_call x3, Pallas kernels, on_device(): pl.pallas_call(functools.partial(middle_kernel, step), out_shape=(y_shape...  18.8 us
    unnamed x28, local copies, waits for them, and re-layouts  16.7 us
    pallas_call x1, Pallas kernels, on_device(): pl.pallas_call(functools.partial(start_kernel, step, peers, cap, col_bloc...  10.5 us

profile of v2, /device:TPU:0, one launch (start us, length us, event | category | flops | bytes accessed | tf_op | source)
XLA Modules:
  0.0 221.4 jit_solution(3004077644281227629)
XLA Ops:
  1.3 4.3 %copy-done.3 = bf16[88,256,256]{2,1,0:T(8,128)(2,1)S(1)} copy-done((bf16[88,256,256]{2,1,0:T(8,128)(2,1)S(1)}, bf16[88,256,256]{2,1,0:T(8,128)(2,1)}, u32[]{:S(2)}) %copy-start.3) | copy-done | bytes 11534360
  9.4 10.5 %start.1 = (bf16[88,256,256]{2,1,0:T(8,128)(2,1)S(1)}, bf16[88,256,256]{2,1,0:T(8,128)(2,1)S(1)}, f32[8,2048]{1,0:T(8,128)S(1)}, f32[8,2048]{1,0:T(8,128)S(1)}, ...) custom-call(s32[88]{0:T(128)S(1)} %copy-done.12, ...), custom_call_target="tpu_custom_call" | custom-call | tf_op jit(solution)/shard_map/start/pallas_call | solution.py:255
  19.9 4.3 %copy-done = bf16[88,256,256]{2,1,0:T(8,128)(2,1)} copy-done((bf16[88,256,256]{2,1,0:T(8,128)(2,1)}, bf16[88,256,256]{2,1,0:T(8,128)(2,1)S(1)}, u32[]{:S(2)}) %copy-start) | copy-done | bytes 11534360
  24.2 11.6 %all_to_all.80.refs_0_ = bf16[100,8,256]{2,1,0:T(8,128)(2,1)S(1)} all-to-all(bf16[100,8,256]{2,1,0:T(8,128)(2,1)S(1)} %get-tuple-element.35), channel_id=1, replica_groups={{0,1,2,3},{4,5,6,7},{8,9,10,11},{12,13,14,15},{16,17,18,19},{20,21,22,2..., dimensions={0} | all-to-all | bytes 819200 | tf_op jit(solution)/shard_map/all_to_all | solution.py:252
  37.6 12.3 %all_to_all.81.got = bf16[48,8,256]{2,1,0:T(8,128)(2,1)S(1)} all-to-all(bf16[48,8,256]{2,1,0:T(8,128)(2,1)S(1)} %get-tuple-element.36), channel_id=1, replica_groups={{0,4,8,12},{1,5,9,13},{2,6,10,14},{3,7,11,15},{16,20,24,28},{17,21,25,2..., dimensions={0} | all-to-all | bytes 393216 | tf_op jit(solution)/shard_map/all_to_all | solution.py:252
  50.0 9.9 %all_to_all.82.blocks = bf16[48,8,256]{2,1,0:T(8,128)(2,1)S(1)} all-to-all(bf16[48,8,256]{2,1,0:T(8,128)(2,1)S(1)} %get-tuple-element.45), channel_id=1, replica_groups={{0,4,8,12},{1,5,9,13},{2,6,10,14},{3,7,11,15},{16,20,24,28},{17,21,25,2..., dimensions={0} | all-to-all | bytes 393216 | tf_op jit(solution)/shard_map/all_to_all | solution.py:252
  60.6 9.8 %all_to_all.83.moved = bf16[96,8,256]{2,1,0:T(8,128)(2,1)S(1)} all-to-all(bf16[96,8,256]{2,1,0:T(8,128)(2,1)S(1)} %pick.4), channel_id=1, replica_groups={{0,1,2,3},{4,5,6,7},{8,9,10,11},{12,13,14,15},{16,17,18,19},{20,21,22,2..., dimensions={0} | all-to-all | bytes 786432 | tf_op jit(solution)/shard_map/all_to_all | solution.py:252
  70.4 4.3 %copy-done.1 = bf16[88,256,256]{2,1,0:T(8,128)(2,1)S(1)} copy-done((bf16[88,256,256]{2,1,0:T(8,128)(2,1)S(1)}, bf16[88,256,256]{2,1,0:T(8,128)(2,1)}, u32[]{:S(2)}) %copy-start.1) | copy-done | bytes 11534360
  74.7 6.1 %middle.3 = (f32[8,2048]{1,0:T(8,128)S(1)}, f32[8,2048]{1,0:T(8,128)S(1)}, bf16[96,8,256]{2,1,0:T(8,128)(2,1)S(1)}) custom-call(s32[88]{0:T(128)S(1)} %get-tuple-element.40.rows, s32[88]{0:T(128)S(1)} %get-tuple-element.41.lands, s32[88]{0:T(128)S(1)} %get-tuple-element.42.slots, bf16[88,256,256]{2,1,0:T(8,128)(2,1)S(1)} %copy-done.1, ...), custom_call_target="tpu_custom_call" | custom-call | tf_op jit(solution)/shard_map/middle/pallas_call | solution.py:316
  80.8 9.8 %all_to_all.84.refs_1_ = bf16[96,8,256]{2,1,0:T(8,128)(2,1)S(1)} all-to-all(bf16[96,8,256]{2,1,0:T(8,128)(2,1)S(1)} %get-tuple-element.48), channel_id=1, replica_groups={{0,1,2,3},{4,5,6,7},{8,9,10,11},{12,13,14,15},{16,17,18,19},{20,21,22,2..., dimensions={0} | all-to-all | bytes 786432 | tf_op jit(solution)/shard_map/all_to_all | solution.py:252
  91.7 9.8 %all_to_all.85.got = bf16[48,8,256]{2,1,0:T(8,128)(2,1)S(1)} all-to-all(bf16[48,8,256]{2,1,0:T(8,128)(2,1)S(1)} %quad_sum.3), channel_id=1, replica_groups={{0,4,8,12},{1,5,9,13},{2,6,10,14},{3,7,11,15},{16,20,24,28},{17,21,25,2..., dimensions={0} | all-to-all | bytes 393216 | tf_op jit(solution)/shard_map/all_to_all | solution.py:252
  101.6 9.8 %all_to_all.86.blocks = bf16[48,8,256]{2,1,0:T(8,128)(2,1)S(1)} all-to-all(bf16[48,8,256]{2,1,0:T(8,128)(2,1)S(1)} %get-tuple-element.51), channel_id=1, replica_groups={{0,4,8,12},{1,5,9,13},{2,6,10,14},{3,7,11,15},{16,20,24,28},{17,21,25,2..., dimensions={0} | all-to-all | bytes 393216 | tf_op jit(solution)/shard_map/all_to_all | solution.py:252
  112.1 9.8 %all_to_all.87.moved = bf16[96,8,256]{2,1,0:T(8,128)(2,1)S(1)} all-to-all(bf16[96,8,256]{2,1,0:T(8,128)(2,1)S(1)} %pick.5), channel_id=1, replica_groups={{0,1,2,3},{4,5,6,7},{8,9,10,11},{12,13,14,15},{16,17,18,19},{20,21,22,2..., dimensions={0} | all-to-all | bytes 786432 | tf_op jit(solution)/shard_map/all_to_all | solution.py:252
  121.9 6.1 %middle.4 = (f32[8,2048]{1,0:T(8,128)S(1)}, f32[8,2048]{1,0:T(8,128)S(1)}, bf16[96,8,256]{2,1,0:T(8,128)(2,1)S(1)}) custom-call(s32[88]{0:T(128)S(1)} %get-tuple-element.40.rows, s32[88]{0:T(128)S(1)} %get-tuple-element.41.lands, s32[88]{0:T(128)S(1)} %get-tuple-element.42.slots, bf16[88,256,256]{2,1,0:T(8,128)(2,1)S(1)} %copy-done.2, ...), custom_call_target="tpu_custom_call" | custom-call | tf_op jit(solution)/shard_map/middle/pallas_call | solution.py:316
  128.1 9.8 %all_to_all.88.refs_1_ = bf16[96,8,256]{2,1,0:T(8,128)(2,1)S(1)} all-to-all(bf16[96,8,256]{2,1,0:T(8,128)(2,1)S(1)} %get-tuple-element.54), channel_id=1, replica_groups={{0,1,2,3},{4,5,6,7},{8,9,10,11},{12,13,14,15},{16,17,18,19},{20,21,22,2..., dimensions={0} | all-to-all | bytes 786432 | tf_op jit(solution)/shard_map/all_to_all | solution.py:252
  139.0 9.8 %all_to_all.89.got = bf16[48,8,256]{2,1,0:T(8,128)(2,1)S(1)} all-to-all(bf16[48,8,256]{2,1,0:T(8,128)(2,1)S(1)} %quad_sum.4), channel_id=1, replica_groups={{0,4,8,12},{1,5,9,13},{2,6,10,14},{3,7,11,15},{16,20,24,28},{17,21,25,2..., dimensions={0} | all-to-all | bytes 393216 | tf_op jit(solution)/shard_map/all_to_all | solution.py:252
  148.9 9.8 %all_to_all.90.blocks = bf16[48,8,256]{2,1,0:T(8,128)(2,1)S(1)} all-to-all(bf16[48,8,256]{2,1,0:T(8,128)(2,1)S(1)} %get-tuple-element.57), channel_id=1, replica_groups={{0,4,8,12},{1,5,9,13},{2,6,10,14},{3,7,11,15},{16,20,24,28},{17,21,25,2..., dimensions={0} | all-to-all | bytes 393216 | tf_op jit(solution)/shard_map/all_to_all | solution.py:252
  159.3 9.8 %all_to_all.91.moved = bf16[96,8,256]{2,1,0:T(8,128)(2,1)S(1)} all-to-all(bf16[96,8,256]{2,1,0:T(8,128)(2,1)S(1)} %pick.6), channel_id=1, replica_groups={{0,1,2,3},{4,5,6,7},{8,9,10,11},{12,13,14,15},{16,17,18,19},{20,21,22,2..., dimensions={0} | all-to-all | bytes 786432 | tf_op jit(solution)/shard_map/all_to_all | solution.py:252
  169.2 6.6 %middle.5 = (f32[8,2048]{1,0:T(8,128)S(1)}, f32[8,2048]{1,0:T(8,128)}, bf16[96,8,256]{2,1,0:T(8,128)(2,1)S(1)}) custom-call(s32[88]{0:T(128)S(1)} %get-tuple-element.40.rows, s32[88]{0:T(128)S(1)} %get-tuple-element.41.lands, s32[88]{0:T(128)S(1)} %get-tuple-element.42.slots, bf16[88,256,256]{2,1,0:T(8,128)(2,1)S(1)} %copy-done.2, ...), custom_call_target="tpu_custom_call" | custom-call | tf_op jit(solution)/shard_map/middle/pallas_call | solution.py:316
  175.7 9.8 %all_to_all.92.refs_1_ = bf16[96,8,256]{2,1,0:T(8,128)(2,1)S(1)} all-to-all(bf16[96,8,256]{2,1,0:T(8,128)(2,1)S(1)} %get-tuple-element.60), channel_id=1, replica_groups={{0,1,2,3},{4,5,6,7},{8,9,10,11},{12,13,14,15},{16,17,18,19},{20,21,22,2..., dimensions={0} | all-to-all | bytes 786432 | tf_op jit(solution)/shard_map/all_to_all | solution.py:252
  186.6 9.8 %all_to_all.93.got = bf16[48,8,256]{2,1,0:T(8,128)(2,1)S(1)} all-to-all(bf16[48,8,256]{2,1,0:T(8,128)(2,1)S(1)} %quad_sum.5), channel_id=1, replica_groups={{0,4,8,12},{1,5,9,13},{2,6,10,14},{3,7,11,15},{16,20,24,28},{17,21,25,2..., dimensions={0} | all-to-all | bytes 393216 | tf_op jit(solution)/shard_map/all_to_all | solution.py:252
  197.2 9.8 %all_to_all.94.blocks = bf16[48,8,256]{2,1,0:T(8,128)(2,1)S(1)} all-to-all(bf16[48,8,256]{2,1,0:T(8,128)(2,1)S(1)} %get-tuple-element.64), channel_id=1, replica_groups={{0,4,8,12},{1,5,9,13},{2,6,10,14},{3,7,11,15},{16,20,24,28},{17,21,25,2..., dimensions={0} | all-to-all | bytes 393216 | tf_op jit(solution)/shard_map/all_to_all | solution.py:252
  207.6 9.8 %all_to_all.95.moved = bf16[96,8,256]{2,1,0:T(8,128)(2,1)S(1)} all-to-all(bf16[96,8,256]{2,1,0:T(8,128)(2,1)S(1)} %pick.7), channel_id=1, replica_groups={{0,1,2,3},{4,5,6,7},{8,9,10,11},{12,13,14,15},{16,17,18,19},{20,21,22,2..., dimensions={0} | all-to-all | bytes 786432 | tf_op jit(solution)/shard_map/all_to_all | solution.py:252
  217.5 4.0 %last.1 = f32[8,2048]{1,0:T(8,128)} custom-call(s32[88]{0:T(128)S(1)} %get-tuple-element.41.lands, s32[88]{0:T(128)S(1)} %get-tuple-element.42.slots, bf16[88,256,256]{2,1,0:T(8,128)(2,1)S(1)} %get-tuple-element.44.turned, bf16[96,8,256]{2,1,0:T(8,128)(2,1)S(1)} %all_to_all.95.moved, f32[8,2048]{1,0:T(8,128)S(1)} %get-tuple-element.65.dy), custom_call_target="tpu_custom_call" | custom-call | tf_op jit(solution)/shard_map/last/pallas_call | solution.py:325
  (37 shorter events, 12.2 us)
Async XLA Ops:
  1.3 4.3 %copy-start.3 = (bf16[88,256,256]{2,1,0:T(8,128)(2,1)S(1)}, bf16[88,256,256]{2,1,0:T(8,128)(2,1)}, u32[]{:S(2)}) copy-start(bf16[88,256,256]{2,1,0:T(8,128)(2,1)} %tiles.1) | copy-start | bytes 34603012
  5.6 0.9 copy-start.5
  6.5 0.7 copy-start.9
  7.2 0.8 copy-start.11
  8.0 0.7 copy-start.12
  8.7 0.7 copy-start.13
  9.4 40.6 %copy-start.4 = (s32[4,8,3072]{2,1,0:T(8,128)S(1)}, s32[4,8,3072]{2,1,0:T(8,128)}, u32[]{:S(2)}) copy-start(s32[4,8,3072]{2,1,0:T(8,128)} %primal_mask.7) | copy-start | bytes 1179652
  9.4 40.6 %copy-start.7 = (f32[8,3072]{1,0:T(8,128)S(1)}, f32[8,3072]{1,0:T(8,128)}, u32[]{:S(2)}) copy-start(f32[8,3072]{1,0:T(8,128)} %cost.1) | copy-start | bytes 294916
  9.4 40.6 %copy-start.8 = (f32[3072]{0:T(1024)S(1)}, f32[3072]{0:T(1024)}, u32[]{:S(2)}) copy-start(f32[3072]{0:T(1024)} %param.15) | copy-start | bytes 36868
  9.4 61.1 %copy-start.6 = (s32[4,8,2048]{2,1,0:T(8,128)S(1)}, s32[4,8,2048]{2,1,0:T(8,128)}, u32[]{:S(2)}) copy-start(s32[4,8,2048]{2,1,0:T(8,128)} %dual_mask.7) | copy-start | bytes 786436
  9.4 61.1 %copy-start.10 = (f32[2048]{0:T(1024)S(1)}, f32[2048]{0:T(1024)}, u32[]{:S(2)}) copy-start(f32[2048]{0:T(1024)} %param.14) | copy-start | bytes 24580
  19.9 4.3 %copy-start = (bf16[88,256,256]{2,1,0:T(8,128)(2,1)}, bf16[88,256,256]{2,1,0:T(8,128)(2,1)S(1)}, u32[]{:S(2)}) copy-start(bf16[88,256,256]{2,1,0:T(8,128)(2,1)S(1)} %get-tuple-element.43.held) | copy-start | bytes 34603012
  70.4 4.3 %copy-start.1 = (bf16[88,256,256]{2,1,0:T(8,128)(2,1)S(1)}, bf16[88,256,256]{2,1,0:T(8,128)(2,1)}, u32[]{:S(2)}) copy-start(bf16[88,256,256]{2,1,0:T(8,128)(2,1)} %copy-done) | copy-start | bytes 34603012
  74.7 47.2 %copy-start.2 = (bf16[88,256,256]{2,1,0:T(8,128)(2,1)S(1)}, bf16[88,256,256]{2,1,0:T(8,128)(2,1)}, u32[]{:S(2)}) copy-start(bf16[88,256,256]{2,1,0:T(8,128)(2,1)} %copy-done) | copy-start | bytes 34603012

commit v3 on v2

v3 whole, which is shorter than its diff:
```python
import functools

import jax
import jax.numpy as jnp
from jax import lax
from jax.experimental import pallas as pl
from jax.experimental.pallas import tpu as pltpu
from jax.sharding import PartitionSpec as P

CHUNK = 8
LANES = 4
HALVES = 2
VM = pl.BlockSpec(memory_space=pltpu.VMEM)
SM = pl.BlockSpec(memory_space=pltpu.SMEM)
HBM = pl.BlockSpec(memory_space=pltpu.HBM)
PARAMS = pltpu.CompilerParams(vmem_limit_bytes=12 * 1024 * 1024)
F32, BF16, I32 = jnp.float32, jnp.bfloat16, jnp.int32


def shape(dims, dtype):
    return jax.ShapeDtypeStruct(dims, dtype)


def cost(moved):
    return pl.CostEstimate(flops=moved * 8, bytes_accessed=moved, transcendentals=0)


def scaled_blocks(side, dy, dual_step, hb, h_into):
    for r in range(hb.shape[0]):
        at = pl.ds(r * side, side)
        h = dual_step[:, at] * dy[:, at]
        hb[r] = h.astype(BF16)
        h_into(at, h)


def transpose_products(first, count, tiles, rows, slots, hb, out):
    for j in range(count):
        t = first + j
        term = jnp.dot(hb[rows[t]], tiles[t], preferred_element_type=F32)
        out[slots[t]] = term.astype(BF16)


def forward_products(turned, lands, places, moved, totals):
    for total in totals:
        total[...] = jnp.zeros_like(total)

    def one_chunk(c, _):
        terms = []
        for j in range(CHUNK):
            t = c * CHUNK + j
            terms.append(jnp.dot(moved[places[t]], turned[t], preferred_element_type=F32))
        for j in range(0, CHUNK, LANES):
            spots = [lands[c * CHUNK + j + i] for i in range(LANES)]
            held = [totals[i][spots[i]] + terms[j + i] for i in range(LANES)]
            for i in range(LANES):
                totals[i][spots[i]] = held[i]
        return 0

    lax.fori_loop(0, turned.shape[0] // CHUNK, one_chunk, 0)


def gathered(totals, r):
    value = totals[0][r]
    for total in totals[1:]:
        value = value + total[r]
    return value


def start_kernel(step, rows_of, peers, cap, col_blocks, count, rows_in, cols_in, tiles, step_in, mask_in, cot_in,
                 held, dy, rhs, slots, places, lands, rows, out, cols, dual_step, dual_mask, cot_y, hb, filled,
                 taken, sems, small):
    tile_slots, side, _ = tiles.shape
    chunks = tile_slots // CHUNK
    minor = [
        pltpu.make_async_copy(src, dst, small.at[i])
        for i, (src, dst) in enumerate((
            (rows_in, rows), (cols_in, cols), (step_in, dual_step), (mask_in.at[step], dual_mask),
            (cot_in, cot_y),
        ))
    ]
    for copy in minor:
        copy.start()

    def tile_copy(c):
        at = pl.ds(c * CHUNK, CHUNK)
        return pltpu.make_async_copy(tiles.at[at], held.at[at], sems.at[c])

    for c in range(chunks):
        tile_copy(c).start()
    for copy in minor:
        copy.wait()
    dy[...] = dual_mask[rows_of].astype(F32) * cot_y[rows_of]

    def h_into(at, h):
        rhs[:, at] = -h

    scaled_blocks(side, dy, dual_step, hb, h_into)

    def clear(o, _):
        filled[o] = 0
        return 0

    lax.fori_loop(0, peers, clear, 0)

    def clear_slot(s, _):
        taken[s] = 0
        return 0

    lax.fori_loop(0, peers * cap, clear_slot, 0)
    lane = lax.broadcasted_iota(I32, out.shape[1:], 1)

    def place_tile(t, plan):
        col = cols[t]
        owner = col // col_blocks
        live = t < count[0]
        rank = filled[owner]
        slot = owner * cap + rank
        slots[t] = jnp.where(live, slot, -1)
        lands[t] = jnp.where(live, rows[t], hb.shape[0])

        @pl.when(live)
        def _():
            filled[owner] = rank + 1
            taken[slot] = 1

        return jnp.where((lane == slot) & live, col - owner * col_blocks, plan)

    plan = lax.fori_loop(0, tile_slots, place_tile, jnp.full(out.shape[1:], -1, I32))
    plan = plan.astype(BF16)
    for p in range(peers):
        out[p * (cap + 1) + cap] = plan
    spare = lax.fori_loop(0, peers * cap, lambda s, best: jnp.where(taken[s] == 0, s, best), 0)

    def settle(t, _):
        slot = jnp.where(slots[t] < 0, spare, slots[t])
        slots[t] = slot
        places[t] = slot + slot // cap
        return 0

    lax.fori_loop(0, tile_slots, settle, 0)

    def one_chunk(c, _):
        tile_copy(c).wait()
        transpose_products(c * CHUNK, CHUNK, held, rows, places, hb, out)
        return 0

    lax.fori_loop(0, chunks, one_chunk, 0)


def second_kernel(step, rows_of, rows, slots, held, dual_step, dual_mask, cot_y, turned, dy, rhs, out, hb):
    side = held.shape[1]
    dy[...] = dual_mask[step, rows_of].astype(F32) * cot_y[rows_of]

    def h_into(at, h):
        rhs[:, at] = -h

    scaled_blocks(side, dy, dual_step, hb, h_into)

    def one_chunk(c, _):
        transpose_products(c * CHUNK, CHUNK, held, rows, slots, hb, out)
        for j in range(CHUNK):
            turned[c * CHUNK + j] = held[c * CHUNK + j].T
        return 0

    lax.fori_loop(0, held.shape[0] // CHUNK, one_chunk, 0)


def primal_kernel(step, rows_of, first, plan_in, cap, *refs):
    refs = list(refs)
    wants = None if plan_in else refs.pop(0)
    primal_mask, primal_step, x, spent, got, new_x, new_spent, out = refs[:8]
    rest = refs[8:]
    if plan_in:
        wants = rest.pop(0)
    moved, totals = rest[0], rest[1:1 + LANES]
    _, batch, side = out.shape
    blocks = new_x.shape[1] // side
    slots = out.shape[0]
    peers = slots // cap
    stride = got.shape[0] // peers
    if plan_in:
        whole, wide, sem = rest[1 + LANES:]
        me = lax.axis_index("rb")
        for p in range(peers):
            plan = got[p * stride + cap][0:1].astype(F32)
            whole[pl.ds(p, 1)] = jnp.where(plan < 0.0, float(blocks), plan).astype(I32)
        copy = pltpu.make_async_copy(whole, wide, sem)
        copy.start()
    for total in totals:
        total[...] = jnp.zeros_like(total)
    if plan_in:
        copy.wait()

        def note(p, _):
            for s in range(cap):
                wants[p * cap + s] = wide[p, me * cap + s]
            return 0

        lax.fori_loop(0, peers, note, 0)
    for s in range(0, slots, LANES):
        spots = [wants[s + i] for i in range(LANES)]
        parts = [got[(s + i) // cap * stride + (s + i) % cap].astype(F32) for i in range(LANES)]
        held = [totals[i][spots[i]] + parts[i] for i in range(LANES)]
        for i in range(LANES):
            totals[i][spots[i]] = held[i]
    for c in range(blocks):
        at = pl.ds(c * side, side)
        u = gathered(totals, c)
        state = x[rows_of, at] if first else x[:, at]
        dx = primal_mask[step, rows_of, at].astype(F32) * (state + 2.0 * u)
        q = primal_step[:, at] * dx
        new_x[:, at] = dx - u
        new_spent[:, at] = -q if first else spent[:, at] - q
        moved[c] = q.astype(BF16)
    moved[blocks] = jnp.zeros(moved.shape[1:], BF16)
    for s in range(0, slots, 2 * LANES):
        values = [moved[wants[s + i]] for i in range(2 * LANES)]
        for i in range(2 * LANES):
            out[s + i] = values[i]


def middle_kernel(step, rows_of, rows, lands, slots, held, turned, dual_step, dual_mask, moved, dy, rhs,
                  new_dy, new_rhs, out, hb, *totals):
    side = held.shape[1]
    forward_products(turned, lands, slots, moved, totals)
    for r in range(hb.shape[0]):
        at = pl.ds(r * side, side)
        new_dy[:, at] = dual_mask[step, rows_of, at].astype(F32) * (dy[:, at] - gathered(totals, r))

    def h_into(at, h):
        new_rhs[:, at] = rhs[:, at] - h

    scaled_blocks(side, new_dy, dual_step, hb, h_into)

    def one_chunk(c, _):
        transpose_products(c * CHUNK, CHUNK, held, rows, slots, hb, out)
        return 0

    lax.fori_loop(0, held.shape[0] // CHUNK, one_chunk, 0)


def last_kernel(lands, slots, turned, moved, dy, new_y, *totals):
    side = turned.shape[1]
    forward_products(turned, lands, slots, moved, totals)
    for r in range(totals[0].shape[0] - 1):
        at = pl.ds(r * side, side)
        new_y[:, at] = dy[:, at] - gathered(totals, r)


def on_device(tiles, tile_rows, tile_cols, tile_counts, dual_step, primal_step, primal_mask, dual_mask, cot_x, cot_y):
    peers = lax.axis_size("rb")
    tile_slots, side, _ = tiles.shape
    whole_batch = cot_x.shape[0]
    batch = whole_batch // HALVES
    row_blocks = dual_step.shape[0] // side
    col_blocks = primal_step.shape[0] // side
    cap = max(2, (tile_slots + peers - 1) // peers)
    slots_all = peers * cap
    steps = primal_mask.shape[0]
    dual_step = dual_step.reshape(1, -1)
    primal_step = primal_step.reshape(1, -1)
    y_shape = shape((batch, cot_y.shape[1]), F32)
    x_shape = shape((batch, cot_x.shape[1]), F32)
    slot_set = shape((slots_all, batch, side), BF16)
    per_tile = shape((tile_slots,), I32)
    hb_scratch = pltpu.VMEM((row_blocks, batch, side), BF16)
    row_totals = [pltpu.VMEM((row_blocks + 1, batch, side), F32)] * LANES
    col_totals = [pltpu.VMEM((col_blocks + 1, batch, side), F32)] * LANES
    moved_scratch = pltpu.VMEM((col_blocks + 1, batch, side), BF16)
    tile_bytes = tiles.size * 2

    def swap(array):
        return lax.all_to_all(array, "rb", 0, 0, tiled=True)

    def rows_of(half):
        return slice(half * batch, (half + 1) * batch)

    step = steps - 1
    held, dy, rhs, slots, places, lands, rows, sent = pl.pallas_call(
        functools.partial(start_kernel, step, rows_of(0), peers, cap, col_blocks),
        out_shape=(
            pltpu.VMEM(tiles.shape, BF16), y_shape, y_shape, per_tile, per_tile, per_tile, per_tile,
            shape((peers * (cap + 1), batch, side), BF16),
        ),
        in_specs=[SM] + [HBM] * 6,
        out_specs=(VM, VM, VM, SM, SM, SM, SM, VM),
        scratch_shapes=[
            pltpu.SMEM((tile_slots,), I32), pltpu.VMEM(dual_step.shape, F32),
            pltpu.VMEM(cot_y.shape, I32), pltpu.VMEM(cot_y.shape, F32), hb_scratch, pltpu.SMEM((peers,), I32),
            pltpu.SMEM((slots_all,), I32), pltpu.SemaphoreType.DMA((tile_slots // CHUNK,)),
            pltpu.SemaphoreType.DMA((5,)),
        ],
        compiler_params=PARAMS,
        cost_estimate=cost(2 * tile_bytes),
        name="start",
    )(tile_counts, *(
        pltpu.with_memory_space_constraint(array, pltpu.HBM)
        for array in (tile_rows, tile_cols, tiles, dual_step, dual_mask, cot_y)
    ))
    state_dy, state_rhs, got = [dy], [rhs], [swap(sent)]
    turned = None
    for half in range(1, HALVES):
        turned, dy, rhs, sent = pl.pallas_call(
            functools.partial(second_kernel, step, rows_of(half)),
            out_shape=(pltpu.VMEM(tiles.shape, BF16), y_shape, y_shape, slot_set),
            in_specs=[SM, SM] + [VM] * 4,
            out_specs=(VM,) * 4,
            scratch_shapes=[hb_scratch],
            compiler_params=PARAMS,
            cost_estimate=cost(2 * tile_bytes),
            name="second",
        )(rows, slots, held, dual_step, dual_mask, cot_y)
        state_dy.append(dy)
        state_rhs.append(rhs)
        got.append(swap(sent))
    state_x, spent, wants = [cot_x] * HALVES, [cot_x] * HALVES, None
    while True:
        moved = []
        for half in range(HALVES):
            first = step == steps - 1
            plan_in = wants is None
            outs = (x_shape, x_shape, slot_set)
            specs = (VM,) * 3
            scratch = [moved_scratch] + col_totals
            if plan_in:
                outs += (shape((slots_all,), I32),)
                specs += (SM,)
                scratch += [
                    pltpu.VMEM((peers, side), I32), pltpu.SMEM((peers, side), I32), pltpu.SemaphoreType.DMA,
                ]
            results = pl.pallas_call(
                functools.partial(primal_kernel, step, rows_of(half), first, plan_in, cap),
                out_shape=outs,
                in_specs=([] if plan_in else [SM]) + [VM] * 5,
                out_specs=specs,
                scratch_shapes=scratch,
                compiler_params=PARAMS,
                cost_estimate=cost(1 << 22),
                name="primal_plan" if plan_in else "primal",
            )(*([] if plan_in else [wants]), primal_mask, primal_step, state_x[half], spent[half], got[half])
            state_x[half], spent[half], sent = results[:3]
            if plan_in:
                wants = results[3]
            moved.append(swap(sent))
        if step == 0:
            break
        step -= 1
        for half in range(HALVES):
            state_dy[half], state_rhs[half], sent = pl.pallas_call(
                functools.partial(middle_kernel, step, rows_of(half)),
                out_shape=(y_shape, y_shape, slot_set),
                in_specs=[SM] * 3 + [VM] * 7,
                out_specs=(VM,) * 3,
                scratch_shapes=[hb_scratch] + row_totals,
                compiler_params=PARAMS,
                cost_estimate=cost(2 * tile_bytes),
                name="middle",
            )(rows, lands, slots, held, turned, dual_step, dual_mask, moved[half], state_dy[half], state_rhs[half])
            got[half] = swap(sent)
    state_y = []
    for half in range(HALVES):
        state_y.append(
            pl.pallas_call(
                last_kernel,
                out_shape=y_shape,
                in_specs=[SM] * 2 + [VM] * 3,
                out_specs=VM,
                scratch_shapes=row_totals,
                compiler_params=PARAMS,
                cost_estimate=cost(tile_bytes),
                name="last",
            )(lands, slots, turned, moved[half], state_dy[half])
        )
    return tuple(jnp.concatenate(parts, axis=0) for parts in (spent, state_rhs, state_x, state_y))


def solution(mesh):
    rb = ("grp", "rb")
    return jax.shard_map(
        on_device,
        mesh=mesh,
        in_specs=(
            P(rb, None, None), P(rb), P(rb), P(rb), P(rb), P(rb),
            P(None, "grp", "rb"), P(None, "grp", "rb"), P("grp", "rb"), P("grp", "rb"),
        ),
        out_specs=(P("grp", "rb"),) * 4,
        check_vma=False,
    )
```

time: 222 us -> 292 us (1.32)
  blocking collectives: 162 us -> 0 us
  starting transfers between devices: 0 us -> 77.5 us
  waiting for transfers between devices: 0 us -> 59.3 us
  local copies, waits for them, and re-layouts: 16.7 us -> 72.5 us
  Pallas kernels: 41.7 us -> 77.4 us
    all_to_all x16 -> x0, blocking collectives: 162 us -> none  [swap(): lax.all_to_all(array, 'rb', 0, 0, axis_index_groups=groups, tiled=True)]
    all_to_all x0 -> x16, starting transfers between devices: none -> 77.5 us  [swap(): return lax.all_to_all(array, 'rb', 0, 0, tiled=True)]
    all_to_all x0 -> x16, waiting for transfers between devices: none -> 59.3 us  [swap(): return lax.all_to_all(array, 'rb', 0, 0, tiled=True)]
    unnamed x28 -> x46, local copies, waits for them, and re-layouts: 16.7 us -> 72.5 us
    pallas_call x16, Pallas kernels: 37.7 us -> 70.7 us  [the longest x6 40.8 us: on_device(): pl.pallas_call(functools.partial(middle_kernel, step, rows_of(half)), out...]
    pallas_call x1 -> x2, Pallas kernels: 3.99 us -> 6.67 us  [on_device(): pl.pallas_call(last_kernel, out_shape=y_shape, in_specs=[SM] * 2 + [VM] *...]
  transfers between devices with their start and end apart: 0 -> 16, of which waited for: 0 -> 8; matrix products, arithmetic and copies ran while one was open for 0% -> 0% of each run, Pallas kernels for 0% -> 21%
where the time goes in v3:
time: 292 us; the launch traced here: 290 us
  starting transfers between devices  77.5 us (27%)
  Pallas kernels  77.4 us (27%)
  local copies, waits for them, and re-layouts  72.5 us (25%)
  waiting for transfers between devices  59.3 us (20%)
    all_to_all x16, starting transfers between devices, swap(): return lax.all_to_all(array, 'rb', 0, 0, tiled=True)  77.5 us
    unnamed x46, local copies, waits for them, and re-layouts  72.5 us
    all_to_all x16, waiting for transfers between devices, swap(): return lax.all_to_all(array, 'rb', 0, 0, tiled=True)  59.3 us
    pallas_call x6, Pallas kernels, on_device(): pl.pallas_call(functools.partial(middle_kernel, step, rows_of(half)), out...  40.8 us
    pallas_call x1, Pallas kernels, on_device(): pl.pallas_call(functools.partial(start_kernel, step, rows_of(0), peers, c...  12.6 us
    pallas_call x8, Pallas kernels, on_device(): pl.pallas_call(functools.partial(primal_kernel, step, rows_of(half), firs...  12.5 us
    pallas_call x2, Pallas kernels, on_device(): pl.pallas_call(last_kernel, out_shape=y_shape, in_specs=[SM] * 2 + [VM] *...  6.67 us
  transfers between devices with their start and end apart: 16, of which 8 were waited for; matrix products, arithmetic and copies ran while one was open for 0% of the time, Pallas kernels for 21%

profile of v3, /device:TPU:0, one launch (start us, length us, event | category | flops | bytes accessed | tf_op | source)
XLA Modules:
  0.0 290.4 jit_solution(11873921295887094916)
XLA Ops:
  1.4 12.6 %start.1 = (bf16[88,256,256]{2,1,0:T(8,128)(2,1)S(1)}, f32[4,2048]{1,0:T(4,128)S(1)}, f32[4,2048]{1,0:T(4,128)S(1)}, s32[88]{0:T(128)S(1)}, s32[88]{0:T(128)}, /...) custom-call(s32[1]{0:T(128)S(6)} %copy.14.count, s32[88]{0:T(128)} %rows_in.1, s32[88]{0:T(128)} %cols_in.1, ...), custom_call_target="tpu_custom_call" | custom-call | flops 184549376 | bytes 23068672 | tf_op jit(solution)/shard_map/start/pallas_call | solution.py:279
  18.2 7.4 %all-to-all-start = ((bf16[112,4,256]{2,1,0:T(4,128)(2,1)}), bf16[112,4,256]{2,1,0:T(4,128)(2,1)S(1)}, u32[]{:S(2)}, u32[]{:S(2)}) async-start(bf16[112,4,256]{2,1,0:T(4,128)(2,1)} %get-tuple-element.58), calls=%async_computation | async-start | bytes 458752 | tf_op jit(solution)/shard_map/all_to_all | solution.py:273
  29.9 4.8 %second.1 = (bf16[88,256,256]{2,1,0:T(8,128)(2,1)S(1)}, f32[4,2048]{1,0:T(4,128)S(1)}, f32[4,2048]{1,0:T(4,128)S(1)}, bf16[96,4,256]{2,1,0:T(4,128)(2,1)}) custom-call(s32[88]{0:T(128)S(1)} %get-tuple-element.62.rows, s32[88]{0:T(128)S(1)} %get-tuple-element.64.slots, bf16[88,256,256]{2,1,0:T(8,128)(2,1)S(1)} %copy-done.10, f32[1,2048]{1,0:T(1,128)S(1)} %bitcast.11, ...), custom_call_target="tpu_custom_call" | custom-call | flops 184549376 | bytes 23068672 | tf_op jit(solution)/shard_map/second/pallas_call | solution.py:303
  38.9 6.0 %all-to-all-start.7 = ((bf16[96,4,256]{2,1,0:T(4,128)(2,1)}), bf16[96,4,256]{2,1,0:T(4,128)(2,1)S(1)}, u32[]{:S(2)}, u32[]{:S(2)}) async-start(bf16[96,4,256]{2,1,0:T(4,128)(2,1)} %get-tuple-element.84), calls=%async_computation.7 | async-start | bytes 393216 | tf_op jit(solution)/shard_map/all_to_all | solution.py:273
  47.1 6.8 %all-to-all-done.7.refs_5_ = bf16[96,4,256]{2,1,0:T(4,128)(2,1)S(1)} async-done(((bf16[96,4,256]{2,1,0:T(4,128)(2,1)}), bf16[96,4,256]{2,1,0:T(4,128)(2,1)S(1)}, u32[]{:S(2)}, u32[]{:S(2)}) %all-to-all-start.7) | async-done | bytes 196640 | tf_op jit(solution)/shard_map/all_to_all | solution.py:273
  58.9 7.5 %all-to-all-done.1.moved = bf16[96,4,256]{2,1,0:T(4,128)(2,1)S(1)} async-done(((bf16[96,4,256]{2,1,0:T(4,128)(2,1)}), bf16[96,4,256]{2,1,0:T(4,128)(2,1)S(1)}, u32[]{:S(2)}, u32[]{:S(2)}) %all-to-all-start.1) | async-done | bytes 196640 | tf_op jit(solution)/shard_map/all_to_all | solution.py:273
  78.5 6.8 %middle.6 = (f32[4,2048]{1,0:T(4,128)S(1)}, f32[4,2048]{1,0:T(4,128)S(1)}, bf16[96,4,256]{2,1,0:T(4,128)(2,1)}) custom-call(s32[88]{0:T(128)S(1)} %get-tuple-element.62.rows, s32[88]{0:T(128)S(1)} %get-tuple-element.63.lands, s32[88]{0:T(128)S(1)} %get-tuple-element.64.slots, bf16[88,256,256]{2,1,0:T(8,128)(2,1)S(1)} %copy-done.11, ...), custom_call_target="tpu_custom_call" | custom-call | flops 184549376 | bytes 23068672 | tf_op jit(solution)/shard_map/middle/pallas_call | solution.py:349
  85.3 6.0 %all-to-all-start.2 = ((bf16[96,4,256]{2,1,0:T(4,128)(2,1)}), bf16[96,4,256]{2,1,0:T(4,128)(2,1)S(1)}, u32[]{:S(2)}, u32[]{:S(2)}) async-start(bf16[96,4,256]{2,1,0:T(4,128)(2,1)} %get-tuple-element.70), calls=%async_computation.2 | async-start | bytes 393216 | tf_op jit(solution)/shard_map/all_to_all | solution.py:273
  99.8 6.8 %middle.9 = (f32[4,2048]{1,0:T(4,128)S(1)}, f32[4,2048]{1,0:T(4,128)S(1)}, bf16[96,4,256]{2,1,0:T(4,128)(2,1)}) custom-call(s32[88]{0:T(128)S(1)} %get-tuple-element.62.rows, s32[88]{0:T(128)S(1)} %get-tuple-element.63.lands, s32[88]{0:T(128)S(1)} %get-tuple-element.64.slots, bf16[88,256,256]{2,1,0:T(8,128)(2,1)S(1)} %copy-done.12, ...), custom_call_target="tpu_custom_call" | custom-call | flops 184549376 | bytes 23068672 | tf_op jit(solution)/shard_map/middle/pallas_call | solution.py:349
  106.6 6.0 %all-to-all-start.9 = ((bf16[96,4,256]{2,1,0:T(4,128)(2,1)}), bf16[96,4,256]{2,1,0:T(4,128)(2,1)S(1)}, u32[]{:S(2)}, u32[]{:S(2)}) async-start(bf16[96,4,256]{2,1,0:T(4,128)(2,1)} %get-tuple-element.90), calls=%async_computation.9 | async-start | bytes 393216 | tf_op jit(solution)/shard_map/all_to_all | solution.py:273
  114.1 7.5 %all-to-all-done.9.refs_5_ = bf16[96,4,256]{2,1,0:T(4,128)(2,1)S(1)} async-done(((bf16[96,4,256]{2,1,0:T(4,128)(2,1)}), bf16[96,4,256]{2,1,0:T(4,128)(2,1)S(1)}, u32[]{:S(2)}, u32[]{:S(2)}) %all-to-all-start.9) | async-done | bytes 196640 | tf_op jit(solution)/shard_map/all_to_all | solution.py:273
  126.6 7.5 %all-to-all-done.3.moved = bf16[96,4,256]{2,1,0:T(4,128)(2,1)S(1)} async-done(((bf16[96,4,256]{2,1,0:T(4,128)(2,1)}), bf16[96,4,256]{2,1,0:T(4,128)(2,1)S(1)}, u32[]{:S(2)}, u32[]{:S(2)}) %all-to-all-start.3) | async-done | bytes 196640 | tf_op jit(solution)/shard_map/all_to_all | solution.py:273
  146.2 6.8 %middle.7 = (f32[4,2048]{1,0:T(4,128)S(1)}, f32[4,2048]{1,0:T(4,128)S(1)}, bf16[96,4,256]{2,1,0:T(4,128)(2,1)}) custom-call(s32[88]{0:T(128)S(1)} %get-tuple-element.62.rows, s32[88]{0:T(128)S(1)} %get-tuple-element.63.lands, s32[88]{0:T(128)S(1)} %get-tuple-element.64.slots, bf16[88,256,256]{2,1,0:T(8,128)(2,1)S(1)} %copy-done.13, ...), custom_call_target="tpu_custom_call" | custom-call | flops 184549376 | bytes 23068672 | tf_op jit(solution)/shard_map/middle/pallas_call | solution.py:349
  153.0 6.0 %all-to-all-start.4 = ((bf16[96,4,256]{2,1,0:T(4,128)(2,1)}), bf16[96,4,256]{2,1,0:T(4,128)(2,1)S(1)}, u32[]{:S(2)}, u32[]{:S(2)}) async-start(bf16[96,4,256]{2,1,0:T(4,128)(2,1)} %get-tuple-element.76), calls=%async_computation.4 | async-start | bytes 393216 | tf_op jit(solution)/shard_map/all_to_all | solution.py:273
  167.5 6.8 %middle.10 = (f32[4,2048]{1,0:T(4,128)S(1)}, f32[4,2048]{1,0:T(4,128)S(1)}, bf16[96,4,256]{2,1,0:T(4,128)(2,1)}) custom-call(s32[88]{0:T(128)S(1)} %get-tuple-element.62.rows, s32[88]{0:T(128)S(1)} %get-tuple-element.63.lands, s32[88]{0:T(128)S(1)} %get-tuple-element.64.slots, bf16[88,256,256]{2,1,0:T(8,128)(2,1)S(1)} %copy-done.14, ...), custom_call_target="tpu_custom_call" | custom-call | flops 184549376 | bytes 23068672 | tf_op jit(solution)/shard_map/middle/pallas_call | solution.py:349
  174.4 6.0 %all-to-all-start.11 = ((bf16[96,4,256]{2,1,0:T(4,128)(2,1)}), bf16[96,4,256]{2,1,0:T(4,128)(2,1)S(1)}, u32[]{:S(2)}, u32[]{:S(2)}) async-start(bf16[96,4,256]{2,1,0:T(4,128)(2,1)} %get-tuple-element.96), calls=%async_computation.11 | async-start | bytes 393216 | tf_op jit(solution)/shard_map/all_to_all | solution.py:273
  181.9 7.5 %all-to-all-done.11.refs_5_ = bf16[96,4,256]{2,1,0:T(4,128)(2,1)S(1)} async-done(((bf16[96,4,256]{2,1,0:T(4,128)(2,1)}), bf16[96,4,256]{2,1,0:T(4,128)(2,1)S(1)}, u32[]{:S(2)}, u32[]{:S(2)}) %all-to-all-start.11) | async-done | bytes 196640 | tf_op jit(solution)/shard_map/all_to_all | solution.py:273
  194.4 7.5 %all-to-all-done.5.moved = bf16[96,4,256]{2,1,0:T(4,128)(2,1)S(1)} async-done(((bf16[96,4,256]{2,1,0:T(4,128)(2,1)}), bf16[96,4,256]{2,1,0:T(4,128)(2,1)S(1)}, u32[]{:S(2)}, u32[]{:S(2)}) %all-to-all-start.5) | async-done | bytes 196640 | tf_op jit(solution)/shard_map/all_to_all | solution.py:273
  213.9 6.8 %middle.8 = (f32[4,2048]{1,0:T(4,128)S(1)}, f32[4,2048]{1,0:T(4,128)S(1)}, bf16[96,4,256]{2,1,0:T(4,128)(2,1)}) custom-call(s32[88]{0:T(128)S(1)} %get-tuple-element.62.rows, s32[88]{0:T(128)S(1)} %get-tuple-element.63.lands, s32[88]{0:T(128)S(1)} %get-tuple-element.64.slots, bf16[88,256,256]{2,1,0:T(8,128)(2,1)S(1)} %copy-done.15, ...), custom_call_target="tpu_custom_call" | custom-call | flops 184549376 | bytes 23068672 | tf_op jit(solution)/shard_map/middle/pallas_call | solution.py:349
  220.8 6.0 %all-to-all-start.6 = ((bf16[96,4,256]{2,1,0:T(4,128)(2,1)}), bf16[96,4,256]{2,1,0:T(4,128)(2,1)S(1)}, u32[]{:S(2)}, u32[]{:S(2)}) async-start(bf16[96,4,256]{2,1,0:T(4,128)(2,1)} %get-tuple-element.82), calls=%async_computation.6 | async-start | bytes 393216 | tf_op jit(solution)/shard_map/all_to_all | solution.py:273
  235.3 6.8 %middle.11 = (f32[4,2048]{1,0:T(4,128)S(1)}, f32[4,2048]{1,0:T(4,128)S(1)}, bf16[96,4,256]{2,1,0:T(4,128)(2,1)}) custom-call(s32[88]{0:T(128)S(1)} %get-tuple-element.62.rows, s32[88]{0:T(128)S(1)} %get-tuple-element.63.lands, s32[88]{0:T(128)S(1)} %get-tuple-element.64.slots, bf16[88,256,256]{2,1,0:T(8,128)(2,1)S(1)} %copy-done.16, ...), custom_call_target="tpu_custom_call" | custom-call | flops 184549376 | bytes 23068672 | tf_op jit(solution)/shard_map/middle/pallas_call | solution.py:349
  242.1 6.0 %all-to-all-start.13 = ((bf16[96,4,256]{2,1,0:T(4,128)(2,1)}), bf16[96,4,256]{2,1,0:T(4,128)(2,1)S(1)}, u32[]{:S(2)}, u32[]{:S(2)}) async-start(bf16[96,4,256]{2,1,0:T(4,128)(2,1)} %get-tuple-element.102), calls=%async_computation.13 | async-start | bytes 393216 | tf_op jit(solution)/shard_map/all_to_all | solution.py:273
  249.6 7.5 %all-to-all-done.13.refs_5_ = bf16[96,4,256]{2,1,0:T(4,128)(2,1)S(1)} async-done(((bf16[96,4,256]{2,1,0:T(4,128)(2,1)}), bf16[96,4,256]{2,1,0:T(4,128)(2,1)S(1)}, u32[]{:S(2)}, u32[]{:S(2)}) %all-to-all-start.13) | async-done | bytes 196640 | tf_op jit(solution)/shard_map/all_to_all | solution.py:273
  262.1 7.5 %all-to-all-done.14.moved = bf16[96,4,256]{2,1,0:T(4,128)(2,1)S(1)} async-done(((bf16[96,4,256]{2,1,0:T(4,128)(2,1)}), bf16[96,4,256]{2,1,0:T(4,128)(2,1)S(1)}, u32[]{:S(2)}, u32[]{:S(2)}) %all-to-all-start.14) | async-done | bytes 196640 | tf_op jit(solution)/shard_map/all_to_all | solution.py:273
  (75 shorter events, 121.9 us)
Async XLA Ops:
  0.6 24.9 %copy-start.18 = (s32[4,8,2048]{2,1,0:T(8,128)S(1)}, s32[4,8,2048]{2,1,0:T(8,128)}, u32[]{:S(2)}) copy-start(s32[4,8,2048]{2,1,0:T(8,128)} %dual_mask.13) | copy-start | bytes 786436
  0.6 24.9 %copy-start.22 = (f32[8,2048]{1,0:T(8,128)S(1)}, f32[8,2048]{1,0:T(8,128)}, u32[]{:S(2)}) copy-start(f32[8,2048]{1,0:T(8,128)} %cot_y.1) | copy-start | bytes 196612
  0.7 24.9 %copy-start.21 = (f32[2048]{0:T(1024)S(1)}, f32[2048]{0:T(1024)}, u32[]{:S(2)}) copy-start(f32[2048]{0:T(1024)} %param.14) | copy-start | bytes 24580
  1.4 43.5 %copy-start.17 = (s32[4,8,3072]{2,1,0:T(8,128)S(1)}, s32[4,8,3072]{2,1,0:T(8,128)}, u32[]{:S(2)}) copy-start(s32[4,8,3072]{2,1,0:T(8,128)} %refs_1_.13) | copy-start | bytes 1179652
  1.4 43.5 %copy-start.19 = (f32[8,3072]{1,0:T(8,128)S(1)}, f32[8,3072]{1,0:T(8,128)}, u32[]{:S(2)}) copy-start(f32[8,3072]{1,0:T(8,128)} %refs_4_.1) | copy-start | bytes 294916
  1.4 43.5 %copy-start.20 = (f32[3072]{0:T(1024)S(1)}, f32[3072]{0:T(1024)}, u32[]{:S(2)}) copy-start(f32[3072]{0:T(1024)} %param.15) | copy-start | bytes 36868
  18.2 20.7 %all-to-all-start = ((bf16[112,4,256]{2,1,0:T(4,128)(2,1)}), bf16[112,4,256]{2,1,0:T(4,128)(2,1)S(1)}, u32[]{:S(2)}, u32[]{:S(2)}) async-start(bf16[112,4,256]{2,1,0:T(4,128)(2,1)} %get-tuple-element.58), calls=%async_computation | async-start | bytes 458752 | tf_op jit(solution)/shard_map/all_to_all | solution.py:273
  25.6 4.3 %copy-start.10 = (bf16[88,256,256]{2,1,0:T(8,128)(2,1)S(1)}, bf16[88,256,256]{2,1,0:T(8,128)(2,1)}, u32[]{:S(2)}) copy-start(bf16[88,256,256]{2,1,0:T(8,128)(2,1)} %copy-done.9) | copy-start | bytes 34603012
  38.9 15.0 %all-to-all-start.7 = ((bf16[96,4,256]{2,1,0:T(4,128)(2,1)}), bf16[96,4,256]{2,1,0:T(4,128)(2,1)S(1)}, u32[]{:S(2)}, u32[]{:S(2)}) async-start(bf16[96,4,256]{2,1,0:T(4,128)(2,1)} %get-tuple-element.84), calls=%async_computation.7 | async-start | bytes 393216 | tf_op jit(solution)/shard_map/all_to_all | solution.py:273
  53.9 12.5 %all-to-all-start.1 = ((bf16[96,4,256]{2,1,0:T(4,128)(2,1)}), bf16[96,4,256]{2,1,0:T(4,128)(2,1)S(1)}, u32[]{:S(2)}, u32[]{:S(2)}) async-start(bf16[96,4,256]{2,1,0:T(4,128)(2,1)} %get-tuple-element.67), calls=%async_computation.1 | async-start | bytes 393216 | tf_op jit(solution)/shard_map/all_to_all | solution.py:273
  66.4 18.9 %all-to-all-start.8 = ((bf16[96,4,256]{2,1,0:T(4,128)(2,1)}), bf16[96,4,256]{2,1,0:T(4,128)(2,1)S(1)}, u32[]{:S(2)}, u32[]{:S(2)}) async-start(bf16[96,4,256]{2,1,0:T(4,128)(2,1)} %get-tuple-element.87), calls=%async_computation.8 | async-start | bytes 393216 | tf_op jit(solution)/shard_map/all_to_all | solution.py:273
  85.3 21.3 %all-to-all-start.2 = ((bf16[96,4,256]{2,1,0:T(4,128)(2,1)}), bf16[96,4,256]{2,1,0:T(4,128)(2,1)S(1)}, u32[]{:S(2)}, u32[]{:S(2)}) async-start(bf16[96,4,256]{2,1,0:T(4,128)(2,1)} %get-tuple-element.70), calls=%async_computation.2 | async-start | bytes 393216 | tf_op jit(solution)/shard_map/all_to_all | solution.py:273
  91.2 4.3 %copy-start.2 = (bf16[88,256,256]{2,1,0:T(8,128)(2,1)S(1)}, bf16[88,256,256]{2,1,0:T(8,128)(2,1)}, u32[]{:S(2)}) copy-start(bf16[88,256,256]{2,1,0:T(8,128)(2,1)} %copy-done) | copy-start | bytes 34603012
  106.6 15.0 %all-to-all-start.9 = ((bf16[96,4,256]{2,1,0:T(4,128)(2,1)}), bf16[96,4,256]{2,1,0:T(4,128)(2,1)S(1)}, u32[]{:S(2)}, u32[]{:S(2)}) async-start(bf16[96,4,256]{2,1,0:T(4,128)(2,1)} %get-tuple-element.90), calls=%async_computation.9 | async-start | bytes 393216 | tf_op jit(solution)/shard_map/all_to_all | solution.py:273
  121.6 12.5 %all-to-all-start.3 = ((bf16[96,4,256]{2,1,0:T(4,128)(2,1)}), bf16[96,4,256]{2,1,0:T(4,128)(2,1)S(1)}, u32[]{:S(2)}, u32[]{:S(2)}) async-start(bf16[96,4,256]{2,1,0:T(4,128)(2,1)} %get-tuple-element.73), calls=%async_computation.3 | async-start | bytes 393216 | tf_op jit(solution)/shard_map/all_to_all | solution.py:273
  134.1 18.9 %all-to-all-start.10 = ((bf16[96,4,256]{2,1,0:T(4,128)(2,1)}), bf16[96,4,256]{2,1,0:T(4,128)(2,1)S(1)}, u32[]{:S(2)}, u32[]{:S(2)}) async-start(bf16[96,4,256]{2,1,0:T(4,128)(2,1)} %get-tuple-element.93), calls=%async_computation.10 | async-start | bytes 393216 | tf_op jit(solution)/shard_map/all_to_all | solution.py:273
  153.0 21.3 %all-to-all-start.4 = ((bf16[96,4,256]{2,1,0:T(4,128)(2,1)}), bf16[96,4,256]{2,1,0:T(4,128)(2,1)S(1)}, u32[]{:S(2)}, u32[]{:S(2)}) async-start(bf16[96,4,256]{2,1,0:T(4,128)(2,1)} %get-tuple-element.76), calls=%async_computation.4 | async-start | bytes 393216 | tf_op jit(solution)/shard_map/all_to_all | solution.py:273
  174.4 15.0 %all-to-all-start.11 = ((bf16[96,4,256]{2,1,0:T(4,128)(2,1)}), bf16[96,4,256]{2,1,0:T(4,128)(2,1)S(1)}, u32[]{:S(2)}, u32[]{:S(2)}) async-start(bf16[96,4,256]{2,1,0:T(4,128)(2,1)} %get-tuple-element.96), calls=%async_computation.11 | async-start | bytes 393216 | tf_op jit(solution)/shard_map/all_to_all | solution.py:273
  189.4 12.5 %all-to-all-start.5 = ((bf16[96,4,256]{2,1,0:T(4,128)(2,1)}), bf16[96,4,256]{2,1,0:T(4,128)(2,1)S(1)}, u32[]{:S(2)}, u32[]{:S(2)}) async-start(bf16[96,4,256]{2,1,0:T(4,128)(2,1)} %get-tuple-element.79), calls=%async_computation.5 | async-start | bytes 393216 | tf_op jit(solution)/shard_map/all_to_all | solution.py:273
  201.9 18.9 %all-to-all-start.12 = ((bf16[96,4,256]{2,1,0:T(4,128)(2,1)}), bf16[96,4,256]{2,1,0:T(4,128)(2,1)S(1)}, u32[]{:S(2)}, u32[]{:S(2)}) async-start(bf16[96,4,256]{2,1,0:T(4,128)(2,1)} %get-tuple-element.99), calls=%async_computation.12 | async-start | bytes 393216 | tf_op jit(solution)/shard_map/all_to_all | solution.py:273
  220.8 21.3 %all-to-all-start.6 = ((bf16[96,4,256]{2,1,0:T(4,128)(2,1)}), bf16[96,4,256]{2,1,0:T(4,128)(2,1)S(1)}, u32[]{:S(2)}, u32[]{:S(2)}) async-start(bf16[96,4,256]{2,1,0:T(4,128)(2,1)} %get-tuple-element.82), calls=%async_computation.6 | async-start | bytes 393216 | tf_op jit(solution)/shard_map/all_to_all | solution.py:273
  242.1 15.0 %all-to-all-start.13 = ((bf16[96,4,256]{2,1,0:T(4,128)(2,1)}), bf16[96,4,256]{2,1,0:T(4,128)(2,1)S(1)}, u32[]{:S(2)}, u32[]{:S(2)}) async-start(bf16[96,4,256]{2,1,0:T(4,128)(2,1)} %get-tuple-element.102), calls=%async_computation.13 | async-start | bytes 393216 | tf_op jit(solution)/shard_map/all_to_all | solution.py:273
  257.1 12.5 %all-to-all-start.14 = ((bf16[96,4,256]{2,1,0:T(4,128)(2,1)}), bf16[96,4,256]{2,1,0:T(4,128)(2,1)S(1)}, u32[]{:S(2)}, u32[]{:S(2)}) async-start(bf16[96,4,256]{2,1,0:T(4,128)(2,1)} %get-tuple-element.108), calls=%async_computation.14 | async-start | bytes 393216 | tf_op jit(solution)/shard_map/all_to_all | solution.py:273
  269.6 12.5 %all-to-all-start.15 = ((bf16[96,4,256]{2,1,0:T(4,128)(2,1)}), bf16[96,4,256]{2,1,0:T(4,128)(2,1)S(1)}, u32[]{:S(2)}, u32[]{:S(2)}) async-start(bf16[96,4,256]{2,1,0:T(4,128)(2,1)} %get-tuple-element.110), calls=%async_computation.15 | async-start | bytes 393216 | tf_op jit(solution)/shard_map/all_to_all | solution.py:273
  (15 other events, 64.0 us)

commit v4 on v1

v4 whole, which is shorter than its diff:
```python
import functools

import jax
import jax.numpy as jnp
from jax import lax
from jax.experimental import pallas as pl
from jax.experimental.pallas import tpu as pltpu
from jax.sharding import PartitionSpec as P

QUAD = 4
CHUNK = 8
LANES = 4
VM = pl.BlockSpec(memory_space=pltpu.VMEM)
SM = pl.BlockSpec(memory_space=pltpu.SMEM)
HBM = pl.BlockSpec(memory_space=pltpu.HBM)
PARAMS = pltpu.CompilerParams(vmem_limit_bytes=12 * 1024 * 1024)
F32, BF16, I32 = jnp.float32, jnp.bfloat16, jnp.int32


def shape(dims, dtype):
    return jax.ShapeDtypeStruct(dims, dtype)


def cost(moved):
    return pl.CostEstimate(flops=moved * 8, bytes_accessed=moved, transcendentals=0)


def scaled_blocks(side, dy, dual_step, hb, h_into):
    for r in range(hb.shape[0]):
        at = pl.ds(r * side, side)
        h = dual_step[:, at] * dy[:, at]
        hb[r] = h.astype(BF16)
        h_into(at, h)


def transpose_products(base, tile_of, row_of, tiles, hb, outs):
    per = outs[0].shape[0]
    for x, out in enumerate(outs):
        for s in range(per):
            slot = base + x * per + s
            out[s] = jnp.dot(hb[row_of[slot]], tiles[tile_of[slot]], preferred_element_type=F32).astype(BF16)


def forward_products(base, tile_of, land_of, turned, moved, totals):
    per = moved[0].shape[0]
    for total in totals:
        total[...] = jnp.zeros_like(total)
    for x, part in enumerate(moved):
        first = base + x * per
        terms = [jnp.dot(part[s], turned[tile_of[first + s]], preferred_element_type=F32) for s in range(per)]
        for s in range(0, per, LANES):
            several = range(min(LANES, per - s))
            spots = [land_of[first + s + i] for i in several]
            held = [totals[i][spots[i]] + terms[s + i] for i in several]
            for i in several:
                totals[i][spots[i]] = held[i]


def gathered(totals, r):
    value = totals[0][r]
    for total in totals[1:]:
        value = value + total[r]
    return value


def start_kernel(step, peers, cap, col_blocks, count, rows_in, cols_in, tiles, step_in, mask_in, cot_in,
                 held, dy, rhs, hb, tile_of, row_of, land_of, wants, o0, o1, o2, o3,
                 rows, cols, dual_step, dual_mask, cot_y, filled, sems, small):
    tile_slots, side, _ = tiles.shape
    group = peers // QUAD
    half = group // 2
    chunks = tile_slots // CHUNK
    minor = [
        pltpu.make_async_copy(src, dst, small.at[i])
        for i, (src, dst) in enumerate((
            (cols_in, cols), (rows_in, rows), (step_in, dual_step), (mask_in.at[step], dual_mask), (cot_in, cot_y),
        ))
    ]
    for copy in minor:
        copy.start()

    def tile_copy(c):
        at = pl.ds(c * CHUNK, CHUNK)
        return pltpu.make_async_copy(tiles.at[at], held.at[at], sems.at[c])

    for c in range(chunks):
        tile_copy(c).start()
    for o in range(peers):
        filled[o] = 0
    for s in range(tile_of.shape[0]):
        tile_of[s] = 0
        row_of[s] = 0
        land_of[s] = hb.shape[0]
    for x in range(QUAD):
        for s in range(group * cap):
            wants[x, s] = col_blocks
    for copy in minor:
        copy.wait()
    me = lax.axis_index("rb").astype(I32)
    scale = (1 << 19) // col_blocks + 1

    def place_tile(t, _):
        col = cols[t]
        owner = (col * scale) >> 19
        rank = filled[owner]
        filled[owner] = rank + 1
        apart = owner ^ me
        high, quad = apart // QUAD, apart % QUAD
        place = high * cap + rank
        near = jnp.where(high < half, 1, 0)
        slot = (near * QUAD + quad) * (half * cap) + place - (1 - near) * (half * cap)
        tile_of[slot] = t
        row_of[slot] = rows[t]
        land_of[slot] = rows[t]
        wants[quad, place] = col - owner * col_blocks
        return 0

    lax.fori_loop(0, count[0], place_tile, 0)
    dy[...] = dual_mask[...].astype(F32) * cot_y[...]

    def h_into(at, h):
        rhs[:, at] = -h

    scaled_blocks(side, dy, dual_step, hb, h_into)
    for c in range(chunks):
        tile_copy(c).wait()
    transpose_products(0, tile_of, row_of, held, hb, (o0, o1, o2, o3))


def turn_kernel(held, turned):
    def one_chunk(c, _):
        for j in range(CHUNK):
            turned[c * CHUNK + j] = held[c * CHUNK + j].T
        return 0

    lax.fori_loop(0, held.shape[0] // CHUNK, one_chunk, 0)


def near_product_kernel(tile_of, row_of, held, hb, o0, o1, o2, o3):
    transpose_products(tile_of.shape[0] // 2, tile_of, row_of, held, hb, (o0, o1, o2, o3))


def sum_kernel(first_high, cap, wants, got1, got2, got3, a0, a1, a2, a3, *rest):
    parts = (a0, a1, a2, a3)
    half = a0.shape[0] // cap
    outs, totals = rest[:half], rest[half:]
    for total in totals:
        total[...] = jnp.zeros_like(total)
    for r in range(cap):
        for pair in range(QUAD // 2):
            jobs = []
            for h in range(half):
                for side in range(2):
                    x = 2 * pair + side
                    want = (wants, got1, got2, got3)[x]
                    spot = want[x, (first_high + h) * cap + r]
                    jobs.append((totals[2 * h + side], spot, parts[x][h * cap + r].astype(F32)))
            values = [total[spot] + part for total, spot, part in jobs]
            for (total, spot, _), value in zip(jobs, values):
                total[spot] = value
    for h, out in enumerate(outs):
        for c in range(out.shape[0]):
            out[c] = (totals[2 * h][c] + totals[2 * h + 1][c]).astype(out.dtype)


def primal_kernel(step, first, primal_mask, primal_step, x, spent, *refs):
    parts, (new_x, new_spent, out) = refs[:-3], refs[-3:]
    blocks, _, side = out.shape
    for c in range(blocks):
        at = pl.ds(c * side, side)
        u = parts[0][c]
        for part in parts[1:]:
            u = u + part[c].astype(F32)
        dx = primal_mask[step, :, at].astype(F32) * (x[:, at] + 2.0 * u)
        q = primal_step[:, at] * dx
        new_x[:, at] = dx - u
        new_spent[:, at] = -q if first else spent[:, at] - q
        out[c] = q.astype(BF16)


def pick_kernel(first_high, cap, wants, got1, got2, got3, *refs):
    blocks, outs = refs[:-QUAD], refs[-QUAD:]
    last = blocks[0].shape[0] - 1
    for x, out in enumerate(outs):
        want = (wants, got1, got2, got3)[x]
        values = [
            blocks[h][jnp.minimum(want[x, (first_high + h) * cap + r], last)]
            for h in range(len(blocks))
            for r in range(cap)
        ]
        for s, value in enumerate(values):
            out[s] = value


def near_forward_kernel(tile_of, land_of, turned, m0, m1, m2, m3, out, *totals):
    forward_products(tile_of.shape[0] // 2, tile_of, land_of, turned, (m0, m1, m2, m3), totals)
    for r in range(out.shape[0]):
        out[r] = gathered(totals, r)


def middle_kernel(step, tile_of, row_of, land_of, held, turned, dual_step, dual_mask, part, dy, rhs, m0, m1, m2, m3,
                  new_dy, new_rhs, hb, o0, o1, o2, o3, *totals):
    side = held.shape[1]
    forward_products(0, tile_of, land_of, turned, (m0, m1, m2, m3), totals)
    for r in range(hb.shape[0]):
        at = pl.ds(r * side, side)
        v = part[r] + gathered(totals, r)
        new_dy[:, at] = dual_mask[step, :, at].astype(F32) * (dy[:, at] - v)

    def h_into(at, h):
        new_rhs[:, at] = rhs[:, at] - h

    scaled_blocks(side, new_dy, dual_step, hb, h_into)
    transpose_products(0, tile_of, row_of, held, hb, (o0, o1, o2, o3))


def last_kernel(tile_of, land_of, turned, part, dy, m0, m1, m2, m3, new_y, *totals):
    side = turned.shape[1]
    forward_products(0, tile_of, land_of, turned, (m0, m1, m2, m3), totals)
    for r in range(part.shape[0]):
        at = pl.ds(r * side, side)
        new_y[:, at] = dy[:, at] - (part[r] + gathered(totals, r))


def on_device(tiles, tile_rows, tile_cols, tile_counts, dual_step, primal_step, primal_mask, dual_mask, cot_x, cot_y):
    peers = lax.axis_size("rb")
    tile_slots, side, _ = tiles.shape
    batch = cot_x.shape[0]
    row_blocks = dual_step.shape[0] // side
    col_blocks = primal_step.shape[0] // side
    cap = max(2, (tile_slots + peers - 1) // peers)
    group = peers // QUAD
    half = group // 2
    slots = peers * cap
    steps = primal_mask.shape[0]
    dual_step = dual_step.reshape(1, -1)
    primal_step = primal_step.reshape(1, -1)
    y_shape = shape(cot_y.shape, F32)
    x_shape = shape(cot_x.shape, F32)
    part_set = (shape((half * cap, batch, side), BF16),) * QUAD
    block_set = shape((col_blocks, batch, side), BF16)
    hb_set = shape((row_blocks, batch, side), BF16)
    per_slot = shape((slots,), I32)
    row_totals = [pltpu.VMEM((row_blocks + 1, batch, side), F32)] * LANES
    col_totals = [pltpu.VMEM((col_blocks + 1, batch, side), F32)] * (2 * half)
    tile_bytes = tiles.size * 2

    def call(kernel, name, moved, ins, outs, args, scratch=()):
        return pl.pallas_call(
            kernel,
            out_shape=outs,
            in_specs=ins,
            out_specs=jax.tree.map(lambda _: VM, outs),
            scratch_shapes=scratch,
            compiler_params=PARAMS,
            cost_estimate=cost(moved),
            name=name,
        )(*args)

    def swap(array, x):
        return lax.ppermute(array, "rb", [(p, p ^ x) for p in range(peers)])

    def near_swaps(parts):
        return [parts[0]] + [swap(parts[x], x) for x in range(1, QUAD)]

    step = steps - 1
    held, dy, rhs, hb, tile_of, row_of, land_of, wants, *far_parts = pl.pallas_call(
        functools.partial(start_kernel, step, peers, cap, col_blocks),
        out_shape=(
            pltpu.VMEM(tiles.shape, BF16), y_shape, y_shape, hb_set, per_slot, per_slot, per_slot,
            shape((QUAD, group * cap), I32),
        ) + part_set,
        in_specs=[SM] + [HBM] * 6,
        out_specs=(VM,) * 4 + (SM,) * 4 + (VM,) * QUAD,
        scratch_shapes=[
            pltpu.SMEM((tile_slots,), I32), pltpu.SMEM((tile_slots,), I32), pltpu.VMEM(dual_step.shape, F32),
            pltpu.VMEM(cot_y.shape, I32), pltpu.VMEM(cot_y.shape, F32), pltpu.SMEM((peers,), I32),
            pltpu.SemaphoreType.DMA((tile_slots // CHUNK,)), pltpu.SemaphoreType.DMA((5,)),
        ],
        compiler_params=PARAMS,
        cost_estimate=cost(2 * tile_bytes),
        name="start",
    )(tile_counts, *(
        pltpu.with_memory_space_constraint(array, pltpu.HBM)
        for array in (tile_rows, tile_cols, tiles, dual_step, dual_mask, cot_y)
    ))
    maps = [wants] + [swap(wants, x) for x in range(1, QUAD)]
    turned = call(turn_kernel, "turn", tile_bytes, [VM], pltpu.VMEM(tiles.shape, BF16), (held,))
    x_state, spent = cot_x, cot_x
    while True:
        far_got = near_swaps(far_parts)
        near_parts = call(near_product_kernel, "near_product", tile_bytes // 2, [SM] * 2 + [VM] * 2, part_set,
                          (tile_of, row_of, held, hb))
        near_got = near_swaps(near_parts)
        far_sums = call(functools.partial(sum_kernel, half, cap), "far_sum", 1 << 20, [SM] * QUAD + [VM] * QUAD,
                        (block_set,) * half, (*maps, *far_got), col_totals)
        got = [swap(far_sums[h], (half + h) * QUAD) for h in reversed(range(half))]
        near_sums = call(functools.partial(sum_kernel, 0, cap), "near_sum", 1 << 20, [SM] * QUAD + [VM] * QUAD,
                         (shape(block_set.shape, F32),) + (block_set,) * (half - 1), (*maps, *near_got), col_totals)
        got += [swap(near_sums[h], h * QUAD) for h in range(1, half)]
        x_state, spent, moved = call(
            functools.partial(primal_kernel, step, step == steps - 1), "primal", 1 << 20, [VM] * (4 + group),
            (x_shape, x_shape, block_set), (primal_mask, primal_step, x_state, spent, near_sums[0], *got))
        blocks = [moved] + [swap(moved, h * QUAD) for h in range(1, group)]
        near_moved = near_swaps(call(functools.partial(pick_kernel, 0, cap), "near_pick", 1 << 20,
                                     [SM] * QUAD + [VM] * half, part_set, (*maps, *blocks[:half])))
        far_moved = near_swaps(call(functools.partial(pick_kernel, half, cap), "far_pick", 1 << 20,
                                    [SM] * QUAD + [VM] * half, part_set, (*maps, *blocks[half:])))
        part = call(near_forward_kernel, "near_forward", tile_bytes // 2, [SM] * 2 + [VM] * (1 + QUAD),
                    shape(hb_set.shape, F32), (tile_of, land_of, turned, *near_moved), row_totals)
        if step == 0:
            break
        step -= 1
        dy, rhs, hb, *far_parts = call(
            functools.partial(middle_kernel, step), "middle", tile_bytes, [SM] * 3 + [VM] * (7 + QUAD),
            (y_shape, y_shape, hb_set) + part_set,
            (tile_of, row_of, land_of, held, turned, dual_step, dual_mask, part, dy, rhs, *far_moved), row_totals)
    y_state = call(last_kernel, "last", tile_bytes // 2, [SM] * 2 + [VM] * (3 + QUAD), y_shape,
                   (tile_of, land_of, turned, part, dy, *far_moved), row_totals)
    return spent, rhs, x_state, y_state


def solution(mesh):
    rb = ("grp", "rb")
    return jax.shard_map(
        on_device,
        mesh=mesh,
        in_specs=(
            P(rb, None, None), P(rb), P(rb), P(rb), P(rb), P(rb),
            P(None, "grp", "rb"), P(None, "grp", "rb"), P("grp", "rb"), P("grp", "rb"),
        ),
        out_specs=(P("grp", "rb"),) * 4,
        check_vma=False,
    )
```

time: 203 us -> 143 us (0.70)
  blocking collectives: 88.1 us -> 0 us
  starting transfers between devices: 28.6 us -> 63.5 us
  local copies, waits for them, and re-layouts: 8.09 us -> 0.03 us
  Pallas kernels: 42 us -> 44.5 us
    all_gather x4 -> x0, blocking collectives: 88.1 us -> none  [on_device(): moved = lax.all_gather(moved, 'rb', axis=0, tiled=True)]
    ppermute x27 -> x75, starting transfers between devices: 28.6 us -> 63.5 us  [swap(): return lax.ppermute(array, 'rb', [(p, p ^ x) for p in range(peers)])]
    unnamed x24 -> x10, local copies, waits for them, and re-layouts: 8.09 us -> 0.03 us
    pallas_call x12 -> x33, Pallas kernels: 34.4 us -> 38.5 us  [call(): pl.pallas_call(kernel, out_shape=outs, in_specs=ins, out_specs=jax.tree.m...]
    ppermute x27 -> x75, waiting for transfers between devices: 34.1 us -> 33.6 us  [swap(): return lax.ppermute(array, 'rb', [(p, p ^ x) for p in range(peers)])]
  transfers between devices with their start and end apart: 27 -> 75, of which waited for: 14 -> 33; matrix products, arithmetic and copies ran while one was open for 0% -> 0% of each run, Pallas kernels for 0% -> 18%
where the time goes in v4:
time: 143 us
  starting transfers between devices  63.5 us (44%)
  Pallas kernels  44.5 us (31%)
  waiting for transfers between devices  33.6 us (23%)
  between operations  1.7 us (1%)
    ppermute x75, starting transfers between devices, swap(): return lax.ppermute(array, 'rb', [(p, p ^ x) for p in range(peers)])  63.5 us
    pallas_call x33, Pallas kernels, call(): pl.pallas_call(kernel, out_shape=outs, in_specs=ins, out_specs=jax.tree.m...  38.5 us
    ppermute x75, waiting for transfers between devices, swap(): return lax.ppermute(array, 'rb', [(p, p ^ x) for p in range(peers)])  33.6 us
    pallas_call x1, Pallas kernels, on_device(): pl.pallas_call(functools.partial(start_kernel, step, peers, cap, col_bloc...  5.92 us
  transfers between devices with their start and end apart: 75, of which 33 were waited for; matrix products, arithmetic and copies ran while one was open for 0% of the time, Pallas kernels for 18%

profile of v4, /device:TPU:0, one launch (start us, length us, event | category | flops | bytes accessed | tf_op | source)
XLA Modules:
  0.0 143.3 jit_solution(6358372028577402660)
XLA Ops:
  1.3 5.9 %start.1 = (bf16[88,256,256]{2,1,0:T(8,128)(2,1)S(1)}, f32[8,2048]{1,0:T(8,128)S(1)}, f32[8,2048]{1,0:T(8,128)S(1)}, bf16[8,8,256]{2,1,0:T(8,128)(2,1)S(1)}, s32...) custom-call(s32[1]{0:T(128)S(6)} %copy.14.count, ...), custom_call_target="tpu_custom_call" | custom-call | flops 184549376 | bytes 23068672 | tf_op jit(solution)/shard_map/start/pallas_call | solution.py:267
  7.8 2.6 %collective-permute-start.2 = (s32[4,24]{1,0:T(4,128)S(1)}, s32[4,24]{1,0:T(4,128)S(1)}, u32[]{:S(2)}, u32[]{:S(2)}) collective-permute-start(s32[4,24]{1,0:T(4,128)S(1)} %get-tuple-element.113.wants), channel_id=1, source_target_pairs={{0,3},{1,2},{2,1},{3,0},{4,7},{5,6},{6,5},{7,4},{8,11},{9,10},{10,... | collective-permute-start | bytes 1160 | tf_op jit(solution)/shard_map/ppermute | solution.py:261
  10.5 1.9 %collective-permute-start.7 = (bf16[12,8,256]{2,1,0:T(8,128)(2,1)S(1)}, bf16[12,8,256]{2,1,0:T(8,128)(2,1)S(1)}, u32[]{:S(2)}, u32[]{:S(2)}) collective-permute-start(bf16[12,8,256]{2,1,0:T(8,128)(2,1)S(1)} %get-tuple-element.125), channel_id=1, source_target_pairs={{0,2},{1,3},{2,0},{3,1},{4,6},{5,7},{6,4},{7,5},{8,10},{9,11},{10,... | collective-permute-start | bytes 147464 | tf_op jit(solution)/shard_map/ppermute | solution.py:261
  17.6 3.7 %collective-permute-start.9 = (bf16[12,8,256]{2,1,0:T(8,128)(2,1)S(1)}, bf16[12,8,256]{2,1,0:T(8,128)(2,1)S(1)}, u32[]{:S(2)}, u32[]{:S(2)}) collective-permute-start(bf16[12,8,256]{2,1,0:T(8,128)(2,1)S(1)} %get-tuple-element.127), channel_id=1, source_target_pairs={{0,12},{1,13},{2,14},{3,15},{4,8},{5,9},{6,10},{7,11},{8,4},{9,5},... | collective-permute-start | bytes 147464 | tf_op jit(solution)/shard_map/ppermute | solution.py:261
  23.6 2.8 %collective-permute-done.10.refs_2_ = bf16[12,8,256]{2,1,0:T(8,128)(2,1)S(1)} collective-permute-done((bf16[12,8,256]{2,1,0:T(8,128)(2,1)S(1)}, bf16[12,8,256]{2,1,0:T(8,128)(2,1)S(1)}, u32[]{:S(2)}, u32[]{:S(2)}) %collective-permute-start.10) | collective-permute-done | bytes 49184 | tf_op jit(solution)/shard_map/ppermute | solution.py:261
  27.6 3.2 %collective-permute-start.17 = (bf16[12,8,256]{2,1,0:T(8,128)(2,1)S(1)}, bf16[12,8,256]{2,1,0:T(8,128)(2,1)S(1)}, u32[]{:S(2)}, u32[]{:S(2)}) collective-permute-start(bf16[12,8,256]{2,1,0:T(8,128)(2,1)S(1)} %get-tuple-element.133.refs_0_), channel_id=1, source_target_pairs={{0,12},{1,13},{2,14},{3,15},{4,8},{5,9},{6,10},{7,11},{8,4},{9,5},... | collective-permute-start | bytes 147464 | tf_op jit(solution)/shard_map/ppermute | solution.py:261
  38.4 3.7 %turn.1.turned = bf16[88,256,256]{2,1,0:T(8,128)(2,1)S(1)} custom-call(bf16[88,256,256]{2,1,0:T(8,128)(2,1)S(1)} %get-tuple-element.116.held), custom_call_target="tpu_custom_call" | custom-call | flops 92274688 | bytes 11534336 | tf_op jit(solution)/shard_map/turn/pallas_call | solution.py:249
  43.8 2.4 %middle.3 = (f32[8,2048]{1,0:T(8,128)S(1)}, f32[8,2048]{1,0:T(8,128)S(1)}, bf16[8,8,256]{2,1,0:T(8,128)(2,1)S(1)}, bf16[12,8,256]{2,1,0:T(8,128)(2,1)S(1)}, bf16...) custom-call(s32[96]{0:T(128)S(1)} %get-tuple-element.114.tile_of, ...), custom_call_target="tpu_custom_call" | custom-call | flops 92274688 | bytes 11534336 | tf_op jit(solution)/shard_map/middle/pallas_call | solution.py:249
  52.4 1.7 %collective-permute-start.27 = (bf16[12,8,256]{2,1,0:T(8,128)(2,1)S(1)}, bf16[12,8,256]{2,1,0:T(8,128)(2,1)S(1)}, u32[]{:S(2)}, u32[]{:S(2)}) collective-permute-start(bf16[12,8,256]{2,1,0:T(8,128)(2,1)S(1)} %get-tuple-element.154), channel_id=1, source_target_pairs={{0,12},{1,13},{2,14},{3,15},{4,8},{5,9},{6,10},{7,11},{8,4},{9,5},... | collective-permute-start | bytes 147464 | tf_op jit(solution)/shard_map/ppermute | solution.py:261
  55.9 1.8 %collective-permute-start.29 = (bf16[12,8,256]{2,1,0:T(8,128)(2,1)S(1)}, bf16[12,8,256]{2,1,0:T(8,128)(2,1)S(1)}, u32[]{:S(2)}, u32[]{:S(2)}) collective-permute-start(bf16[12,8,256]{2,1,0:T(8,128)(2,1)S(1)} %get-tuple-element.156), channel_id=1, source_target_pairs={{0,4},{1,5},{2,6},{3,7},{4,0},{5,1},{6,2},{7,3},{8,12},{9,13},{10,... | collective-permute-start | bytes 147464 | tf_op jit(solution)/shard_map/ppermute | solution.py:261
  59.0 1.9 %collective-permute-done.28.refs_2_ = bf16[12,8,256]{2,1,0:T(8,128)(2,1)S(1)} collective-permute-done((bf16[12,8,256]{2,1,0:T(8,128)(2,1)S(1)}, bf16[12,8,256]{2,1,0:T(8,128)(2,1)S(1)}, u32[]{:S(2)}, u32[]{:S(2)}) %collective-permute-start.28) | collective-permute-done | bytes 49184 | tf_op jit(solution)/shard_map/ppermute | solution.py:261
  62.0 1.7 %collective-permute-start.35 = (bf16[12,8,256]{2,1,0:T(8,128)(2,1)S(1)}, bf16[12,8,256]{2,1,0:T(8,128)(2,1)S(1)}, u32[]{:S(2)}, u32[]{:S(2)}) collective-permute-start(bf16[12,8,256]{2,1,0:T(8,128)(2,1)S(1)} %get-tuple-element.159.refs_0_), channel_id=1, source_target_pairs={{0,12},{1,13},{2,14},{3,15},{4,8},{5,9},{6,10},{7,11},{8,4},{9,5},... | collective-permute-start | bytes 147464 | tf_op jit(solution)/shard_map/ppermute | solution.py:261
  75.2 2.4 %middle.4 = (f32[8,2048]{1,0:T(8,128)S(1)}, f32[8,2048]{1,0:T(8,128)S(1)}, bf16[8,8,256]{2,1,0:T(8,128)(2,1)S(1)}, bf16[12,8,256]{2,1,0:T(8,128)(2,1)S(1)}, bf16...) custom-call(s32[96]{0:T(128)S(1)} %get-tuple-element.114.tile_of, ...), custom_call_target="tpu_custom_call" | custom-call | flops 92274688 | bytes 11534336 | tf_op jit(solution)/shard_map/middle/pallas_call | solution.py:249
  83.6 1.8 %collective-permute-start.45 = (bf16[12,8,256]{2,1,0:T(8,128)(2,1)S(1)}, bf16[12,8,256]{2,1,0:T(8,128)(2,1)S(1)}, u32[]{:S(2)}, u32[]{:S(2)}) collective-permute-start(bf16[12,8,256]{2,1,0:T(8,128)(2,1)S(1)} %get-tuple-element.180), channel_id=1, source_target_pairs={{0,12},{1,13},{2,14},{3,15},{4,8},{5,9},{6,10},{7,11},{8,4},{9,5},... | collective-permute-start | bytes 147464 | tf_op jit(solution)/shard_map/ppermute | solution.py:261
  87.1 1.8 %collective-permute-start.47 = (bf16[12,8,256]{2,1,0:T(8,128)(2,1)S(1)}, bf16[12,8,256]{2,1,0:T(8,128)(2,1)S(1)}, u32[]{:S(2)}, u32[]{:S(2)}) collective-permute-start(bf16[12,8,256]{2,1,0:T(8,128)(2,1)S(1)} %get-tuple-element.182), channel_id=1, source_target_pairs={{0,4},{1,5},{2,6},{3,7},{4,0},{5,1},{6,2},{7,3},{8,12},{9,13},{10,... | collective-permute-start | bytes 147464 | tf_op jit(solution)/shard_map/ppermute | solution.py:261
  90.2 1.9 %collective-permute-done.46.refs_2_ = bf16[12,8,256]{2,1,0:T(8,128)(2,1)S(1)} collective-permute-done((bf16[12,8,256]{2,1,0:T(8,128)(2,1)S(1)}, bf16[12,8,256]{2,1,0:T(8,128)(2,1)S(1)}, u32[]{:S(2)}, u32[]{:S(2)}) %collective-permute-start.46) | collective-permute-done | bytes 49184 | tf_op jit(solution)/shard_map/ppermute | solution.py:261
  93.1 1.8 %collective-permute-start.53 = (bf16[12,8,256]{2,1,0:T(8,128)(2,1)S(1)}, bf16[12,8,256]{2,1,0:T(8,128)(2,1)S(1)}, u32[]{:S(2)}, u32[]{:S(2)}) collective-permute-start(bf16[12,8,256]{2,1,0:T(8,128)(2,1)S(1)} %get-tuple-element.185.refs_0_), channel_id=1, source_target_pairs={{0,12},{1,13},{2,14},{3,15},{4,8},{5,9},{6,10},{7,11},{8,4},{9,5},... | collective-permute-start | bytes 147464 | tf_op jit(solution)/shard_map/ppermute | solution.py:261
  103.2 1.5 %near_forward.6.part = f32[8,8,256]{2,1,0:T(8,128)S(1)} custom-call(s32[96]{0:T(128)S(1)} %get-tuple-element.114.tile_of, s32[96]{0:T(128)S(1)} %get-tuple-element.132.land_of, bf16[88,256,256]{2,1,0:T(8,128)(2,1)S(1)} %turn.1.turned, bf16[12,8,256]{2,1,0:T(8,128)(2,1)S(1)} %get-tuple-element.186.m0, bf16[12,8,256]{2,1,0:T(8,128)(2,1)S(1)} %collective-permute-done.49.m1, ...), custom_call_target="tpu_custom_call" | custom-call | flops 46137344 | bytes 5767168 | tf_op jit(solution)/shard_map/near_forward/pallas_call | solution.py:249
  106.3 3.0 %middle.5 = (f32[8,2048]{1,0:T(8,128)S(1)}, f32[8,2048]{1,0:T(8,128)}, bf16[8,8,256]{2,1,0:T(8,128)(2,1)S(1)}, bf16[12,8,256]{2,1,0:T(8,128)(2,1)S(1)}, bf16[12,...) custom-call(s32[96]{0:T(128)S(1)} %get-tuple-element.114.tile_of, ...), custom_call_target="tpu_custom_call" | custom-call | flops 92274688 | bytes 11534336 | tf_op jit(solution)/shard_map/middle/pallas_call | solution.py:249
  118.8 2.1 %collective-permute-start.63 = (bf16[12,8,256]{2,1,0:T(8,128)(2,1)S(1)}, bf16[12,8,256]{2,1,0:T(8,128)(2,1)S(1)}, u32[]{:S(2)}, u32[]{:S(2)}) collective-permute-start(bf16[12,8,256]{2,1,0:T(8,128)(2,1)S(1)} %get-tuple-element.206), channel_id=1, source_target_pairs={{0,12},{1,13},{2,14},{3,15},{4,8},{5,9},{6,10},{7,11},{8,4},{9,5},... | collective-permute-start | bytes 147464 | tf_op jit(solution)/shard_map/ppermute | solution.py:261
  121.0 4.0 %collective-permute-done.63.refs_1_ = bf16[12,8,256]{2,1,0:T(8,128)(2,1)S(1)} collective-permute-done((bf16[12,8,256]{2,1,0:T(8,128)(2,1)S(1)}, bf16[12,8,256]{2,1,0:T(8,128)(2,1)S(1)}, u32[]{:S(2)}, u32[]{:S(2)}) %collective-permute-start.63) | collective-permute-done | bytes 49184 | tf_op jit(solution)/shard_map/ppermute | solution.py:261
  125.0 1.5 %collective-permute-done.64.refs_2_ = bf16[12,8,256]{2,1,0:T(8,128)(2,1)S(1)} collective-permute-done((bf16[12,8,256]{2,1,0:T(8,128)(2,1)S(1)}, bf16[12,8,256]{2,1,0:T(8,128)(2,1)S(1)}, u32[]{:S(2)}, u32[]{:S(2)}) %collective-permute-start.64) | collective-permute-done | bytes 49184 | tf_op jit(solution)/shard_map/ppermute | solution.py:261
  127.2 2.0 %collective-permute-start.71 = (bf16[12,8,256]{2,1,0:T(8,128)(2,1)S(1)}, bf16[12,8,256]{2,1,0:T(8,128)(2,1)S(1)}, u32[]{:S(2)}, u32[]{:S(2)}) collective-permute-start(bf16[12,8,256]{2,1,0:T(8,128)(2,1)S(1)} %get-tuple-element.212.refs_0_), channel_id=1, source_target_pairs={{0,12},{1,13},{2,14},{3,15},{4,8},{5,9},{6,10},{7,11},{8,4},{9,5},... | collective-permute-start | bytes 147464 | tf_op jit(solution)/shard_map/ppermute | solution.py:261
  141.2 2.1 %last.1 = f32[8,2048]{1,0:T(8,128)} custom-call(s32[96]{0:T(128)S(1)} %get-tuple-element.114.tile_of, s32[96]{0:T(128)S(1)} %get-tuple-element.132.land_of, bf16[88,256,256]{2,1,0:T(8,128)(2,1)S(1)} %turn.1.turned, f32[8,8,256]{2,1,0:T(8,128)S(1)} %near_forward.7.part, f32[8,2048]{1,0:T(8,128)S(1)} %get-tuple-element.217.dy, ...), custom_call_target="tpu_custom_call" | custom-call | flops 46137344 | bytes 5767168 | tf_op jit(solution)/shard_map/last/pallas_call | solution.py:249
  (170 shorter events, 82.2 us)
Async XLA Ops:
  7.2 8.9 %collective-permute-start.6 = (bf16[12,8,256]{2,1,0:T(8,128)(2,1)S(1)}, bf16[12,8,256]{2,1,0:T(8,128)(2,1)S(1)}, u32[]{:S(2)}, u32[]{:S(2)}) collective-permute-start(bf16[12,8,256]{2,1,0:T(8,128)(2,1)S(1)} %get-tuple-element.124), channel_id=1, source_target_pairs={{0,1},{1,0},{2,3},{3,2},{4,5},{5,4},{6,7},{7,6},{8,9},{9,8},{10,11... | collective-permute-start | bytes 147464 | tf_op jit(solution)/shard_map/ppermute | solution.py:261
  10.5 6.3 %collective-permute-start.7 = (bf16[12,8,256]{2,1,0:T(8,128)(2,1)S(1)}, bf16[12,8,256]{2,1,0:T(8,128)(2,1)S(1)}, u32[]{:S(2)}, u32[]{:S(2)}) collective-permute-start(bf16[12,8,256]{2,1,0:T(8,128)(2,1)S(1)} %get-tuple-element.125), channel_id=1, source_target_pairs={{0,2},{1,3},{2,0},{3,1},{4,6},{5,7},{6,4},{7,5},{8,10},{9,11},{10,... | collective-permute-start | bytes 147464 | tf_op jit(solution)/shard_map/ppermute | solution.py:261
  14.9 6.4 %collective-permute-start.3 = (bf16[12,8,256]{2,1,0:T(8,128)(2,1)S(1)}, bf16[12,8,256]{2,1,0:T(8,128)(2,1)S(1)}, u32[]{:S(2)}, u32[]{:S(2)}) collective-permute-start(bf16[12,8,256]{2,1,0:T(8,128)(2,1)S(1)} %get-tuple-element.119), channel_id=1, source_target_pairs={{0,1},{1,0},{2,3},{3,2},{4,5},{5,4},{6,7},{7,6},{8,9},{9,8},{10,11... | collective-permute-start | bytes 147464 | tf_op jit(solution)/shard_map/ppermute | solution.py:261
  15.0 6.3 %collective-permute-start.4 = (bf16[12,8,256]{2,1,0:T(8,128)(2,1)S(1)}, bf16[12,8,256]{2,1,0:T(8,128)(2,1)S(1)}, u32[]{:S(2)}, u32[]{:S(2)}) collective-permute-start(bf16[12,8,256]{2,1,0:T(8,128)(2,1)S(1)} %get-tuple-element.120), channel_id=1, source_target_pairs={{0,2},{1,3},{2,0},{3,1},{4,6},{5,7},{6,4},{7,5},{8,10},{9,11},{10,... | collective-permute-start | bytes 147464 | tf_op jit(solution)/shard_map/ppermute | solution.py:261
  17.6 6.0 %collective-permute-start.9 = (bf16[12,8,256]{2,1,0:T(8,128)(2,1)S(1)}, bf16[12,8,256]{2,1,0:T(8,128)(2,1)S(1)}, u32[]{:S(2)}, u32[]{:S(2)}) collective-permute-start(bf16[12,8,256]{2,1,0:T(8,128)(2,1)S(1)} %get-tuple-element.127), channel_id=1, source_target_pairs={{0,12},{1,13},{2,14},{3,15},{4,8},{5,9},{6,10},{7,11},{8,4},{9,5},... | collective-permute-start | bytes 147464 | tf_op jit(solution)/shard_map/ppermute | solution.py:261
  27.6 6.8 %collective-permute-start.17 = (bf16[12,8,256]{2,1,0:T(8,128)(2,1)S(1)}, bf16[12,8,256]{2,1,0:T(8,128)(2,1)S(1)}, u32[]{:S(2)}, u32[]{:S(2)}) collective-permute-start(bf16[12,8,256]{2,1,0:T(8,128)(2,1)S(1)} %get-tuple-element.133.refs_0_), channel_id=1, source_target_pairs={{0,12},{1,13},{2,14},{3,15},{4,8},{5,9},{6,10},{7,11},{8,4},{9,5},... | collective-permute-start | bytes 147464 | tf_op jit(solution)/shard_map/ppermute | solution.py:261
  32.5 9.7 %collective-permute-start.14 = (bf16[12,8,256]{2,1,0:T(8,128)(2,1)S(1)}, bf16[12,8,256]{2,1,0:T(8,128)(2,1)S(1)}, u32[]{:S(2)}, u32[]{:S(2)}) collective-permute-start(bf16[12,8,256]{2,1,0:T(8,128)(2,1)S(1)} %get-tuple-element.136), channel_id=1, source_target_pairs={{0,2},{1,3},{2,0},{3,1},{4,6},{5,7},{6,4},{7,5},{8,10},{9,11},{10,... | collective-permute-start | bytes 147464 | tf_op jit(solution)/shard_map/ppermute | solution.py:261
  33.1 9.1 %collective-permute-start.15 = (bf16[12,8,256]{2,1,0:T(8,128)(2,1)S(1)}, bf16[12,8,256]{2,1,0:T(8,128)(2,1)S(1)}, u32[]{:S(2)}, u32[]{:S(2)}) collective-permute-start(bf16[12,8,256]{2,1,0:T(8,128)(2,1)S(1)} %get-tuple-element.137), channel_id=1, source_target_pairs={{0,3},{1,2},{2,1},{3,0},{4,7},{5,6},{6,5},{7,4},{8,11},{9,10},{10,... | collective-permute-start | bytes 147464 | tf_op jit(solution)/shard_map/ppermute | solution.py:261
  36.5 7.2 %collective-permute-start.18 = (bf16[12,8,256]{2,1,0:T(8,128)(2,1)S(1)}, bf16[12,8,256]{2,1,0:T(8,128)(2,1)S(1)}, u32[]{:S(2)}, u32[]{:S(2)}) collective-permute-start(bf16[12,8,256]{2,1,0:T(8,128)(2,1)S(1)} %get-tuple-element.141), channel_id=1, source_target_pairs={{0,1},{1,0},{2,3},{3,2},{4,5},{5,4},{6,7},{7,6},{8,9},{9,8},{10,11... | collective-permute-start | bytes 147464 | tf_op jit(solution)/shard_map/ppermute | solution.py:261
  36.6 7.2 %collective-permute-start.19 = (bf16[12,8,256]{2,1,0:T(8,128)(2,1)S(1)}, bf16[12,8,256]{2,1,0:T(8,128)(2,1)S(1)}, u32[]{:S(2)}, u32[]{:S(2)}) collective-permute-start(bf16[12,8,256]{2,1,0:T(8,128)(2,1)S(1)} %get-tuple-element.142), channel_id=1, source_target_pairs={{0,2},{1,3},{2,0},{3,1},{4,6},{5,7},{6,4},{7,5},{8,10},{9,11},{10,... | collective-permute-start | bytes 147464 | tf_op jit(solution)/shard_map/ppermute | solution.py:261
  37.5 6.3 %collective-permute-start.20 = (bf16[12,8,256]{2,1,0:T(8,128)(2,1)S(1)}, bf16[12,8,256]{2,1,0:T(8,128)(2,1)S(1)}, u32[]{:S(2)}, u32[]{:S(2)}) collective-permute-start(bf16[12,8,256]{2,1,0:T(8,128)(2,1)S(1)} %get-tuple-element.143), channel_id=1, source_target_pairs={{0,3},{1,2},{2,1},{3,0},{4,7},{5,6},{6,5},{7,4},{8,11},{9,10},{10,... | collective-permute-start | bytes 147464 | tf_op jit(solution)/shard_map/ppermute | solution.py:261
  52.4 6.6 %collective-permute-start.27 = (bf16[12,8,256]{2,1,0:T(8,128)(2,1)S(1)}, bf16[12,8,256]{2,1,0:T(8,128)(2,1)S(1)}, u32[]{:S(2)}, u32[]{:S(2)}) collective-permute-start(bf16[12,8,256]{2,1,0:T(8,128)(2,1)S(1)} %get-tuple-element.154), channel_id=1, source_target_pairs={{0,12},{1,13},{2,14},{3,15},{4,8},{5,9},{6,10},{7,11},{8,4},{9,5},... | collective-permute-start | bytes 147464 | tf_op jit(solution)/shard_map/ppermute | solution.py:261
  54.2 6.7 %collective-permute-start.28 = (bf16[12,8,256]{2,1,0:T(8,128)(2,1)S(1)}, bf16[12,8,256]{2,1,0:T(8,128)(2,1)S(1)}, u32[]{:S(2)}, u32[]{:S(2)}) collective-permute-start(bf16[12,8,256]{2,1,0:T(8,128)(2,1)S(1)} %get-tuple-element.155), channel_id=1, source_target_pairs={{0,8},{1,9},{2,10},{3,11},{4,12},{5,13},{6,14},{7,15},{8,0},{9,1},... | collective-permute-start | bytes 147464 | tf_op jit(solution)/shard_map/ppermute | solution.py:261
  62.0 6.0 %collective-permute-start.35 = (bf16[12,8,256]{2,1,0:T(8,128)(2,1)S(1)}, bf16[12,8,256]{2,1,0:T(8,128)(2,1)S(1)}, u32[]{:S(2)}, u32[]{:S(2)}) collective-permute-start(bf16[12,8,256]{2,1,0:T(8,128)(2,1)S(1)} %get-tuple-element.159.refs_0_), channel_id=1, source_target_pairs={{0,12},{1,13},{2,14},{3,15},{4,8},{5,9},{6,10},{7,11},{8,4},{9,5},... | collective-permute-start | bytes 147464 | tf_op jit(solution)/shard_map/ppermute | solution.py:261
  63.6 5.7 %collective-permute-start.34 = (bf16[12,8,256]{2,1,0:T(8,128)(2,1)S(1)}, bf16[12,8,256]{2,1,0:T(8,128)(2,1)S(1)}, u32[]{:S(2)}, u32[]{:S(2)}) collective-permute-start(bf16[12,8,256]{2,1,0:T(8,128)(2,1)S(1)} %get-tuple-element.159.refs_0_), channel_id=1, source_target_pairs={{0,8},{1,9},{2,10},{3,11},{4,12},{5,13},{6,14},{7,15},{8,0},{9,1},... | collective-permute-start | bytes 147464 | tf_op jit(solution)/shard_map/ppermute | solution.py:261
  66.0 6.0 %collective-permute-start.32 = (bf16[12,8,256]{2,1,0:T(8,128)(2,1)S(1)}, bf16[12,8,256]{2,1,0:T(8,128)(2,1)S(1)}, u32[]{:S(2)}, u32[]{:S(2)}) collective-permute-start(bf16[12,8,256]{2,1,0:T(8,128)(2,1)S(1)} %get-tuple-element.162), channel_id=1, source_target_pairs={{0,2},{1,3},{2,0},{3,1},{4,6},{5,7},{6,4},{7,5},{8,10},{9,11},{10,... | collective-permute-start | bytes 147464 | tf_op jit(solution)/shard_map/ppermute | solution.py:261
  83.6 6.6 %collective-permute-start.45 = (bf16[12,8,256]{2,1,0:T(8,128)(2,1)S(1)}, bf16[12,8,256]{2,1,0:T(8,128)(2,1)S(1)}, u32[]{:S(2)}, u32[]{:S(2)}) collective-permute-start(bf16[12,8,256]{2,1,0:T(8,128)(2,1)S(1)} %get-tuple-element.180), channel_id=1, source_target_pairs={{0,12},{1,13},{2,14},{3,15},{4,8},{5,9},{6,10},{7,11},{8,4},{9,5},... | collective-permute-start | bytes 147464 | tf_op jit(solution)/shard_map/ppermute | solution.py:261
  85.4 6.6 %collective-permute-start.46 = (bf16[12,8,256]{2,1,0:T(8,128)(2,1)S(1)}, bf16[12,8,256]{2,1,0:T(8,128)(2,1)S(1)}, u32[]{:S(2)}, u32[]{:S(2)}) collective-permute-start(bf16[12,8,256]{2,1,0:T(8,128)(2,1)S(1)} %get-tuple-element.181), channel_id=1, source_target_pairs={{0,8},{1,9},{2,10},{3,11},{4,12},{5,13},{6,14},{7,15},{8,0},{9,1},... | collective-permute-start | bytes 147464 | tf_op jit(solution)/shard_map/ppermute | solution.py:261
  93.1 5.9 %collective-permute-start.53 = (bf16[12,8,256]{2,1,0:T(8,128)(2,1)S(1)}, bf16[12,8,256]{2,1,0:T(8,128)(2,1)S(1)}, u32[]{:S(2)}, u32[]{:S(2)}) collective-permute-start(bf16[12,8,256]{2,1,0:T(8,128)(2,1)S(1)} %get-tuple-element.185.refs_0_), channel_id=1, source_target_pairs={{0,12},{1,13},{2,14},{3,15},{4,8},{5,9},{6,10},{7,11},{8,4},{9,5},... | collective-permute-start | bytes 147464 | tf_op jit(solution)/shard_map/ppermute | solution.py:261
  97.2 6.0 %collective-permute-start.50 = (bf16[12,8,256]{2,1,0:T(8,128)(2,1)S(1)}, bf16[12,8,256]{2,1,0:T(8,128)(2,1)S(1)}, u32[]{:S(2)}, u32[]{:S(2)}) collective-permute-start(bf16[12,8,256]{2,1,0:T(8,128)(2,1)S(1)} %get-tuple-element.188), channel_id=1, source_target_pairs={{0,2},{1,3},{2,0},{3,1},{4,6},{5,7},{6,4},{7,5},{8,10},{9,11},{10,... | collective-permute-start | bytes 147464 | tf_op jit(solution)/shard_map/ppermute | solution.py:261
  118.8 6.2 %collective-permute-start.63 = (bf16[12,8,256]{2,1,0:T(8,128)(2,1)S(1)}, bf16[12,8,256]{2,1,0:T(8,128)(2,1)S(1)}, u32[]{:S(2)}, u32[]{:S(2)}) collective-permute-start(bf16[12,8,256]{2,1,0:T(8,128)(2,1)S(1)} %get-tuple-element.206), channel_id=1, source_target_pairs={{0,12},{1,13},{2,14},{3,15},{4,8},{5,9},{6,10},{7,11},{8,4},{9,5},... | collective-permute-start | bytes 147464 | tf_op jit(solution)/shard_map/ppermute | solution.py:261
  127.2 6.8 %collective-permute-start.71 = (bf16[12,8,256]{2,1,0:T(8,128)(2,1)S(1)}, bf16[12,8,256]{2,1,0:T(8,128)(2,1)S(1)}, u32[]{:S(2)}, u32[]{:S(2)}) collective-permute-start(bf16[12,8,256]{2,1,0:T(8,128)(2,1)S(1)} %get-tuple-element.212.refs_0_), channel_id=1, source_target_pairs={{0,12},{1,13},{2,14},{3,15},{4,8},{5,9},{6,10},{7,11},{8,4},{9,5},... | collective-permute-start | bytes 147464 | tf_op jit(solution)/shard_map/ppermute | solution.py:261
  129.3 6.1 %collective-permute-start.70 = (bf16[12,8,256]{2,1,0:T(8,128)(2,1)S(1)}, bf16[12,8,256]{2,1,0:T(8,128)(2,1)S(1)}, u32[]{:S(2)}, u32[]{:S(2)}) collective-permute-start(bf16[12,8,256]{2,1,0:T(8,128)(2,1)S(1)} %get-tuple-element.212.refs_0_), channel_id=1, source_target_pairs={{0,8},{1,9},{2,10},{3,11},{4,12},{5,13},{6,14},{7,15},{8,0},{9,1},... | collective-permute-start | bytes 147464 | tf_op jit(solution)/shard_map/ppermute | solution.py:261
  132.1 6.0 %collective-permute-start.68 = (bf16[12,8,256]{2,1,0:T(8,128)(2,1)S(1)}, bf16[12,8,256]{2,1,0:T(8,128)(2,1)S(1)}, u32[]{:S(2)}, u32[]{:S(2)}) collective-permute-start(bf16[12,8,256]{2,1,0:T(8,128)(2,1)S(1)} %get-tuple-element.215), channel_id=1, source_target_pairs={{0,2},{1,3},{2,0},{3,1},{4,6},{5,7},{6,4},{7,5},{8,10},{9,11},{10,... | collective-permute-start | bytes 147464 | tf_op jit(solution)/shard_map/ppermute | solution.py:261
  (56 other events, 309.3 us)

commit v5 on v4

--- a/solution.py
+++ b/solution.py
@@ -93,7 +93,7 @@
         land_of[s] = hb.shape[0]
     for x in range(QUAD):
         for s in range(group * cap):
-            wants[x, s] = col_blocks
+            wants[x * group * cap + s] = col_blocks
     for copy in minor:
         copy.wait()
     me = lax.axis_index("rb").astype(I32)
@@ -112,7 +112,7 @@
         tile_of[slot] = t
         row_of[slot] = rows[t]
         land_of[slot] = rows[t]
-        wants[quad, place] = col - owner * col_blocks
+        wants[quad * (group * cap) + place] = col - owner * col_blocks
         return 0
 
     lax.fori_loop(0, count[0], place_tile, 0)
@@ -140,9 +140,17 @@
     transpose_products(tile_of.shape[0] // 2, tile_of, row_of, held, hb, (o0, o1, o2, o3))
 
 
-def sum_kernel(first_high, cap, wants, got1, got2, got3, a0, a1, a2, a3, *rest):
+def map_kernel(own, got1, got2, got3, wants):
+    per = own.shape[0] // QUAD
+    for x, got in enumerate((own, got1, got2, got3)):
+        for s in range(per):
+            wants[x * per + s] = got[x * per + s]
+
+
+def sum_kernel(first_high, cap, wants, a0, a1, a2, a3, *rest):
     parts = (a0, a1, a2, a3)
     half = a0.shape[0] // cap
+    per = wants.shape[0] // QUAD
     outs, totals = rest[:half], rest[half:]
     for total in totals:
         total[...] = jnp.zeros_like(total)
@@ -152,8 +160,7 @@
             for h in range(half):
                 for side in range(2):
                     x = 2 * pair + side
-                    want = (wants, got1, got2, got3)[x]
-                    spot = want[x, (first_high + h) * cap + r]
+                    spot = wants[x * per + (first_high + h) * cap + r]
                     jobs.append((totals[2 * h + side], spot, parts[x][h * cap + r].astype(F32)))
             values = [total[spot] + part for total, spot, part in jobs]
             for (total, spot, _), value in zip(jobs, values):
@@ -178,13 +185,13 @@
         out[c] = q.astype(BF16)
 
 
-def pick_kernel(first_high, cap, wants, got1, got2, got3, *refs):
+def pick_kernel(first_high, cap, wants, *refs):
     blocks, outs = refs[:-QUAD], refs[-QUAD:]
+    per = wants.shape[0] // QUAD
     last = blocks[0].shape[0] - 1
     for x, out in enumerate(outs):
-        want = (wants, got1, got2, got3)[x]
         values = [
-            blocks[h][jnp.minimum(want[x, (first_high + h) * cap + r], last)]
+            blocks[h][jnp.minimum(wants[x * per + (first_high + h) * cap + r], last)]
             for h in range(len(blocks))
             for r in range(cap)
         ]
@@ -240,7 +247,7 @@
     part_set = (shape((half * cap, batch, side), BF16),) * QUAD
     block_set = shape((col_blocks, batch, side), BF16)
     hb_set = shape((row_blocks, batch, side), BF16)
-    per_slot = shape((slots,), I32)
+    per_slot = pltpu.SMEM((slots,), I32)
     row_totals = [pltpu.VMEM((row_blocks + 1, batch, side), F32)] * LANES
     col_totals = [pltpu.VMEM((col_blocks + 1, batch, side), F32)] * (2 * half)
     tile_bytes = tiles.size * 2
@@ -268,7 +275,7 @@
         functools.partial(start_kernel, step, peers, cap, col_blocks),
         out_shape=(
             pltpu.VMEM(tiles.shape, BF16), y_shape, y_shape, hb_set, per_slot, per_slot, per_slot,
-            shape((QUAD, group * cap), I32),
+            shape((QUAD * group * cap,), I32),
         ) + part_set,
         in_specs=[SM] + [HBM] * 6,
         out_specs=(VM,) * 4 + (SM,) * 4 + (VM,) * QUAD,
@@ -284,7 +291,14 @@
         pltpu.with_memory_space_constraint(array, pltpu.HBM)
         for array in (tile_rows, tile_cols, tiles, dual_step, dual_mask, cot_y)
     ))
-    maps = [wants] + [swap(wants, x) for x in range(1, QUAD)]
+    wants = pl.pallas_call(
+        map_kernel,
+        out_shape=pltpu.SMEM((slots,), I32),
+        in_specs=[SM] * QUAD,
+        out_specs=SM,
+        compiler_params=PARAMS,
+        name="maps",
+    )(wants, *(swap(wants, x) for x in range(1, QUAD)))
     turned = call(turn_kernel, "turn", tile_bytes, [VM], pltpu.VMEM(tiles.shape, BF16), (held,))
     x_state, spent = cot_x, cot_x
     while True:
@@ -292,20 +306,22 @@
         near_parts = call(near_product_kernel, "near_product", tile_bytes // 2, [SM] * 2 + [VM] * 2, part_set,
                           (tile_of, row_of, held, hb))
         near_got = near_swaps(near_parts)
-        far_sums = call(functools.partial(sum_kernel, half, cap), "far_sum", 1 << 20, [SM] * QUAD + [VM] * QUAD,
-                        (block_set,) * half, (*maps, *far_got), col_totals)
+        far_sums = call(functools.partial(sum_kernel, half, cap), "far_sum", 1 << 20, [SM] + [VM] * QUAD,
+                        (block_set,) * half, (wants, *far_got), col_totals)
         got = [swap(far_sums[h], (half + h) * QUAD) for h in reversed(range(half))]
-        near_sums = call(functools.partial(sum_kernel, 0, cap), "near_sum", 1 << 20, [SM] * QUAD + [VM] * QUAD,
-                         (shape(block_set.shape, F32),) + (block_set,) * (half - 1), (*maps, *near_got), col_totals)
+        near_sums = call(functools.partial(sum_kernel, 0, cap), "near_sum", 1 << 20, [SM] + [VM] * QUAD,
+                         (shape(block_set.shape, F32),) + (block_set,) * (half - 1), (wants, *near_got), col_totals)
         got += [swap(near_sums[h], h * QUAD) for h in range(1, half)]
+        if step == steps - 1:
+            turned, x_state = lax.optimization_barrier((turned, x_state))
         x_state, spent, moved = call(
             functools.partial(primal_kernel, step, step == steps - 1), "primal", 1 << 20, [VM] * (4 + group),
             (x_shape, x_shape, block_set), (primal_mask, primal_step, x_state, spent, near_sums[0], *got))
         blocks = [moved] + [swap(moved, h * QUAD) for h in range(1, group)]
         near_moved = near_swaps(call(functools.partial(pick_kernel, 0, cap), "near_pick", 1 << 20,
-                                     [SM] * QUAD + [VM] * half, part_set, (*maps, *blocks[:half])))
+                                     [SM] + [VM] * half, part_set, (wants, *blocks[:half])))
         far_moved = near_swaps(call(functools.partial(pick_kernel, half, cap), "far_pick", 1 << 20,
-                                    [SM] * QUAD + [VM] * half, part_set, (*maps, *blocks[half:])))
+                                    [SM] + [VM] * half, part_set, (wants, *blocks[half:])))
         part = call(near_forward_kernel, "near_forward", tile_bytes // 2, [SM] * 2 + [VM] * (1 + QUAD),
                     shape(hb_set.shape, F32), (tile_of, land_of, turned, *near_moved), row_totals)
         if step == 0:

time: 143 us -> 132 us (0.923)
  Pallas kernels: 44.5 us -> 27.8 us
  waiting for transfers between devices: 33.6 us -> 39.2 us
    pallas_call x33, Pallas kernels: 38.5 us -> 21.4 us  [call(): pl.pallas_call(kernel, out_shape=outs, in_specs=ins, out_specs=jax.tree.m...]
    ppermute x75, waiting for transfers between devices: 33.6 us -> 39.2 us  [swap(): return lax.ppermute(array, 'rb', [(p, p ^ x) for p in range(peers)])]
  transfers between devices with their start and end apart: 75 -> 75, of which waited for: 33 -> 39; matrix products, arithmetic and copies ran while one was open for 0% -> 0% of each run, Pallas kernels for 18% -> 9%
where the time goes in v5:
time: 132 us; the launch traced here: 131 us
  starting transfers between devices  62.7 us (48%)
  waiting for transfers between devices  39.2 us (30%)
  Pallas kernels  27.8 us (21%)
  between operations  1.68 us (1%)
    ppermute x75, starting transfers between devices, swap(): return lax.ppermute(array, 'rb', [(p, p ^ x) for p in range(peers)])  62.7 us
    ppermute x75, waiting for transfers between devices, swap(): return lax.ppermute(array, 'rb', [(p, p ^ x) for p in range(peers)])  39.2 us
    pallas_call x33, Pallas kernels, call(): pl.pallas_call(kernel, out_shape=outs, in_specs=ins, out_specs=jax.tree.m...  21.4 us
    pallas_call x1, Pallas kernels, on_device(): pl.pallas_call(functools.partial(start_kernel, step, peers, cap, col_bloc...  5.81 us
  transfers between devices with their start and end apart: 75, of which 39 were waited for; matrix products, arithmetic and copies ran while one was open for 0% of the time, Pallas kernels for 9%

profile of v5, /device:TPU:0, one launch (start us, length us, event | category | flops | bytes accessed | tf_op | source)
XLA Modules:
  0.0 131.4 jit_solution(902719147087860325)
XLA Ops:
  1.3 5.8 %start.1 = (bf16[88,256,256]{2,1,0:T(8,128)(2,1)S(1)}, f32[8,2048]{1,0:T(8,128)S(1)}, f32[8,2048]{1,0:T(8,128)S(1)}, bf16[8,8,256]{2,1,0:T(8,128)(2,1)S(1)}, s32...) custom-call(s32[1]{0:T(128)S(6)} %copy.14.count, ...), custom_call_target="tpu_custom_call" | custom-call | flops 184549376 | bytes 23068672 | tf_op jit(solution)/shard_map/start/pallas_call | solution.py:274
  7.6 2.6 %collective-permute-start.2 = (s32[96]{0:T(128)S(1)}, s32[96]{0:T(128)S(1)}, u32[]{:S(2)}, u32[]{:S(2)}) collective-permute-start(s32[96]{0:T(128)S(1)} %get-tuple-element.117.own), channel_id=1, source_target_pairs={{0,3},{1,2},{2,1},{3,0},{4,7},{5,6},{6,5},{7,4},{8,11},{9,10},{10,... | collective-permute-start | bytes 1160 | tf_op jit(solution)/shard_map/ppermute | solution.py:268
  10.4 1.9 %collective-permute-start.7 = (bf16[12,8,256]{2,1,0:T(8,128)(2,1)S(1)}, bf16[12,8,256]{2,1,0:T(8,128)(2,1)S(1)}, u32[]{:S(2)}, u32[]{:S(2)}) collective-permute-start(bf16[12,8,256]{2,1,0:T(8,128)(2,1)S(1)} %get-tuple-element.128), channel_id=1, source_target_pairs={{0,2},{1,3},{2,0},{3,1},{4,6},{5,7},{6,4},{7,5},{8,10},{9,11},{10,... | collective-permute-start | bytes 147464 | tf_op jit(solution)/shard_map/ppermute | solution.py:268
  16.9 3.7 %collective-permute-start.9 = (bf16[12,8,256]{2,1,0:T(8,128)(2,1)S(1)}, bf16[12,8,256]{2,1,0:T(8,128)(2,1)S(1)}, u32[]{:S(2)}, u32[]{:S(2)}) collective-permute-start(bf16[12,8,256]{2,1,0:T(8,128)(2,1)S(1)} %get-tuple-element.130), channel_id=1, source_target_pairs={{0,12},{1,13},{2,14},{3,15},{4,8},{5,9},{6,10},{7,11},{8,4},{9,5},... | collective-permute-start | bytes 147464 | tf_op jit(solution)/shard_map/ppermute | solution.py:268
  21.6 3.7 %turn.1.turned = bf16[88,256,256]{2,1,0:T(8,128)(2,1)S(1)} custom-call(bf16[88,256,256]{2,1,0:T(8,128)(2,1)S(1)} %get-tuple-element.115.held), custom_call_target="tpu_custom_call" | custom-call | flops 92274688 | bytes 11534336 | tf_op jit(solution)/shard_map/turn/pallas_call | solution.py:256
  26.8 2.6 %collective-permute-start.17 = (bf16[12,8,256]{2,1,0:T(8,128)(2,1)S(1)}, bf16[12,8,256]{2,1,0:T(8,128)(2,1)S(1)}, u32[]{:S(2)}, u32[]{:S(2)}) collective-permute-start(bf16[12,8,256]{2,1,0:T(8,128)(2,1)S(1)} %get-tuple-element.137.refs_0_), channel_id=1, source_target_pairs={{0,12},{1,13},{2,14},{3,15},{4,8},{5,9},{6,10},{7,11},{8,4},{9,5},... | collective-permute-start | bytes 147464 | tf_op jit(solution)/shard_map/ppermute | solution.py:268
  33.3 1.6 %collective-permute-done.16.refs_0_ = bf16[12,8,256]{2,1,0:T(8,128)(2,1)S(1)} collective-permute-done((bf16[12,8,256]{2,1,0:T(8,128)(2,1)S(1)}, bf16[12,8,256]{2,1,0:T(8,128)(2,1)S(1)}, u32[]{:S(2)}, u32[]{:S(2)}) %collective-permute-start.16) | collective-permute-done | bytes 49184 | tf_op jit(solution)/shard_map/ppermute | solution.py:268
  40.1 1.9 %middle.3 = (f32[8,2048]{1,0:T(8,128)S(1)}, f32[8,2048]{1,0:T(8,128)S(1)}, bf16[8,8,256]{2,1,0:T(8,128)(2,1)S(1)}, bf16[12,8,256]{2,1,0:T(8,128)(2,1)S(1)}, bf16...) custom-call(s32[96]{0:T(128)S(4)} %get-tuple-element.118.tile_of, ...), custom_call_target="tpu_custom_call" | custom-call | flops 92274688 | bytes 11534336 | tf_op jit(solution)/shard_map/middle/pallas_call | solution.py:256
  47.1 1.9 %collective-permute-start.27 = (bf16[12,8,256]{2,1,0:T(8,128)(2,1)S(1)}, bf16[12,8,256]{2,1,0:T(8,128)(2,1)S(1)}, u32[]{:S(2)}, u32[]{:S(2)}) collective-permute-start(bf16[12,8,256]{2,1,0:T(8,128)(2,1)S(1)} %get-tuple-element.158), channel_id=1, source_target_pairs={{0,12},{1,13},{2,14},{3,15},{4,8},{5,9},{6,10},{7,11},{8,4},{9,5},... | collective-permute-start | bytes 147464 | tf_op jit(solution)/shard_map/ppermute | solution.py:268
  51.7 1.8 %collective-permute-done.27.refs_1_ = bf16[12,8,256]{2,1,0:T(8,128)(2,1)S(1)} collective-permute-done((bf16[12,8,256]{2,1,0:T(8,128)(2,1)S(1)}, bf16[12,8,256]{2,1,0:T(8,128)(2,1)S(1)}, u32[]{:S(2)}, u32[]{:S(2)}) %collective-permute-start.27) | collective-permute-done | bytes 49184 | tf_op jit(solution)/shard_map/ppermute | solution.py:268
  53.6 1.6 %collective-permute-done.28.refs_2_ = bf16[12,8,256]{2,1,0:T(8,128)(2,1)S(1)} collective-permute-done((bf16[12,8,256]{2,1,0:T(8,128)(2,1)S(1)}, bf16[12,8,256]{2,1,0:T(8,128)(2,1)S(1)}, u32[]{:S(2)}, u32[]{:S(2)}) %collective-permute-start.28) | collective-permute-done | bytes 49184 | tf_op jit(solution)/shard_map/ppermute | solution.py:268
  55.9 1.8 %collective-permute-start.35 = (bf16[12,8,256]{2,1,0:T(8,128)(2,1)S(1)}, bf16[12,8,256]{2,1,0:T(8,128)(2,1)S(1)}, u32[]{:S(2)}, u32[]{:S(2)}) collective-permute-start(bf16[12,8,256]{2,1,0:T(8,128)(2,1)S(1)} %get-tuple-element.163.refs_0_), channel_id=1, source_target_pairs={{0,12},{1,13},{2,14},{3,15},{4,8},{5,9},{6,10},{7,11},{8,4},{9,5},... | collective-permute-start | bytes 147464 | tf_op jit(solution)/shard_map/ppermute | solution.py:268
  61.8 1.7 %collective-permute-done.34.refs_0_ = bf16[12,8,256]{2,1,0:T(8,128)(2,1)S(1)} collective-permute-done((bf16[12,8,256]{2,1,0:T(8,128)(2,1)S(1)}, bf16[12,8,256]{2,1,0:T(8,128)(2,1)S(1)}, u32[]{:S(2)}, u32[]{:S(2)}) %collective-permute-start.34) | collective-permute-done | bytes 49184 | tf_op jit(solution)/shard_map/ppermute | solution.py:268
  68.6 1.9 %middle.4 = (f32[8,2048]{1,0:T(8,128)S(1)}, f32[8,2048]{1,0:T(8,128)S(1)}, bf16[8,8,256]{2,1,0:T(8,128)(2,1)S(1)}, bf16[12,8,256]{2,1,0:T(8,128)(2,1)S(1)}, bf16...) custom-call(s32[96]{0:T(128)S(4)} %get-tuple-element.118.tile_of, ...), custom_call_target="tpu_custom_call" | custom-call | flops 92274688 | bytes 11534336 | tf_op jit(solution)/shard_map/middle/pallas_call | solution.py:256
  75.7 2.0 %collective-permute-start.45 = (bf16[12,8,256]{2,1,0:T(8,128)(2,1)S(1)}, bf16[12,8,256]{2,1,0:T(8,128)(2,1)S(1)}, u32[]{:S(2)}, u32[]{:S(2)}) collective-permute-start(bf16[12,8,256]{2,1,0:T(8,128)(2,1)S(1)} %get-tuple-element.184), channel_id=1, source_target_pairs={{0,12},{1,13},{2,14},{3,15},{4,8},{5,9},{6,10},{7,11},{8,4},{9,5},... | collective-permute-start | bytes 147464 | tf_op jit(solution)/shard_map/ppermute | solution.py:268
  80.4 1.8 %collective-permute-done.45.refs_1_ = bf16[12,8,256]{2,1,0:T(8,128)(2,1)S(1)} collective-permute-done((bf16[12,8,256]{2,1,0:T(8,128)(2,1)S(1)}, bf16[12,8,256]{2,1,0:T(8,128)(2,1)S(1)}, u32[]{:S(2)}, u32[]{:S(2)}) %collective-permute-start.45) | collective-permute-done | bytes 49184 | tf_op jit(solution)/shard_map/ppermute | solution.py:268
  84.6 1.9 %collective-permute-start.53 = (bf16[12,8,256]{2,1,0:T(8,128)(2,1)S(1)}, bf16[12,8,256]{2,1,0:T(8,128)(2,1)S(1)}, u32[]{:S(2)}, u32[]{:S(2)}) collective-permute-start(bf16[12,8,256]{2,1,0:T(8,128)(2,1)S(1)} %get-tuple-element.189.refs_0_), channel_id=1, source_target_pairs={{0,12},{1,13},{2,14},{3,15},{4,8},{5,9},{6,10},{7,11},{8,4},{9,5},... | collective-permute-start | bytes 147464 | tf_op jit(solution)/shard_map/ppermute | solution.py:268
  90.5 1.8 %collective-permute-done.52.refs_0_ = bf16[12,8,256]{2,1,0:T(8,128)(2,1)S(1)} collective-permute-done((bf16[12,8,256]{2,1,0:T(8,128)(2,1)S(1)}, bf16[12,8,256]{2,1,0:T(8,128)(2,1)S(1)}, u32[]{:S(2)}, u32[]{:S(2)}) %collective-permute-start.52) | collective-permute-done | bytes 49184 | tf_op jit(solution)/shard_map/ppermute | solution.py:268
  97.4 2.5 %middle.5 = (f32[8,2048]{1,0:T(8,128)S(1)}, f32[8,2048]{1,0:T(8,128)}, bf16[8,8,256]{2,1,0:T(8,128)(2,1)S(1)}, bf16[12,8,256]{2,1,0:T(8,128)(2,1)S(1)}, bf16[12,...) custom-call(s32[96]{0:T(128)S(4)} %get-tuple-element.118.tile_of, ...), custom_call_target="tpu_custom_call" | custom-call | flops 92274688 | bytes 11534336 | tf_op jit(solution)/shard_map/middle/pallas_call | solution.py:256
  108.1 2.1 %collective-permute-start.63 = (bf16[12,8,256]{2,1,0:T(8,128)(2,1)S(1)}, bf16[12,8,256]{2,1,0:T(8,128)(2,1)S(1)}, u32[]{:S(2)}, u32[]{:S(2)}) collective-permute-start(bf16[12,8,256]{2,1,0:T(8,128)(2,1)S(1)} %get-tuple-element.210), channel_id=1, source_target_pairs={{0,12},{1,13},{2,14},{3,15},{4,8},{5,9},{6,10},{7,11},{8,4},{9,5},... | collective-permute-start | bytes 147464 | tf_op jit(solution)/shard_map/ppermute | solution.py:268
  110.3 4.1 %collective-permute-done.63.refs_1_ = bf16[12,8,256]{2,1,0:T(8,128)(2,1)S(1)} collective-permute-done((bf16[12,8,256]{2,1,0:T(8,128)(2,1)S(1)}, bf16[12,8,256]{2,1,0:T(8,128)(2,1)S(1)}, u32[]{:S(2)}, u32[]{:S(2)}) %collective-permute-start.63) | collective-permute-done | bytes 49184 | tf_op jit(solution)/shard_map/ppermute | solution.py:268
  116.6 2.1 %collective-permute-start.71 = (bf16[12,8,256]{2,1,0:T(8,128)(2,1)S(1)}, bf16[12,8,256]{2,1,0:T(8,128)(2,1)S(1)}, u32[]{:S(2)}, u32[]{:S(2)}) collective-permute-start(bf16[12,8,256]{2,1,0:T(8,128)(2,1)S(1)} %get-tuple-element.216.refs_0_), channel_id=1, source_target_pairs={{0,12},{1,13},{2,14},{3,15},{4,8},{5,9},{6,10},{7,11},{8,4},{9,5},... | collective-permute-start | bytes 147464 | tf_op jit(solution)/shard_map/ppermute | solution.py:268
  122.9 1.9 %collective-permute-done.70.refs_0_ = bf16[12,8,256]{2,1,0:T(8,128)(2,1)S(1)} collective-permute-done((bf16[12,8,256]{2,1,0:T(8,128)(2,1)S(1)}, bf16[12,8,256]{2,1,0:T(8,128)(2,1)S(1)}, u32[]{:S(2)}, u32[]{:S(2)}) %collective-permute-start.70) | collective-permute-done | bytes 49184 | tf_op jit(solution)/shard_map/ppermute | solution.py:268
  129.8 1.6 %last.1 = f32[8,2048]{1,0:T(8,128)} custom-call(s32[96]{0:T(128)S(4)} %get-tuple-element.118.tile_of, s32[96]{0:T(128)S(4)} %get-tuple-element.135.land_of, bf16[88,256,256]{2,1,0:T(8,128)(2,1)S(1)} %turn.1.turned, f32[8,8,256]{2,1,0:T(8,128)S(1)} %near_forward.7.part, f32[8,2048]{1,0:T(8,128)S(1)} %get-tuple-element.221.dy, ...), custom_call_target="tpu_custom_call" | custom-call | flops 46137344 | bytes 5767168 | tf_op jit(solution)/shard_map/last/pallas_call | solution.py:256
  (171 shorter events, 73.4 us)
Async XLA Ops:
  7.1 8.3 %collective-permute-start.6 = (bf16[12,8,256]{2,1,0:T(8,128)(2,1)S(1)}, bf16[12,8,256]{2,1,0:T(8,128)(2,1)S(1)}, u32[]{:S(2)}, u32[]{:S(2)}) collective-permute-start(bf16[12,8,256]{2,1,0:T(8,128)(2,1)S(1)} %get-tuple-element.127), channel_id=1, source_target_pairs={{0,1},{1,0},{2,3},{3,2},{4,5},{5,4},{6,7},{7,6},{8,9},{9,8},{10,11... | collective-permute-start | bytes 147464 | tf_op jit(solution)/shard_map/ppermute | solution.py:268
  10.4 6.3 %collective-permute-start.7 = (bf16[12,8,256]{2,1,0:T(8,128)(2,1)S(1)}, bf16[12,8,256]{2,1,0:T(8,128)(2,1)S(1)}, u32[]{:S(2)}, u32[]{:S(2)}) collective-permute-start(bf16[12,8,256]{2,1,0:T(8,128)(2,1)S(1)} %get-tuple-element.128), channel_id=1, source_target_pairs={{0,2},{1,3},{2,0},{3,1},{4,6},{5,7},{6,4},{7,5},{8,10},{9,11},{10,... | collective-permute-start | bytes 147464 | tf_op jit(solution)/shard_map/ppermute | solution.py:268
  14.1 6.4 %collective-permute-start.3 = (bf16[12,8,256]{2,1,0:T(8,128)(2,1)S(1)}, bf16[12,8,256]{2,1,0:T(8,128)(2,1)S(1)}, u32[]{:S(2)}, u32[]{:S(2)}) collective-permute-start(bf16[12,8,256]{2,1,0:T(8,128)(2,1)S(1)} %get-tuple-element.122), channel_id=1, source_target_pairs={{0,1},{1,0},{2,3},{3,2},{4,5},{5,4},{6,7},{7,6},{8,9},{9,8},{10,11... | collective-permute-start | bytes 147464 | tf_op jit(solution)/shard_map/ppermute | solution.py:268
  14.3 6.3 %collective-permute-start.4 = (bf16[12,8,256]{2,1,0:T(8,128)(2,1)S(1)}, bf16[12,8,256]{2,1,0:T(8,128)(2,1)S(1)}, u32[]{:S(2)}, u32[]{:S(2)}) collective-permute-start(bf16[12,8,256]{2,1,0:T(8,128)(2,1)S(1)} %get-tuple-element.123), channel_id=1, source_target_pairs={{0,2},{1,3},{2,0},{3,1},{4,6},{5,7},{6,4},{7,5},{8,10},{9,11},{10,... | collective-permute-start | bytes 147464 | tf_op jit(solution)/shard_map/ppermute | solution.py:268
  16.9 8.5 %collective-permute-start.9 = (bf16[12,8,256]{2,1,0:T(8,128)(2,1)S(1)}, bf16[12,8,256]{2,1,0:T(8,128)(2,1)S(1)}, u32[]{:S(2)}, u32[]{:S(2)}) collective-permute-start(bf16[12,8,256]{2,1,0:T(8,128)(2,1)S(1)} %get-tuple-element.130), channel_id=1, source_target_pairs={{0,12},{1,13},{2,14},{3,15},{4,8},{5,9},{6,10},{7,11},{8,4},{9,5},... | collective-permute-start | bytes 147464 | tf_op jit(solution)/shard_map/ppermute | solution.py:268
  26.8 6.5 %collective-permute-start.17 = (bf16[12,8,256]{2,1,0:T(8,128)(2,1)S(1)}, bf16[12,8,256]{2,1,0:T(8,128)(2,1)S(1)}, u32[]{:S(2)}, u32[]{:S(2)}) collective-permute-start(bf16[12,8,256]{2,1,0:T(8,128)(2,1)S(1)} %get-tuple-element.137.refs_0_), channel_id=1, source_target_pairs={{0,12},{1,13},{2,14},{3,15},{4,8},{5,9},{6,10},{7,11},{8,4},{9,5},... | collective-permute-start | bytes 147464 | tf_op jit(solution)/shard_map/ppermute | solution.py:268
  30.2 5.8 %collective-permute-start.13 = (bf16[12,8,256]{2,1,0:T(8,128)(2,1)S(1)}, bf16[12,8,256]{2,1,0:T(8,128)(2,1)S(1)}, u32[]{:S(2)}, u32[]{:S(2)}) collective-permute-start(bf16[12,8,256]{2,1,0:T(8,128)(2,1)S(1)} %get-tuple-element.139), channel_id=1, source_target_pairs={{0,1},{1,0},{2,3},{3,2},{4,5},{5,4},{6,7},{7,6},{8,9},{9,8},{10,11... | collective-permute-start | bytes 147464 | tf_op jit(solution)/shard_map/ppermute | solution.py:268
  30.3 6.6 %collective-permute-start.14 = (bf16[12,8,256]{2,1,0:T(8,128)(2,1)S(1)}, bf16[12,8,256]{2,1,0:T(8,128)(2,1)S(1)}, u32[]{:S(2)}, u32[]{:S(2)}) collective-permute-start(bf16[12,8,256]{2,1,0:T(8,128)(2,1)S(1)} %get-tuple-element.140), channel_id=1, source_target_pairs={{0,2},{1,3},{2,0},{3,1},{4,6},{5,7},{6,4},{7,5},{8,10},{9,11},{10,... | collective-permute-start | bytes 147464 | tf_op jit(solution)/shard_map/ppermute | solution.py:268
  31.3 5.7 %collective-permute-start.15 = (bf16[12,8,256]{2,1,0:T(8,128)(2,1)S(1)}, bf16[12,8,256]{2,1,0:T(8,128)(2,1)S(1)}, u32[]{:S(2)}, u32[]{:S(2)}) collective-permute-start(bf16[12,8,256]{2,1,0:T(8,128)(2,1)S(1)} %get-tuple-element.141), channel_id=1, source_target_pairs={{0,3},{1,2},{2,1},{3,0},{4,7},{5,6},{6,5},{7,4},{8,11},{9,10},{10,... | collective-permute-start | bytes 147464 | tf_op jit(solution)/shard_map/ppermute | solution.py:268
  47.1 6.5 %collective-permute-start.27 = (bf16[12,8,256]{2,1,0:T(8,128)(2,1)S(1)}, bf16[12,8,256]{2,1,0:T(8,128)(2,1)S(1)}, u32[]{:S(2)}, u32[]{:S(2)}) collective-permute-start(bf16[12,8,256]{2,1,0:T(8,128)(2,1)S(1)} %get-tuple-element.158), channel_id=1, source_target_pairs={{0,12},{1,13},{2,14},{3,15},{4,8},{5,9},{6,10},{7,11},{8,4},{9,5},... | collective-permute-start | bytes 147464 | tf_op jit(solution)/shard_map/ppermute | solution.py:268
  49.0 6.2 %collective-permute-start.28 = (bf16[12,8,256]{2,1,0:T(8,128)(2,1)S(1)}, bf16[12,8,256]{2,1,0:T(8,128)(2,1)S(1)}, u32[]{:S(2)}, u32[]{:S(2)}) collective-permute-start(bf16[12,8,256]{2,1,0:T(8,128)(2,1)S(1)} %get-tuple-element.159), channel_id=1, source_target_pairs={{0,8},{1,9},{2,10},{3,11},{4,12},{5,13},{6,14},{7,15},{8,0},{9,1},... | collective-permute-start | bytes 147464 | tf_op jit(solution)/shard_map/ppermute | solution.py:268
  55.9 5.9 %collective-permute-start.35 = (bf16[12,8,256]{2,1,0:T(8,128)(2,1)S(1)}, bf16[12,8,256]{2,1,0:T(8,128)(2,1)S(1)}, u32[]{:S(2)}, u32[]{:S(2)}) collective-permute-start(bf16[12,8,256]{2,1,0:T(8,128)(2,1)S(1)} %get-tuple-element.163.refs_0_), channel_id=1, source_target_pairs={{0,12},{1,13},{2,14},{3,15},{4,8},{5,9},{6,10},{7,11},{8,4},{9,5},... | collective-permute-start | bytes 147464 | tf_op jit(solution)/shard_map/ppermute | solution.py:268
  57.8 5.8 %collective-permute-start.34 = (bf16[12,8,256]{2,1,0:T(8,128)(2,1)S(1)}, bf16[12,8,256]{2,1,0:T(8,128)(2,1)S(1)}, u32[]{:S(2)}, u32[]{:S(2)}) collective-permute-start(bf16[12,8,256]{2,1,0:T(8,128)(2,1)S(1)} %get-tuple-element.163.refs_0_), channel_id=1, source_target_pairs={{0,8},{1,9},{2,10},{3,11},{4,12},{5,13},{6,14},{7,15},{8,0},{9,1},... | collective-permute-start | bytes 147464 | tf_op jit(solution)/shard_map/ppermute | solution.py:268
  59.7 5.9 %collective-permute-start.32 = (bf16[12,8,256]{2,1,0:T(8,128)(2,1)S(1)}, bf16[12,8,256]{2,1,0:T(8,128)(2,1)S(1)}, u32[]{:S(2)}, u32[]{:S(2)}) collective-permute-start(bf16[12,8,256]{2,1,0:T(8,128)(2,1)S(1)} %get-tuple-element.166), channel_id=1, source_target_pairs={{0,2},{1,3},{2,0},{3,1},{4,6},{5,7},{6,4},{7,5},{8,10},{9,11},{10,... | collective-permute-start | bytes 147464 | tf_op jit(solution)/shard_map/ppermute | solution.py:268
  75.7 6.4 %collective-permute-start.45 = (bf16[12,8,256]{2,1,0:T(8,128)(2,1)S(1)}, bf16[12,8,256]{2,1,0:T(8,128)(2,1)S(1)}, u32[]{:S(2)}, u32[]{:S(2)}) collective-permute-start(bf16[12,8,256]{2,1,0:T(8,128)(2,1)S(1)} %get-tuple-element.184), channel_id=1, source_target_pairs={{0,12},{1,13},{2,14},{3,15},{4,8},{5,9},{6,10},{7,11},{8,4},{9,5},... | collective-permute-start | bytes 147464 | tf_op jit(solution)/shard_map/ppermute | solution.py:268
  77.7 5.9 %collective-permute-start.46 = (bf16[12,8,256]{2,1,0:T(8,128)(2,1)S(1)}, bf16[12,8,256]{2,1,0:T(8,128)(2,1)S(1)}, u32[]{:S(2)}, u32[]{:S(2)}) collective-permute-start(bf16[12,8,256]{2,1,0:T(8,128)(2,1)S(1)} %get-tuple-element.185), channel_id=1, source_target_pairs={{0,8},{1,9},{2,10},{3,11},{4,12},{5,13},{6,14},{7,15},{8,0},{9,1},... | collective-permute-start | bytes 147464 | tf_op jit(solution)/shard_map/ppermute | solution.py:268
  84.6 5.9 %collective-permute-start.53 = (bf16[12,8,256]{2,1,0:T(8,128)(2,1)S(1)}, bf16[12,8,256]{2,1,0:T(8,128)(2,1)S(1)}, u32[]{:S(2)}, u32[]{:S(2)}) collective-permute-start(bf16[12,8,256]{2,1,0:T(8,128)(2,1)S(1)} %get-tuple-element.189.refs_0_), channel_id=1, source_target_pairs={{0,12},{1,13},{2,14},{3,15},{4,8},{5,9},{6,10},{7,11},{8,4},{9,5},... | collective-permute-start | bytes 147464 | tf_op jit(solution)/shard_map/ppermute | solution.py:268
  86.5 5.8 %collective-permute-start.52 = (bf16[12,8,256]{2,1,0:T(8,128)(2,1)S(1)}, bf16[12,8,256]{2,1,0:T(8,128)(2,1)S(1)}, u32[]{:S(2)}, u32[]{:S(2)}) collective-permute-start(bf16[12,8,256]{2,1,0:T(8,128)(2,1)S(1)} %get-tuple-element.189.refs_0_), channel_id=1, source_target_pairs={{0,8},{1,9},{2,10},{3,11},{4,12},{5,13},{6,14},{7,15},{8,0},{9,1},... | collective-permute-start | bytes 147464 | tf_op jit(solution)/shard_map/ppermute | solution.py:268
  88.6 5.7 %collective-permute-start.50 = (bf16[12,8,256]{2,1,0:T(8,128)(2,1)S(1)}, bf16[12,8,256]{2,1,0:T(8,128)(2,1)S(1)}, u32[]{:S(2)}, u32[]{:S(2)}) collective-permute-start(bf16[12,8,256]{2,1,0:T(8,128)(2,1)S(1)} %get-tuple-element.192), channel_id=1, source_target_pairs={{0,2},{1,3},{2,0},{3,1},{4,6},{5,7},{6,4},{7,5},{8,10},{9,11},{10,... | collective-permute-start | bytes 147464 | tf_op jit(solution)/shard_map/ppermute | solution.py:268
  108.1 6.2 %collective-permute-start.63 = (bf16[12,8,256]{2,1,0:T(8,128)(2,1)S(1)}, bf16[12,8,256]{2,1,0:T(8,128)(2,1)S(1)}, u32[]{:S(2)}, u32[]{:S(2)}) collective-permute-start(bf16[12,8,256]{2,1,0:T(8,128)(2,1)S(1)} %get-tuple-element.210), channel_id=1, source_target_pairs={{0,12},{1,13},{2,14},{3,15},{4,8},{5,9},{6,10},{7,11},{8,4},{9,5},... | collective-permute-start | bytes 147464 | tf_op jit(solution)/shard_map/ppermute | solution.py:268
  110.3 5.6 %collective-permute-start.64 = (bf16[12,8,256]{2,1,0:T(8,128)(2,1)S(1)}, bf16[12,8,256]{2,1,0:T(8,128)(2,1)S(1)}, u32[]{:S(2)}, u32[]{:S(2)}) collective-permute-start(bf16[12,8,256]{2,1,0:T(8,128)(2,1)S(1)} %get-tuple-element.211), channel_id=1, source_target_pairs={{0,8},{1,9},{2,10},{3,11},{4,12},{5,13},{6,14},{7,15},{8,0},{9,1},... | collective-permute-start | bytes 147464 | tf_op jit(solution)/shard_map/ppermute | solution.py:268
  116.6 6.3 %collective-permute-start.71 = (bf16[12,8,256]{2,1,0:T(8,128)(2,1)S(1)}, bf16[12,8,256]{2,1,0:T(8,128)(2,1)S(1)}, u32[]{:S(2)}, u32[]{:S(2)}) collective-permute-start(bf16[12,8,256]{2,1,0:T(8,128)(2,1)S(1)} %get-tuple-element.216.refs_0_), channel_id=1, source_target_pairs={{0,12},{1,13},{2,14},{3,15},{4,8},{5,9},{6,10},{7,11},{8,4},{9,5},... | collective-permute-start | bytes 147464 | tf_op jit(solution)/shard_map/ppermute | solution.py:268
  118.7 6.1 %collective-permute-start.70 = (bf16[12,8,256]{2,1,0:T(8,128)(2,1)S(1)}, bf16[12,8,256]{2,1,0:T(8,128)(2,1)S(1)}, u32[]{:S(2)}, u32[]{:S(2)}) collective-permute-start(bf16[12,8,256]{2,1,0:T(8,128)(2,1)S(1)} %get-tuple-element.216.refs_0_), channel_id=1, source_target_pairs={{0,8},{1,9},{2,10},{3,11},{4,12},{5,13},{6,14},{7,15},{8,0},{9,1},... | collective-permute-start | bytes 147464 | tf_op jit(solution)/shard_map/ppermute | solution.py:268
  120.8 6.0 %collective-permute-start.68 = (bf16[12,8,256]{2,1,0:T(8,128)(2,1)S(1)}, bf16[12,8,256]{2,1,0:T(8,128)(2,1)S(1)}, u32[]{:S(2)}, u32[]{:S(2)}) collective-permute-start(bf16[12,8,256]{2,1,0:T(8,128)(2,1)S(1)} %get-tuple-element.219), channel_id=1, source_target_pairs={{0,2},{1,3},{2,0},{3,1},{4,6},{5,7},{6,4},{7,5},{8,10},{9,11},{10,... | collective-permute-start | bytes 147464 | tf_op jit(solution)/shard_map/ppermute | solution.py:268
  (56 other events, 262.3 us)

commit v6 on v4

--- a/solution.py
+++ b/solution.py
@@ -34,7 +34,7 @@
 
 
 def transpose_products(base, tile_of, row_of, tiles, hb, outs):
-    per = outs[0].shape[0]
+    per = tile_of.shape[0] // (2 * QUAD)
     for x, out in enumerate(outs):
         for s in range(per):
             slot = base + x * per + s
@@ -64,7 +64,7 @@
 
 
 def start_kernel(step, peers, cap, col_blocks, count, rows_in, cols_in, tiles, step_in, mask_in, cot_in,
-                 held, dy, rhs, hb, tile_of, row_of, land_of, wants, o0, o1, o2, o3,
+                 held, dy, rhs, hb, tile_of, row_of, land_of, o0, o1, o2, o3,
                  rows, cols, dual_step, dual_mask, cot_y, filled, sems, small):
     tile_slots, side, _ = tiles.shape
     group = peers // QUAD
@@ -91,31 +91,30 @@
         tile_of[s] = 0
         row_of[s] = 0
         land_of[s] = hb.shape[0]
-    for x in range(QUAD):
-        for s in range(group * cap):
-            wants[x, s] = col_blocks
     for copy in minor:
         copy.wait()
     me = lax.axis_index("rb").astype(I32)
     scale = (1 << 19) // col_blocks + 1
 
-    def place_tile(t, _):
+    lane = lax.broadcasted_iota(I32, o0.shape[1:], 1)
+    line = lax.broadcasted_iota(I32, o0.shape[1:], 0)
+
+    def place_tile(t, plan):
         col = cols[t]
         owner = (col * scale) >> 19
         rank = filled[owner]
         filled[owner] = rank + 1
         apart = owner ^ me
         high, quad = apart // QUAD, apart % QUAD
-        place = high * cap + rank
-        near = jnp.where(high < half, 1, 0)
-        slot = (near * QUAD + quad) * (half * cap) + place - (1 - near) * (half * cap)
+        slot = ((1 - high % 2) * QUAD + quad) * (half * cap) + high // 2 * cap + rank
         tile_of[slot] = t
         row_of[slot] = rows[t]
         land_of[slot] = rows[t]
-        wants[quad, place] = col - owner * col_blocks
-        return 0
-
-    lax.fori_loop(0, count[0], place_tile, 0)
+        return jnp.where((line == quad) & (lane == high * cap + rank), col - owner * col_blocks, plan)
+
+    plan = lax.fori_loop(0, count[0], place_tile, jnp.full(o0.shape[1:], col_blocks, I32)).astype(BF16)
+    for out in (o0, o1, o2, o3):
+        out[half * cap] = plan
     dy[...] = dual_mask[...].astype(F32) * cot_y[...]
 
     def h_into(at, h):
@@ -140,27 +139,41 @@
     transpose_products(tile_of.shape[0] // 2, tile_of, row_of, held, hb, (o0, o1, o2, o3))
 
 
-def sum_kernel(first_high, cap, wants, got1, got2, got3, a0, a1, a2, a3, *rest):
+def map_kernel(a0, a1, a2, a3, wants, whole, sem):
+    for x, part in enumerate((a0, a1, a2, a3)):
+        plan = part[part.shape[0] - 1].astype(F32)
+        whole[pl.ds(x, 1)] = plan[x:x + 1].astype(I32)
+    whole[pl.ds(QUAD, QUAD)] = jnp.zeros((QUAD, whole.shape[1]), I32)
+    copy = pltpu.make_async_copy(whole, wants, sem)
+    copy.start()
+    copy.wait()
+
+
+def sum_kernel(highs, cap, wants, a0, a1, a2, a3, *rest):
     parts = (a0, a1, a2, a3)
-    half = a0.shape[0] // cap
-    outs, totals = rest[:half], rest[half:]
+    count = len(highs)
+    totals = rest[len(rest) - 2 * count:]
+    outs = rest[len(rest) - 3 * count:len(rest) - 2 * count]
+    passed = rest[:len(rest) - 3 * count]
     for total in totals:
         total[...] = jnp.zeros_like(total)
     for r in range(cap):
         for pair in range(QUAD // 2):
             jobs = []
-            for h in range(half):
+            for h in range(count):
                 for side in range(2):
                     x = 2 * pair + side
-                    want = (wants, got1, got2, got3)[x]
-                    spot = want[x, (first_high + h) * cap + r]
+                    spot = wants[x, highs[h] * cap + r]
                     jobs.append((totals[2 * h + side], spot, parts[x][h * cap + r].astype(F32)))
             values = [total[spot] + part for total, spot, part in jobs]
             for (total, spot, _), value in zip(jobs, values):
                 total[spot] = value
     for h, out in enumerate(outs):
         for c in range(out.shape[0]):
-            out[c] = (totals[2 * h][c] + totals[2 * h + 1][c]).astype(out.dtype)
+            value = totals[2 * h][c] + totals[2 * h + 1][c]
+            if passed and h > 0:
+                value = value + passed[h - 1][c].astype(F32)
+            out[c] = value.astype(out.dtype)
 
 
 def primal_kernel(step, first, primal_mask, primal_step, x, spent, *refs):
@@ -178,15 +191,12 @@
         out[c] = q.astype(BF16)
 
 
-def pick_kernel(first_high, cap, wants, got1, got2, got3, *refs):
+def pick_kernel(highs, cap, wants, *refs):
     blocks, outs = refs[:-QUAD], refs[-QUAD:]
     last = blocks[0].shape[0] - 1
     for x, out in enumerate(outs):
-        want = (wants, got1, got2, got3)[x]
         values = [
-            blocks[h][jnp.minimum(want[x, (first_high + h) * cap + r], last)]
-            for h in range(len(blocks))
-            for r in range(cap)
+            block[jnp.minimum(wants[x, high * cap + r], last)] for high, block in zip(highs, blocks) for r in range(cap)
         ]
         for s, value in enumerate(values):
             out[s] = value
@@ -240,7 +250,7 @@
     part_set = (shape((half * cap, batch, side), BF16),) * QUAD
     block_set = shape((col_blocks, batch, side), BF16)
     hb_set = shape((row_blocks, batch, side), BF16)
-    per_slot = shape((slots,), I32)
+    per_slot = pltpu.SMEM((slots,), I32)
     row_totals = [pltpu.VMEM((row_blocks + 1, batch, side), F32)] * LANES
     col_totals = [pltpu.VMEM((col_blocks + 1, batch, side), F32)] * (2 * half)
     tile_bytes = tiles.size * 2
@@ -264,14 +274,13 @@
         return [parts[0]] + [swap(parts[x], x) for x in range(1, QUAD)]
 
     step = steps - 1
-    held, dy, rhs, hb, tile_of, row_of, land_of, wants, *far_parts = pl.pallas_call(
+    held, dy, rhs, hb, tile_of, row_of, land_of, *far_parts = pl.pallas_call(
         functools.partial(start_kernel, step, peers, cap, col_blocks),
         out_shape=(
             pltpu.VMEM(tiles.shape, BF16), y_shape, y_shape, hb_set, per_slot, per_slot, per_slot,
-            shape((QUAD, group * cap), I32),
-        ) + part_set,
+        ) + (shape((half * cap + 1, batch, side), BF16),) * QUAD,
         in_specs=[SM] + [HBM] * 6,
-        out_specs=(VM,) * 4 + (SM,) * 4 + (VM,) * QUAD,
+        out_specs=(VM,) * 4 + (SM,) * 3 + (VM,) * QUAD,
         scratch_shapes=[
             pltpu.SMEM((tile_slots,), I32), pltpu.SMEM((tile_slots,), I32), pltpu.VMEM(dual_step.shape, F32),
             pltpu.VMEM(cot_y.shape, I32), pltpu.VMEM(cot_y.shape, F32), pltpu.SMEM((peers,), I32),
@@ -284,28 +293,43 @@
         pltpu.with_memory_space_constraint(array, pltpu.HBM)
         for array in (tile_rows, tile_cols, tiles, dual_step, dual_mask, cot_y)
     ))
-    maps = [wants] + [swap(wants, x) for x in range(1, QUAD)]
     turned = call(turn_kernel, "turn", tile_bytes, [VM], pltpu.VMEM(tiles.shape, BF16), (held,))
-    x_state, spent = cot_x, cot_x
+    x_state, spent, wants = cot_x, cot_x, None
+    odd, even = tuple(range(1, group, 2)), tuple(range(0, group, 2))
     while True:
         far_got = near_swaps(far_parts)
         near_parts = call(near_product_kernel, "near_product", tile_bytes // 2, [SM] * 2 + [VM] * 2, part_set,
                           (tile_of, row_of, held, hb))
         near_got = near_swaps(near_parts)
-        far_sums = call(functools.partial(sum_kernel, half, cap), "far_sum", 1 << 20, [SM] * QUAD + [VM] * QUAD,
-                        (block_set,) * half, (*maps, *far_got), col_totals)
-        got = [swap(far_sums[h], (half + h) * QUAD) for h in reversed(range(half))]
-        near_sums = call(functools.partial(sum_kernel, 0, cap), "near_sum", 1 << 20, [SM] * QUAD + [VM] * QUAD,
-                         (shape(block_set.shape, F32),) + (block_set,) * (half - 1), (*maps, *near_got), col_totals)
-        got += [swap(near_sums[h], h * QUAD) for h in range(1, half)]
+        if wants is None:
+            wants = pl.pallas_call(
+                map_kernel,
+                out_shape=pltpu.SMEM((2 * QUAD, side), I32),
+                in_specs=[VM] * QUAD,
+                out_specs=SM,
+                scratch_shapes=[pltpu.VMEM((2 * QUAD, side), I32), pltpu.SemaphoreType.DMA],
+                compiler_params=PARAMS,
+                name="maps",
+            )(*far_got)
+        far_sums = call(functools.partial(sum_kernel, odd, cap), "odd_sum", 1 << 20, [SM] + [VM] * QUAD,
+                        (block_set,) * half, (wants, *far_got), col_totals)
+        passed = [swap(far_sums[j], QUAD) for j in range(1, half)]
+        beside = swap(far_sums[0], QUAD)
+        near_sums = call(functools.partial(sum_kernel, even, cap), "even_sum", 1 << 20, [SM] + [VM] * (QUAD + half - 1),
+                         (shape(block_set.shape, F32),) + (block_set,) * (half - 1), (wants, *near_got, *passed),
+                         col_totals)
+        got = [beside] + [swap(near_sums[j], 2 * j * QUAD) for j in range(1, half)]
+        if step == steps - 1:
+            turned, x_state = lax.optimization_barrier((turned, x_state))
         x_state, spent, moved = call(
-            functools.partial(primal_kernel, step, step == steps - 1), "primal", 1 << 20, [VM] * (4 + group),
+            functools.partial(primal_kernel, step, step == steps - 1), "primal", 1 << 20, [VM] * (5 + half),
             (x_shape, x_shape, block_set), (primal_mask, primal_step, x_state, spent, near_sums[0], *got))
-        blocks = [moved] + [swap(moved, h * QUAD) for h in range(1, group)]
-        near_moved = near_swaps(call(functools.partial(pick_kernel, 0, cap), "near_pick", 1 << 20,
-                                     [SM] * QUAD + [VM] * half, part_set, (*maps, *blocks[:half])))
-        far_moved = near_swaps(call(functools.partial(pick_kernel, half, cap), "far_pick", 1 << 20,
-                                    [SM] * QUAD + [VM] * half, part_set, (*maps, *blocks[half:])))
+        blocks = [moved] + [swap(moved, 2 * j * QUAD) for j in range(1, half)]
+        beside = [swap(block, QUAD) for block in blocks]
+        near_moved = near_swaps(call(functools.partial(pick_kernel, even, cap), "even_pick", 1 << 20,
+                                     [SM] + [VM] * half, part_set, (wants, *blocks)))
+        far_moved = near_swaps(call(functools.partial(pick_kernel, odd, cap), "odd_pick", 1 << 20,
+                                    [SM] + [VM] * half, part_set, (wants, *beside)))
         part = call(near_forward_kernel, "near_forward", tile_bytes // 2, [SM] * 2 + [VM] * (1 + QUAD),
                     shape(hb_set.shape, F32), (tile_of, land_of, turned, *near_moved), row_totals)
         if step == 0:

time: 143 us -> 138 us (0.965)
  Pallas kernels: 44.5 us -> 29.2 us
  waiting for transfers between devices: 33.6 us -> 39.3 us
  starting transfers between devices: 63.5 us -> 68.5 us
    pallas_call x33, Pallas kernels: 38.5 us -> 21.4 us  [call(): pl.pallas_call(kernel, out_shape=outs, in_specs=ins, out_specs=jax.tree.m...]
    ppermute x75 -> x72, waiting for transfers between devices: 33.6 us -> 39.3 us  [swap(): return lax.ppermute(array, 'rb', [(p, p ^ x) for p in range(peers)])]
    ppermute x75 -> x72, starting transfers between devices: 63.5 us -> 68.5 us  [swap(): return lax.ppermute(array, 'rb', [(p, p ^ x) for p in range(peers)])]
  transfers between devices with their start and end apart: 75 -> 72, of which waited for: 33 -> 41; matrix products, arithmetic and copies ran while one was open for 0% -> 0% of each run, Pallas kernels for 18% -> 10%
where the time goes in v6:
time: 138 us; the launch traced here: 139 us
  starting transfers between devices  68.5 us (50%)
  waiting for transfers between devices  39.3 us (28%)
  Pallas kernels  29.2 us (21%)
  between operations  1.66 us (1%)
    ppermute x72, starting transfers between devices, swap(): return lax.ppermute(array, 'rb', [(p, p ^ x) for p in range(peers)])  68.5 us
    ppermute x72, waiting for transfers between devices, swap(): return lax.ppermute(array, 'rb', [(p, p ^ x) for p in range(peers)])  39.3 us
    pallas_call x33, Pallas kernels, call(): pl.pallas_call(kernel, out_shape=outs, in_specs=ins, out_specs=jax.tree.m...  21.4 us
    pallas_call x1, Pallas kernels, on_device(): pl.pallas_call(functools.partial(start_kernel, step, peers, cap, col_bloc...  7.05 us
  transfers between devices with their start and end apart: 72, of which 41 were waited for; matrix products, arithmetic and copies ran while one was open for 0% of the time, Pallas kernels for 10%

profile of v6, /device:TPU:0, one launch (start us, length us, event | category | flops | bytes accessed | tf_op | source)
XLA Modules:
  0.0 138.7 jit_solution(11291967093703207695)
XLA Ops:
  1.3 7.0 %start.1 = (bf16[88,256,256]{2,1,0:T(8,128)(2,1)S(1)}, f32[8,2048]{1,0:T(8,128)S(1)}, f32[8,2048]{1,0:T(8,128)S(1)}, bf16[8,8,256]{2,1,0:T(8,128)(2,1)S(1)}, s32...) custom-call(s32[1]{0:T(128)S(6)} %copy.14.count, ...), custom_call_target="tpu_custom_call" | custom-call | flops 184549376 | bytes 23068672 | tf_op jit(solution)/shard_map/start/pallas_call | solution.py:277
  8.4 2.2 %collective-permute-start.1 = (bf16[13,8,256]{2,1,0:T(8,128)(2,1)S(1)}, bf16[13,8,256]{2,1,0:T(8,128)(2,1)S(1)}, u32[]{:S(2)}, u32[]{:S(2)}) collective-permute-start(bf16[13,8,256]{2,1,0:T(8,128)(2,1)S(1)} %get-tuple-element.118), channel_id=1, source_target_pairs={{0,2},{1,3},{2,0},{3,1},{4,6},{5,7},{6,4},{7,5},{8,10},{9,11},{10,... | collective-permute-start | bytes 159752 | tf_op jit(solution)/shard_map/ppermute | solution.py:271
  11.7 2.0 %collective-permute-start.4 = (bf16[12,8,256]{2,1,0:T(8,128)(2,1)S(1)}, bf16[12,8,256]{2,1,0:T(8,128)(2,1)S(1)}, u32[]{:S(2)}, u32[]{:S(2)}) collective-permute-start(bf16[12,8,256]{2,1,0:T(8,128)(2,1)S(1)} %get-tuple-element.125), channel_id=1, source_target_pairs={{0,2},{1,3},{2,0},{3,1},{4,6},{5,7},{6,4},{7,5},{8,10},{9,11},{10,... | collective-permute-start | bytes 147464 | tf_op jit(solution)/shard_map/ppermute | solution.py:271
  15.4 2.0 %collective-permute-start.6 = (bf16[12,8,256]{2,1,0:T(8,128)(2,1)S(1)}, bf16[12,8,256]{2,1,0:T(8,128)(2,1)S(1)}, u32[]{:S(2)}, u32[]{:S(2)}) collective-permute-start(bf16[12,8,256]{2,1,0:T(8,128)(2,1)S(1)} %get-tuple-element.127), channel_id=1, source_target_pairs={{0,4},{1,5},{2,6},{3,7},{4,0},{5,1},{6,2},{7,3},{8,12},{9,13},{10,... | collective-permute-start | bytes 147464 | tf_op jit(solution)/shard_map/ppermute | solution.py:271
  17.7 2.0 %collective-permute-done.6.rest_0_ = bf16[12,8,256]{2,1,0:T(8,128)(2,1)S(1)} collective-permute-done((bf16[12,8,256]{2,1,0:T(8,128)(2,1)S(1)}, bf16[12,8,256]{2,1,0:T(8,128)(2,1)S(1)}, u32[]{:S(2)}, u32[]{:S(2)}) %collective-permute-start.6) | collective-permute-done | bytes 49184 | tf_op jit(solution)/shard_map/ppermute | solution.py:271
  19.9 3.4 %collective-permute-start.8 = (bf16[12,8,256]{2,1,0:T(8,128)(2,1)S(1)}, bf16[12,8,256]{2,1,0:T(8,128)(2,1)S(1)}, u32[]{:S(2)}, u32[]{:S(2)}) collective-permute-start(bf16[12,8,256]{2,1,0:T(8,128)(2,1)S(1)} %get-tuple-element.130), channel_id=1, source_target_pairs={{0,8},{1,9},{2,10},{3,11},{4,12},{5,13},{6,14},{7,15},{8,0},{9,1},... | collective-permute-start | bytes 147464 | tf_op jit(solution)/shard_map/ppermute | solution.py:271
  23.3 3.7 %turn.1.turned = bf16[88,256,256]{2,1,0:T(8,128)(2,1)S(1)} custom-call(bf16[88,256,256]{2,1,0:T(8,128)(2,1)S(1)} %get-tuple-element.114.held), custom_call_target="tpu_custom_call" | custom-call | flops 92274688 | bytes 11534336 | tf_op jit(solution)/shard_map/turn/pallas_call | solution.py:259
  28.5 2.0 %collective-permute-start.13 = (bf16[12,8,256]{2,1,0:T(8,128)(2,1)S(1)}, bf16[12,8,256]{2,1,0:T(8,128)(2,1)S(1)}, u32[]{:S(2)}, u32[]{:S(2)}) collective-permute-start(bf16[12,8,256]{2,1,0:T(8,128)(2,1)S(1)} %get-tuple-element.135.refs_0_), channel_id=1, source_target_pairs={{0,4},{1,5},{2,6},{3,7},{4,0},{5,1},{6,2},{7,3},{8,12},{9,13},{10,... | collective-permute-start | bytes 147464 | tf_op jit(solution)/shard_map/ppermute | solution.py:271
  30.4 1.8 %collective-permute-done.9.refs_1_ = bf16[12,8,256]{2,1,0:T(8,128)(2,1)S(1)} collective-permute-done((bf16[12,8,256]{2,1,0:T(8,128)(2,1)S(1)}, bf16[12,8,256]{2,1,0:T(8,128)(2,1)S(1)}, u32[]{:S(2)}, u32[]{:S(2)}) %collective-permute-start.9) | collective-permute-done | bytes 49184 | tf_op jit(solution)/shard_map/ppermute | solution.py:271
  32.3 1.8 %collective-permute-start.14 = (bf16[12,8,256]{2,1,0:T(8,128)(2,1)S(1)}, bf16[12,8,256]{2,1,0:T(8,128)(2,1)S(1)}, u32[]{:S(2)}, u32[]{:S(2)}) collective-permute-start(bf16[12,8,256]{2,1,0:T(8,128)(2,1)S(1)} %collective-permute-done.9.refs_1_), channel_id=1, source_target_pairs={{0,4},{1,5},{2,6},{3,7},{4,0},{5,1},{6,2},{7,3},{8,12},{9,13},{10,... | collective-permute-start | bytes 147464 | tf_op jit(solution)/shard_map/ppermute | solution.py:271
  41.4 1.9 %middle.3 = (f32[8,2048]{1,0:T(8,128)S(1)}, f32[8,2048]{1,0:T(8,128)S(1)}, bf16[8,8,256]{2,1,0:T(8,128)(2,1)S(1)}, bf16[12,8,256]{2,1,0:T(8,128)(2,1)S(1)}, bf16...) custom-call(s32[96]{0:T(128)S(4)} %get-tuple-element.120.tile_of, ...), custom_call_target="tpu_custom_call" | custom-call | flops 92274688 | bytes 11534336 | tf_op jit(solution)/shard_map/middle/pallas_call | solution.py:259
  48.6 1.8 %collective-permute-start.24 = (bf16[12,8,256]{2,1,0:T(8,128)(2,1)S(1)}, bf16[12,8,256]{2,1,0:T(8,128)(2,1)S(1)}, u32[]{:S(2)}, u32[]{:S(2)}) collective-permute-start(bf16[12,8,256]{2,1,0:T(8,128)(2,1)S(1)} %get-tuple-element.155), channel_id=1, source_target_pairs={{0,4},{1,5},{2,6},{3,7},{4,0},{5,1},{6,2},{7,3},{8,12},{9,13},{10,... | collective-permute-start | bytes 147464 | tf_op jit(solution)/shard_map/ppermute | solution.py:271
  54.6 3.3 %collective-permute-done.26.refs_2_ = bf16[12,8,256]{2,1,0:T(8,128)(2,1)S(1)} collective-permute-done((bf16[12,8,256]{2,1,0:T(8,128)(2,1)S(1)}, bf16[12,8,256]{2,1,0:T(8,128)(2,1)S(1)}, u32[]{:S(2)}, u32[]{:S(2)}) %collective-permute-start.26) | collective-permute-done | bytes 49184 | tf_op jit(solution)/shard_map/ppermute | solution.py:271
  59.7 2.0 %collective-permute-start.31 = (bf16[12,8,256]{2,1,0:T(8,128)(2,1)S(1)}, bf16[12,8,256]{2,1,0:T(8,128)(2,1)S(1)}, u32[]{:S(2)}, u32[]{:S(2)}) collective-permute-start(bf16[12,8,256]{2,1,0:T(8,128)(2,1)S(1)} %get-tuple-element.161.refs_0_), channel_id=1, source_target_pairs={{0,4},{1,5},{2,6},{3,7},{4,0},{5,1},{6,2},{7,3},{8,12},{9,13},{10,... | collective-permute-start | bytes 147464 | tf_op jit(solution)/shard_map/ppermute | solution.py:271
  63.1 2.5 %collective-permute-start.32 = (bf16[12,8,256]{2,1,0:T(8,128)(2,1)S(1)}, bf16[12,8,256]{2,1,0:T(8,128)(2,1)S(1)}, u32[]{:S(2)}, u32[]{:S(2)}) collective-permute-start(bf16[12,8,256]{2,1,0:T(8,128)(2,1)S(1)} %collective-permute-done.27.refs_1_), channel_id=1, source_target_pairs={{0,4},{1,5},{2,6},{3,7},{4,0},{5,1},{6,2},{7,3},{8,12},{9,13},{10,... | collective-permute-start | bytes 147464 | tf_op jit(solution)/shard_map/ppermute | solution.py:271
  73.1 1.9 %middle.4 = (f32[8,2048]{1,0:T(8,128)S(1)}, f32[8,2048]{1,0:T(8,128)S(1)}, bf16[8,8,256]{2,1,0:T(8,128)(2,1)S(1)}, bf16[12,8,256]{2,1,0:T(8,128)(2,1)S(1)}, bf16...) custom-call(s32[96]{0:T(128)S(4)} %get-tuple-element.120.tile_of, ...), custom_call_target="tpu_custom_call" | custom-call | flops 92274688 | bytes 11534336 | tf_op jit(solution)/shard_map/middle/pallas_call | solution.py:259
  86.0 3.5 %collective-permute-done.44.refs_2_ = bf16[12,8,256]{2,1,0:T(8,128)(2,1)S(1)} collective-permute-done((bf16[12,8,256]{2,1,0:T(8,128)(2,1)S(1)}, bf16[12,8,256]{2,1,0:T(8,128)(2,1)S(1)}, u32[]{:S(2)}, u32[]{:S(2)}) %collective-permute-start.44) | collective-permute-done | bytes 49184 | tf_op jit(solution)/shard_map/ppermute | solution.py:271
  90.8 2.1 %collective-permute-start.49 = (bf16[12,8,256]{2,1,0:T(8,128)(2,1)S(1)}, bf16[12,8,256]{2,1,0:T(8,128)(2,1)S(1)}, u32[]{:S(2)}, u32[]{:S(2)}) collective-permute-start(bf16[12,8,256]{2,1,0:T(8,128)(2,1)S(1)} %get-tuple-element.187.refs_0_), channel_id=1, source_target_pairs={{0,4},{1,5},{2,6},{3,7},{4,0},{5,1},{6,2},{7,3},{8,12},{9,13},{10,... | collective-permute-start | bytes 147464 | tf_op jit(solution)/shard_map/ppermute | solution.py:271
  94.6 2.1 %collective-permute-start.50 = (bf16[12,8,256]{2,1,0:T(8,128)(2,1)S(1)}, bf16[12,8,256]{2,1,0:T(8,128)(2,1)S(1)}, u32[]{:S(2)}, u32[]{:S(2)}) collective-permute-start(bf16[12,8,256]{2,1,0:T(8,128)(2,1)S(1)} %collective-permute-done.45.refs_1_), channel_id=1, source_target_pairs={{0,4},{1,5},{2,6},{3,7},{4,0},{5,1},{6,2},{7,3},{8,12},{9,13},{10,... | collective-permute-start | bytes 147464 | tf_op jit(solution)/shard_map/ppermute | solution.py:271
  104.5 2.5 %middle.5 = (f32[8,2048]{1,0:T(8,128)S(1)}, f32[8,2048]{1,0:T(8,128)}, bf16[8,8,256]{2,1,0:T(8,128)(2,1)S(1)}, bf16[12,8,256]{2,1,0:T(8,128)(2,1)S(1)}, bf16[12,...) custom-call(s32[96]{0:T(128)S(4)} %get-tuple-element.120.tile_of, ...), custom_call_target="tpu_custom_call" | custom-call | flops 92274688 | bytes 11534336 | tf_op jit(solution)/shard_map/middle/pallas_call | solution.py:259
  118.0 3.5 %collective-permute-done.62.refs_2_ = bf16[12,8,256]{2,1,0:T(8,128)(2,1)S(1)} collective-permute-done((bf16[12,8,256]{2,1,0:T(8,128)(2,1)S(1)}, bf16[12,8,256]{2,1,0:T(8,128)(2,1)S(1)}, u32[]{:S(2)}, u32[]{:S(2)}) %collective-permute-start.62) | collective-permute-done | bytes 49184 | tf_op jit(solution)/shard_map/ppermute | solution.py:271
  123.2 2.1 %collective-permute-start.67 = (bf16[12,8,256]{2,1,0:T(8,128)(2,1)S(1)}, bf16[12,8,256]{2,1,0:T(8,128)(2,1)S(1)}, u32[]{:S(2)}, u32[]{:S(2)}) collective-permute-start(bf16[12,8,256]{2,1,0:T(8,128)(2,1)S(1)} %get-tuple-element.214.refs_0_), channel_id=1, source_target_pairs={{0,4},{1,5},{2,6},{3,7},{4,0},{5,1},{6,2},{7,3},{8,12},{9,13},{10,... | collective-permute-start | bytes 147464 | tf_op jit(solution)/shard_map/ppermute | solution.py:271
  125.2 2.1 %collective-permute-done.63.refs_1_ = bf16[12,8,256]{2,1,0:T(8,128)(2,1)S(1)} collective-permute-done((bf16[12,8,256]{2,1,0:T(8,128)(2,1)S(1)}, bf16[12,8,256]{2,1,0:T(8,128)(2,1)S(1)}, u32[]{:S(2)}, u32[]{:S(2)}) %collective-permute-start.63) | collective-permute-done | bytes 49184 | tf_op jit(solution)/shard_map/ppermute | solution.py:271
  127.3 1.9 %collective-permute-start.68 = (bf16[12,8,256]{2,1,0:T(8,128)(2,1)S(1)}, bf16[12,8,256]{2,1,0:T(8,128)(2,1)S(1)}, u32[]{:S(2)}, u32[]{:S(2)}) collective-permute-start(bf16[12,8,256]{2,1,0:T(8,128)(2,1)S(1)} %collective-permute-done.63.refs_1_), channel_id=1, source_target_pairs={{0,4},{1,5},{2,6},{3,7},{4,0},{5,1},{6,2},{7,3},{8,12},{9,13},{10,... | collective-permute-start | bytes 147464 | tf_op jit(solution)/shard_map/ppermute | solution.py:271
  (165 shorter events, 76.0 us)
Async XLA Ops:
  8.3 5.3 %collective-permute-start = (bf16[13,8,256]{2,1,0:T(8,128)(2,1)S(1)}, bf16[13,8,256]{2,1,0:T(8,128)(2,1)S(1)}, u32[]{:S(2)}, u32[]{:S(2)}) collective-permute-start(bf16[13,8,256]{2,1,0:T(8,128)(2,1)S(1)} %get-tuple-element.117), channel_id=1, source_target_pairs={{0,1},{1,0},{2,3},{3,2},{4,5},{5,4},{6,7},{7,6},{8,9},{9,8},{10,11... | collective-permute-start | bytes 159752 | tf_op jit(solution)/shard_map/ppermute | solution.py:271
  8.4 5.2 %collective-permute-start.1 = (bf16[13,8,256]{2,1,0:T(8,128)(2,1)S(1)}, bf16[13,8,256]{2,1,0:T(8,128)(2,1)S(1)}, u32[]{:S(2)}, u32[]{:S(2)}) collective-permute-start(bf16[13,8,256]{2,1,0:T(8,128)(2,1)S(1)} %get-tuple-element.118), channel_id=1, source_target_pairs={{0,2},{1,3},{2,0},{3,1},{4,6},{5,7},{6,4},{7,5},{8,10},{9,11},{10,... | collective-permute-start | bytes 159752 | tf_op jit(solution)/shard_map/ppermute | solution.py:271
  11.5 6.0 %collective-permute-start.3 = (bf16[12,8,256]{2,1,0:T(8,128)(2,1)S(1)}, bf16[12,8,256]{2,1,0:T(8,128)(2,1)S(1)}, u32[]{:S(2)}, u32[]{:S(2)}) collective-permute-start(bf16[12,8,256]{2,1,0:T(8,128)(2,1)S(1)} %get-tuple-element.124), channel_id=1, source_target_pairs={{0,1},{1,0},{2,3},{3,2},{4,5},{5,4},{6,7},{7,6},{8,9},{9,8},{10,11... | collective-permute-start | bytes 147464 | tf_op jit(solution)/shard_map/ppermute | solution.py:271
  11.7 5.9 %collective-permute-start.4 = (bf16[12,8,256]{2,1,0:T(8,128)(2,1)S(1)}, bf16[12,8,256]{2,1,0:T(8,128)(2,1)S(1)}, u32[]{:S(2)}, u32[]{:S(2)}) collective-permute-start(bf16[12,8,256]{2,1,0:T(8,128)(2,1)S(1)} %get-tuple-element.125), channel_id=1, source_target_pairs={{0,2},{1,3},{2,0},{3,1},{4,6},{5,7},{6,4},{7,5},{8,10},{9,11},{10,... | collective-permute-start | bytes 147464 | tf_op jit(solution)/shard_map/ppermute | solution.py:271
  17.4 9.6 %collective-permute-start.7 = (bf16[12,8,256]{2,1,0:T(8,128)(2,1)S(1)}, bf16[12,8,256]{2,1,0:T(8,128)(2,1)S(1)}, u32[]{:S(2)}, u32[]{:S(2)}) collective-permute-start(bf16[12,8,256]{2,1,0:T(8,128)(2,1)S(1)} %get-tuple-element.129), channel_id=1, source_target_pairs={{0,4},{1,5},{2,6},{3,7},{4,0},{5,1},{6,2},{7,3},{8,12},{9,13},{10,... | collective-permute-start | bytes 147464 | tf_op jit(solution)/shard_map/ppermute | solution.py:271
  19.9 7.2 %collective-permute-start.8 = (bf16[12,8,256]{2,1,0:T(8,128)(2,1)S(1)}, bf16[12,8,256]{2,1,0:T(8,128)(2,1)S(1)}, u32[]{:S(2)}, u32[]{:S(2)}) collective-permute-start(bf16[12,8,256]{2,1,0:T(8,128)(2,1)S(1)} %get-tuple-element.130), channel_id=1, source_target_pairs={{0,8},{1,9},{2,10},{3,11},{4,12},{5,13},{6,14},{7,15},{8,0},{9,1},... | collective-permute-start | bytes 147464 | tf_op jit(solution)/shard_map/ppermute | solution.py:271
  27.2 5.1 %collective-permute-start.9 = (bf16[12,8,256]{2,1,0:T(8,128)(2,1)S(1)}, bf16[12,8,256]{2,1,0:T(8,128)(2,1)S(1)}, u32[]{:S(2)}, u32[]{:S(2)}) collective-permute-start(bf16[12,8,256]{2,1,0:T(8,128)(2,1)S(1)} %get-tuple-element.135.refs_0_), channel_id=1, source_target_pairs={{0,8},{1,9},{2,10},{3,11},{4,12},{5,13},{6,14},{7,15},{8,0},{9,1},... | collective-permute-start | bytes 147464 | tf_op jit(solution)/shard_map/ppermute | solution.py:271
  28.5 7.6 %collective-permute-start.13 = (bf16[12,8,256]{2,1,0:T(8,128)(2,1)S(1)}, bf16[12,8,256]{2,1,0:T(8,128)(2,1)S(1)}, u32[]{:S(2)}, u32[]{:S(2)}) collective-permute-start(bf16[12,8,256]{2,1,0:T(8,128)(2,1)S(1)} %get-tuple-element.135.refs_0_), channel_id=1, source_target_pairs={{0,4},{1,5},{2,6},{3,7},{4,0},{5,1},{6,2},{7,3},{8,12},{9,13},{10,... | collective-permute-start | bytes 147464 | tf_op jit(solution)/shard_map/ppermute | solution.py:271
  43.3 4.5 %collective-permute-start.21 = (bf16[12,8,256]{2,1,0:T(8,128)(2,1)S(1)}, bf16[12,8,256]{2,1,0:T(8,128)(2,1)S(1)}, u32[]{:S(2)}, u32[]{:S(2)}) collective-permute-start(bf16[12,8,256]{2,1,0:T(8,128)(2,1)S(1)} %get-tuple-element.152), channel_id=1, source_target_pairs={{0,1},{1,0},{2,3},{3,2},{4,5},{5,4},{6,7},{7,6},{8,9},{9,8},{10,11... | collective-permute-start | bytes 147464 | tf_op jit(solution)/shard_map/ppermute | solution.py:271
  43.4 4.5 %collective-permute-start.22 = (bf16[12,8,256]{2,1,0:T(8,128)(2,1)S(1)}, bf16[12,8,256]{2,1,0:T(8,128)(2,1)S(1)}, u32[]{:S(2)}, u32[]{:S(2)}) collective-permute-start(bf16[12,8,256]{2,1,0:T(8,128)(2,1)S(1)} %get-tuple-element.153), channel_id=1, source_target_pairs={{0,2},{1,3},{2,0},{3,1},{4,6},{5,7},{6,4},{7,5},{8,10},{9,11},{10,... | collective-permute-start | bytes 147464 | tf_op jit(solution)/shard_map/ppermute | solution.py:271
  46.1 4.6 %collective-permute-start.18 = (bf16[12,8,256]{2,1,0:T(8,128)(2,1)S(1)}, bf16[12,8,256]{2,1,0:T(8,128)(2,1)S(1)}, u32[]{:S(2)}, u32[]{:S(2)}) collective-permute-start(bf16[12,8,256]{2,1,0:T(8,128)(2,1)S(1)} %get-tuple-element.148), channel_id=1, source_target_pairs={{0,1},{1,0},{2,3},{3,2},{4,5},{5,4},{6,7},{7,6},{8,9},{9,8},{10,11... | collective-permute-start | bytes 147464 | tf_op jit(solution)/shard_map/ppermute | solution.py:271
  52.9 5.1 %collective-permute-start.26 = (bf16[12,8,256]{2,1,0:T(8,128)(2,1)S(1)}, bf16[12,8,256]{2,1,0:T(8,128)(2,1)S(1)}, u32[]{:S(2)}, u32[]{:S(2)}) collective-permute-start(bf16[12,8,256]{2,1,0:T(8,128)(2,1)S(1)} %get-tuple-element.158), channel_id=1, source_target_pairs={{0,8},{1,9},{2,10},{3,11},{4,12},{5,13},{6,14},{7,15},{8,0},{9,1},... | collective-permute-start | bytes 147464 | tf_op jit(solution)/shard_map/ppermute | solution.py:271
  58.0 5.2 %collective-permute-start.27 = (bf16[12,8,256]{2,1,0:T(8,128)(2,1)S(1)}, bf16[12,8,256]{2,1,0:T(8,128)(2,1)S(1)}, u32[]{:S(2)}, u32[]{:S(2)}) collective-permute-start(bf16[12,8,256]{2,1,0:T(8,128)(2,1)S(1)} %get-tuple-element.161.refs_0_), channel_id=1, source_target_pairs={{0,8},{1,9},{2,10},{3,11},{4,12},{5,13},{6,14},{7,15},{8,0},{9,1},... | collective-permute-start | bytes 147464 | tf_op jit(solution)/shard_map/ppermute | solution.py:271
  59.7 7.9 %collective-permute-start.31 = (bf16[12,8,256]{2,1,0:T(8,128)(2,1)S(1)}, bf16[12,8,256]{2,1,0:T(8,128)(2,1)S(1)}, u32[]{:S(2)}, u32[]{:S(2)}) collective-permute-start(bf16[12,8,256]{2,1,0:T(8,128)(2,1)S(1)} %get-tuple-element.161.refs_0_), channel_id=1, source_target_pairs={{0,4},{1,5},{2,6},{3,7},{4,0},{5,1},{6,2},{7,3},{8,12},{9,13},{10,... | collective-permute-start | bytes 147464 | tf_op jit(solution)/shard_map/ppermute | solution.py:271
  63.1 4.5 %collective-permute-start.32 = (bf16[12,8,256]{2,1,0:T(8,128)(2,1)S(1)}, bf16[12,8,256]{2,1,0:T(8,128)(2,1)S(1)}, u32[]{:S(2)}, u32[]{:S(2)}) collective-permute-start(bf16[12,8,256]{2,1,0:T(8,128)(2,1)S(1)} %collective-permute-done.27.refs_1_), channel_id=1, source_target_pairs={{0,4},{1,5},{2,6},{3,7},{4,0},{5,1},{6,2},{7,3},{8,12},{9,13},{10,... | collective-permute-start | bytes 147464 | tf_op jit(solution)/shard_map/ppermute | solution.py:271
  75.0 4.5 %collective-permute-start.40 = (bf16[12,8,256]{2,1,0:T(8,128)(2,1)S(1)}, bf16[12,8,256]{2,1,0:T(8,128)(2,1)S(1)}, u32[]{:S(2)}, u32[]{:S(2)}) collective-permute-start(bf16[12,8,256]{2,1,0:T(8,128)(2,1)S(1)} %get-tuple-element.179), channel_id=1, source_target_pairs={{0,2},{1,3},{2,0},{3,1},{4,6},{5,7},{6,4},{7,5},{8,10},{9,11},{10,... | collective-permute-start | bytes 147464 | tf_op jit(solution)/shard_map/ppermute | solution.py:271
  77.7 4.5 %collective-permute-start.36 = (bf16[12,8,256]{2,1,0:T(8,128)(2,1)S(1)}, bf16[12,8,256]{2,1,0:T(8,128)(2,1)S(1)}, u32[]{:S(2)}, u32[]{:S(2)}) collective-permute-start(bf16[12,8,256]{2,1,0:T(8,128)(2,1)S(1)} %get-tuple-element.174), channel_id=1, source_target_pairs={{0,1},{1,0},{2,3},{3,2},{4,5},{5,4},{6,7},{7,6},{8,9},{9,8},{10,11... | collective-permute-start | bytes 147464 | tf_op jit(solution)/shard_map/ppermute | solution.py:271
  84.4 5.1 %collective-permute-start.44 = (bf16[12,8,256]{2,1,0:T(8,128)(2,1)S(1)}, bf16[12,8,256]{2,1,0:T(8,128)(2,1)S(1)}, u32[]{:S(2)}, u32[]{:S(2)}) collective-permute-start(bf16[12,8,256]{2,1,0:T(8,128)(2,1)S(1)} %get-tuple-element.184), channel_id=1, source_target_pairs={{0,8},{1,9},{2,10},{3,11},{4,12},{5,13},{6,14},{7,15},{8,0},{9,1},... | collective-permute-start | bytes 147464 | tf_op jit(solution)/shard_map/ppermute | solution.py:271
  89.5 5.1 %collective-permute-start.45 = (bf16[12,8,256]{2,1,0:T(8,128)(2,1)S(1)}, bf16[12,8,256]{2,1,0:T(8,128)(2,1)S(1)}, u32[]{:S(2)}, u32[]{:S(2)}) collective-permute-start(bf16[12,8,256]{2,1,0:T(8,128)(2,1)S(1)} %get-tuple-element.187.refs_0_), channel_id=1, source_target_pairs={{0,8},{1,9},{2,10},{3,11},{4,12},{5,13},{6,14},{7,15},{8,0},{9,1},... | collective-permute-start | bytes 147464 | tf_op jit(solution)/shard_map/ppermute | solution.py:271
  90.8 7.9 %collective-permute-start.49 = (bf16[12,8,256]{2,1,0:T(8,128)(2,1)S(1)}, bf16[12,8,256]{2,1,0:T(8,128)(2,1)S(1)}, u32[]{:S(2)}, u32[]{:S(2)}) collective-permute-start(bf16[12,8,256]{2,1,0:T(8,128)(2,1)S(1)} %get-tuple-element.187.refs_0_), channel_id=1, source_target_pairs={{0,4},{1,5},{2,6},{3,7},{4,0},{5,1},{6,2},{7,3},{8,12},{9,13},{10,... | collective-permute-start | bytes 147464 | tf_op jit(solution)/shard_map/ppermute | solution.py:271
  107.2 4.5 %collective-permute-start.58 = (bf16[12,8,256]{2,1,0:T(8,128)(2,1)S(1)}, bf16[12,8,256]{2,1,0:T(8,128)(2,1)S(1)}, u32[]{:S(2)}, u32[]{:S(2)}) collective-permute-start(bf16[12,8,256]{2,1,0:T(8,128)(2,1)S(1)} %get-tuple-element.205), channel_id=1, source_target_pairs={{0,2},{1,3},{2,0},{3,1},{4,6},{5,7},{6,4},{7,5},{8,10},{9,11},{10,... | collective-permute-start | bytes 147464 | tf_op jit(solution)/shard_map/ppermute | solution.py:271
  116.5 5.1 %collective-permute-start.62 = (bf16[12,8,256]{2,1,0:T(8,128)(2,1)S(1)}, bf16[12,8,256]{2,1,0:T(8,128)(2,1)S(1)}, u32[]{:S(2)}, u32[]{:S(2)}) collective-permute-start(bf16[12,8,256]{2,1,0:T(8,128)(2,1)S(1)} %get-tuple-element.210), channel_id=1, source_target_pairs={{0,8},{1,9},{2,10},{3,11},{4,12},{5,13},{6,14},{7,15},{8,0},{9,1},... | collective-permute-start | bytes 147464 | tf_op jit(solution)/shard_map/ppermute | solution.py:271
  122.3 5.0 %collective-permute-start.63 = (bf16[12,8,256]{2,1,0:T(8,128)(2,1)S(1)}, bf16[12,8,256]{2,1,0:T(8,128)(2,1)S(1)}, u32[]{:S(2)}, u32[]{:S(2)}) collective-permute-start(bf16[12,8,256]{2,1,0:T(8,128)(2,1)S(1)} %get-tuple-element.214.refs_0_), channel_id=1, source_target_pairs={{0,8},{1,9},{2,10},{3,11},{4,12},{5,13},{6,14},{7,15},{8,0},{9,1},... | collective-permute-start | bytes 147464 | tf_op jit(solution)/shard_map/ppermute | solution.py:271
  123.2 8.1 %collective-permute-start.67 = (bf16[12,8,256]{2,1,0:T(8,128)(2,1)S(1)}, bf16[12,8,256]{2,1,0:T(8,128)(2,1)S(1)}, u32[]{:S(2)}, u32[]{:S(2)}) collective-permute-start(bf16[12,8,256]{2,1,0:T(8,128)(2,1)S(1)} %get-tuple-element.214.refs_0_), channel_id=1, source_target_pairs={{0,4},{1,5},{2,6},{3,7},{4,0},{5,1},{6,2},{7,3},{8,12},{9,13},{10,... | collective-permute-start | bytes 147464 | tf_op jit(solution)/shard_map/ppermute | solution.py:271
  (53 other events, 243.9 us)

commit v7 on v5

--- a/solution.py
+++ b/solution.py
@@ -34,7 +34,7 @@
 
 
 def transpose_products(base, tile_of, row_of, tiles, hb, outs):
-    per = outs[0].shape[0]
+    per = tile_of.shape[0] // (2 * QUAD)
     for x, out in enumerate(outs):
         for s in range(per):
             slot = base + x * per + s
@@ -46,7 +46,7 @@
     for total in totals:
         total[...] = jnp.zeros_like(total)
     for x, part in enumerate(moved):
-        first = base + x * per
+        first = base + x * (tile_of.shape[0] // (2 * QUAD))
         terms = [jnp.dot(part[s], turned[tile_of[first + s]], preferred_element_type=F32) for s in range(per)]
         for s in range(0, per, LANES):
             several = range(min(LANES, per - s))
@@ -64,8 +64,8 @@
 
 
 def start_kernel(step, peers, cap, col_blocks, count, rows_in, cols_in, tiles, step_in, mask_in, cot_in,
-                 held, dy, rhs, hb, tile_of, row_of, land_of, wants, o0, o1, o2, o3,
-                 rows, cols, dual_step, dual_mask, cot_y, filled, sems, small):
+                 held, dy, rhs, hb, tile_of, row_of, land_of, o0, o1, o2, o3,
+                 rows, cols, dual_step, dual_mask, cot_y, filled, wants, plan, sems, small):
     tile_slots, side, _ = tiles.shape
     group = peers // QUAD
     half = group // 2
@@ -93,7 +93,7 @@
         land_of[s] = hb.shape[0]
     for x in range(QUAD):
         for s in range(group * cap):
-            wants[x * group * cap + s] = col_blocks
+            wants[x, s] = col_blocks
     for copy in minor:
         copy.wait()
     me = lax.axis_index("rb").astype(I32)
@@ -112,16 +112,21 @@
         tile_of[slot] = t
         row_of[slot] = rows[t]
         land_of[slot] = rows[t]
-        wants[quad * (group * cap) + place] = col - owner * col_blocks
+        wants[quad, place] = col - owner * col_blocks
         return 0
 
     lax.fori_loop(0, count[0], place_tile, 0)
+    chart = pltpu.make_async_copy(wants, plan, small.at[len(minor)])
+    chart.start()
     dy[...] = dual_mask[...].astype(F32) * cot_y[...]
 
     def h_into(at, h):
         rhs[:, at] = -h
 
     scaled_blocks(side, dy, dual_step, hb, h_into)
+    chart.wait()
+    for out in (o0, o1, o2, o3):
+        out[half * cap] = plan[...].astype(BF16)
     for c in range(chunks):
         tile_copy(c).wait()
     transpose_products(0, tile_of, row_of, held, hb, (o0, o1, o2, o3))
@@ -140,17 +145,19 @@
     transpose_products(tile_of.shape[0] // 2, tile_of, row_of, held, hb, (o0, o1, o2, o3))
 
 
-def map_kernel(own, got1, got2, got3, wants):
-    per = own.shape[0] // QUAD
-    for x, got in enumerate((own, got1, got2, got3)):
-        for s in range(per):
-            wants[x * per + s] = got[x * per + s]
+def map_kernel(a0, a1, a2, a3, wants, whole, sem):
+    for x, part in enumerate((a0, a1, a2, a3)):
+        plan = part[part.shape[0] - 1].astype(F32)
+        whole[pl.ds(x, 1)] = plan[x:x + 1].astype(I32)
+    whole[pl.ds(QUAD, QUAD)] = jnp.zeros((QUAD, whole.shape[1]), I32)
+    copy = pltpu.make_async_copy(whole, wants, sem)
+    copy.start()
+    copy.wait()
 
 
 def sum_kernel(first_high, cap, wants, a0, a1, a2, a3, *rest):
     parts = (a0, a1, a2, a3)
-    half = a0.shape[0] // cap
-    per = wants.shape[0] // QUAD
+    half = len(rest) // 3
     outs, totals = rest[:half], rest[half:]
     for total in totals:
         total[...] = jnp.zeros_like(total)
@@ -160,7 +167,7 @@
             for h in range(half):
                 for side in range(2):
                     x = 2 * pair + side
-                    spot = wants[x * per + (first_high + h) * cap + r]
+                    spot = wants[x, (first_high + h) * cap + r]
                     jobs.append((totals[2 * h + side], spot, parts[x][h * cap + r].astype(F32)))
             values = [total[spot] + part for total, spot, part in jobs]
             for (total, spot, _), value in zip(jobs, values):
@@ -187,11 +194,10 @@
 
 def pick_kernel(first_high, cap, wants, *refs):
     blocks, outs = refs[:-QUAD], refs[-QUAD:]
-    per = wants.shape[0] // QUAD
     last = blocks[0].shape[0] - 1
     for x, out in enumerate(outs):
         values = [
-            blocks[h][jnp.minimum(wants[x * per + (first_high + h) * cap + r], last)]
+            blocks[h][jnp.minimum(wants[x, (first_high + h) * cap + r], last)]
             for h in range(len(blocks))
             for r in range(cap)
         ]
@@ -199,16 +205,18 @@
             out[s] = value
 
 
-def near_forward_kernel(tile_of, land_of, turned, m0, m1, m2, m3, out, *totals):
-    forward_products(tile_of.shape[0] // 2, tile_of, land_of, turned, (m0, m1, m2, m3), totals)
+def near_forward_kernel(base, tile_of, land_of, turned, m0, m1, m2, m3, *rest):
+    out, totals = rest[-LANES - 1], rest[-LANES:]
+    forward_products(base, tile_of, land_of, turned, (m0, m1, m2, m3), totals)
     for r in range(out.shape[0]):
-        out[r] = gathered(totals, r)
-
-
-def middle_kernel(step, tile_of, row_of, land_of, held, turned, dual_step, dual_mask, part, dy, rhs, m0, m1, m2, m3,
+        value = gathered(totals, r)
+        out[r] = value + rest[0][r] if len(rest) > LANES + 1 else value
+
+
+def middle_kernel(step, base, tile_of, row_of, land_of, held, turned, dual_step, dual_mask, part, dy, rhs, m0, m1, m2, m3,
                   new_dy, new_rhs, hb, o0, o1, o2, o3, *totals):
     side = held.shape[1]
-    forward_products(0, tile_of, land_of, turned, (m0, m1, m2, m3), totals)
+    forward_products(base, tile_of, land_of, turned, (m0, m1, m2, m3), totals)
     for r in range(hb.shape[0]):
         at = pl.ds(r * side, side)
         v = part[r] + gathered(totals, r)
@@ -221,9 +229,9 @@
     transpose_products(0, tile_of, row_of, held, hb, (o0, o1, o2, o3))
 
 
-def last_kernel(tile_of, land_of, turned, part, dy, m0, m1, m2, m3, new_y, *totals):
+def last_kernel(base, tile_of, land_of, turned, part, dy, m0, m1, m2, m3, new_y, *totals):
     side = turned.shape[1]
-    forward_products(0, tile_of, land_of, turned, (m0, m1, m2, m3), totals)
+    forward_products(base, tile_of, land_of, turned, (m0, m1, m2, m3), totals)
     for r in range(part.shape[0]):
         at = pl.ds(r * side, side)
         new_y[:, at] = dy[:, at] - (part[r] + gathered(totals, r))
@@ -271,18 +279,18 @@
         return [parts[0]] + [swap(parts[x], x) for x in range(1, QUAD)]
 
     step = steps - 1
-    held, dy, rhs, hb, tile_of, row_of, land_of, wants, *far_parts = pl.pallas_call(
+    held, dy, rhs, hb, tile_of, row_of, land_of, *far_parts = pl.pallas_call(
         functools.partial(start_kernel, step, peers, cap, col_blocks),
         out_shape=(
             pltpu.VMEM(tiles.shape, BF16), y_shape, y_shape, hb_set, per_slot, per_slot, per_slot,
-            shape((QUAD * group * cap,), I32),
-        ) + part_set,
+        ) + (shape((half * cap + 1, batch, side), BF16),) * QUAD,
         in_specs=[SM] + [HBM] * 6,
-        out_specs=(VM,) * 4 + (SM,) * 4 + (VM,) * QUAD,
+        out_specs=(VM,) * 4 + (SM,) * 3 + (VM,) * QUAD,
         scratch_shapes=[
             pltpu.SMEM((tile_slots,), I32), pltpu.SMEM((tile_slots,), I32), pltpu.VMEM(dual_step.shape, F32),
             pltpu.VMEM(cot_y.shape, I32), pltpu.VMEM(cot_y.shape, F32), pltpu.SMEM((peers,), I32),
-            pltpu.SemaphoreType.DMA((tile_slots // CHUNK,)), pltpu.SemaphoreType.DMA((5,)),
+            pltpu.SMEM((2 * QUAD, side), I32), pltpu.VMEM((2 * QUAD, side), I32),
+            pltpu.SemaphoreType.DMA((tile_slots // CHUNK,)), pltpu.SemaphoreType.DMA((6,)),
         ],
         compiler_params=PARAMS,
         cost_estimate=cost(2 * tile_bytes),
@@ -291,21 +299,25 @@
         pltpu.with_memory_space_constraint(array, pltpu.HBM)
         for array in (tile_rows, tile_cols, tiles, dual_step, dual_mask, cot_y)
     ))
-    wants = pl.pallas_call(
-        map_kernel,
-        out_shape=pltpu.SMEM((slots,), I32),
-        in_specs=[SM] * QUAD,
-        out_specs=SM,
-        compiler_params=PARAMS,
-        name="maps",
-    )(wants, *(swap(wants, x) for x in range(1, QUAD)))
     turned = call(turn_kernel, "turn", tile_bytes, [VM], pltpu.VMEM(tiles.shape, BF16), (held,))
-    x_state, spent = cot_x, cot_x
+    x_state, spent, wants = cot_x, cot_x, None
+    middle_high = half + half // 2
+    late = half // 2 * cap
     while True:
         far_got = near_swaps(far_parts)
         near_parts = call(near_product_kernel, "near_product", tile_bytes // 2, [SM] * 2 + [VM] * 2, part_set,
                           (tile_of, row_of, held, hb))
         near_got = near_swaps(near_parts)
+        if wants is None:
+            wants = pl.pallas_call(
+                map_kernel,
+                out_shape=pltpu.SMEM((2 * QUAD, side), I32),
+                in_specs=[VM] * QUAD,
+                out_specs=SM,
+                scratch_shapes=[pltpu.VMEM((2 * QUAD, side), I32), pltpu.SemaphoreType.DMA],
+                compiler_params=PARAMS,
+                name="maps",
+            )(*far_got)
         far_sums = call(functools.partial(sum_kernel, half, cap), "far_sum", 1 << 20, [SM] + [VM] * QUAD,
                         (block_set,) * half, (wants, *far_got), col_totals)
         got = [swap(far_sums[h], (half + h) * QUAD) for h in reversed(range(half))]
@@ -320,19 +332,26 @@
         blocks = [moved] + [swap(moved, h * QUAD) for h in range(1, group)]
         near_moved = near_swaps(call(functools.partial(pick_kernel, 0, cap), "near_pick", 1 << 20,
                                      [SM] + [VM] * half, part_set, (wants, *blocks[:half])))
-        far_moved = near_swaps(call(functools.partial(pick_kernel, half, cap), "far_pick", 1 << 20,
-                                    [SM] + [VM] * half, part_set, (wants, *blocks[half:])))
-        part = call(near_forward_kernel, "near_forward", tile_bytes // 2, [SM] * 2 + [VM] * (1 + QUAD),
-                    shape(hb_set.shape, F32), (tile_of, land_of, turned, *near_moved), row_totals)
+        early_moved, late_moved = (
+            near_swaps(call(functools.partial(pick_kernel, low, cap), name, 1 << 20, [SM] + [VM] * (top - low),
+                            (shape(((top - low) * cap, batch, side), BF16),) * QUAD, (wants, *blocks[low:top])))
+            for name, low, top in (("early_pick", half, middle_high), ("late_pick", middle_high, group))
+        )
+        part = call(functools.partial(near_forward_kernel, slots // 2), "near_forward", tile_bytes // 2,
+                    [SM] * 2 + [VM] * (1 + QUAD), shape(hb_set.shape, F32), (tile_of, land_of, turned, *near_moved),
+                    row_totals)
+        part = call(functools.partial(near_forward_kernel, 0), "early_forward", tile_bytes // 4,
+                    [SM] * 2 + [VM] * (2 + QUAD), shape(hb_set.shape, F32),
+                    (tile_of, land_of, turned, *early_moved, part), row_totals)
         if step == 0:
             break
         step -= 1
         dy, rhs, hb, *far_parts = call(
-            functools.partial(middle_kernel, step), "middle", tile_bytes, [SM] * 3 + [VM] * (7 + QUAD),
+            functools.partial(middle_kernel, step, late), "middle", tile_bytes, [SM] * 3 + [VM] * (7 + QUAD),
             (y_shape, y_shape, hb_set) + part_set,
-            (tile_of, row_of, land_of, held, turned, dual_step, dual_mask, part, dy, rhs, *far_moved), row_totals)
-    y_state = call(last_kernel, "last", tile_bytes // 2, [SM] * 2 + [VM] * (3 + QUAD), y_shape,
-                   (tile_of, land_of, turned, part, dy, *far_moved), row_totals)
+            (tile_of, row_of, land_of, held, turned, dual_step, dual_mask, part, dy, rhs, *late_moved), row_totals)
+    y_state = call(functools.partial(last_kernel, late), "last", tile_bytes // 2, [SM] * 2 + [VM] * (3 + QUAD), y_shape,
+                   (tile_of, land_of, turned, part, dy, *late_moved), row_totals)
     return spent, rhs, x_state, y_state
 
 

time: 132 us -> 135 us (1.023)
  starting transfers between devices: 62.7 us -> 70.6 us
  waiting for transfers between devices: 39.2 us -> 33.6 us
    ppermute x75 -> x84, starting transfers between devices: 62.7 us -> 70.6 us  [swap(): return lax.ppermute(array, 'rb', [(p, p ^ x) for p in range(peers)])]
    ppermute x75 -> x84, waiting for transfers between devices: 39.2 us -> 33.6 us  [swap(): return lax.ppermute(array, 'rb', [(p, p ^ x) for p in range(peers)])]
    pallas_call x33 -> x41, Pallas kernels: 21.4 us -> 22 us  [call(): pl.pallas_call(kernel, out_shape=outs, in_specs=ins, out_specs=jax.tree.m...]
  transfers between devices with their start and end apart: 75 -> 84, of which waited for: 39 -> 35; matrix products, arithmetic and copies ran while one was open for 0% -> 0% of each run, Pallas kernels for 9% -> 11%
where the time goes in v7:
time: 135 us
  starting transfers between devices  70.6 us (52%)
  waiting for transfers between devices  33.6 us (25%)
  Pallas kernels  28.6 us (21%)
  between operations  1.8 us (1%)
    ppermute x84, starting transfers between devices, swap(): return lax.ppermute(array, 'rb', [(p, p ^ x) for p in range(peers)])  70.6 us
    ppermute x84, waiting for transfers between devices, swap(): return lax.ppermute(array, 'rb', [(p, p ^ x) for p in range(peers)])  33.6 us
    pallas_call x41, Pallas kernels, call(): pl.pallas_call(kernel, out_shape=outs, in_specs=ins, out_specs=jax.tree.m...  22 us
    pallas_call x1, Pallas kernels, on_device(): pl.pallas_call(functools.partial(start_kernel, step, peers, cap, col_bloc...  5.87 us
  transfers between devices with their start and end apart: 84, of which 35 were waited for; matrix products, arithmetic and copies ran while one was open for 0% of the time, Pallas kernels for 11%

profile of v7, /device:TPU:0, one launch (start us, length us, event | category | flops | bytes accessed | tf_op | source)
XLA Modules:
  0.0 134.6 jit_solution(7786996853521614293)
XLA Ops:
  1.3 5.9 %start.1 = (bf16[88,256,256]{2,1,0:T(8,128)(2,1)S(1)}, f32[8,2048]{1,0:T(8,128)S(1)}, f32[8,2048]{1,0:T(8,128)S(1)}, bf16[8,8,256]{2,1,0:T(8,128)(2,1)S(1)}, s32...) custom-call(s32[1]{0:T(128)S(6)} %copy.14.count, ...), custom_call_target="tpu_custom_call" | custom-call | flops 184549376 | bytes 23068672 | tf_op jit(solution)/shard_map/start/pallas_call | solution.py:282
  7.7 2.6 %collective-permute-start.1 = (bf16[13,8,256]{2,1,0:T(8,128)(2,1)S(1)}, bf16[13,8,256]{2,1,0:T(8,128)(2,1)S(1)}, u32[]{:S(2)}, u32[]{:S(2)}) collective-permute-start(bf16[13,8,256]{2,1,0:T(8,128)(2,1)S(1)} %get-tuple-element.134), channel_id=1, source_target_pairs={{0,2},{1,3},{2,0},{3,1},{4,6},{5,7},{6,4},{7,5},{8,10},{9,11},{10,... | collective-permute-start | bytes 159752 | tf_op jit(solution)/shard_map/ppermute | solution.py:276
  11.4 1.9 %collective-permute-start.4 = (bf16[12,8,256]{2,1,0:T(8,128)(2,1)S(1)}, bf16[12,8,256]{2,1,0:T(8,128)(2,1)S(1)}, u32[]{:S(2)}, u32[]{:S(2)}) collective-permute-start(bf16[12,8,256]{2,1,0:T(8,128)(2,1)S(1)} %get-tuple-element.141), channel_id=1, source_target_pairs={{0,2},{1,3},{2,0},{3,1},{4,6},{5,7},{6,4},{7,5},{8,10},{9,11},{10,... | collective-permute-start | bytes 147464 | tf_op jit(solution)/shard_map/ppermute | solution.py:276
  14.9 3.7 %collective-permute-start.6 = (bf16[12,8,256]{2,1,0:T(8,128)(2,1)S(1)}, bf16[12,8,256]{2,1,0:T(8,128)(2,1)S(1)}, u32[]{:S(2)}, u32[]{:S(2)}) collective-permute-start(bf16[12,8,256]{2,1,0:T(8,128)(2,1)S(1)} %get-tuple-element.144), channel_id=1, source_target_pairs={{0,12},{1,13},{2,14},{3,15},{4,8},{5,9},{6,10},{7,11},{8,4},{9,5},... | collective-permute-start | bytes 147464 | tf_op jit(solution)/shard_map/ppermute | solution.py:276
  19.6 3.7 %turn.1.turned = bf16[88,256,256]{2,1,0:T(8,128)(2,1)S(1)} custom-call(bf16[88,256,256]{2,1,0:T(8,128)(2,1)S(1)} %get-tuple-element.130.held), custom_call_target="tpu_custom_call" | custom-call | flops 92274688 | bytes 11534336 | tf_op jit(solution)/shard_map/turn/pallas_call | solution.py:264
  24.8 2.9 %collective-permute-start.9 = (bf16[12,8,256]{2,1,0:T(8,128)(2,1)S(1)}, bf16[12,8,256]{2,1,0:T(8,128)(2,1)S(1)}, u32[]{:S(2)}, u32[]{:S(2)}) collective-permute-start(bf16[12,8,256]{2,1,0:T(8,128)(2,1)S(1)} %get-tuple-element.151.refs_0_), channel_id=1, source_target_pairs={{0,8},{1,9},{2,10},{3,11},{4,12},{5,13},{6,14},{7,15},{8,0},{9,1},... | collective-permute-start | bytes 147464 | tf_op jit(solution)/shard_map/ppermute | solution.py:276
  31.0 2.6 %collective-permute-done.17.refs_0_ = bf16[12,8,256]{2,1,0:T(8,128)(2,1)S(1)} collective-permute-done((bf16[12,8,256]{2,1,0:T(8,128)(2,1)S(1)}, bf16[12,8,256]{2,1,0:T(8,128)(2,1)S(1)}, u32[]{:S(2)}, u32[]{:S(2)}) %collective-permute-start.17) | collective-permute-done | bytes 49184 | tf_op jit(solution)/shard_map/ppermute | solution.py:276
  40.4 1.5 %middle.3 = (f32[8,2048]{1,0:T(8,128)S(1)}, f32[8,2048]{1,0:T(8,128)S(1)}, bf16[8,8,256]{2,1,0:T(8,128)(2,1)S(1)}, bf16[12,8,256]{2,1,0:T(8,128)(2,1)S(1)}, bf16...) custom-call(s32[96]{0:T(128)S(4)} %get-tuple-element.136.tile_of, ...), custom_call_target="tpu_custom_call" | custom-call | flops 92274688 | bytes 11534336 | tf_op jit(solution)/shard_map/middle/pallas_call | solution.py:264
  47.8 1.5 %collective-permute-done.22.a2 = bf16[12,8,256]{2,1,0:T(8,128)(2,1)S(1)} collective-permute-done((bf16[12,8,256]{2,1,0:T(8,128)(2,1)S(1)}, bf16[12,8,256]{2,1,0:T(8,128)(2,1)S(1)}, u32[]{:S(2)}, u32[]{:S(2)}) %collective-permute-start.22) | collective-permute-done | bytes 49184 | tf_op jit(solution)/shard_map/ppermute | solution.py:276
  50.1 1.6 %collective-permute-start.29 = (bf16[12,8,256]{2,1,0:T(8,128)(2,1)S(1)}, bf16[12,8,256]{2,1,0:T(8,128)(2,1)S(1)}, u32[]{:S(2)}, u32[]{:S(2)}) collective-permute-start(bf16[12,8,256]{2,1,0:T(8,128)(2,1)S(1)} %get-tuple-element.178), channel_id=1, source_target_pairs={{0,4},{1,5},{2,6},{3,7},{4,0},{5,1},{6,2},{7,3},{8,12},{9,13},{10,... | collective-permute-start | bytes 147464 | tf_op jit(solution)/shard_map/ppermute | solution.py:276
  51.7 1.9 %collective-permute-done.27.refs_1_ = bf16[12,8,256]{2,1,0:T(8,128)(2,1)S(1)} collective-permute-done((bf16[12,8,256]{2,1,0:T(8,128)(2,1)S(1)}, bf16[12,8,256]{2,1,0:T(8,128)(2,1)S(1)}, u32[]{:S(2)}, u32[]{:S(2)}) %collective-permute-start.27) | collective-permute-done | bytes 49184 | tf_op jit(solution)/shard_map/ppermute | solution.py:276
  56.9 2.5 %collective-permute-start.38 = (bf16[12,8,256]{2,1,0:T(8,128)(2,1)S(1)}, bf16[12,8,256]{2,1,0:T(8,128)(2,1)S(1)}, u32[]{:S(2)}, u32[]{:S(2)}) collective-permute-start(bf16[12,8,256]{2,1,0:T(8,128)(2,1)S(1)} %get-tuple-element.181.refs_0_), channel_id=1, source_target_pairs={{0,12},{1,13},{2,14},{3,15},{4,8},{5,9},{6,10},{7,11},{8,4},{9,5},... | collective-permute-start | bytes 147464 | tf_op jit(solution)/shard_map/ppermute | solution.py:276
  76.0 2.5 %collective-permute-start.48 = (bf16[12,8,256]{2,1,0:T(8,128)(2,1)S(1)}, bf16[12,8,256]{2,1,0:T(8,128)(2,1)S(1)}, u32[]{:S(2)}, u32[]{:S(2)}) collective-permute-start(bf16[12,8,256]{2,1,0:T(8,128)(2,1)S(1)} %get-tuple-element.206), channel_id=1, source_target_pairs={{0,12},{1,13},{2,14},{3,15},{4,8},{5,9},{6,10},{7,11},{8,4},{9,5},... | collective-permute-start | bytes 147464 | tf_op jit(solution)/shard_map/ppermute | solution.py:276
  80.7 1.8 %collective-permute-done.48.refs_1_ = bf16[12,8,256]{2,1,0:T(8,128)(2,1)S(1)} collective-permute-done((bf16[12,8,256]{2,1,0:T(8,128)(2,1)S(1)}, bf16[12,8,256]{2,1,0:T(8,128)(2,1)S(1)}, u32[]{:S(2)}, u32[]{:S(2)}) %collective-permute-start.48) | collective-permute-done | bytes 49184 | tf_op jit(solution)/shard_map/ppermute | solution.py:276
  82.5 1.6 %collective-permute-done.49.refs_2_ = bf16[12,8,256]{2,1,0:T(8,128)(2,1)S(1)} collective-permute-done((bf16[12,8,256]{2,1,0:T(8,128)(2,1)S(1)}, bf16[12,8,256]{2,1,0:T(8,128)(2,1)S(1)}, u32[]{:S(2)}, u32[]{:S(2)}) %collective-permute-start.49) | collective-permute-done | bytes 49184 | tf_op jit(solution)/shard_map/ppermute | solution.py:276
  84.9 2.6 %collective-permute-start.51 = (bf16[12,8,256]{2,1,0:T(8,128)(2,1)S(1)}, bf16[12,8,256]{2,1,0:T(8,128)(2,1)S(1)}, u32[]{:S(2)}, u32[]{:S(2)}) collective-permute-start(bf16[12,8,256]{2,1,0:T(8,128)(2,1)S(1)} %get-tuple-element.211.refs_0_), channel_id=1, source_target_pairs={{0,8},{1,9},{2,10},{3,11},{4,12},{5,13},{6,14},{7,15},{8,0},{9,1},... | collective-permute-start | bytes 147464 | tf_op jit(solution)/shard_map/ppermute | solution.py:276
  87.5 1.5 %collective-permute-start.59 = (bf16[12,8,256]{2,1,0:T(8,128)(2,1)S(1)}, bf16[12,8,256]{2,1,0:T(8,128)(2,1)S(1)}, u32[]{:S(2)}, u32[]{:S(2)}) collective-permute-start(bf16[12,8,256]{2,1,0:T(8,128)(2,1)S(1)} %get-tuple-element.211.refs_0_), channel_id=1, source_target_pairs={{0,12},{1,13},{2,14},{3,15},{4,8},{5,9},{6,10},{7,11},{8,4},{9,5},... | collective-permute-start | bytes 147464 | tf_op jit(solution)/shard_map/ppermute | solution.py:276
  91.5 1.9 %collective-permute-done.59.refs_0_ = bf16[12,8,256]{2,1,0:T(8,128)(2,1)S(1)} collective-permute-done((bf16[12,8,256]{2,1,0:T(8,128)(2,1)S(1)}, bf16[12,8,256]{2,1,0:T(8,128)(2,1)S(1)}, u32[]{:S(2)}, u32[]{:S(2)}) %collective-permute-start.59) | collective-permute-done | bytes 49184 | tf_op jit(solution)/shard_map/ppermute | solution.py:276
  100.2 1.9 %middle.5 = (f32[8,2048]{1,0:T(8,128)S(1)}, f32[8,2048]{1,0:T(8,128)}, bf16[8,8,256]{2,1,0:T(8,128)(2,1)S(1)}, bf16[12,8,256]{2,1,0:T(8,128)(2,1)S(1)}, bf16[12,...) custom-call(s32[96]{0:T(128)S(4)} %get-tuple-element.136.tile_of, ...), custom_call_target="tpu_custom_call" | custom-call | flops 92274688 | bytes 11534336 | tf_op jit(solution)/shard_map/middle/pallas_call | solution.py:264
  110.3 1.5 %collective-permute-start.69 = (bf16[12,8,256]{2,1,0:T(8,128)(2,1)S(1)}, bf16[12,8,256]{2,1,0:T(8,128)(2,1)S(1)}, u32[]{:S(2)}, u32[]{:S(2)}) collective-permute-start(bf16[12,8,256]{2,1,0:T(8,128)(2,1)S(1)} %get-tuple-element.236), channel_id=1, source_target_pairs={{0,12},{1,13},{2,14},{3,15},{4,8},{5,9},{6,10},{7,11},{8,4},{9,5},... | collective-permute-start | bytes 147464 | tf_op jit(solution)/shard_map/ppermute | solution.py:276
  112.3 4.3 %collective-permute-done.69.refs_1_ = bf16[12,8,256]{2,1,0:T(8,128)(2,1)S(1)} collective-permute-done((bf16[12,8,256]{2,1,0:T(8,128)(2,1)S(1)}, bf16[12,8,256]{2,1,0:T(8,128)(2,1)S(1)}, u32[]{:S(2)}, u32[]{:S(2)}) %collective-permute-start.69) | collective-permute-done | bytes 49184 | tf_op jit(solution)/shard_map/ppermute | solution.py:276
  116.6 1.5 %collective-permute-done.70.refs_2_ = bf16[12,8,256]{2,1,0:T(8,128)(2,1)S(1)} collective-permute-done((bf16[12,8,256]{2,1,0:T(8,128)(2,1)S(1)}, bf16[12,8,256]{2,1,0:T(8,128)(2,1)S(1)}, u32[]{:S(2)}, u32[]{:S(2)}) %collective-permute-start.70) | collective-permute-done | bytes 49184 | tf_op jit(solution)/shard_map/ppermute | solution.py:276
  118.8 2.1 %collective-permute-start.72 = (bf16[12,8,256]{2,1,0:T(8,128)(2,1)S(1)}, bf16[12,8,256]{2,1,0:T(8,128)(2,1)S(1)}, u32[]{:S(2)}, u32[]{:S(2)}) collective-permute-start(bf16[12,8,256]{2,1,0:T(8,128)(2,1)S(1)} %get-tuple-element.242.refs_0_), channel_id=1, source_target_pairs={{0,8},{1,9},{2,10},{3,11},{4,12},{5,13},{6,14},{7,15},{8,0},{9,1},... | collective-permute-start | bytes 147464 | tf_op jit(solution)/shard_map/ppermute | solution.py:276
  120.8 2.3 %collective-permute-start.80 = (bf16[12,8,256]{2,1,0:T(8,128)(2,1)S(1)}, bf16[12,8,256]{2,1,0:T(8,128)(2,1)S(1)}, u32[]{:S(2)}, u32[]{:S(2)}) collective-permute-start(bf16[12,8,256]{2,1,0:T(8,128)(2,1)S(1)} %get-tuple-element.242.refs_0_), channel_id=1, source_target_pairs={{0,12},{1,13},{2,14},{3,15},{4,8},{5,9},{6,10},{7,11},{8,4},{9,5},... | collective-permute-start | bytes 147464 | tf_op jit(solution)/shard_map/ppermute | solution.py:276
  (197 shorter events, 75.1 us)
Async XLA Ops:
  7.2 6.2 %collective-permute-start = (bf16[13,8,256]{2,1,0:T(8,128)(2,1)S(1)}, bf16[13,8,256]{2,1,0:T(8,128)(2,1)S(1)}, u32[]{:S(2)}, u32[]{:S(2)}) collective-permute-start(bf16[13,8,256]{2,1,0:T(8,128)(2,1)S(1)} %get-tuple-element.133), channel_id=1, source_target_pairs={{0,1},{1,0},{2,3},{3,2},{4,5},{5,4},{6,7},{7,6},{8,9},{9,8},{10,11... | collective-permute-start | bytes 159752 | tf_op jit(solution)/shard_map/ppermute | solution.py:276
  7.7 5.7 %collective-permute-start.1 = (bf16[13,8,256]{2,1,0:T(8,128)(2,1)S(1)}, bf16[13,8,256]{2,1,0:T(8,128)(2,1)S(1)}, u32[]{:S(2)}, u32[]{:S(2)}) collective-permute-start(bf16[13,8,256]{2,1,0:T(8,128)(2,1)S(1)} %get-tuple-element.134), channel_id=1, source_target_pairs={{0,2},{1,3},{2,0},{3,1},{4,6},{5,7},{6,4},{7,5},{8,10},{9,11},{10,... | collective-permute-start | bytes 159752 | tf_op jit(solution)/shard_map/ppermute | solution.py:276
  11.3 7.3 %collective-permute-start.3 = (bf16[12,8,256]{2,1,0:T(8,128)(2,1)S(1)}, bf16[12,8,256]{2,1,0:T(8,128)(2,1)S(1)}, u32[]{:S(2)}, u32[]{:S(2)}) collective-permute-start(bf16[12,8,256]{2,1,0:T(8,128)(2,1)S(1)} %get-tuple-element.140), channel_id=1, source_target_pairs={{0,1},{1,0},{2,3},{3,2},{4,5},{5,4},{6,7},{7,6},{8,9},{9,8},{10,11... | collective-permute-start | bytes 147464 | tf_op jit(solution)/shard_map/ppermute | solution.py:276
  11.4 7.1 %collective-permute-start.4 = (bf16[12,8,256]{2,1,0:T(8,128)(2,1)S(1)}, bf16[12,8,256]{2,1,0:T(8,128)(2,1)S(1)}, u32[]{:S(2)}, u32[]{:S(2)}) collective-permute-start(bf16[12,8,256]{2,1,0:T(8,128)(2,1)S(1)} %get-tuple-element.141), channel_id=1, source_target_pairs={{0,2},{1,3},{2,0},{3,1},{4,6},{5,7},{6,4},{7,5},{8,10},{9,11},{10,... | collective-permute-start | bytes 147464 | tf_op jit(solution)/shard_map/ppermute | solution.py:276
  14.9 8.4 %collective-permute-start.6 = (bf16[12,8,256]{2,1,0:T(8,128)(2,1)S(1)}, bf16[12,8,256]{2,1,0:T(8,128)(2,1)S(1)}, u32[]{:S(2)}, u32[]{:S(2)}) collective-permute-start(bf16[12,8,256]{2,1,0:T(8,128)(2,1)S(1)} %get-tuple-element.144), channel_id=1, source_target_pairs={{0,12},{1,13},{2,14},{3,15},{4,8},{5,9},{6,10},{7,11},{8,4},{9,5},... | collective-permute-start | bytes 147464 | tf_op jit(solution)/shard_map/ppermute | solution.py:276
  24.8 5.8 %collective-permute-start.9 = (bf16[12,8,256]{2,1,0:T(8,128)(2,1)S(1)}, bf16[12,8,256]{2,1,0:T(8,128)(2,1)S(1)}, u32[]{:S(2)}, u32[]{:S(2)}) collective-permute-start(bf16[12,8,256]{2,1,0:T(8,128)(2,1)S(1)} %get-tuple-element.151.refs_0_), channel_id=1, source_target_pairs={{0,8},{1,9},{2,10},{3,11},{4,12},{5,13},{6,14},{7,15},{8,0},{9,1},... | collective-permute-start | bytes 147464 | tf_op jit(solution)/shard_map/ppermute | solution.py:276
  27.7 5.9 %collective-permute-start.17 = (bf16[12,8,256]{2,1,0:T(8,128)(2,1)S(1)}, bf16[12,8,256]{2,1,0:T(8,128)(2,1)S(1)}, u32[]{:S(2)}, u32[]{:S(2)}) collective-permute-start(bf16[12,8,256]{2,1,0:T(8,128)(2,1)S(1)} %get-tuple-element.151.refs_0_), channel_id=1, source_target_pairs={{0,12},{1,13},{2,14},{3,15},{4,8},{5,9},{6,10},{7,11},{8,4},{9,5},... | collective-permute-start | bytes 147464 | tf_op jit(solution)/shard_map/ppermute | solution.py:276
  28.6 6.1 %collective-permute-start.14 = (bf16[12,8,256]{2,1,0:T(8,128)(2,1)S(1)}, bf16[12,8,256]{2,1,0:T(8,128)(2,1)S(1)}, u32[]{:S(2)}, u32[]{:S(2)}) collective-permute-start(bf16[12,8,256]{2,1,0:T(8,128)(2,1)S(1)} %get-tuple-element.157), channel_id=1, source_target_pairs={{0,1},{1,0},{2,3},{3,2},{4,5},{5,4},{6,7},{7,6},{8,9},{9,8},{10,11... | collective-permute-start | bytes 147464 | tf_op jit(solution)/shard_map/ppermute | solution.py:276
  28.7 7.1 %collective-permute-start.15 = (bf16[12,8,256]{2,1,0:T(8,128)(2,1)S(1)}, bf16[12,8,256]{2,1,0:T(8,128)(2,1)S(1)}, u32[]{:S(2)}, u32[]{:S(2)}) collective-permute-start(bf16[12,8,256]{2,1,0:T(8,128)(2,1)S(1)} %get-tuple-element.158), channel_id=1, source_target_pairs={{0,2},{1,3},{2,0},{3,1},{4,6},{5,7},{6,4},{7,5},{8,10},{9,11},{10,... | collective-permute-start | bytes 147464 | tf_op jit(solution)/shard_map/ppermute | solution.py:276
  29.9 7.0 %collective-permute-start.16 = (bf16[12,8,256]{2,1,0:T(8,128)(2,1)S(1)}, bf16[12,8,256]{2,1,0:T(8,128)(2,1)S(1)}, u32[]{:S(2)}, u32[]{:S(2)}) collective-permute-start(bf16[12,8,256]{2,1,0:T(8,128)(2,1)S(1)} %get-tuple-element.159), channel_id=1, source_target_pairs={{0,3},{1,2},{2,1},{3,0},{4,7},{5,6},{6,5},{7,4},{8,11},{9,10},{10,... | collective-permute-start | bytes 147464 | tf_op jit(solution)/shard_map/ppermute | solution.py:276
  47.0 6.6 %collective-permute-start.27 = (bf16[12,8,256]{2,1,0:T(8,128)(2,1)S(1)}, bf16[12,8,256]{2,1,0:T(8,128)(2,1)S(1)}, u32[]{:S(2)}, u32[]{:S(2)}) collective-permute-start(bf16[12,8,256]{2,1,0:T(8,128)(2,1)S(1)} %get-tuple-element.176), channel_id=1, source_target_pairs={{0,12},{1,13},{2,14},{3,15},{4,8},{5,9},{6,10},{7,11},{8,4},{9,5},... | collective-permute-start | bytes 147464 | tf_op jit(solution)/shard_map/ppermute | solution.py:276
  47.8 6.8 %collective-permute-start.28 = (bf16[12,8,256]{2,1,0:T(8,128)(2,1)S(1)}, bf16[12,8,256]{2,1,0:T(8,128)(2,1)S(1)}, u32[]{:S(2)}, u32[]{:S(2)}) collective-permute-start(bf16[12,8,256]{2,1,0:T(8,128)(2,1)S(1)} %get-tuple-element.177), channel_id=1, source_target_pairs={{0,8},{1,9},{2,10},{3,11},{4,12},{5,13},{6,14},{7,15},{8,0},{9,1},... | collective-permute-start | bytes 147464 | tf_op jit(solution)/shard_map/ppermute | solution.py:276
  55.9 5.6 %collective-permute-start.30 = (bf16[12,8,256]{2,1,0:T(8,128)(2,1)S(1)}, bf16[12,8,256]{2,1,0:T(8,128)(2,1)S(1)}, u32[]{:S(2)}, u32[]{:S(2)}) collective-permute-start(bf16[12,8,256]{2,1,0:T(8,128)(2,1)S(1)} %get-tuple-element.181.refs_0_), channel_id=1, source_target_pairs={{0,8},{1,9},{2,10},{3,11},{4,12},{5,13},{6,14},{7,15},{8,0},{9,1},... | collective-permute-start | bytes 147464 | tf_op jit(solution)/shard_map/ppermute | solution.py:276
  56.9 5.9 %collective-permute-start.38 = (bf16[12,8,256]{2,1,0:T(8,128)(2,1)S(1)}, bf16[12,8,256]{2,1,0:T(8,128)(2,1)S(1)}, u32[]{:S(2)}, u32[]{:S(2)}) collective-permute-start(bf16[12,8,256]{2,1,0:T(8,128)(2,1)S(1)} %get-tuple-element.181.refs_0_), channel_id=1, source_target_pairs={{0,12},{1,13},{2,14},{3,15},{4,8},{5,9},{6,10},{7,11},{8,4},{9,5},... | collective-permute-start | bytes 147464 | tf_op jit(solution)/shard_map/ppermute | solution.py:276
  60.4 5.5 %collective-permute-start.37 = (bf16[12,8,256]{2,1,0:T(8,128)(2,1)S(1)}, bf16[12,8,256]{2,1,0:T(8,128)(2,1)S(1)}, u32[]{:S(2)}, u32[]{:S(2)}) collective-permute-start(bf16[12,8,256]{2,1,0:T(8,128)(2,1)S(1)} %get-tuple-element.189), channel_id=1, source_target_pairs={{0,3},{1,2},{2,1},{3,0},{4,7},{5,6},{6,5},{7,4},{8,11},{9,10},{10,... | collective-permute-start | bytes 147464 | tf_op jit(solution)/shard_map/ppermute | solution.py:276
  76.0 6.4 %collective-permute-start.48 = (bf16[12,8,256]{2,1,0:T(8,128)(2,1)S(1)}, bf16[12,8,256]{2,1,0:T(8,128)(2,1)S(1)}, u32[]{:S(2)}, u32[]{:S(2)}) collective-permute-start(bf16[12,8,256]{2,1,0:T(8,128)(2,1)S(1)} %get-tuple-element.206), channel_id=1, source_target_pairs={{0,12},{1,13},{2,14},{3,15},{4,8},{5,9},{6,10},{7,11},{8,4},{9,5},... | collective-permute-start | bytes 147464 | tf_op jit(solution)/shard_map/ppermute | solution.py:276
  84.9 6.1 %collective-permute-start.51 = (bf16[12,8,256]{2,1,0:T(8,128)(2,1)S(1)}, bf16[12,8,256]{2,1,0:T(8,128)(2,1)S(1)}, u32[]{:S(2)}, u32[]{:S(2)}) collective-permute-start(bf16[12,8,256]{2,1,0:T(8,128)(2,1)S(1)} %get-tuple-element.211.refs_0_), channel_id=1, source_target_pairs={{0,8},{1,9},{2,10},{3,11},{4,12},{5,13},{6,14},{7,15},{8,0},{9,1},... | collective-permute-start | bytes 147464 | tf_op jit(solution)/shard_map/ppermute | solution.py:276
  87.5 5.9 %collective-permute-start.59 = (bf16[12,8,256]{2,1,0:T(8,128)(2,1)S(1)}, bf16[12,8,256]{2,1,0:T(8,128)(2,1)S(1)}, u32[]{:S(2)}, u32[]{:S(2)}) collective-permute-start(bf16[12,8,256]{2,1,0:T(8,128)(2,1)S(1)} %get-tuple-element.211.refs_0_), channel_id=1, source_target_pairs={{0,12},{1,13},{2,14},{3,15},{4,8},{5,9},{6,10},{7,11},{8,4},{9,5},... | collective-permute-start | bytes 147464 | tf_op jit(solution)/shard_map/ppermute | solution.py:276
  89.2 6.5 %collective-permute-start.57 = (bf16[12,8,256]{2,1,0:T(8,128)(2,1)S(1)}, bf16[12,8,256]{2,1,0:T(8,128)(2,1)S(1)}, u32[]{:S(2)}, u32[]{:S(2)}) collective-permute-start(bf16[12,8,256]{2,1,0:T(8,128)(2,1)S(1)} %get-tuple-element.218), channel_id=1, source_target_pairs={{0,2},{1,3},{2,0},{3,1},{4,6},{5,7},{6,4},{7,5},{8,10},{9,11},{10,... | collective-permute-start | bytes 147464 | tf_op jit(solution)/shard_map/ppermute | solution.py:276
  90.2 6.5 %collective-permute-start.58 = (bf16[12,8,256]{2,1,0:T(8,128)(2,1)S(1)}, bf16[12,8,256]{2,1,0:T(8,128)(2,1)S(1)}, u32[]{:S(2)}, u32[]{:S(2)}) collective-permute-start(bf16[12,8,256]{2,1,0:T(8,128)(2,1)S(1)} %get-tuple-element.219), channel_id=1, source_target_pairs={{0,3},{1,2},{2,1},{3,0},{4,7},{5,6},{6,5},{7,4},{8,11},{9,10},{10,... | collective-permute-start | bytes 147464 | tf_op jit(solution)/shard_map/ppermute | solution.py:276
  110.3 6.2 %collective-permute-start.69 = (bf16[12,8,256]{2,1,0:T(8,128)(2,1)S(1)}, bf16[12,8,256]{2,1,0:T(8,128)(2,1)S(1)}, u32[]{:S(2)}, u32[]{:S(2)}) collective-permute-start(bf16[12,8,256]{2,1,0:T(8,128)(2,1)S(1)} %get-tuple-element.236), channel_id=1, source_target_pairs={{0,12},{1,13},{2,14},{3,15},{4,8},{5,9},{6,10},{7,11},{8,4},{9,5},... | collective-permute-start | bytes 147464 | tf_op jit(solution)/shard_map/ppermute | solution.py:276
  111.9 6.2 %collective-permute-start.70 = (bf16[12,8,256]{2,1,0:T(8,128)(2,1)S(1)}, bf16[12,8,256]{2,1,0:T(8,128)(2,1)S(1)}, u32[]{:S(2)}, u32[]{:S(2)}) collective-permute-start(bf16[12,8,256]{2,1,0:T(8,128)(2,1)S(1)} %get-tuple-element.237), channel_id=1, source_target_pairs={{0,8},{1,9},{2,10},{3,11},{4,12},{5,13},{6,14},{7,15},{8,0},{9,1},... | collective-permute-start | bytes 147464 | tf_op jit(solution)/shard_map/ppermute | solution.py:276
  118.8 6.7 %collective-permute-start.72 = (bf16[12,8,256]{2,1,0:T(8,128)(2,1)S(1)}, bf16[12,8,256]{2,1,0:T(8,128)(2,1)S(1)}, u32[]{:S(2)}, u32[]{:S(2)}) collective-permute-start(bf16[12,8,256]{2,1,0:T(8,128)(2,1)S(1)} %get-tuple-element.242.refs_0_), channel_id=1, source_target_pairs={{0,8},{1,9},{2,10},{3,11},{4,12},{5,13},{6,14},{7,15},{8,0},{9,1},... | collective-permute-start | bytes 147464 | tf_op jit(solution)/shard_map/ppermute | solution.py:276
  120.8 5.9 %collective-permute-start.80 = (bf16[12,8,256]{2,1,0:T(8,128)(2,1)S(1)}, bf16[12,8,256]{2,1,0:T(8,128)(2,1)S(1)}, u32[]{:S(2)}, u32[]{:S(2)}) collective-permute-start(bf16[12,8,256]{2,1,0:T(8,128)(2,1)S(1)} %get-tuple-element.242.refs_0_), channel_id=1, source_target_pairs={{0,12},{1,13},{2,14},{3,15},{4,8},{5,9},{6,10},{7,11},{8,4},{9,5},... | collective-permute-start | bytes 147464 | tf_op jit(solution)/shard_map/ppermute | solution.py:276
  (65 other events, 273.3 us)

commit v8 on v7

--- a/solution.py
+++ b/solution.py
@@ -33,20 +33,20 @@
         h_into(at, h)
 
 
-def transpose_products(base, tile_of, row_of, tiles, hb, outs):
+def transpose_products(base, tile_of, row_of, tiles, hb, outs, xs=range(QUAD)):
     per = tile_of.shape[0] // (2 * QUAD)
-    for x, out in enumerate(outs):
+    for x, out in zip(xs, outs):
         for s in range(per):
             slot = base + x * per + s
             out[s] = jnp.dot(hb[row_of[slot]], tiles[tile_of[slot]], preferred_element_type=F32).astype(BF16)
 
 
-def forward_products(base, tile_of, land_of, turned, moved, totals):
-    per = moved[0].shape[0]
+def forward_products(base, tile_of, land_of, turned, moved, totals, xs=range(QUAD)):
+    per = tile_of.shape[0] // (2 * QUAD)
     for total in totals:
         total[...] = jnp.zeros_like(total)
-    for x, part in enumerate(moved):
-        first = base + x * (tile_of.shape[0] // (2 * QUAD))
+    for x, part in zip(xs, moved):
+        first = base + x * per
         terms = [jnp.dot(part[s], turned[tile_of[first + s]], preferred_element_type=F32) for s in range(per)]
         for s in range(0, per, LANES):
             several = range(min(LANES, per - s))
@@ -192,31 +192,35 @@
         out[c] = q.astype(BF16)
 
 
-def pick_kernel(first_high, cap, wants, *refs):
-    blocks, outs = refs[:-QUAD], refs[-QUAD:]
-    last = blocks[0].shape[0] - 1
+def pick_kernel(highs, cap, wants, *refs):
+    blocks, outs = dict(zip(highs, refs[:-QUAD])), refs[-QUAD:]
+    last = refs[0].shape[0] - 1
     for x, out in enumerate(outs):
-        values = [
-            blocks[h][jnp.minimum(wants[x, (first_high + h) * cap + r], last)]
-            for h in range(len(blocks))
-            for r in range(cap)
-        ]
+        values = [blocks[h][jnp.minimum(wants[x, h * cap + r], last)] for h in sorted(highs) for r in range(cap)]
         for s, value in enumerate(values):
             out[s] = value
 
 
-def near_forward_kernel(base, tile_of, land_of, turned, m0, m1, m2, m3, *rest):
-    out, totals = rest[-LANES - 1], rest[-LANES:]
-    forward_products(base, tile_of, land_of, turned, (m0, m1, m2, m3), totals)
+def near_forward_kernel(tile_of, land_of, turned, m0, m1, m2, m3, out, *totals):
+    forward_products(tile_of.shape[0] // 2, tile_of, land_of, turned, (m0, m1, m2, m3), totals)
     for r in range(out.shape[0]):
-        value = gathered(totals, r)
-        out[r] = value + rest[0][r] if len(rest) > LANES + 1 else value
-
-
-def middle_kernel(step, base, tile_of, row_of, land_of, held, turned, dual_step, dual_mask, part, dy, rhs, m0, m1, m2, m3,
-                  new_dy, new_rhs, hb, o0, o1, o2, o3, *totals):
+        out[r] = gathered(totals, r)
+
+
+def chip_forward_kernel(tile_of, land_of, turned, part, m0, m1, out, *totals):
+    forward_products(0, tile_of, land_of, turned, (m0, m1), totals, (0, 1))
+    for r in range(out.shape[0]):
+        out[r] = part[r] + gathered(totals, r)
+
+
+def rest_product_kernel(tile_of, row_of, held, hb, o0, o1, o3):
+    transpose_products(0, tile_of, row_of, held, hb, (o3, o1, o0), (3, 1, 0))
+
+
+def middle_kernel(step, tile_of, row_of, land_of, held, turned, dual_step, dual_mask, part, dy, rhs, m2, m3,
+                  new_dy, new_rhs, hb, o2, *totals):
     side = held.shape[1]
-    forward_products(base, tile_of, land_of, turned, (m0, m1, m2, m3), totals)
+    forward_products(0, tile_of, land_of, turned, (m2, m3), totals, (2, 3))
     for r in range(hb.shape[0]):
         at = pl.ds(r * side, side)
         v = part[r] + gathered(totals, r)
@@ -226,12 +230,12 @@
         new_rhs[:, at] = rhs[:, at] - h
 
     scaled_blocks(side, new_dy, dual_step, hb, h_into)
-    transpose_products(0, tile_of, row_of, held, hb, (o0, o1, o2, o3))
-
-
-def last_kernel(base, tile_of, land_of, turned, part, dy, m0, m1, m2, m3, new_y, *totals):
+    transpose_products(0, tile_of, row_of, held, hb, (o2,), (2,))
+
+
+def last_kernel(tile_of, land_of, turned, part, dy, m2, m3, new_y, *totals):
     side = turned.shape[1]
-    forward_products(base, tile_of, land_of, turned, (m0, m1, m2, m3), totals)
+    forward_products(0, tile_of, land_of, turned, (m2, m3), totals, (2, 3))
     for r in range(part.shape[0]):
         at = pl.ds(r * side, side)
         new_y[:, at] = dy[:, at] - (part[r] + gathered(totals, r))
@@ -301,8 +305,7 @@
     ))
     turned = call(turn_kernel, "turn", tile_bytes, [VM], pltpu.VMEM(tiles.shape, BF16), (held,))
     x_state, spent, wants = cot_x, cot_x, None
-    middle_high = half + half // 2
-    late = half // 2 * cap
+    near_highs, far_highs = tuple(range(half)), tuple(reversed(range(half, group)))
     while True:
         far_got = near_swaps(far_parts)
         near_parts = call(near_product_kernel, "near_product", tile_bytes // 2, [SM] * 2 + [VM] * 2, part_set,
@@ -330,28 +333,27 @@
             functools.partial(primal_kernel, step, step == steps - 1), "primal", 1 << 20, [VM] * (4 + group),
             (x_shape, x_shape, block_set), (primal_mask, primal_step, x_state, spent, near_sums[0], *got))
         blocks = [moved] + [swap(moved, h * QUAD) for h in range(1, group)]
-        near_moved = near_swaps(call(functools.partial(pick_kernel, 0, cap), "near_pick", 1 << 20,
-                                     [SM] + [VM] * half, part_set, (wants, *blocks[:half])))
-        early_moved, late_moved = (
-            near_swaps(call(functools.partial(pick_kernel, low, cap), name, 1 << 20, [SM] + [VM] * (top - low),
-                            (shape(((top - low) * cap, batch, side), BF16),) * QUAD, (wants, *blocks[low:top])))
-            for name, low, top in (("early_pick", half, middle_high), ("late_pick", middle_high, group))
+        near_moved, far_moved = (
+            near_swaps(call(functools.partial(pick_kernel, highs, cap), name, 1 << 20, [SM] + [VM] * half, part_set,
+                            (wants, *(blocks[h] for h in highs))))
+            for name, highs in (("near_pick", near_highs), ("far_pick", far_highs))
         )
-        part = call(functools.partial(near_forward_kernel, slots // 2), "near_forward", tile_bytes // 2,
-                    [SM] * 2 + [VM] * (1 + QUAD), shape(hb_set.shape, F32), (tile_of, land_of, turned, *near_moved),
-                    row_totals)
-        part = call(functools.partial(near_forward_kernel, 0), "early_forward", tile_bytes // 4,
-                    [SM] * 2 + [VM] * (2 + QUAD), shape(hb_set.shape, F32),
-                    (tile_of, land_of, turned, *early_moved, part), row_totals)
+        part = call(near_forward_kernel, "near_forward", tile_bytes // 2, [SM] * 2 + [VM] * (1 + QUAD),
+                    shape(hb_set.shape, F32), (tile_of, land_of, turned, *near_moved), row_totals)
+        part = call(chip_forward_kernel, "chip_forward", tile_bytes // 4, [SM] * 2 + [VM] * 4,
+                    shape(hb_set.shape, F32), (tile_of, land_of, turned, part, *far_moved[:2]), row_totals)
         if step == 0:
             break
         step -= 1
-        dy, rhs, hb, *far_parts = call(
-            functools.partial(middle_kernel, step, late), "middle", tile_bytes, [SM] * 3 + [VM] * (7 + QUAD),
-            (y_shape, y_shape, hb_set) + part_set,
-            (tile_of, row_of, land_of, held, turned, dual_step, dual_mask, part, dy, rhs, *late_moved), row_totals)
-    y_state = call(functools.partial(last_kernel, late), "last", tile_bytes // 2, [SM] * 2 + [VM] * (3 + QUAD), y_shape,
-                   (tile_of, land_of, turned, part, dy, *late_moved), row_totals)
+        dy, rhs, hb, across = call(
+            functools.partial(middle_kernel, step), "middle", tile_bytes // 2, [SM] * 3 + [VM] * 9,
+            (y_shape, y_shape, hb_set, part_set[0]),
+            (tile_of, row_of, land_of, held, turned, dual_step, dual_mask, part, dy, rhs, *far_moved[2:]), row_totals)
+        own, beside, aslant = call(rest_product_kernel, "rest_product", tile_bytes // 4, [SM] * 2 + [VM] * 2,
+                                   part_set[:3], (tile_of, row_of, held, hb))
+        far_parts = [own, beside, across, aslant]
+    y_state = call(last_kernel, "last", tile_bytes // 4, [SM] * 2 + [VM] * 5, y_shape,
+                   (tile_of, land_of, turned, part, dy, *far_moved[2:]), row_totals)
     return spent, rhs, x_state, y_state
 
 

time: 135 us -> 126 us (0.933)
  starting transfers between devices: 70.6 us -> 64.4 us
  waiting for transfers between devices: 33.6 us -> 30.4 us
    ppermute x84 -> x72, starting transfers between devices: 70.6 us -> 64.4 us  [swap(): return lax.ppermute(array, 'rb', [(p, p ^ x) for p in range(peers)])]
    ppermute x84 -> x72, waiting for transfers between devices: 33.6 us -> 30.4 us  [swap(): return lax.ppermute(array, 'rb', [(p, p ^ x) for p in range(peers)])]
    pallas_call x41 -> x40, Pallas kernels: 22 us -> 22.3 us  [call(): pl.pallas_call(kernel, out_shape=outs, in_specs=ins, out_specs=jax.tree.m...]
  transfers between devices with their start and end apart: 84 -> 72, of which waited for: 35 -> 30; matrix products, arithmetic and copies ran while one was open for 0% -> 0% of each run, Pallas kernels for 11% -> 14%
where the time goes in v8:
time: 126 us; the launch traced here: 125 us
  starting transfers between devices  64.4 us (51%)
  waiting for transfers between devices  30.4 us (24%)
  Pallas kernels  28.8 us (23%)
  between operations  1.72 us (1%)
    ppermute x72, starting transfers between devices, swap(): return lax.ppermute(array, 'rb', [(p, p ^ x) for p in range(peers)])  64.4 us
    ppermute x72, waiting for transfers between devices, swap(): return lax.ppermute(array, 'rb', [(p, p ^ x) for p in range(peers)])  30.4 us
    pallas_call x40, Pallas kernels, call(): pl.pallas_call(kernel, out_shape=outs, in_specs=ins, out_specs=jax.tree.m...  22.3 us
    pallas_call x1, Pallas kernels, on_device(): pl.pallas_call(functools.partial(start_kernel, step, peers, cap, col_bloc...  5.87 us
  transfers between devices with their start and end apart: 72, of which 30 were waited for; matrix products, arithmetic and copies ran while one was open for 0% of the time, Pallas kernels for 14%

profile of v8, /device:TPU:0, one launch (start us, length us, event | category | flops | bytes accessed | tf_op | source)
XLA Modules:
  0.0 125.4 jit_solution(6271647080059671271)
XLA Ops:
  1.3 5.9 %start.1 = (bf16[88,256,256]{2,1,0:T(8,128)(2,1)S(1)}, f32[8,2048]{1,0:T(8,128)S(1)}, f32[8,2048]{1,0:T(8,128)S(1)}, bf16[8,8,256]{2,1,0:T(8,128)(2,1)S(1)}, s32...) custom-call(s32[1]{0:T(128)S(6)} %copy.14.count, ...), custom_call_target="tpu_custom_call" | custom-call | flops 184549376 | bytes 23068672 | tf_op jit(solution)/shard_map/start/pallas_call | solution.py:286
  7.7 2.6 %collective-permute-start.1 = (bf16[13,8,256]{2,1,0:T(8,128)(2,1)S(1)}, bf16[13,8,256]{2,1,0:T(8,128)(2,1)S(1)}, u32[]{:S(2)}, u32[]{:S(2)}) collective-permute-start(bf16[13,8,256]{2,1,0:T(8,128)(2,1)S(1)} %get-tuple-element.118), channel_id=1, source_target_pairs={{0,2},{1,3},{2,0},{3,1},{4,6},{5,7},{6,4},{7,5},{8,10},{9,11},{10,... | collective-permute-start | bytes 159752 | tf_op jit(solution)/shard_map/ppermute | solution.py:280
  11.4 1.9 %collective-permute-start.4 = (bf16[12,8,256]{2,1,0:T(8,128)(2,1)S(1)}, bf16[12,8,256]{2,1,0:T(8,128)(2,1)S(1)}, u32[]{:S(2)}, u32[]{:S(2)}) collective-permute-start(bf16[12,8,256]{2,1,0:T(8,128)(2,1)S(1)} %get-tuple-element.125), channel_id=1, source_target_pairs={{0,2},{1,3},{2,0},{3,1},{4,6},{5,7},{6,4},{7,5},{8,10},{9,11},{10,... | collective-permute-start | bytes 147464 | tf_op jit(solution)/shard_map/ppermute | solution.py:280
  14.9 3.7 %collective-permute-start.6 = (bf16[12,8,256]{2,1,0:T(8,128)(2,1)S(1)}, bf16[12,8,256]{2,1,0:T(8,128)(2,1)S(1)}, u32[]{:S(2)}, u32[]{:S(2)}) collective-permute-start(bf16[12,8,256]{2,1,0:T(8,128)(2,1)S(1)} %get-tuple-element.128), channel_id=1, source_target_pairs={{0,12},{1,13},{2,14},{3,15},{4,8},{5,9},{6,10},{7,11},{8,4},{9,5},... | collective-permute-start | bytes 147464 | tf_op jit(solution)/shard_map/ppermute | solution.py:280
  19.6 3.7 %turn.1.turned = bf16[88,256,256]{2,1,0:T(8,128)(2,1)S(1)} custom-call(bf16[88,256,256]{2,1,0:T(8,128)(2,1)S(1)} %get-tuple-element.114.held), custom_call_target="tpu_custom_call" | custom-call | flops 92274688 | bytes 11534336 | tf_op jit(solution)/shard_map/turn/pallas_call | solution.py:268
  24.8 2.9 %collective-permute-start.14 = (bf16[12,8,256]{2,1,0:T(8,128)(2,1)S(1)}, bf16[12,8,256]{2,1,0:T(8,128)(2,1)S(1)}, u32[]{:S(2)}, u32[]{:S(2)}) collective-permute-start(bf16[12,8,256]{2,1,0:T(8,128)(2,1)S(1)} %get-tuple-element.135.refs_0_), channel_id=1, source_target_pairs={{0,8},{1,9},{2,10},{3,11},{4,12},{5,13},{6,14},{7,15},{8,0},{9,1},... | collective-permute-start | bytes 147464 | tf_op jit(solution)/shard_map/ppermute | solution.py:280
  30.6 3.0 %collective-permute-done.13.refs_0_ = bf16[12,8,256]{2,1,0:T(8,128)(2,1)S(1)} collective-permute-done((bf16[12,8,256]{2,1,0:T(8,128)(2,1)S(1)}, bf16[12,8,256]{2,1,0:T(8,128)(2,1)S(1)}, u32[]{:S(2)}, u32[]{:S(2)}) %collective-permute-start.13) | collective-permute-done | bytes 49184 | tf_op jit(solution)/shard_map/ppermute | solution.py:280
  48.4 1.5 %collective-permute-start.26 = (bf16[12,8,256]{2,1,0:T(8,128)(2,1)S(1)}, bf16[12,8,256]{2,1,0:T(8,128)(2,1)S(1)}, u32[]{:S(2)}, u32[]{:S(2)}) collective-permute-start(bf16[12,8,256]{2,1,0:T(8,128)(2,1)S(1)} %get-tuple-element.158), channel_id=1, source_target_pairs={{0,4},{1,5},{2,6},{3,7},{4,0},{5,1},{6,2},{7,3},{8,12},{9,13},{10,... | collective-permute-start | bytes 147464 | tf_op jit(solution)/shard_map/ppermute | solution.py:280
  49.9 1.9 %collective-permute-done.24.refs_1_ = bf16[12,8,256]{2,1,0:T(8,128)(2,1)S(1)} collective-permute-done((bf16[12,8,256]{2,1,0:T(8,128)(2,1)S(1)}, bf16[12,8,256]{2,1,0:T(8,128)(2,1)S(1)}, u32[]{:S(2)}, u32[]{:S(2)}) %collective-permute-start.24) | collective-permute-done | bytes 49184 | tf_op jit(solution)/shard_map/ppermute | solution.py:280
  55.2 2.5 %collective-permute-start.31 = (bf16[12,8,256]{2,1,0:T(8,128)(2,1)S(1)}, bf16[12,8,256]{2,1,0:T(8,128)(2,1)S(1)}, u32[]{:S(2)}, u32[]{:S(2)}) collective-permute-start(bf16[12,8,256]{2,1,0:T(8,128)(2,1)S(1)} %get-tuple-element.161.refs_0_), channel_id=1, source_target_pairs={{0,12},{1,13},{2,14},{3,15},{4,8},{5,9},{6,10},{7,11},{8,4},{9,5},... | collective-permute-start | bytes 147464 | tf_op jit(solution)/shard_map/ppermute | solution.py:280
  72.8 2.5 %collective-permute-start.42 = (bf16[12,8,256]{2,1,0:T(8,128)(2,1)S(1)}, bf16[12,8,256]{2,1,0:T(8,128)(2,1)S(1)}, u32[]{:S(2)}, u32[]{:S(2)}) collective-permute-start(bf16[12,8,256]{2,1,0:T(8,128)(2,1)S(1)} %get-tuple-element.182), channel_id=1, source_target_pairs={{0,12},{1,13},{2,14},{3,15},{4,8},{5,9},{6,10},{7,11},{8,4},{9,5},... | collective-permute-start | bytes 147464 | tf_op jit(solution)/shard_map/ppermute | solution.py:280
  76.0 1.5 %collective-permute-start.44 = (bf16[12,8,256]{2,1,0:T(8,128)(2,1)S(1)}, bf16[12,8,256]{2,1,0:T(8,128)(2,1)S(1)}, u32[]{:S(2)}, u32[]{:S(2)}) collective-permute-start(bf16[12,8,256]{2,1,0:T(8,128)(2,1)S(1)} %get-tuple-element.184), channel_id=1, source_target_pairs={{0,4},{1,5},{2,6},{3,7},{4,0},{5,1},{6,2},{7,3},{8,12},{9,13},{10,... | collective-permute-start | bytes 147464 | tf_op jit(solution)/shard_map/ppermute | solution.py:280
  77.5 1.8 %collective-permute-done.42.refs_1_ = bf16[12,8,256]{2,1,0:T(8,128)(2,1)S(1)} collective-permute-done((bf16[12,8,256]{2,1,0:T(8,128)(2,1)S(1)}, bf16[12,8,256]{2,1,0:T(8,128)(2,1)S(1)}, u32[]{:S(2)}, u32[]{:S(2)}) %collective-permute-start.42) | collective-permute-done | bytes 49184 | tf_op jit(solution)/shard_map/ppermute | solution.py:280
  79.3 1.6 %collective-permute-done.43.refs_2_ = bf16[12,8,256]{2,1,0:T(8,128)(2,1)S(1)} collective-permute-done((bf16[12,8,256]{2,1,0:T(8,128)(2,1)S(1)}, bf16[12,8,256]{2,1,0:T(8,128)(2,1)S(1)}, u32[]{:S(2)}, u32[]{:S(2)}) %collective-permute-start.43) | collective-permute-done | bytes 49184 | tf_op jit(solution)/shard_map/ppermute | solution.py:280
  81.7 2.5 %collective-permute-start.50 = (bf16[12,8,256]{2,1,0:T(8,128)(2,1)S(1)}, bf16[12,8,256]{2,1,0:T(8,128)(2,1)S(1)}, u32[]{:S(2)}, u32[]{:S(2)}) collective-permute-start(bf16[12,8,256]{2,1,0:T(8,128)(2,1)S(1)} %get-tuple-element.187.refs_0_), channel_id=1, source_target_pairs={{0,8},{1,9},{2,10},{3,11},{4,12},{5,13},{6,14},{7,15},{8,0},{9,1},... | collective-permute-start | bytes 147464 | tf_op jit(solution)/shard_map/ppermute | solution.py:280
  84.2 1.5 %collective-permute-start.49 = (bf16[12,8,256]{2,1,0:T(8,128)(2,1)S(1)}, bf16[12,8,256]{2,1,0:T(8,128)(2,1)S(1)}, u32[]{:S(2)}, u32[]{:S(2)}) collective-permute-start(bf16[12,8,256]{2,1,0:T(8,128)(2,1)S(1)} %get-tuple-element.187.refs_0_), channel_id=1, source_target_pairs={{0,12},{1,13},{2,14},{3,15},{4,8},{5,9},{6,10},{7,11},{8,4},{9,5},... | collective-permute-start | bytes 147464 | tf_op jit(solution)/shard_map/ppermute | solution.py:280
  87.7 2.4 %collective-permute-done.49.refs_0_ = bf16[12,8,256]{2,1,0:T(8,128)(2,1)S(1)} collective-permute-done((bf16[12,8,256]{2,1,0:T(8,128)(2,1)S(1)}, bf16[12,8,256]{2,1,0:T(8,128)(2,1)S(1)}, u32[]{:S(2)}, u32[]{:S(2)}) %collective-permute-start.49) | collective-permute-done | bytes 49184 | tf_op jit(solution)/shard_map/ppermute | solution.py:280
  102.2 1.5 %collective-permute-start.60 = (bf16[12,8,256]{2,1,0:T(8,128)(2,1)S(1)}, bf16[12,8,256]{2,1,0:T(8,128)(2,1)S(1)}, u32[]{:S(2)}, u32[]{:S(2)}) collective-permute-start(bf16[12,8,256]{2,1,0:T(8,128)(2,1)S(1)} %get-tuple-element.208), channel_id=1, source_target_pairs={{0,12},{1,13},{2,14},{3,15},{4,8},{5,9},{6,10},{7,11},{8,4},{9,5},... | collective-permute-start | bytes 147464 | tf_op jit(solution)/shard_map/ppermute | solution.py:280
  105.4 1.4 %collective-permute-start.62 = (bf16[12,8,256]{2,1,0:T(8,128)(2,1)S(1)}, bf16[12,8,256]{2,1,0:T(8,128)(2,1)S(1)}, u32[]{:S(2)}, u32[]{:S(2)}) collective-permute-start(bf16[12,8,256]{2,1,0:T(8,128)(2,1)S(1)} %get-tuple-element.210), channel_id=1, source_target_pairs={{0,4},{1,5},{2,6},{3,7},{4,0},{5,1},{6,2},{7,3},{8,12},{9,13},{10,... | collective-permute-start | bytes 147464 | tf_op jit(solution)/shard_map/ppermute | solution.py:280
  106.8 1.8 %collective-permute-done.60.refs_1_ = bf16[12,8,256]{2,1,0:T(8,128)(2,1)S(1)} collective-permute-done((bf16[12,8,256]{2,1,0:T(8,128)(2,1)S(1)}, bf16[12,8,256]{2,1,0:T(8,128)(2,1)S(1)}, u32[]{:S(2)}, u32[]{:S(2)}) %collective-permute-start.60) | collective-permute-done | bytes 49184 | tf_op jit(solution)/shard_map/ppermute | solution.py:280
  108.7 1.5 %collective-permute-done.61.refs_2_ = bf16[12,8,256]{2,1,0:T(8,128)(2,1)S(1)} collective-permute-done((bf16[12,8,256]{2,1,0:T(8,128)(2,1)S(1)}, bf16[12,8,256]{2,1,0:T(8,128)(2,1)S(1)}, u32[]{:S(2)}, u32[]{:S(2)}) %collective-permute-start.61) | collective-permute-done | bytes 49184 | tf_op jit(solution)/shard_map/ppermute | solution.py:280
  111.7 1.6 %collective-permute-start.68 = (bf16[12,8,256]{2,1,0:T(8,128)(2,1)S(1)}, bf16[12,8,256]{2,1,0:T(8,128)(2,1)S(1)}, u32[]{:S(2)}, u32[]{:S(2)}) collective-permute-start(bf16[12,8,256]{2,1,0:T(8,128)(2,1)S(1)} %get-tuple-element.214.refs_0_), channel_id=1, source_target_pairs={{0,8},{1,9},{2,10},{3,11},{4,12},{5,13},{6,14},{7,15},{8,0},{9,1},... | collective-permute-start | bytes 147464 | tf_op jit(solution)/shard_map/ppermute | solution.py:280
  113.3 2.3 %collective-permute-start.67 = (bf16[12,8,256]{2,1,0:T(8,128)(2,1)S(1)}, bf16[12,8,256]{2,1,0:T(8,128)(2,1)S(1)}, u32[]{:S(2)}, u32[]{:S(2)}) collective-permute-start(bf16[12,8,256]{2,1,0:T(8,128)(2,1)S(1)} %get-tuple-element.214.refs_0_), channel_id=1, source_target_pairs={{0,12},{1,13},{2,14},{3,15},{4,8},{5,9},{6,10},{7,11},{8,4},{9,5},... | collective-permute-start | bytes 147464 | tf_op jit(solution)/shard_map/ppermute | solution.py:280
  117.6 1.6 %collective-permute-done.67.refs_0_ = bf16[12,8,256]{2,1,0:T(8,128)(2,1)S(1)} collective-permute-done((bf16[12,8,256]{2,1,0:T(8,128)(2,1)S(1)}, bf16[12,8,256]{2,1,0:T(8,128)(2,1)S(1)}, u32[]{:S(2)}, u32[]{:S(2)}) %collective-permute-start.67) | collective-permute-done | bytes 49184 | tf_op jit(solution)/shard_map/ppermute | solution.py:280
  (172 shorter events, 68.6 us)
Async XLA Ops:
  7.2 6.2 %collective-permute-start = (bf16[13,8,256]{2,1,0:T(8,128)(2,1)S(1)}, bf16[13,8,256]{2,1,0:T(8,128)(2,1)S(1)}, u32[]{:S(2)}, u32[]{:S(2)}) collective-permute-start(bf16[13,8,256]{2,1,0:T(8,128)(2,1)S(1)} %get-tuple-element.117), channel_id=1, source_target_pairs={{0,1},{1,0},{2,3},{3,2},{4,5},{5,4},{6,7},{7,6},{8,9},{9,8},{10,11... | collective-permute-start | bytes 159752 | tf_op jit(solution)/shard_map/ppermute | solution.py:280
  7.7 5.7 %collective-permute-start.1 = (bf16[13,8,256]{2,1,0:T(8,128)(2,1)S(1)}, bf16[13,8,256]{2,1,0:T(8,128)(2,1)S(1)}, u32[]{:S(2)}, u32[]{:S(2)}) collective-permute-start(bf16[13,8,256]{2,1,0:T(8,128)(2,1)S(1)} %get-tuple-element.118), channel_id=1, source_target_pairs={{0,2},{1,3},{2,0},{3,1},{4,6},{5,7},{6,4},{7,5},{8,10},{9,11},{10,... | collective-permute-start | bytes 159752 | tf_op jit(solution)/shard_map/ppermute | solution.py:280
  11.3 7.3 %collective-permute-start.3 = (bf16[12,8,256]{2,1,0:T(8,128)(2,1)S(1)}, bf16[12,8,256]{2,1,0:T(8,128)(2,1)S(1)}, u32[]{:S(2)}, u32[]{:S(2)}) collective-permute-start(bf16[12,8,256]{2,1,0:T(8,128)(2,1)S(1)} %get-tuple-element.124), channel_id=1, source_target_pairs={{0,1},{1,0},{2,3},{3,2},{4,5},{5,4},{6,7},{7,6},{8,9},{9,8},{10,11... | collective-permute-start | bytes 147464 | tf_op jit(solution)/shard_map/ppermute | solution.py:280
  11.4 7.1 %collective-permute-start.4 = (bf16[12,8,256]{2,1,0:T(8,128)(2,1)S(1)}, bf16[12,8,256]{2,1,0:T(8,128)(2,1)S(1)}, u32[]{:S(2)}, u32[]{:S(2)}) collective-permute-start(bf16[12,8,256]{2,1,0:T(8,128)(2,1)S(1)} %get-tuple-element.125), channel_id=1, source_target_pairs={{0,2},{1,3},{2,0},{3,1},{4,6},{5,7},{6,4},{7,5},{8,10},{9,11},{10,... | collective-permute-start | bytes 147464 | tf_op jit(solution)/shard_map/ppermute | solution.py:280
  14.9 8.4 %collective-permute-start.6 = (bf16[12,8,256]{2,1,0:T(8,128)(2,1)S(1)}, bf16[12,8,256]{2,1,0:T(8,128)(2,1)S(1)}, u32[]{:S(2)}, u32[]{:S(2)}) collective-permute-start(bf16[12,8,256]{2,1,0:T(8,128)(2,1)S(1)} %get-tuple-element.128), channel_id=1, source_target_pairs={{0,12},{1,13},{2,14},{3,15},{4,8},{5,9},{6,10},{7,11},{8,4},{9,5},... | collective-permute-start | bytes 147464 | tf_op jit(solution)/shard_map/ppermute | solution.py:280
  24.8 5.8 %collective-permute-start.14 = (bf16[12,8,256]{2,1,0:T(8,128)(2,1)S(1)}, bf16[12,8,256]{2,1,0:T(8,128)(2,1)S(1)}, u32[]{:S(2)}, u32[]{:S(2)}) collective-permute-start(bf16[12,8,256]{2,1,0:T(8,128)(2,1)S(1)} %get-tuple-element.135.refs_0_), channel_id=1, source_target_pairs={{0,8},{1,9},{2,10},{3,11},{4,12},{5,13},{6,14},{7,15},{8,0},{9,1},... | collective-permute-start | bytes 147464 | tf_op jit(solution)/shard_map/ppermute | solution.py:280
  27.7 5.9 %collective-permute-start.13 = (bf16[12,8,256]{2,1,0:T(8,128)(2,1)S(1)}, bf16[12,8,256]{2,1,0:T(8,128)(2,1)S(1)}, u32[]{:S(2)}, u32[]{:S(2)}) collective-permute-start(bf16[12,8,256]{2,1,0:T(8,128)(2,1)S(1)} %get-tuple-element.135.refs_0_), channel_id=1, source_target_pairs={{0,12},{1,13},{2,14},{3,15},{4,8},{5,9},{6,10},{7,11},{8,4},{9,5},... | collective-permute-start | bytes 147464 | tf_op jit(solution)/shard_map/ppermute | solution.py:280
  28.6 6.3 %collective-permute-start.10 = (bf16[12,8,256]{2,1,0:T(8,128)(2,1)S(1)}, bf16[12,8,256]{2,1,0:T(8,128)(2,1)S(1)}, u32[]{:S(2)}, u32[]{:S(2)}) collective-permute-start(bf16[12,8,256]{2,1,0:T(8,128)(2,1)S(1)} %get-tuple-element.137), channel_id=1, source_target_pairs={{0,1},{1,0},{2,3},{3,2},{4,5},{5,4},{6,7},{7,6},{8,9},{9,8},{10,11... | collective-permute-start | bytes 147464 | tf_op jit(solution)/shard_map/ppermute | solution.py:280
  28.7 6.9 %collective-permute-start.11 = (bf16[12,8,256]{2,1,0:T(8,128)(2,1)S(1)}, bf16[12,8,256]{2,1,0:T(8,128)(2,1)S(1)}, u32[]{:S(2)}, u32[]{:S(2)}) collective-permute-start(bf16[12,8,256]{2,1,0:T(8,128)(2,1)S(1)} %get-tuple-element.138), channel_id=1, source_target_pairs={{0,2},{1,3},{2,0},{3,1},{4,6},{5,7},{6,4},{7,5},{8,10},{9,11},{10,... | collective-permute-start | bytes 147464 | tf_op jit(solution)/shard_map/ppermute | solution.py:280
  29.9 5.7 %collective-permute-start.12 = (bf16[12,8,256]{2,1,0:T(8,128)(2,1)S(1)}, bf16[12,8,256]{2,1,0:T(8,128)(2,1)S(1)}, u32[]{:S(2)}, u32[]{:S(2)}) collective-permute-start(bf16[12,8,256]{2,1,0:T(8,128)(2,1)S(1)} %get-tuple-element.139), channel_id=1, source_target_pairs={{0,3},{1,2},{2,1},{3,0},{4,7},{5,6},{6,5},{7,4},{8,11},{9,10},{10,... | collective-permute-start | bytes 147464 | tf_op jit(solution)/shard_map/ppermute | solution.py:280
  45.3 6.6 %collective-permute-start.24 = (bf16[12,8,256]{2,1,0:T(8,128)(2,1)S(1)}, bf16[12,8,256]{2,1,0:T(8,128)(2,1)S(1)}, u32[]{:S(2)}, u32[]{:S(2)}) collective-permute-start(bf16[12,8,256]{2,1,0:T(8,128)(2,1)S(1)} %get-tuple-element.156), channel_id=1, source_target_pairs={{0,12},{1,13},{2,14},{3,15},{4,8},{5,9},{6,10},{7,11},{8,4},{9,5},... | collective-permute-start | bytes 147464 | tf_op jit(solution)/shard_map/ppermute | solution.py:280
  46.1 6.7 %collective-permute-start.25 = (bf16[12,8,256]{2,1,0:T(8,128)(2,1)S(1)}, bf16[12,8,256]{2,1,0:T(8,128)(2,1)S(1)}, u32[]{:S(2)}, u32[]{:S(2)}) collective-permute-start(bf16[12,8,256]{2,1,0:T(8,128)(2,1)S(1)} %get-tuple-element.157), channel_id=1, source_target_pairs={{0,8},{1,9},{2,10},{3,11},{4,12},{5,13},{6,14},{7,15},{8,0},{9,1},... | collective-permute-start | bytes 147464 | tf_op jit(solution)/shard_map/ppermute | solution.py:280
  54.1 5.5 %collective-permute-start.32 = (bf16[12,8,256]{2,1,0:T(8,128)(2,1)S(1)}, bf16[12,8,256]{2,1,0:T(8,128)(2,1)S(1)}, u32[]{:S(2)}, u32[]{:S(2)}) collective-permute-start(bf16[12,8,256]{2,1,0:T(8,128)(2,1)S(1)} %get-tuple-element.161.refs_0_), channel_id=1, source_target_pairs={{0,8},{1,9},{2,10},{3,11},{4,12},{5,13},{6,14},{7,15},{8,0},{9,1},... | collective-permute-start | bytes 147464 | tf_op jit(solution)/shard_map/ppermute | solution.py:280
  55.2 5.9 %collective-permute-start.31 = (bf16[12,8,256]{2,1,0:T(8,128)(2,1)S(1)}, bf16[12,8,256]{2,1,0:T(8,128)(2,1)S(1)}, u32[]{:S(2)}, u32[]{:S(2)}) collective-permute-start(bf16[12,8,256]{2,1,0:T(8,128)(2,1)S(1)} %get-tuple-element.161.refs_0_), channel_id=1, source_target_pairs={{0,12},{1,13},{2,14},{3,15},{4,8},{5,9},{6,10},{7,11},{8,4},{9,5},... | collective-permute-start | bytes 147464 | tf_op jit(solution)/shard_map/ppermute | solution.py:280
  72.8 6.4 %collective-permute-start.42 = (bf16[12,8,256]{2,1,0:T(8,128)(2,1)S(1)}, bf16[12,8,256]{2,1,0:T(8,128)(2,1)S(1)}, u32[]{:S(2)}, u32[]{:S(2)}) collective-permute-start(bf16[12,8,256]{2,1,0:T(8,128)(2,1)S(1)} %get-tuple-element.182), channel_id=1, source_target_pairs={{0,12},{1,13},{2,14},{3,15},{4,8},{5,9},{6,10},{7,11},{8,4},{9,5},... | collective-permute-start | bytes 147464 | tf_op jit(solution)/shard_map/ppermute | solution.py:280
  75.3 5.6 %collective-permute-start.43 = (bf16[12,8,256]{2,1,0:T(8,128)(2,1)S(1)}, bf16[12,8,256]{2,1,0:T(8,128)(2,1)S(1)}, u32[]{:S(2)}, u32[]{:S(2)}) collective-permute-start(bf16[12,8,256]{2,1,0:T(8,128)(2,1)S(1)} %get-tuple-element.183), channel_id=1, source_target_pairs={{0,8},{1,9},{2,10},{3,11},{4,12},{5,13},{6,14},{7,15},{8,0},{9,1},... | collective-permute-start | bytes 147464 | tf_op jit(solution)/shard_map/ppermute | solution.py:280
  81.7 6.0 %collective-permute-start.50 = (bf16[12,8,256]{2,1,0:T(8,128)(2,1)S(1)}, bf16[12,8,256]{2,1,0:T(8,128)(2,1)S(1)}, u32[]{:S(2)}, u32[]{:S(2)}) collective-permute-start(bf16[12,8,256]{2,1,0:T(8,128)(2,1)S(1)} %get-tuple-element.187.refs_0_), channel_id=1, source_target_pairs={{0,8},{1,9},{2,10},{3,11},{4,12},{5,13},{6,14},{7,15},{8,0},{9,1},... | collective-permute-start | bytes 147464 | tf_op jit(solution)/shard_map/ppermute | solution.py:280
  84.2 5.9 %collective-permute-start.49 = (bf16[12,8,256]{2,1,0:T(8,128)(2,1)S(1)}, bf16[12,8,256]{2,1,0:T(8,128)(2,1)S(1)}, u32[]{:S(2)}, u32[]{:S(2)}) collective-permute-start(bf16[12,8,256]{2,1,0:T(8,128)(2,1)S(1)} %get-tuple-element.187.refs_0_), channel_id=1, source_target_pairs={{0,12},{1,13},{2,14},{3,15},{4,8},{5,9},{6,10},{7,11},{8,4},{9,5},... | collective-permute-start | bytes 147464 | tf_op jit(solution)/shard_map/ppermute | solution.py:280
  85.7 5.7 %collective-permute-start.46 = (bf16[12,8,256]{2,1,0:T(8,128)(2,1)S(1)}, bf16[12,8,256]{2,1,0:T(8,128)(2,1)S(1)}, u32[]{:S(2)}, u32[]{:S(2)}) collective-permute-start(bf16[12,8,256]{2,1,0:T(8,128)(2,1)S(1)} %get-tuple-element.189), channel_id=1, source_target_pairs={{0,1},{1,0},{2,3},{3,2},{4,5},{5,4},{6,7},{7,6},{8,9},{9,8},{10,11... | collective-permute-start | bytes 147464 | tf_op jit(solution)/shard_map/ppermute | solution.py:280
  85.8 6.3 %collective-permute-start.47 = (bf16[12,8,256]{2,1,0:T(8,128)(2,1)S(1)}, bf16[12,8,256]{2,1,0:T(8,128)(2,1)S(1)}, u32[]{:S(2)}, u32[]{:S(2)}) collective-permute-start(bf16[12,8,256]{2,1,0:T(8,128)(2,1)S(1)} %get-tuple-element.190), channel_id=1, source_target_pairs={{0,2},{1,3},{2,0},{3,1},{4,6},{5,7},{6,4},{7,5},{8,10},{9,11},{10,... | collective-permute-start | bytes 147464 | tf_op jit(solution)/shard_map/ppermute | solution.py:280
  102.2 6.5 %collective-permute-start.60 = (bf16[12,8,256]{2,1,0:T(8,128)(2,1)S(1)}, bf16[12,8,256]{2,1,0:T(8,128)(2,1)S(1)}, u32[]{:S(2)}, u32[]{:S(2)}) collective-permute-start(bf16[12,8,256]{2,1,0:T(8,128)(2,1)S(1)} %get-tuple-element.208), channel_id=1, source_target_pairs={{0,12},{1,13},{2,14},{3,15},{4,8},{5,9},{6,10},{7,11},{8,4},{9,5},... | collective-permute-start | bytes 147464 | tf_op jit(solution)/shard_map/ppermute | solution.py:280
  103.7 6.5 %collective-permute-start.61 = (bf16[12,8,256]{2,1,0:T(8,128)(2,1)S(1)}, bf16[12,8,256]{2,1,0:T(8,128)(2,1)S(1)}, u32[]{:S(2)}, u32[]{:S(2)}) collective-permute-start(bf16[12,8,256]{2,1,0:T(8,128)(2,1)S(1)} %get-tuple-element.209), channel_id=1, source_target_pairs={{0,8},{1,9},{2,10},{3,11},{4,12},{5,13},{6,14},{7,15},{8,0},{9,1},... | collective-permute-start | bytes 147464 | tf_op jit(solution)/shard_map/ppermute | solution.py:280
  111.7 5.9 %collective-permute-start.68 = (bf16[12,8,256]{2,1,0:T(8,128)(2,1)S(1)}, bf16[12,8,256]{2,1,0:T(8,128)(2,1)S(1)}, u32[]{:S(2)}, u32[]{:S(2)}) collective-permute-start(bf16[12,8,256]{2,1,0:T(8,128)(2,1)S(1)} %get-tuple-element.214.refs_0_), channel_id=1, source_target_pairs={{0,8},{1,9},{2,10},{3,11},{4,12},{5,13},{6,14},{7,15},{8,0},{9,1},... | collective-permute-start | bytes 147464 | tf_op jit(solution)/shard_map/ppermute | solution.py:280
  113.3 5.9 %collective-permute-start.67 = (bf16[12,8,256]{2,1,0:T(8,128)(2,1)S(1)}, bf16[12,8,256]{2,1,0:T(8,128)(2,1)S(1)}, u32[]{:S(2)}, u32[]{:S(2)}) collective-permute-start(bf16[12,8,256]{2,1,0:T(8,128)(2,1)S(1)} %get-tuple-element.214.refs_0_), channel_id=1, source_target_pairs={{0,12},{1,13},{2,14},{3,15},{4,8},{5,9},{6,10},{7,11},{8,4},{9,5},... | collective-permute-start | bytes 147464 | tf_op jit(solution)/shard_map/ppermute | solution.py:280
  (53 other events, 223.0 us)

commit v9 on v8

--- a/solution.py
+++ b/solution.py
@@ -126,7 +126,7 @@
     scaled_blocks(side, dy, dual_step, hb, h_into)
     chart.wait()
     for out in (o0, o1, o2, o3):
-        out[half * cap] = plan[...].astype(BF16)
+        out[half * cap, :, pl.ds(0, plan.shape[1])] = plan[...].astype(BF16)
     for c in range(chunks):
         tile_copy(c).wait()
     transpose_products(0, tile_of, row_of, held, hb, (o0, o1, o2, o3))
@@ -148,7 +148,7 @@
 def map_kernel(a0, a1, a2, a3, wants, whole, sem):
     for x, part in enumerate((a0, a1, a2, a3)):
         plan = part[part.shape[0] - 1].astype(F32)
-        whole[pl.ds(x, 1)] = plan[x:x + 1].astype(I32)
+        whole[pl.ds(x, 1)] = plan[x:x + 1, :whole.shape[1]].astype(I32)
     whole[pl.ds(QUAD, QUAD)] = jnp.zeros((QUAD, whole.shape[1]), I32)
     copy = pltpu.make_async_copy(whole, wants, sem)
     copy.start()
@@ -251,6 +251,7 @@
     group = peers // QUAD
     half = group // 2
     slots = peers * cap
+    places = -(-group * cap // 128) * 128
     steps = primal_mask.shape[0]
     dual_step = dual_step.reshape(1, -1)
     primal_step = primal_step.reshape(1, -1)
@@ -293,7 +294,7 @@
         scratch_shapes=[
             pltpu.SMEM((tile_slots,), I32), pltpu.SMEM((tile_slots,), I32), pltpu.VMEM(dual_step.shape, F32),
             pltpu.VMEM(cot_y.shape, I32), pltpu.VMEM(cot_y.shape, F32), pltpu.SMEM((peers,), I32),
-            pltpu.SMEM((2 * QUAD, side), I32), pltpu.VMEM((2 * QUAD, side), I32),
+            pltpu.SMEM((2 * QUAD, places), I32), pltpu.VMEM((2 * QUAD, places), I32),
             pltpu.SemaphoreType.DMA((tile_slots // CHUNK,)), pltpu.SemaphoreType.DMA((6,)),
         ],
         compiler_params=PARAMS,
@@ -314,16 +315,16 @@
         if wants is None:
             wants = pl.pallas_call(
                 map_kernel,
-                out_shape=pltpu.SMEM((2 * QUAD, side), I32),
+                out_shape=pltpu.SMEM((2 * QUAD, places), I32),
                 in_specs=[VM] * QUAD,
                 out_specs=SM,
-                scratch_shapes=[pltpu.VMEM((2 * QUAD, side), I32), pltpu.SemaphoreType.DMA],
+                scratch_shapes=[pltpu.VMEM((2 * QUAD, places), I32), pltpu.SemaphoreType.DMA],
                 compiler_params=PARAMS,
                 name="maps",
             )(*far_got)
         far_sums = call(functools.partial(sum_kernel, half, cap), "far_sum", 1 << 20, [SM] + [VM] * QUAD,
                         (block_set,) * half, (wants, *far_got), col_totals)
-        got = [swap(far_sums[h], (half + h) * QUAD) for h in reversed(range(half))]
+        got = [swap(far_sums[h], (half + h) * QUAD) for h in range(half)]
         near_sums = call(functools.partial(sum_kernel, 0, cap), "near_sum", 1 << 20, [SM] + [VM] * QUAD,
                          (shape(block_set.shape, F32),) + (block_set,) * (half - 1), (wants, *near_got), col_totals)
         got += [swap(near_sums[h], h * QUAD) for h in range(1, half)]

time: 126 us -> 123 us (0.976)
    ppermute x72, starting transfers between devices: 64.4 us -> 63.2 us  [swap(): return lax.ppermute(array, 'rb', [(p, p ^ x) for p in range(peers)])]
  transfers between devices with their start and end apart: 72 -> 72, of which waited for: 30 -> 31; matrix products, arithmetic and copies ran while one was open for 0% -> 0% of each run, Pallas kernels for 14% -> 15%
where the time goes in v9:
time: 123 us
  starting transfers between devices  63.2 us (51%)
  waiting for transfers between devices  29.6 us (24%)
  Pallas kernels  28.7 us (23%)
  between operations  1.71 us (1%)
    ppermute x72, starting transfers between devices, swap(): return lax.ppermute(array, 'rb', [(p, p ^ x) for p in range(peers)])  63.2 us
    ppermute x72, waiting for transfers between devices, swap(): return lax.ppermute(array, 'rb', [(p, p ^ x) for p in range(peers)])  29.6 us
    pallas_call x40, Pallas kernels, call(): pl.pallas_call(kernel, out_shape=outs, in_specs=ins, out_specs=jax.tree.m...  22.3 us
    pallas_call x1, Pallas kernels, on_device(): pl.pallas_call(functools.partial(start_kernel, step, peers, cap, col_bloc...  5.8 us
  transfers between devices with their start and end apart: 72, of which 31 were waited for; matrix products, arithmetic and copies ran while one was open for 0% of the time, Pallas kernels for 15%

profile of v9, /device:TPU:0, one launch (start us, length us, event | category | flops | bytes accessed | tf_op | source)
XLA Modules:
  0.0 123.2 jit_solution(7339372198248693835)
XLA Ops:
  1.3 5.8 %start.1 = (bf16[88,256,256]{2,1,0:T(8,128)(2,1)S(1)}, f32[8,2048]{1,0:T(8,128)S(1)}, f32[8,2048]{1,0:T(8,128)S(1)}, bf16[8,8,256]{2,1,0:T(8,128)(2,1)S(1)}, s32...) custom-call(s32[1]{0:T(128)S(6)} %copy.14.count, ...), custom_call_target="tpu_custom_call" | custom-call | flops 184549376 | bytes 23068672 | tf_op jit(solution)/shard_map/start/pallas_call | solution.py:287
  7.6 2.6 %collective-permute-start.1 = (bf16[13,8,256]{2,1,0:T(8,128)(2,1)S(1)}, bf16[13,8,256]{2,1,0:T(8,128)(2,1)S(1)}, u32[]{:S(2)}, u32[]{:S(2)}) collective-permute-start(bf16[13,8,256]{2,1,0:T(8,128)(2,1)S(1)} %get-tuple-element.118), channel_id=1, source_target_pairs={{0,2},{1,3},{2,0},{3,1},{4,6},{5,7},{6,4},{7,5},{8,10},{9,11},{10,... | collective-permute-start | bytes 159752 | tf_op jit(solution)/shard_map/ppermute | solution.py:281
  11.3 1.9 %collective-permute-start.4 = (bf16[12,8,256]{2,1,0:T(8,128)(2,1)S(1)}, bf16[12,8,256]{2,1,0:T(8,128)(2,1)S(1)}, u32[]{:S(2)}, u32[]{:S(2)}) collective-permute-start(bf16[12,8,256]{2,1,0:T(8,128)(2,1)S(1)} %get-tuple-element.125), channel_id=1, source_target_pairs={{0,2},{1,3},{2,0},{3,1},{4,6},{5,7},{6,4},{7,5},{8,10},{9,11},{10,... | collective-permute-start | bytes 147464 | tf_op jit(solution)/shard_map/ppermute | solution.py:281
  14.7 2.6 %collective-permute-start.6 = (bf16[12,8,256]{2,1,0:T(8,128)(2,1)S(1)}, bf16[12,8,256]{2,1,0:T(8,128)(2,1)S(1)}, u32[]{:S(2)}, u32[]{:S(2)}) collective-permute-start(bf16[12,8,256]{2,1,0:T(8,128)(2,1)S(1)} %get-tuple-element.128), channel_id=1, source_target_pairs={{0,8},{1,9},{2,10},{3,11},{4,12},{5,13},{6,14},{7,15},{8,0},{9,1},... | collective-permute-start | bytes 147464 | tf_op jit(solution)/shard_map/ppermute | solution.py:281
  17.4 1.3 %collective-permute-start.7 = (bf16[12,8,256]{2,1,0:T(8,128)(2,1)S(1)}, bf16[12,8,256]{2,1,0:T(8,128)(2,1)S(1)}, u32[]{:S(2)}, u32[]{:S(2)}) collective-permute-start(bf16[12,8,256]{2,1,0:T(8,128)(2,1)S(1)} %get-tuple-element.129), channel_id=1, source_target_pairs={{0,12},{1,13},{2,14},{3,15},{4,8},{5,9},{6,10},{7,11},{8,4},{9,5},... | collective-permute-start | bytes 147464 | tf_op jit(solution)/shard_map/ppermute | solution.py:281
  19.2 3.7 %turn.1.turned = bf16[88,256,256]{2,1,0:T(8,128)(2,1)S(1)} custom-call(bf16[88,256,256]{2,1,0:T(8,128)(2,1)S(1)} %get-tuple-element.114.held), custom_call_target="tpu_custom_call" | custom-call | flops 92274688 | bytes 11534336 | tf_op jit(solution)/shard_map/turn/pallas_call | solution.py:269
  24.9 1.9 %collective-permute-start.14 = (bf16[12,8,256]{2,1,0:T(8,128)(2,1)S(1)}, bf16[12,8,256]{2,1,0:T(8,128)(2,1)S(1)}, u32[]{:S(2)}, u32[]{:S(2)}) collective-permute-start(bf16[12,8,256]{2,1,0:T(8,128)(2,1)S(1)} %get-tuple-element.135.refs_0_), channel_id=1, source_target_pairs={{0,8},{1,9},{2,10},{3,11},{4,12},{5,13},{6,14},{7,15},{8,0},{9,1},... | collective-permute-start | bytes 147464 | tf_op jit(solution)/shard_map/ppermute | solution.py:281
  30.5 2.3 %collective-permute-done.13.refs_0_ = bf16[12,8,256]{2,1,0:T(8,128)(2,1)S(1)} collective-permute-done((bf16[12,8,256]{2,1,0:T(8,128)(2,1)S(1)}, bf16[12,8,256]{2,1,0:T(8,128)(2,1)S(1)}, u32[]{:S(2)}, u32[]{:S(2)}) %collective-permute-start.13) | collective-permute-done | bytes 49184 | tf_op jit(solution)/shard_map/ppermute | solution.py:281
  32.9 1.3 %collective-permute-start.16 = (bf16[12,8,256]{2,1,0:T(8,128)(2,1)S(1)}, bf16[12,8,256]{2,1,0:T(8,128)(2,1)S(1)}, u32[]{:S(2)}, u32[]{:S(2)}) collective-permute-start(bf16[12,8,256]{2,1,0:T(8,128)(2,1)S(1)} %get-tuple-element.144), channel_id=1, source_target_pairs={{0,2},{1,3},{2,0},{3,1},{4,6},{5,7},{6,4},{7,5},{8,10},{9,11},{10,... | collective-permute-start | bytes 147464 | tf_op jit(solution)/shard_map/ppermute | solution.py:281
  48.4 2.3 %collective-permute-done.24.refs_1_ = bf16[12,8,256]{2,1,0:T(8,128)(2,1)S(1)} collective-permute-done((bf16[12,8,256]{2,1,0:T(8,128)(2,1)S(1)}, bf16[12,8,256]{2,1,0:T(8,128)(2,1)S(1)}, u32[]{:S(2)}, u32[]{:S(2)}) %collective-permute-start.24) | collective-permute-done | bytes 49184 | tf_op jit(solution)/shard_map/ppermute | solution.py:281
  52.6 2.0 %collective-permute-start.32 = (bf16[12,8,256]{2,1,0:T(8,128)(2,1)S(1)}, bf16[12,8,256]{2,1,0:T(8,128)(2,1)S(1)}, u32[]{:S(2)}, u32[]{:S(2)}) collective-permute-start(bf16[12,8,256]{2,1,0:T(8,128)(2,1)S(1)} %get-tuple-element.161.refs_0_), channel_id=1, source_target_pairs={{0,8},{1,9},{2,10},{3,11},{4,12},{5,13},{6,14},{7,15},{8,0},{9,1},... | collective-permute-start | bytes 147464 | tf_op jit(solution)/shard_map/ppermute | solution.py:281
  54.6 2.0 %collective-permute-start.31 = (bf16[12,8,256]{2,1,0:T(8,128)(2,1)S(1)}, bf16[12,8,256]{2,1,0:T(8,128)(2,1)S(1)}, u32[]{:S(2)}, u32[]{:S(2)}) collective-permute-start(bf16[12,8,256]{2,1,0:T(8,128)(2,1)S(1)} %get-tuple-element.161.refs_0_), channel_id=1, source_target_pairs={{0,12},{1,13},{2,14},{3,15},{4,8},{5,9},{6,10},{7,11},{8,4},{9,5},... | collective-permute-start | bytes 147464 | tf_op jit(solution)/shard_map/ppermute | solution.py:281
  58.7 1.8 %collective-permute-done.31.refs_0_ = bf16[12,8,256]{2,1,0:T(8,128)(2,1)S(1)} collective-permute-done((bf16[12,8,256]{2,1,0:T(8,128)(2,1)S(1)}, bf16[12,8,256]{2,1,0:T(8,128)(2,1)S(1)}, u32[]{:S(2)}, u32[]{:S(2)}) %collective-permute-start.31) | collective-permute-done | bytes 49184 | tf_op jit(solution)/shard_map/ppermute | solution.py:281
  72.4 2.0 %collective-permute-start.43 = (bf16[12,8,256]{2,1,0:T(8,128)(2,1)S(1)}, bf16[12,8,256]{2,1,0:T(8,128)(2,1)S(1)}, u32[]{:S(2)}, u32[]{:S(2)}) collective-permute-start(bf16[12,8,256]{2,1,0:T(8,128)(2,1)S(1)} %get-tuple-element.183), channel_id=1, source_target_pairs={{0,12},{1,13},{2,14},{3,15},{4,8},{5,9},{6,10},{7,11},{8,4},{9,5},... | collective-permute-start | bytes 147464 | tf_op jit(solution)/shard_map/ppermute | solution.py:281
  76.0 2.9 %collective-permute-done.42.refs_1_ = bf16[12,8,256]{2,1,0:T(8,128)(2,1)S(1)} collective-permute-done((bf16[12,8,256]{2,1,0:T(8,128)(2,1)S(1)}, bf16[12,8,256]{2,1,0:T(8,128)(2,1)S(1)}, u32[]{:S(2)}, u32[]{:S(2)}) %collective-permute-start.42) | collective-permute-done | bytes 49184 | tf_op jit(solution)/shard_map/ppermute | solution.py:281
  80.4 1.9 %collective-permute-start.50 = (bf16[12,8,256]{2,1,0:T(8,128)(2,1)S(1)}, bf16[12,8,256]{2,1,0:T(8,128)(2,1)S(1)}, u32[]{:S(2)}, u32[]{:S(2)}) collective-permute-start(bf16[12,8,256]{2,1,0:T(8,128)(2,1)S(1)} %get-tuple-element.187.refs_0_), channel_id=1, source_target_pairs={{0,8},{1,9},{2,10},{3,11},{4,12},{5,13},{6,14},{7,15},{8,0},{9,1},... | collective-permute-start | bytes 147464 | tf_op jit(solution)/shard_map/ppermute | solution.py:281
  82.3 1.9 %collective-permute-start.49 = (bf16[12,8,256]{2,1,0:T(8,128)(2,1)S(1)}, bf16[12,8,256]{2,1,0:T(8,128)(2,1)S(1)}, u32[]{:S(2)}, u32[]{:S(2)}) collective-permute-start(bf16[12,8,256]{2,1,0:T(8,128)(2,1)S(1)} %get-tuple-element.187.refs_0_), channel_id=1, source_target_pairs={{0,12},{1,13},{2,14},{3,15},{4,8},{5,9},{6,10},{7,11},{8,4},{9,5},... | collective-permute-start | bytes 147464 | tf_op jit(solution)/shard_map/ppermute | solution.py:281
  86.7 1.5 %collective-permute-done.49.refs_0_ = bf16[12,8,256]{2,1,0:T(8,128)(2,1)S(1)} collective-permute-done((bf16[12,8,256]{2,1,0:T(8,128)(2,1)S(1)}, bf16[12,8,256]{2,1,0:T(8,128)(2,1)S(1)}, u32[]{:S(2)}, u32[]{:S(2)}) %collective-permute-start.49) | collective-permute-done | bytes 49184 | tf_op jit(solution)/shard_map/ppermute | solution.py:281
  88.4 1.3 %collective-permute-start.52 = (bf16[12,8,256]{2,1,0:T(8,128)(2,1)S(1)}, bf16[12,8,256]{2,1,0:T(8,128)(2,1)S(1)}, u32[]{:S(2)}, u32[]{:S(2)}) collective-permute-start(bf16[12,8,256]{2,1,0:T(8,128)(2,1)S(1)} %get-tuple-element.196), channel_id=1, source_target_pairs={{0,2},{1,3},{2,0},{3,1},{4,6},{5,7},{6,4},{7,5},{8,10},{9,11},{10,... | collective-permute-start | bytes 147464 | tf_op jit(solution)/shard_map/ppermute | solution.py:281
  100.8 1.8 %collective-permute-start.61 = (bf16[12,8,256]{2,1,0:T(8,128)(2,1)S(1)}, bf16[12,8,256]{2,1,0:T(8,128)(2,1)S(1)}, u32[]{:S(2)}, u32[]{:S(2)}) collective-permute-start(bf16[12,8,256]{2,1,0:T(8,128)(2,1)S(1)} %get-tuple-element.209), channel_id=1, source_target_pairs={{0,12},{1,13},{2,14},{3,15},{4,8},{5,9},{6,10},{7,11},{8,4},{9,5},... | collective-permute-start | bytes 147464 | tf_op jit(solution)/shard_map/ppermute | solution.py:281
  104.2 2.9 %collective-permute-done.60.refs_1_ = bf16[12,8,256]{2,1,0:T(8,128)(2,1)S(1)} collective-permute-done((bf16[12,8,256]{2,1,0:T(8,128)(2,1)S(1)}, bf16[12,8,256]{2,1,0:T(8,128)(2,1)S(1)}, u32[]{:S(2)}, u32[]{:S(2)}) %collective-permute-start.60) | collective-permute-done | bytes 49184 | tf_op jit(solution)/shard_map/ppermute | solution.py:281
  109.1 2.0 %collective-permute-start.68 = (bf16[12,8,256]{2,1,0:T(8,128)(2,1)S(1)}, bf16[12,8,256]{2,1,0:T(8,128)(2,1)S(1)}, u32[]{:S(2)}, u32[]{:S(2)}) collective-permute-start(bf16[12,8,256]{2,1,0:T(8,128)(2,1)S(1)} %get-tuple-element.214.refs_0_), channel_id=1, source_target_pairs={{0,8},{1,9},{2,10},{3,11},{4,12},{5,13},{6,14},{7,15},{8,0},{9,1},... | collective-permute-start | bytes 147464 | tf_op jit(solution)/shard_map/ppermute | solution.py:281
  111.1 1.9 %collective-permute-start.67 = (bf16[12,8,256]{2,1,0:T(8,128)(2,1)S(1)}, bf16[12,8,256]{2,1,0:T(8,128)(2,1)S(1)}, u32[]{:S(2)}, u32[]{:S(2)}) collective-permute-start(bf16[12,8,256]{2,1,0:T(8,128)(2,1)S(1)} %get-tuple-element.214.refs_0_), channel_id=1, source_target_pairs={{0,12},{1,13},{2,14},{3,15},{4,8},{5,9},{6,10},{7,11},{8,4},{9,5},... | collective-permute-start | bytes 147464 | tf_op jit(solution)/shard_map/ppermute | solution.py:281
  115.2 1.8 %collective-permute-done.67.refs_0_ = bf16[12,8,256]{2,1,0:T(8,128)(2,1)S(1)} collective-permute-done((bf16[12,8,256]{2,1,0:T(8,128)(2,1)S(1)}, bf16[12,8,256]{2,1,0:T(8,128)(2,1)S(1)}, u32[]{:S(2)}, u32[]{:S(2)}) %collective-permute-start.67) | collective-permute-done | bytes 49184 | tf_op jit(solution)/shard_map/ppermute | solution.py:281
  (172 shorter events, 67.8 us)
Async XLA Ops:
  7.1 6.2 %collective-permute-start = (bf16[13,8,256]{2,1,0:T(8,128)(2,1)S(1)}, bf16[13,8,256]{2,1,0:T(8,128)(2,1)S(1)}, u32[]{:S(2)}, u32[]{:S(2)}) collective-permute-start(bf16[13,8,256]{2,1,0:T(8,128)(2,1)S(1)} %get-tuple-element.117), channel_id=1, source_target_pairs={{0,1},{1,0},{2,3},{3,2},{4,5},{5,4},{6,7},{7,6},{8,9},{9,8},{10,11... | collective-permute-start | bytes 159752 | tf_op jit(solution)/shard_map/ppermute | solution.py:281
  7.6 5.7 %collective-permute-start.1 = (bf16[13,8,256]{2,1,0:T(8,128)(2,1)S(1)}, bf16[13,8,256]{2,1,0:T(8,128)(2,1)S(1)}, u32[]{:S(2)}, u32[]{:S(2)}) collective-permute-start(bf16[13,8,256]{2,1,0:T(8,128)(2,1)S(1)} %get-tuple-element.118), channel_id=1, source_target_pairs={{0,2},{1,3},{2,0},{3,1},{4,6},{5,7},{6,4},{7,5},{8,10},{9,11},{10,... | collective-permute-start | bytes 159752 | tf_op jit(solution)/shard_map/ppermute | solution.py:281
  11.2 7.5 %collective-permute-start.3 = (bf16[12,8,256]{2,1,0:T(8,128)(2,1)S(1)}, bf16[12,8,256]{2,1,0:T(8,128)(2,1)S(1)}, u32[]{:S(2)}, u32[]{:S(2)}) collective-permute-start(bf16[12,8,256]{2,1,0:T(8,128)(2,1)S(1)} %get-tuple-element.124), channel_id=1, source_target_pairs={{0,1},{1,0},{2,3},{3,2},{4,5},{5,4},{6,7},{7,6},{8,9},{9,8},{10,11... | collective-permute-start | bytes 147464 | tf_op jit(solution)/shard_map/ppermute | solution.py:281
  11.3 7.4 %collective-permute-start.4 = (bf16[12,8,256]{2,1,0:T(8,128)(2,1)S(1)}, bf16[12,8,256]{2,1,0:T(8,128)(2,1)S(1)}, u32[]{:S(2)}, u32[]{:S(2)}) collective-permute-start(bf16[12,8,256]{2,1,0:T(8,128)(2,1)S(1)} %get-tuple-element.125), channel_id=1, source_target_pairs={{0,2},{1,3},{2,0},{3,1},{4,6},{5,7},{6,4},{7,5},{8,10},{9,11},{10,... | collective-permute-start | bytes 147464 | tf_op jit(solution)/shard_map/ppermute | solution.py:281
  14.7 8.2 %collective-permute-start.6 = (bf16[12,8,256]{2,1,0:T(8,128)(2,1)S(1)}, bf16[12,8,256]{2,1,0:T(8,128)(2,1)S(1)}, u32[]{:S(2)}, u32[]{:S(2)}) collective-permute-start(bf16[12,8,256]{2,1,0:T(8,128)(2,1)S(1)} %get-tuple-element.128), channel_id=1, source_target_pairs={{0,8},{1,9},{2,10},{3,11},{4,12},{5,13},{6,14},{7,15},{8,0},{9,1},... | collective-permute-start | bytes 147464 | tf_op jit(solution)/shard_map/ppermute | solution.py:281
  17.4 6.0 %collective-permute-start.7 = (bf16[12,8,256]{2,1,0:T(8,128)(2,1)S(1)}, bf16[12,8,256]{2,1,0:T(8,128)(2,1)S(1)}, u32[]{:S(2)}, u32[]{:S(2)}) collective-permute-start(bf16[12,8,256]{2,1,0:T(8,128)(2,1)S(1)} %get-tuple-element.129), channel_id=1, source_target_pairs={{0,12},{1,13},{2,14},{3,15},{4,8},{5,9},{6,10},{7,11},{8,4},{9,5},... | collective-permute-start | bytes 147464 | tf_op jit(solution)/shard_map/ppermute | solution.py:281
  26.9 5.9 %collective-permute-start.13 = (bf16[12,8,256]{2,1,0:T(8,128)(2,1)S(1)}, bf16[12,8,256]{2,1,0:T(8,128)(2,1)S(1)}, u32[]{:S(2)}, u32[]{:S(2)}) collective-permute-start(bf16[12,8,256]{2,1,0:T(8,128)(2,1)S(1)} %get-tuple-element.135.refs_0_), channel_id=1, source_target_pairs={{0,12},{1,13},{2,14},{3,15},{4,8},{5,9},{6,10},{7,11},{8,4},{9,5},... | collective-permute-start | bytes 147464 | tf_op jit(solution)/shard_map/ppermute | solution.py:281
  28.4 5.8 %collective-permute-start.10 = (bf16[12,8,256]{2,1,0:T(8,128)(2,1)S(1)}, bf16[12,8,256]{2,1,0:T(8,128)(2,1)S(1)}, u32[]{:S(2)}, u32[]{:S(2)}) collective-permute-start(bf16[12,8,256]{2,1,0:T(8,128)(2,1)S(1)} %get-tuple-element.137), channel_id=1, source_target_pairs={{0,1},{1,0},{2,3},{3,2},{4,5},{5,4},{6,7},{7,6},{8,9},{9,8},{10,11... | collective-permute-start | bytes 147464 | tf_op jit(solution)/shard_map/ppermute | solution.py:281
  28.5 6.3 %collective-permute-start.11 = (bf16[12,8,256]{2,1,0:T(8,128)(2,1)S(1)}, bf16[12,8,256]{2,1,0:T(8,128)(2,1)S(1)}, u32[]{:S(2)}, u32[]{:S(2)}) collective-permute-start(bf16[12,8,256]{2,1,0:T(8,128)(2,1)S(1)} %get-tuple-element.138), channel_id=1, source_target_pairs={{0,2},{1,3},{2,0},{3,1},{4,6},{5,7},{6,4},{7,5},{8,10},{9,11},{10,... | collective-permute-start | bytes 147464 | tf_op jit(solution)/shard_map/ppermute | solution.py:281
  44.6 6.1 %collective-permute-start.24 = (bf16[12,8,256]{2,1,0:T(8,128)(2,1)S(1)}, bf16[12,8,256]{2,1,0:T(8,128)(2,1)S(1)}, u32[]{:S(2)}, u32[]{:S(2)}) collective-permute-start(bf16[12,8,256]{2,1,0:T(8,128)(2,1)S(1)} %get-tuple-element.156), channel_id=1, source_target_pairs={{0,8},{1,9},{2,10},{3,11},{4,12},{5,13},{6,14},{7,15},{8,0},{9,1},... | collective-permute-start | bytes 147464 | tf_op jit(solution)/shard_map/ppermute | solution.py:281
  45.3 6.4 %collective-permute-start.25 = (bf16[12,8,256]{2,1,0:T(8,128)(2,1)S(1)}, bf16[12,8,256]{2,1,0:T(8,128)(2,1)S(1)}, u32[]{:S(2)}, u32[]{:S(2)}) collective-permute-start(bf16[12,8,256]{2,1,0:T(8,128)(2,1)S(1)} %get-tuple-element.157), channel_id=1, source_target_pairs={{0,12},{1,13},{2,14},{3,15},{4,8},{5,9},{6,10},{7,11},{8,4},{9,5},... | collective-permute-start | bytes 147464 | tf_op jit(solution)/shard_map/ppermute | solution.py:281
  52.6 6.1 %collective-permute-start.32 = (bf16[12,8,256]{2,1,0:T(8,128)(2,1)S(1)}, bf16[12,8,256]{2,1,0:T(8,128)(2,1)S(1)}, u32[]{:S(2)}, u32[]{:S(2)}) collective-permute-start(bf16[12,8,256]{2,1,0:T(8,128)(2,1)S(1)} %get-tuple-element.161.refs_0_), channel_id=1, source_target_pairs={{0,8},{1,9},{2,10},{3,11},{4,12},{5,13},{6,14},{7,15},{8,0},{9,1},... | collective-permute-start | bytes 147464 | tf_op jit(solution)/shard_map/ppermute | solution.py:281
  54.6 5.9 %collective-permute-start.31 = (bf16[12,8,256]{2,1,0:T(8,128)(2,1)S(1)}, bf16[12,8,256]{2,1,0:T(8,128)(2,1)S(1)}, u32[]{:S(2)}, u32[]{:S(2)}) collective-permute-start(bf16[12,8,256]{2,1,0:T(8,128)(2,1)S(1)} %get-tuple-element.161.refs_0_), channel_id=1, source_target_pairs={{0,12},{1,13},{2,14},{3,15},{4,8},{5,9},{6,10},{7,11},{8,4},{9,5},... | collective-permute-start | bytes 147464 | tf_op jit(solution)/shard_map/ppermute | solution.py:281
  56.8 5.7 %collective-permute-start.29 = (bf16[12,8,256]{2,1,0:T(8,128)(2,1)S(1)}, bf16[12,8,256]{2,1,0:T(8,128)(2,1)S(1)}, u32[]{:S(2)}, u32[]{:S(2)}) collective-permute-start(bf16[12,8,256]{2,1,0:T(8,128)(2,1)S(1)} %get-tuple-element.164), channel_id=1, source_target_pairs={{0,2},{1,3},{2,0},{3,1},{4,6},{5,7},{6,4},{7,5},{8,10},{9,11},{10,... | collective-permute-start | bytes 147464 | tf_op jit(solution)/shard_map/ppermute | solution.py:281
  72.3 6.6 %collective-permute-start.42 = (bf16[12,8,256]{2,1,0:T(8,128)(2,1)S(1)}, bf16[12,8,256]{2,1,0:T(8,128)(2,1)S(1)}, u32[]{:S(2)}, u32[]{:S(2)}) collective-permute-start(bf16[12,8,256]{2,1,0:T(8,128)(2,1)S(1)} %get-tuple-element.182), channel_id=1, source_target_pairs={{0,8},{1,9},{2,10},{3,11},{4,12},{5,13},{6,14},{7,15},{8,0},{9,1},... | collective-permute-start | bytes 147464 | tf_op jit(solution)/shard_map/ppermute | solution.py:281
  72.4 6.5 %collective-permute-start.43 = (bf16[12,8,256]{2,1,0:T(8,128)(2,1)S(1)}, bf16[12,8,256]{2,1,0:T(8,128)(2,1)S(1)}, u32[]{:S(2)}, u32[]{:S(2)}) collective-permute-start(bf16[12,8,256]{2,1,0:T(8,128)(2,1)S(1)} %get-tuple-element.183), channel_id=1, source_target_pairs={{0,12},{1,13},{2,14},{3,15},{4,8},{5,9},{6,10},{7,11},{8,4},{9,5},... | collective-permute-start | bytes 147464 | tf_op jit(solution)/shard_map/ppermute | solution.py:281
  80.4 6.3 %collective-permute-start.50 = (bf16[12,8,256]{2,1,0:T(8,128)(2,1)S(1)}, bf16[12,8,256]{2,1,0:T(8,128)(2,1)S(1)}, u32[]{:S(2)}, u32[]{:S(2)}) collective-permute-start(bf16[12,8,256]{2,1,0:T(8,128)(2,1)S(1)} %get-tuple-element.187.refs_0_), channel_id=1, source_target_pairs={{0,8},{1,9},{2,10},{3,11},{4,12},{5,13},{6,14},{7,15},{8,0},{9,1},... | collective-permute-start | bytes 147464 | tf_op jit(solution)/shard_map/ppermute | solution.py:281
  82.3 5.9 %collective-permute-start.49 = (bf16[12,8,256]{2,1,0:T(8,128)(2,1)S(1)}, bf16[12,8,256]{2,1,0:T(8,128)(2,1)S(1)}, u32[]{:S(2)}, u32[]{:S(2)}) collective-permute-start(bf16[12,8,256]{2,1,0:T(8,128)(2,1)S(1)} %get-tuple-element.187.refs_0_), channel_id=1, source_target_pairs={{0,12},{1,13},{2,14},{3,15},{4,8},{5,9},{6,10},{7,11},{8,4},{9,5},... | collective-permute-start | bytes 147464 | tf_op jit(solution)/shard_map/ppermute | solution.py:281
  84.6 5.6 %collective-permute-start.47 = (bf16[12,8,256]{2,1,0:T(8,128)(2,1)S(1)}, bf16[12,8,256]{2,1,0:T(8,128)(2,1)S(1)}, u32[]{:S(2)}, u32[]{:S(2)}) collective-permute-start(bf16[12,8,256]{2,1,0:T(8,128)(2,1)S(1)} %get-tuple-element.190), channel_id=1, source_target_pairs={{0,2},{1,3},{2,0},{3,1},{4,6},{5,7},{6,4},{7,5},{8,10},{9,11},{10,... | collective-permute-start | bytes 147464 | tf_op jit(solution)/shard_map/ppermute | solution.py:281
  100.5 6.6 %collective-permute-start.60 = (bf16[12,8,256]{2,1,0:T(8,128)(2,1)S(1)}, bf16[12,8,256]{2,1,0:T(8,128)(2,1)S(1)}, u32[]{:S(2)}, u32[]{:S(2)}) collective-permute-start(bf16[12,8,256]{2,1,0:T(8,128)(2,1)S(1)} %get-tuple-element.208), channel_id=1, source_target_pairs={{0,8},{1,9},{2,10},{3,11},{4,12},{5,13},{6,14},{7,15},{8,0},{9,1},... | collective-permute-start | bytes 147464 | tf_op jit(solution)/shard_map/ppermute | solution.py:281
  100.8 6.3 %collective-permute-start.61 = (bf16[12,8,256]{2,1,0:T(8,128)(2,1)S(1)}, bf16[12,8,256]{2,1,0:T(8,128)(2,1)S(1)}, u32[]{:S(2)}, u32[]{:S(2)}) collective-permute-start(bf16[12,8,256]{2,1,0:T(8,128)(2,1)S(1)} %get-tuple-element.209), channel_id=1, source_target_pairs={{0,12},{1,13},{2,14},{3,15},{4,8},{5,9},{6,10},{7,11},{8,4},{9,5},... | collective-permute-start | bytes 147464 | tf_op jit(solution)/shard_map/ppermute | solution.py:281
  109.1 6.1 %collective-permute-start.68 = (bf16[12,8,256]{2,1,0:T(8,128)(2,1)S(1)}, bf16[12,8,256]{2,1,0:T(8,128)(2,1)S(1)}, u32[]{:S(2)}, u32[]{:S(2)}) collective-permute-start(bf16[12,8,256]{2,1,0:T(8,128)(2,1)S(1)} %get-tuple-element.214.refs_0_), channel_id=1, source_target_pairs={{0,8},{1,9},{2,10},{3,11},{4,12},{5,13},{6,14},{7,15},{8,0},{9,1},... | collective-permute-start | bytes 147464 | tf_op jit(solution)/shard_map/ppermute | solution.py:281
  111.1 5.9 %collective-permute-start.67 = (bf16[12,8,256]{2,1,0:T(8,128)(2,1)S(1)}, bf16[12,8,256]{2,1,0:T(8,128)(2,1)S(1)}, u32[]{:S(2)}, u32[]{:S(2)}) collective-permute-start(bf16[12,8,256]{2,1,0:T(8,128)(2,1)S(1)} %get-tuple-element.214.refs_0_), channel_id=1, source_target_pairs={{0,12},{1,13},{2,14},{3,15},{4,8},{5,9},{6,10},{7,11},{8,4},{9,5},... | collective-permute-start | bytes 147464 | tf_op jit(solution)/shard_map/ppermute | solution.py:281
  113.3 5.7 %collective-permute-start.65 = (bf16[12,8,256]{2,1,0:T(8,128)(2,1)S(1)}, bf16[12,8,256]{2,1,0:T(8,128)(2,1)S(1)}, u32[]{:S(2)}, u32[]{:S(2)}) collective-permute-start(bf16[12,8,256]{2,1,0:T(8,128)(2,1)S(1)} %get-tuple-element.217), channel_id=1, source_target_pairs={{0,2},{1,3},{2,0},{3,1},{4,6},{5,7},{6,4},{7,5},{8,10},{9,11},{10,... | collective-permute-start | bytes 147464 | tf_op jit(solution)/shard_map/ppermute | solution.py:281
  (53 other events, 222.8 us)

commit v10 on v9

--- a/solution.py
+++ b/solution.py
@@ -25,12 +25,13 @@
     return pl.CostEstimate(flops=moved * 8, bytes_accessed=moved, transcendentals=0)
 
 
-def scaled_blocks(side, dy, dual_step, hb, h_into):
+def scaled_blocks(side, dy, dual_step, hb, h_into=None):
     for r in range(hb.shape[0]):
         at = pl.ds(r * side, side)
         h = dual_step[:, at] * dy[:, at]
         hb[r] = h.astype(BF16)
-        h_into(at, h)
+        if h_into is not None:
+            h_into(at, h)
 
 
 def transpose_products(base, tile_of, row_of, tiles, hb, outs, xs=range(QUAD)):
@@ -177,8 +178,8 @@
             out[c] = (totals[2 * h][c] + totals[2 * h + 1][c]).astype(out.dtype)
 
 
-def primal_kernel(step, first, primal_mask, primal_step, x, spent, *refs):
-    parts, (new_x, new_spent, out) = refs[:-3], refs[-3:]
+def primal_kernel(step, primal_mask, primal_step, x, *refs):
+    parts, (u_out, dx_out, out) = refs[:-3], refs[-3:]
     blocks, _, side = out.shape
     for c in range(blocks):
         at = pl.ds(c * side, side)
@@ -186,10 +187,19 @@
         for part in parts[1:]:
             u = u + part[c].astype(F32)
         dx = primal_mask[step, :, at].astype(F32) * (x[:, at] + 2.0 * u)
-        q = primal_step[:, at] * dx
-        new_x[:, at] = dx - u
-        new_spent[:, at] = -q if first else spent[:, at] - q
-        out[c] = q.astype(BF16)
+        u_out[:, at] = u
+        dx_out[:, at] = dx
+        out[c] = (primal_step[:, at] * dx).astype(BF16)
+
+
+def settle_kernel(first, primal_step, u, dx, spent, new_x, new_spent):
+    new_x[...] = dx[...] - u[...]
+    q = primal_step[...] * dx[...]
+    new_spent[...] = -q if first else spent[...] - q
+
+
+def settle_dual_kernel(dual_step, dy, rhs, new_rhs):
+    new_rhs[...] = rhs[...] - dual_step[...] * dy[...]
 
 
 def pick_kernel(highs, cap, wants, *refs):
@@ -217,8 +227,8 @@
     transpose_products(0, tile_of, row_of, held, hb, (o3, o1, o0), (3, 1, 0))
 
 
-def middle_kernel(step, tile_of, row_of, land_of, held, turned, dual_step, dual_mask, part, dy, rhs, m2, m3,
-                  new_dy, new_rhs, hb, o2, *totals):
+def middle_kernel(step, tile_of, row_of, land_of, held, turned, dual_step, dual_mask, part, dy, m2, m3,
+                  new_dy, hb, o2, *totals):
     side = held.shape[1]
     forward_products(0, tile_of, land_of, turned, (m2, m3), totals, (2, 3))
     for r in range(hb.shape[0]):
@@ -226,10 +236,7 @@
         v = part[r] + gathered(totals, r)
         new_dy[:, at] = dual_mask[step, :, at].astype(F32) * (dy[:, at] - v)
 
-    def h_into(at, h):
-        new_rhs[:, at] = rhs[:, at] - h
-
-    scaled_blocks(side, new_dy, dual_step, hb, h_into)
+    scaled_blocks(side, new_dy, dual_step, hb)
     transpose_products(0, tile_of, row_of, held, hb, (o2,), (2,))
 
 
@@ -330,9 +337,11 @@
         got += [swap(near_sums[h], h * QUAD) for h in range(1, half)]
         if step == steps - 1:
             turned, x_state = lax.optimization_barrier((turned, x_state))
-        x_state, spent, moved = call(
-            functools.partial(primal_kernel, step, step == steps - 1), "primal", 1 << 20, [VM] * (4 + group),
-            (x_shape, x_shape, block_set), (primal_mask, primal_step, x_state, spent, near_sums[0], *got))
+        u, dx, moved = call(
+            functools.partial(primal_kernel, step), "primal", 1 << 20, [VM] * (3 + group),
+            (x_shape, x_shape, block_set), (primal_mask, primal_step, x_state, near_sums[0], *got))
+        x_state, spent = call(functools.partial(settle_kernel, step == steps - 1), "settle", 1 << 20, [VM] * 4,
+                              (x_shape, x_shape), (primal_step, u, dx, spent))
         blocks = [moved] + [swap(moved, h * QUAD) for h in range(1, group)]
         near_moved, far_moved = (
             near_swaps(call(functools.partial(pick_kernel, highs, cap), name, 1 << 20, [SM] + [VM] * half, part_set,
@@ -346,10 +355,11 @@
         if step == 0:
             break
         step -= 1
-        dy, rhs, hb, across = call(
-            functools.partial(middle_kernel, step), "middle", tile_bytes // 2, [SM] * 3 + [VM] * 9,
-            (y_shape, y_shape, hb_set, part_set[0]),
-            (tile_of, row_of, land_of, held, turned, dual_step, dual_mask, part, dy, rhs, *far_moved[2:]), row_totals)
+        dy, hb, across = call(
+            functools.partial(middle_kernel, step), "middle", tile_bytes // 2, [SM] * 3 + [VM] * 8,
+            (y_shape, hb_set, part_set[0]),
+            (tile_of, row_of, land_of, held, turned, dual_step, dual_mask, part, dy, *far_moved[2:]), row_totals)
+        rhs = call(settle_dual_kernel, "settle_dual", 1 << 20, [VM] * 3, y_shape, (dual_step, dy, rhs))
         own, beside, aslant = call(rest_product_kernel, "rest_product", tile_bytes // 4, [SM] * 2 + [VM] * 2,
                                    part_set[:3], (tile_of, row_of, held, hb))
         far_parts = [own, beside, across, aslant]

time: 123 us -> 122 us (level)
  waiting for transfers between devices: 29.6 us -> 28.1 us
    ppermute x72, waiting for transfers between devices: 29.6 us -> 28.1 us  [swap(): return lax.ppermute(array, 'rb', [(p, p ^ x) for p in range(peers)])]
    pallas_call x40 -> x47, Pallas kernels: 22.3 us -> 22.6 us  [call(): pl.pallas_call(kernel, out_shape=outs, in_specs=ins, out_specs=jax.tree.m...]
  transfers between devices with their start and end apart: 72 -> 72, of which waited for: 31 -> 29; matrix products, arithmetic and copies ran while one was open for 0% -> 0% of each run, Pallas kernels for 15% -> 16%
where the time goes in v10:
time: 122 us
  starting transfers between devices  63.2 us (52%)
  Pallas kernels  29 us (24%)
  waiting for transfers between devices  28.1 us (23%)
  between operations  1.75 us (1%)
    ppermute x72, starting transfers between devices, swap(): return lax.ppermute(array, 'rb', [(p, p ^ x) for p in range(peers)])  63.2 us
    ppermute x72, waiting for transfers between devices, swap(): return lax.ppermute(array, 'rb', [(p, p ^ x) for p in range(peers)])  28.1 us
    pallas_call x47, Pallas kernels, call(): pl.pallas_call(kernel, out_shape=outs, in_specs=ins, out_specs=jax.tree.m...  22.6 us
    pallas_call x1, Pallas kernels, on_device(): pl.pallas_call(functools.partial(start_kernel, step, peers, cap, col_bloc...  5.8 us
  transfers between devices with their start and end apart: 72, of which 29 were waited for; matrix products, arithmetic and copies ran while one was open for 0% of the time, Pallas kernels for 16%

profile of v10, /device:TPU:0, one launch (start us, length us, event | category | flops | bytes accessed | tf_op | source)
XLA Modules:
  0.0 122.1 jit_solution(15129174385268805887)
XLA Ops:
  1.3 5.8 %start.1 = (bf16[88,256,256]{2,1,0:T(8,128)(2,1)S(1)}, f32[8,2048]{1,0:T(8,128)S(1)}, f32[8,2048]{1,0:T(8,128)S(1)}, bf16[8,8,256]{2,1,0:T(8,128)(2,1)S(1)}, s32...) custom-call(s32[1]{0:T(128)S(6)} %copy.14.count, ...), custom_call_target="tpu_custom_call" | custom-call | flops 184549376 | bytes 23068672 | tf_op jit(solution)/shard_map/start/pallas_call | solution.py:294
  7.6 2.6 %collective-permute-start.1 = (bf16[13,8,256]{2,1,0:T(8,128)(2,1)S(1)}, bf16[13,8,256]{2,1,0:T(8,128)(2,1)S(1)}, u32[]{:S(2)}, u32[]{:S(2)}) collective-permute-start(bf16[13,8,256]{2,1,0:T(8,128)(2,1)S(1)} %get-tuple-element.123), channel_id=1, source_target_pairs={{0,2},{1,3},{2,0},{3,1},{4,6},{5,7},{6,4},{7,5},{8,10},{9,11},{10,... | collective-permute-start | bytes 159752 | tf_op jit(solution)/shard_map/ppermute | solution.py:288
  11.3 1.9 %collective-permute-start.4 = (bf16[12,8,256]{2,1,0:T(8,128)(2,1)S(1)}, bf16[12,8,256]{2,1,0:T(8,128)(2,1)S(1)}, u32[]{:S(2)}, u32[]{:S(2)}) collective-permute-start(bf16[12,8,256]{2,1,0:T(8,128)(2,1)S(1)} %get-tuple-element.130), channel_id=1, source_target_pairs={{0,2},{1,3},{2,0},{3,1},{4,6},{5,7},{6,4},{7,5},{8,10},{9,11},{10,... | collective-permute-start | bytes 147464 | tf_op jit(solution)/shard_map/ppermute | solution.py:288
  14.7 2.6 %collective-permute-start.6 = (bf16[12,8,256]{2,1,0:T(8,128)(2,1)S(1)}, bf16[12,8,256]{2,1,0:T(8,128)(2,1)S(1)}, u32[]{:S(2)}, u32[]{:S(2)}) collective-permute-start(bf16[12,8,256]{2,1,0:T(8,128)(2,1)S(1)} %get-tuple-element.133), channel_id=1, source_target_pairs={{0,8},{1,9},{2,10},{3,11},{4,12},{5,13},{6,14},{7,15},{8,0},{9,1},... | collective-permute-start | bytes 147464 | tf_op jit(solution)/shard_map/ppermute | solution.py:288
  17.4 1.3 %collective-permute-start.7 = (bf16[12,8,256]{2,1,0:T(8,128)(2,1)S(1)}, bf16[12,8,256]{2,1,0:T(8,128)(2,1)S(1)}, u32[]{:S(2)}, u32[]{:S(2)}) collective-permute-start(bf16[12,8,256]{2,1,0:T(8,128)(2,1)S(1)} %get-tuple-element.134), channel_id=1, source_target_pairs={{0,12},{1,13},{2,14},{3,15},{4,8},{5,9},{6,10},{7,11},{8,4},{9,5},... | collective-permute-start | bytes 147464 | tf_op jit(solution)/shard_map/ppermute | solution.py:288
  19.2 3.7 %turn.1.turned = bf16[88,256,256]{2,1,0:T(8,128)(2,1)S(1)} custom-call(bf16[88,256,256]{2,1,0:T(8,128)(2,1)S(1)} %get-tuple-element.119.held), custom_call_target="tpu_custom_call" | custom-call | flops 92274688 | bytes 11534336 | tf_op jit(solution)/shard_map/turn/pallas_call | solution.py:276
  24.9 1.9 %collective-permute-start.14 = (bf16[12,8,256]{2,1,0:T(8,128)(2,1)S(1)}, bf16[12,8,256]{2,1,0:T(8,128)(2,1)S(1)}, u32[]{:S(2)}, u32[]{:S(2)}) collective-permute-start(bf16[12,8,256]{2,1,0:T(8,128)(2,1)S(1)} %get-tuple-element.141.refs_0_), channel_id=1, source_target_pairs={{0,8},{1,9},{2,10},{3,11},{4,12},{5,13},{6,14},{7,15},{8,0},{9,1},... | collective-permute-start | bytes 147464 | tf_op jit(solution)/shard_map/ppermute | solution.py:288
  30.6 2.2 %collective-permute-done.13.refs_0_ = bf16[12,8,256]{2,1,0:T(8,128)(2,1)S(1)} collective-permute-done((bf16[12,8,256]{2,1,0:T(8,128)(2,1)S(1)}, bf16[12,8,256]{2,1,0:T(8,128)(2,1)S(1)}, u32[]{:S(2)}, u32[]{:S(2)}) %collective-permute-start.13) | collective-permute-done | bytes 49184 | tf_op jit(solution)/shard_map/ppermute | solution.py:288
  32.9 1.3 %collective-permute-start.16 = (bf16[12,8,256]{2,1,0:T(8,128)(2,1)S(1)}, bf16[12,8,256]{2,1,0:T(8,128)(2,1)S(1)}, u32[]{:S(2)}, u32[]{:S(2)}) collective-permute-start(bf16[12,8,256]{2,1,0:T(8,128)(2,1)S(1)} %get-tuple-element.149), channel_id=1, source_target_pairs={{0,2},{1,3},{2,0},{3,1},{4,6},{5,7},{6,4},{7,5},{8,10},{9,11},{10,... | collective-permute-start | bytes 147464 | tf_op jit(solution)/shard_map/ppermute | solution.py:288
  48.4 2.3 %collective-permute-done.24.refs_1_ = bf16[12,8,256]{2,1,0:T(8,128)(2,1)S(1)} collective-permute-done((bf16[12,8,256]{2,1,0:T(8,128)(2,1)S(1)}, bf16[12,8,256]{2,1,0:T(8,128)(2,1)S(1)}, u32[]{:S(2)}, u32[]{:S(2)}) %collective-permute-start.24) | collective-permute-done | bytes 49184 | tf_op jit(solution)/shard_map/ppermute | solution.py:288
  52.6 2.0 %collective-permute-start.32 = (bf16[12,8,256]{2,1,0:T(8,128)(2,1)S(1)}, bf16[12,8,256]{2,1,0:T(8,128)(2,1)S(1)}, u32[]{:S(2)}, u32[]{:S(2)}) collective-permute-start(bf16[12,8,256]{2,1,0:T(8,128)(2,1)S(1)} %get-tuple-element.168.refs_0_), channel_id=1, source_target_pairs={{0,8},{1,9},{2,10},{3,11},{4,12},{5,13},{6,14},{7,15},{8,0},{9,1},... | collective-permute-start | bytes 147464 | tf_op jit(solution)/shard_map/ppermute | solution.py:288
  54.6 2.0 %collective-permute-start.31 = (bf16[12,8,256]{2,1,0:T(8,128)(2,1)S(1)}, bf16[12,8,256]{2,1,0:T(8,128)(2,1)S(1)}, u32[]{:S(2)}, u32[]{:S(2)}) collective-permute-start(bf16[12,8,256]{2,1,0:T(8,128)(2,1)S(1)} %get-tuple-element.168.refs_0_), channel_id=1, source_target_pairs={{0,12},{1,13},{2,14},{3,15},{4,8},{5,9},{6,10},{7,11},{8,4},{9,5},... | collective-permute-start | bytes 147464 | tf_op jit(solution)/shard_map/ppermute | solution.py:288
  58.7 1.8 %collective-permute-done.31.refs_0_ = bf16[12,8,256]{2,1,0:T(8,128)(2,1)S(1)} collective-permute-done((bf16[12,8,256]{2,1,0:T(8,128)(2,1)S(1)}, bf16[12,8,256]{2,1,0:T(8,128)(2,1)S(1)}, u32[]{:S(2)}, u32[]{:S(2)}) %collective-permute-start.31) | collective-permute-done | bytes 49184 | tf_op jit(solution)/shard_map/ppermute | solution.py:288
  60.6 1.3 %collective-permute-start.34 = (bf16[12,8,256]{2,1,0:T(8,128)(2,1)S(1)}, bf16[12,8,256]{2,1,0:T(8,128)(2,1)S(1)}, u32[]{:S(2)}, u32[]{:S(2)}) collective-permute-start(bf16[12,8,256]{2,1,0:T(8,128)(2,1)S(1)} %get-tuple-element.176), channel_id=1, source_target_pairs={{0,2},{1,3},{2,0},{3,1},{4,6},{5,7},{6,4},{7,5},{8,10},{9,11},{10,... | collective-permute-start | bytes 147464 | tf_op jit(solution)/shard_map/ppermute | solution.py:288
  72.4 2.0 %collective-permute-start.43 = (bf16[12,8,256]{2,1,0:T(8,128)(2,1)S(1)}, bf16[12,8,256]{2,1,0:T(8,128)(2,1)S(1)}, u32[]{:S(2)}, u32[]{:S(2)}) collective-permute-start(bf16[12,8,256]{2,1,0:T(8,128)(2,1)S(1)} %get-tuple-element.189), channel_id=1, source_target_pairs={{0,12},{1,13},{2,14},{3,15},{4,8},{5,9},{6,10},{7,11},{8,4},{9,5},... | collective-permute-start | bytes 147464 | tf_op jit(solution)/shard_map/ppermute | solution.py:288
  76.1 2.8 %collective-permute-done.42.refs_1_ = bf16[12,8,256]{2,1,0:T(8,128)(2,1)S(1)} collective-permute-done((bf16[12,8,256]{2,1,0:T(8,128)(2,1)S(1)}, bf16[12,8,256]{2,1,0:T(8,128)(2,1)S(1)}, u32[]{:S(2)}, u32[]{:S(2)}) %collective-permute-start.42) | collective-permute-done | bytes 49184 | tf_op jit(solution)/shard_map/ppermute | solution.py:288
  80.4 1.9 %collective-permute-start.50 = (bf16[12,8,256]{2,1,0:T(8,128)(2,1)S(1)}, bf16[12,8,256]{2,1,0:T(8,128)(2,1)S(1)}, u32[]{:S(2)}, u32[]{:S(2)}) collective-permute-start(bf16[12,8,256]{2,1,0:T(8,128)(2,1)S(1)} %get-tuple-element.195.refs_0_), channel_id=1, source_target_pairs={{0,8},{1,9},{2,10},{3,11},{4,12},{5,13},{6,14},{7,15},{8,0},{9,1},... | collective-permute-start | bytes 147464 | tf_op jit(solution)/shard_map/ppermute | solution.py:288
  82.3 1.9 %collective-permute-start.49 = (bf16[12,8,256]{2,1,0:T(8,128)(2,1)S(1)}, bf16[12,8,256]{2,1,0:T(8,128)(2,1)S(1)}, u32[]{:S(2)}, u32[]{:S(2)}) collective-permute-start(bf16[12,8,256]{2,1,0:T(8,128)(2,1)S(1)} %get-tuple-element.195.refs_0_), channel_id=1, source_target_pairs={{0,12},{1,13},{2,14},{3,15},{4,8},{5,9},{6,10},{7,11},{8,4},{9,5},... | collective-permute-start | bytes 147464 | tf_op jit(solution)/shard_map/ppermute | solution.py:288
  86.4 1.8 %collective-permute-done.49.refs_0_ = bf16[12,8,256]{2,1,0:T(8,128)(2,1)S(1)} collective-permute-done((bf16[12,8,256]{2,1,0:T(8,128)(2,1)S(1)}, bf16[12,8,256]{2,1,0:T(8,128)(2,1)S(1)}, u32[]{:S(2)}, u32[]{:S(2)}) %collective-permute-start.49) | collective-permute-done | bytes 49184 | tf_op jit(solution)/shard_map/ppermute | solution.py:288
  100.3 1.8 %collective-permute-start.61 = (bf16[12,8,256]{2,1,0:T(8,128)(2,1)S(1)}, bf16[12,8,256]{2,1,0:T(8,128)(2,1)S(1)}, u32[]{:S(2)}, u32[]{:S(2)}) collective-permute-start(bf16[12,8,256]{2,1,0:T(8,128)(2,1)S(1)} %get-tuple-element.216), channel_id=1, source_target_pairs={{0,12},{1,13},{2,14},{3,15},{4,8},{5,9},{6,10},{7,11},{8,4},{9,5},... | collective-permute-start | bytes 147464 | tf_op jit(solution)/shard_map/ppermute | solution.py:288
  103.8 2.8 %collective-permute-done.60.refs_1_ = bf16[12,8,256]{2,1,0:T(8,128)(2,1)S(1)} collective-permute-done((bf16[12,8,256]{2,1,0:T(8,128)(2,1)S(1)}, bf16[12,8,256]{2,1,0:T(8,128)(2,1)S(1)}, u32[]{:S(2)}, u32[]{:S(2)}) %collective-permute-start.60) | collective-permute-done | bytes 49184 | tf_op jit(solution)/shard_map/ppermute | solution.py:288
  108.1 2.0 %collective-permute-start.68 = (bf16[12,8,256]{2,1,0:T(8,128)(2,1)S(1)}, bf16[12,8,256]{2,1,0:T(8,128)(2,1)S(1)}, u32[]{:S(2)}, u32[]{:S(2)}) collective-permute-start(bf16[12,8,256]{2,1,0:T(8,128)(2,1)S(1)} %get-tuple-element.225.refs_0_), channel_id=1, source_target_pairs={{0,8},{1,9},{2,10},{3,11},{4,12},{5,13},{6,14},{7,15},{8,0},{9,1},... | collective-permute-start | bytes 147464 | tf_op jit(solution)/shard_map/ppermute | solution.py:288
  110.0 1.9 %collective-permute-start.67 = (bf16[12,8,256]{2,1,0:T(8,128)(2,1)S(1)}, bf16[12,8,256]{2,1,0:T(8,128)(2,1)S(1)}, u32[]{:S(2)}, u32[]{:S(2)}) collective-permute-start(bf16[12,8,256]{2,1,0:T(8,128)(2,1)S(1)} %get-tuple-element.225.refs_0_), channel_id=1, source_target_pairs={{0,12},{1,13},{2,14},{3,15},{4,8},{5,9},{6,10},{7,11},{8,4},{9,5},... | collective-permute-start | bytes 147464 | tf_op jit(solution)/shard_map/ppermute | solution.py:288
  114.2 1.8 %collective-permute-done.67.refs_0_ = bf16[12,8,256]{2,1,0:T(8,128)(2,1)S(1)} collective-permute-done((bf16[12,8,256]{2,1,0:T(8,128)(2,1)S(1)}, bf16[12,8,256]{2,1,0:T(8,128)(2,1)S(1)}, u32[]{:S(2)}, u32[]{:S(2)}) %collective-permute-start.67) | collective-permute-done | bytes 49184 | tf_op jit(solution)/shard_map/ppermute | solution.py:288
  (179 shorter events, 66.6 us)
Async XLA Ops:
  7.1 6.2 %collective-permute-start = (bf16[13,8,256]{2,1,0:T(8,128)(2,1)S(1)}, bf16[13,8,256]{2,1,0:T(8,128)(2,1)S(1)}, u32[]{:S(2)}, u32[]{:S(2)}) collective-permute-start(bf16[13,8,256]{2,1,0:T(8,128)(2,1)S(1)} %get-tuple-element.122), channel_id=1, source_target_pairs={{0,1},{1,0},{2,3},{3,2},{4,5},{5,4},{6,7},{7,6},{8,9},{9,8},{10,11... | collective-permute-start | bytes 159752 | tf_op jit(solution)/shard_map/ppermute | solution.py:288
  7.6 5.7 %collective-permute-start.1 = (bf16[13,8,256]{2,1,0:T(8,128)(2,1)S(1)}, bf16[13,8,256]{2,1,0:T(8,128)(2,1)S(1)}, u32[]{:S(2)}, u32[]{:S(2)}) collective-permute-start(bf16[13,8,256]{2,1,0:T(8,128)(2,1)S(1)} %get-tuple-element.123), channel_id=1, source_target_pairs={{0,2},{1,3},{2,0},{3,1},{4,6},{5,7},{6,4},{7,5},{8,10},{9,11},{10,... | collective-permute-start | bytes 159752 | tf_op jit(solution)/shard_map/ppermute | solution.py:288
  11.2 7.5 %collective-permute-start.3 = (bf16[12,8,256]{2,1,0:T(8,128)(2,1)S(1)}, bf16[12,8,256]{2,1,0:T(8,128)(2,1)S(1)}, u32[]{:S(2)}, u32[]{:S(2)}) collective-permute-start(bf16[12,8,256]{2,1,0:T(8,128)(2,1)S(1)} %get-tuple-element.129), channel_id=1, source_target_pairs={{0,1},{1,0},{2,3},{3,2},{4,5},{5,4},{6,7},{7,6},{8,9},{9,8},{10,11... | collective-permute-start | bytes 147464 | tf_op jit(solution)/shard_map/ppermute | solution.py:288
  11.3 7.4 %collective-permute-start.4 = (bf16[12,8,256]{2,1,0:T(8,128)(2,1)S(1)}, bf16[12,8,256]{2,1,0:T(8,128)(2,1)S(1)}, u32[]{:S(2)}, u32[]{:S(2)}) collective-permute-start(bf16[12,8,256]{2,1,0:T(8,128)(2,1)S(1)} %get-tuple-element.130), channel_id=1, source_target_pairs={{0,2},{1,3},{2,0},{3,1},{4,6},{5,7},{6,4},{7,5},{8,10},{9,11},{10,... | collective-permute-start | bytes 147464 | tf_op jit(solution)/shard_map/ppermute | solution.py:288
  14.7 8.2 %collective-permute-start.6 = (bf16[12,8,256]{2,1,0:T(8,128)(2,1)S(1)}, bf16[12,8,256]{2,1,0:T(8,128)(2,1)S(1)}, u32[]{:S(2)}, u32[]{:S(2)}) collective-permute-start(bf16[12,8,256]{2,1,0:T(8,128)(2,1)S(1)} %get-tuple-element.133), channel_id=1, source_target_pairs={{0,8},{1,9},{2,10},{3,11},{4,12},{5,13},{6,14},{7,15},{8,0},{9,1},... | collective-permute-start | bytes 147464 | tf_op jit(solution)/shard_map/ppermute | solution.py:288
  17.4 6.0 %collective-permute-start.7 = (bf16[12,8,256]{2,1,0:T(8,128)(2,1)S(1)}, bf16[12,8,256]{2,1,0:T(8,128)(2,1)S(1)}, u32[]{:S(2)}, u32[]{:S(2)}) collective-permute-start(bf16[12,8,256]{2,1,0:T(8,128)(2,1)S(1)} %get-tuple-element.134), channel_id=1, source_target_pairs={{0,12},{1,13},{2,14},{3,15},{4,8},{5,9},{6,10},{7,11},{8,4},{9,5},... | collective-permute-start | bytes 147464 | tf_op jit(solution)/shard_map/ppermute | solution.py:288
  26.9 5.9 %collective-permute-start.13 = (bf16[12,8,256]{2,1,0:T(8,128)(2,1)S(1)}, bf16[12,8,256]{2,1,0:T(8,128)(2,1)S(1)}, u32[]{:S(2)}, u32[]{:S(2)}) collective-permute-start(bf16[12,8,256]{2,1,0:T(8,128)(2,1)S(1)} %get-tuple-element.141.refs_0_), channel_id=1, source_target_pairs={{0,12},{1,13},{2,14},{3,15},{4,8},{5,9},{6,10},{7,11},{8,4},{9,5},... | collective-permute-start | bytes 147464 | tf_op jit(solution)/shard_map/ppermute | solution.py:288
  28.4 5.8 %collective-permute-start.10 = (bf16[12,8,256]{2,1,0:T(8,128)(2,1)S(1)}, bf16[12,8,256]{2,1,0:T(8,128)(2,1)S(1)}, u32[]{:S(2)}, u32[]{:S(2)}) collective-permute-start(bf16[12,8,256]{2,1,0:T(8,128)(2,1)S(1)} %get-tuple-element.143), channel_id=1, source_target_pairs={{0,1},{1,0},{2,3},{3,2},{4,5},{5,4},{6,7},{7,6},{8,9},{9,8},{10,11... | collective-permute-start | bytes 147464 | tf_op jit(solution)/shard_map/ppermute | solution.py:288
  28.5 6.3 %collective-permute-start.11 = (bf16[12,8,256]{2,1,0:T(8,128)(2,1)S(1)}, bf16[12,8,256]{2,1,0:T(8,128)(2,1)S(1)}, u32[]{:S(2)}, u32[]{:S(2)}) collective-permute-start(bf16[12,8,256]{2,1,0:T(8,128)(2,1)S(1)} %get-tuple-element.144), channel_id=1, source_target_pairs={{0,2},{1,3},{2,0},{3,1},{4,6},{5,7},{6,4},{7,5},{8,10},{9,11},{10,... | collective-permute-start | bytes 147464 | tf_op jit(solution)/shard_map/ppermute | solution.py:288
  44.6 6.1 %collective-permute-start.24 = (bf16[12,8,256]{2,1,0:T(8,128)(2,1)S(1)}, bf16[12,8,256]{2,1,0:T(8,128)(2,1)S(1)}, u32[]{:S(2)}, u32[]{:S(2)}) collective-permute-start(bf16[12,8,256]{2,1,0:T(8,128)(2,1)S(1)} %get-tuple-element.161), channel_id=1, source_target_pairs={{0,8},{1,9},{2,10},{3,11},{4,12},{5,13},{6,14},{7,15},{8,0},{9,1},... | collective-permute-start | bytes 147464 | tf_op jit(solution)/shard_map/ppermute | solution.py:288
  45.3 6.4 %collective-permute-start.25 = (bf16[12,8,256]{2,1,0:T(8,128)(2,1)S(1)}, bf16[12,8,256]{2,1,0:T(8,128)(2,1)S(1)}, u32[]{:S(2)}, u32[]{:S(2)}) collective-permute-start(bf16[12,8,256]{2,1,0:T(8,128)(2,1)S(1)} %get-tuple-element.162), channel_id=1, source_target_pairs={{0,12},{1,13},{2,14},{3,15},{4,8},{5,9},{6,10},{7,11},{8,4},{9,5},... | collective-permute-start | bytes 147464 | tf_op jit(solution)/shard_map/ppermute | solution.py:288
  52.6 6.1 %collective-permute-start.32 = (bf16[12,8,256]{2,1,0:T(8,128)(2,1)S(1)}, bf16[12,8,256]{2,1,0:T(8,128)(2,1)S(1)}, u32[]{:S(2)}, u32[]{:S(2)}) collective-permute-start(bf16[12,8,256]{2,1,0:T(8,128)(2,1)S(1)} %get-tuple-element.168.refs_0_), channel_id=1, source_target_pairs={{0,8},{1,9},{2,10},{3,11},{4,12},{5,13},{6,14},{7,15},{8,0},{9,1},... | collective-permute-start | bytes 147464 | tf_op jit(solution)/shard_map/ppermute | solution.py:288
  54.6 5.9 %collective-permute-start.31 = (bf16[12,8,256]{2,1,0:T(8,128)(2,1)S(1)}, bf16[12,8,256]{2,1,0:T(8,128)(2,1)S(1)}, u32[]{:S(2)}, u32[]{:S(2)}) collective-permute-start(bf16[12,8,256]{2,1,0:T(8,128)(2,1)S(1)} %get-tuple-element.168.refs_0_), channel_id=1, source_target_pairs={{0,12},{1,13},{2,14},{3,15},{4,8},{5,9},{6,10},{7,11},{8,4},{9,5},... | collective-permute-start | bytes 147464 | tf_op jit(solution)/shard_map/ppermute | solution.py:288
  56.8 5.7 %collective-permute-start.29 = (bf16[12,8,256]{2,1,0:T(8,128)(2,1)S(1)}, bf16[12,8,256]{2,1,0:T(8,128)(2,1)S(1)}, u32[]{:S(2)}, u32[]{:S(2)}) collective-permute-start(bf16[12,8,256]{2,1,0:T(8,128)(2,1)S(1)} %get-tuple-element.171), channel_id=1, source_target_pairs={{0,2},{1,3},{2,0},{3,1},{4,6},{5,7},{6,4},{7,5},{8,10},{9,11},{10,... | collective-permute-start | bytes 147464 | tf_op jit(solution)/shard_map/ppermute | solution.py:288
  72.3 6.6 %collective-permute-start.42 = (bf16[12,8,256]{2,1,0:T(8,128)(2,1)S(1)}, bf16[12,8,256]{2,1,0:T(8,128)(2,1)S(1)}, u32[]{:S(2)}, u32[]{:S(2)}) collective-permute-start(bf16[12,8,256]{2,1,0:T(8,128)(2,1)S(1)} %get-tuple-element.188), channel_id=1, source_target_pairs={{0,8},{1,9},{2,10},{3,11},{4,12},{5,13},{6,14},{7,15},{8,0},{9,1},... | collective-permute-start | bytes 147464 | tf_op jit(solution)/shard_map/ppermute | solution.py:288
  72.4 6.6 %collective-permute-start.43 = (bf16[12,8,256]{2,1,0:T(8,128)(2,1)S(1)}, bf16[12,8,256]{2,1,0:T(8,128)(2,1)S(1)}, u32[]{:S(2)}, u32[]{:S(2)}) collective-permute-start(bf16[12,8,256]{2,1,0:T(8,128)(2,1)S(1)} %get-tuple-element.189), channel_id=1, source_target_pairs={{0,12},{1,13},{2,14},{3,15},{4,8},{5,9},{6,10},{7,11},{8,4},{9,5},... | collective-permute-start | bytes 147464 | tf_op jit(solution)/shard_map/ppermute | solution.py:288
  80.4 6.1 %collective-permute-start.50 = (bf16[12,8,256]{2,1,0:T(8,128)(2,1)S(1)}, bf16[12,8,256]{2,1,0:T(8,128)(2,1)S(1)}, u32[]{:S(2)}, u32[]{:S(2)}) collective-permute-start(bf16[12,8,256]{2,1,0:T(8,128)(2,1)S(1)} %get-tuple-element.195.refs_0_), channel_id=1, source_target_pairs={{0,8},{1,9},{2,10},{3,11},{4,12},{5,13},{6,14},{7,15},{8,0},{9,1},... | collective-permute-start | bytes 147464 | tf_op jit(solution)/shard_map/ppermute | solution.py:288
  82.3 5.9 %collective-permute-start.49 = (bf16[12,8,256]{2,1,0:T(8,128)(2,1)S(1)}, bf16[12,8,256]{2,1,0:T(8,128)(2,1)S(1)}, u32[]{:S(2)}, u32[]{:S(2)}) collective-permute-start(bf16[12,8,256]{2,1,0:T(8,128)(2,1)S(1)} %get-tuple-element.195.refs_0_), channel_id=1, source_target_pairs={{0,12},{1,13},{2,14},{3,15},{4,8},{5,9},{6,10},{7,11},{8,4},{9,5},... | collective-permute-start | bytes 147464 | tf_op jit(solution)/shard_map/ppermute | solution.py:288
  100.0 6.6 %collective-permute-start.60 = (bf16[12,8,256]{2,1,0:T(8,128)(2,1)S(1)}, bf16[12,8,256]{2,1,0:T(8,128)(2,1)S(1)}, u32[]{:S(2)}, u32[]{:S(2)}) collective-permute-start(bf16[12,8,256]{2,1,0:T(8,128)(2,1)S(1)} %get-tuple-element.215), channel_id=1, source_target_pairs={{0,8},{1,9},{2,10},{3,11},{4,12},{5,13},{6,14},{7,15},{8,0},{9,1},... | collective-permute-start | bytes 147464 | tf_op jit(solution)/shard_map/ppermute | solution.py:288
  100.3 6.3 %collective-permute-start.61 = (bf16[12,8,256]{2,1,0:T(8,128)(2,1)S(1)}, bf16[12,8,256]{2,1,0:T(8,128)(2,1)S(1)}, u32[]{:S(2)}, u32[]{:S(2)}) collective-permute-start(bf16[12,8,256]{2,1,0:T(8,128)(2,1)S(1)} %get-tuple-element.216), channel_id=1, source_target_pairs={{0,12},{1,13},{2,14},{3,15},{4,8},{5,9},{6,10},{7,11},{8,4},{9,5},... | collective-permute-start | bytes 147464 | tf_op jit(solution)/shard_map/ppermute | solution.py:288
  108.1 6.1 %collective-permute-start.68 = (bf16[12,8,256]{2,1,0:T(8,128)(2,1)S(1)}, bf16[12,8,256]{2,1,0:T(8,128)(2,1)S(1)}, u32[]{:S(2)}, u32[]{:S(2)}) collective-permute-start(bf16[12,8,256]{2,1,0:T(8,128)(2,1)S(1)} %get-tuple-element.225.refs_0_), channel_id=1, source_target_pairs={{0,8},{1,9},{2,10},{3,11},{4,12},{5,13},{6,14},{7,15},{8,0},{9,1},... | collective-permute-start | bytes 147464 | tf_op jit(solution)/shard_map/ppermute | solution.py:288
  110.0 5.9 %collective-permute-start.67 = (bf16[12,8,256]{2,1,0:T(8,128)(2,1)S(1)}, bf16[12,8,256]{2,1,0:T(8,128)(2,1)S(1)}, u32[]{:S(2)}, u32[]{:S(2)}) collective-permute-start(bf16[12,8,256]{2,1,0:T(8,128)(2,1)S(1)} %get-tuple-element.225.refs_0_), channel_id=1, source_target_pairs={{0,12},{1,13},{2,14},{3,15},{4,8},{5,9},{6,10},{7,11},{8,4},{9,5},... | collective-permute-start | bytes 147464 | tf_op jit(solution)/shard_map/ppermute | solution.py:288
  112.3 7.0 %collective-permute-start.65 = (bf16[12,8,256]{2,1,0:T(8,128)(2,1)S(1)}, bf16[12,8,256]{2,1,0:T(8,128)(2,1)S(1)}, u32[]{:S(2)}, u32[]{:S(2)}) collective-permute-start(bf16[12,8,256]{2,1,0:T(8,128)(2,1)S(1)} %get-tuple-element.228), channel_id=1, source_target_pairs={{0,2},{1,3},{2,0},{3,1},{4,6},{5,7},{6,4},{7,5},{8,10},{9,11},{10,... | collective-permute-start | bytes 147464 | tf_op jit(solution)/shard_map/ppermute | solution.py:288
  113.5 5.8 %collective-permute-start.66 = (bf16[12,8,256]{2,1,0:T(8,128)(2,1)S(1)}, bf16[12,8,256]{2,1,0:T(8,128)(2,1)S(1)}, u32[]{:S(2)}, u32[]{:S(2)}) collective-permute-start(bf16[12,8,256]{2,1,0:T(8,128)(2,1)S(1)} %get-tuple-element.229), channel_id=1, source_target_pairs={{0,3},{1,2},{2,1},{3,0},{4,7},{5,6},{6,5},{7,4},{8,11},{9,10},{10,... | collective-permute-start | bytes 147464 | tf_op jit(solution)/shard_map/ppermute | solution.py:288
  (53 other events, 225.7 us)

commit v11 on v10

--- a/solution.py
+++ b/solution.py
@@ -34,24 +34,31 @@
             h_into(at, h)
 
 
-def transpose_products(base, tile_of, row_of, tiles, hb, outs, xs=range(QUAD)):
-    per = tile_of.shape[0] // (2 * QUAD)
+def slot_at(cap, group, x, high, rank):
+    if high == 0:
+        return QUAD * (group - 1) * cap + x * cap + rank
+    return x * (group - 1) * cap + (high - 1) * cap + rank
+
+
+def transpose_products(cap, highs, tile_of, row_of, tiles, hb, outs, xs=range(QUAD)):
+    group = tile_of.shape[0] // (QUAD * cap)
     for x, out in zip(xs, outs):
-        for s in range(per):
-            slot = base + x * per + s
+        for s in range(len(highs) * cap):
+            slot = slot_at(cap, group, x, highs[s // cap], s % cap)
             out[s] = jnp.dot(hb[row_of[slot]], tiles[tile_of[slot]], preferred_element_type=F32).astype(BF16)
 
 
-def forward_products(base, tile_of, land_of, turned, moved, totals, xs=range(QUAD)):
-    per = tile_of.shape[0] // (2 * QUAD)
+def forward_products(cap, highs, tile_of, land_of, turned, moved, totals, xs=range(QUAD)):
+    group = tile_of.shape[0] // (QUAD * cap)
+    per = len(highs) * cap
     for total in totals:
         total[...] = jnp.zeros_like(total)
     for x, part in zip(xs, moved):
-        first = base + x * per
-        terms = [jnp.dot(part[s], turned[tile_of[first + s]], preferred_element_type=F32) for s in range(per)]
+        at = [slot_at(cap, group, x, high, rank) for high in highs for rank in range(cap)]
+        terms = [jnp.dot(part[s], turned[tile_of[at[s]]], preferred_element_type=F32) for s in range(per)]
         for s in range(0, per, LANES):
             several = range(min(LANES, per - s))
-            spots = [land_of[first + s + i] for i in several]
+            spots = [land_of[at[s + i]] for i in several]
             held = [totals[i][spots[i]] + terms[s + i] for i in several]
             for i in several:
                 totals[i][spots[i]] = held[i]
@@ -69,7 +76,7 @@
                  rows, cols, dual_step, dual_mask, cot_y, filled, wants, plan, sems, small):
     tile_slots, side, _ = tiles.shape
     group = peers // QUAD
-    half = group // 2
+    most = (group - 1) * cap
     chunks = tile_slots // CHUNK
     minor = [
         pltpu.make_async_copy(src, dst, small.at[i])
@@ -108,8 +115,7 @@
         apart = owner ^ me
         high, quad = apart // QUAD, apart % QUAD
         place = high * cap + rank
-        near = jnp.where(high < half, 1, 0)
-        slot = (near * QUAD + quad) * (half * cap) + place - (1 - near) * (half * cap)
+        slot = jnp.where(high == 0, QUAD * most + quad * cap + rank, quad * most + place - cap)
         tile_of[slot] = t
         row_of[slot] = rows[t]
         land_of[slot] = rows[t]
@@ -127,10 +133,10 @@
     scaled_blocks(side, dy, dual_step, hb, h_into)
     chart.wait()
     for out in (o0, o1, o2, o3):
-        out[half * cap, :, pl.ds(0, plan.shape[1])] = plan[...].astype(BF16)
+        out[most, :, pl.ds(0, plan.shape[1])] = plan[...].astype(BF16)
     for c in range(chunks):
         tile_copy(c).wait()
-    transpose_products(0, tile_of, row_of, held, hb, (o0, o1, o2, o3))
+    transpose_products(cap, range(1, group), tile_of, row_of, held, hb, (o0, o1, o2, o3))
 
 
 def turn_kernel(held, turned):
@@ -142,8 +148,8 @@
     lax.fori_loop(0, held.shape[0] // CHUNK, one_chunk, 0)
 
 
-def near_product_kernel(tile_of, row_of, held, hb, o0, o1, o2, o3):
-    transpose_products(tile_of.shape[0] // 2, tile_of, row_of, held, hb, (o0, o1, o2, o3))
+def near_product_kernel(cap, tile_of, row_of, held, hb, o0, o1, o2, o3):
+    transpose_products(cap, (0,), tile_of, row_of, held, hb, (o0, o1, o2, o3))
 
 
 def map_kernel(a0, a1, a2, a3, wants, whole, sem):
@@ -211,38 +217,38 @@
             out[s] = value
 
 
-def near_forward_kernel(tile_of, land_of, turned, m0, m1, m2, m3, out, *totals):
-    forward_products(tile_of.shape[0] // 2, tile_of, land_of, turned, (m0, m1, m2, m3), totals)
+def near_forward_kernel(cap, highs, tile_of, land_of, turned, m0, m1, m2, m3, out, *totals):
+    forward_products(cap, highs, tile_of, land_of, turned, (m0, m1, m2, m3), totals)
     for r in range(out.shape[0]):
         out[r] = gathered(totals, r)
 
 
-def chip_forward_kernel(tile_of, land_of, turned, part, m0, m1, out, *totals):
-    forward_products(0, tile_of, land_of, turned, (m0, m1), totals, (0, 1))
+def chip_forward_kernel(cap, highs, tile_of, land_of, turned, part, m0, m1, out, *totals):
+    forward_products(cap, highs, tile_of, land_of, turned, (m0, m1), totals, (0, 1))
     for r in range(out.shape[0]):
         out[r] = part[r] + gathered(totals, r)
 
 
-def rest_product_kernel(tile_of, row_of, held, hb, o0, o1, o3):
-    transpose_products(0, tile_of, row_of, held, hb, (o3, o1, o0), (3, 1, 0))
-
-
-def middle_kernel(step, tile_of, row_of, land_of, held, turned, dual_step, dual_mask, part, dy, m2, m3,
+def rest_product_kernel(cap, highs, tile_of, row_of, held, hb, o0, o1, o3):
+    transpose_products(cap, highs, tile_of, row_of, held, hb, (o3, o1, o0), (3, 1, 0))
+
+
+def middle_kernel(step, cap, highs, sent, tile_of, row_of, land_of, held, turned, dual_step, dual_mask, part, dy, m2, m3,
                   new_dy, hb, o2, *totals):
     side = held.shape[1]
-    forward_products(0, tile_of, land_of, turned, (m2, m3), totals, (2, 3))
+    forward_products(cap, highs, tile_of, land_of, turned, (m2, m3), totals, (2, 3))
     for r in range(hb.shape[0]):
         at = pl.ds(r * side, side)
         v = part[r] + gathered(totals, r)
         new_dy[:, at] = dual_mask[step, :, at].astype(F32) * (dy[:, at] - v)
 
     scaled_blocks(side, new_dy, dual_step, hb)
-    transpose_products(0, tile_of, row_of, held, hb, (o2,), (2,))
-
-
-def last_kernel(tile_of, land_of, turned, part, dy, m2, m3, new_y, *totals):
+    transpose_products(cap, sent, tile_of, row_of, held, hb, (o2,), (2,))
+
+
+def last_kernel(cap, highs, tile_of, land_of, turned, part, dy, m2, m3, new_y, *totals):
     side = turned.shape[1]
-    forward_products(0, tile_of, land_of, turned, (m2, m3), totals, (2, 3))
+    forward_products(cap, highs, tile_of, land_of, turned, (m2, m3), totals, (2, 3))
     for r in range(part.shape[0]):
         at = pl.ds(r * side, side)
         new_y[:, at] = dy[:, at] - (part[r] + gathered(totals, r))
@@ -264,12 +270,12 @@
     primal_step = primal_step.reshape(1, -1)
     y_shape = shape(cot_y.shape, F32)
     x_shape = shape(cot_x.shape, F32)
-    part_set = (shape((half * cap, batch, side), BF16),) * QUAD
+    part_set, most_set, own_set = ((shape((n * cap, batch, side), BF16),) * QUAD for n in (half, group - 1, 1))
     block_set = shape((col_blocks, batch, side), BF16)
     hb_set = shape((row_blocks, batch, side), BF16)
     per_slot = pltpu.SMEM((slots,), I32)
     row_totals = [pltpu.VMEM((row_blocks + 1, batch, side), F32)] * LANES
-    col_totals = [pltpu.VMEM((col_blocks + 1, batch, side), F32)] * (2 * half)
+    col_totals = [pltpu.VMEM((col_blocks + 1, batch, side), F32)] * (2 * (group - 1))
     tile_bytes = tiles.size * 2
 
     def call(kernel, name, moved, ins, outs, args, scratch=()):
@@ -295,7 +301,7 @@
         functools.partial(start_kernel, step, peers, cap, col_blocks),
         out_shape=(
             pltpu.VMEM(tiles.shape, BF16), y_shape, y_shape, hb_set, per_slot, per_slot, per_slot,
-        ) + (shape((half * cap + 1, batch, side), BF16),) * QUAD,
+        ) + (shape(((group - 1) * cap + 1, batch, side), BF16),) * QUAD,
         in_specs=[SM] + [HBM] * 6,
         out_specs=(VM,) * 4 + (SM,) * 3 + (VM,) * QUAD,
         scratch_shapes=[
@@ -313,10 +319,11 @@
     ))
     turned = call(turn_kernel, "turn", tile_bytes, [VM], pltpu.VMEM(tiles.shape, BF16), (held,))
     x_state, spent, wants = cot_x, cot_x, None
-    near_highs, far_highs = tuple(range(half)), tuple(reversed(range(half, group)))
+    near_highs, late_highs = tuple(range(half)), tuple(range(half, group))
+    far_highs = tuple(reversed(late_highs))
     while True:
         far_got = near_swaps(far_parts)
-        near_parts = call(near_product_kernel, "near_product", tile_bytes // 2, [SM] * 2 + [VM] * 2, part_set,
+        near_parts = call(functools.partial(near_product_kernel, cap), "near_product", tile_bytes // 4, [SM] * 2 + [VM] * 2, own_set,
                           (tile_of, row_of, held, hb))
         near_got = near_swaps(near_parts)
         if wants is None:
@@ -329,17 +336,16 @@
                 compiler_params=PARAMS,
                 name="maps",
             )(*far_got)
-        far_sums = call(functools.partial(sum_kernel, half, cap), "far_sum", 1 << 20, [SM] + [VM] * QUAD,
-                        (block_set,) * half, (wants, *far_got), col_totals)
-        got = [swap(far_sums[h], (half + h) * QUAD) for h in range(half)]
-        near_sums = call(functools.partial(sum_kernel, 0, cap), "near_sum", 1 << 20, [SM] + [VM] * QUAD,
-                         (shape(block_set.shape, F32),) + (block_set,) * (half - 1), (wants, *near_got), col_totals)
-        got += [swap(near_sums[h], h * QUAD) for h in range(1, half)]
+        far_sums = call(functools.partial(sum_kernel, 1, cap), "far_sum", 1 << 20, [SM] + [VM] * QUAD,
+                        (block_set,) * (group - 1), (wants, *far_got), col_totals)
+        own_sum = call(functools.partial(sum_kernel, 0, cap), "own_sum", 1 << 20, [SM] + [VM] * QUAD,
+                       (shape(block_set.shape, F32),), (wants, *near_got), col_totals[:2])
+        got = [swap(far_sums[h - 1], h * QUAD) for h in (*range(half, group), *range(1, half))]
         if step == steps - 1:
             turned, x_state = lax.optimization_barrier((turned, x_state))
         u, dx, moved = call(
             functools.partial(primal_kernel, step), "primal", 1 << 20, [VM] * (3 + group),
-            (x_shape, x_shape, block_set), (primal_mask, primal_step, x_state, near_sums[0], *got))
+            (x_shape, x_shape, block_set), (primal_mask, primal_step, x_state, *own_sum, *got))
         x_state, spent = call(functools.partial(settle_kernel, step == steps - 1), "settle", 1 << 20, [VM] * 4,
                               (x_shape, x_shape), (primal_step, u, dx, spent))
         blocks = [moved] + [swap(moved, h * QUAD) for h in range(1, group)]
@@ -348,22 +354,22 @@
                             (wants, *(blocks[h] for h in highs))))
             for name, highs in (("near_pick", near_highs), ("far_pick", far_highs))
         )
-        part = call(near_forward_kernel, "near_forward", tile_bytes // 2, [SM] * 2 + [VM] * (1 + QUAD),
+        part = call(functools.partial(near_forward_kernel, cap, near_highs), "near_forward", tile_bytes // 2, [SM] * 2 + [VM] * (1 + QUAD),
                     shape(hb_set.shape, F32), (tile_of, land_of, turned, *near_moved), row_totals)
-        part = call(chip_forward_kernel, "chip_forward", tile_bytes // 4, [SM] * 2 + [VM] * 4,
+        part = call(functools.partial(chip_forward_kernel, cap, late_highs), "chip_forward", tile_bytes // 4, [SM] * 2 + [VM] * 4,
                     shape(hb_set.shape, F32), (tile_of, land_of, turned, part, *far_moved[:2]), row_totals)
         if step == 0:
             break
         step -= 1
         dy, hb, across = call(
-            functools.partial(middle_kernel, step), "middle", tile_bytes // 2, [SM] * 3 + [VM] * 8,
-            (y_shape, hb_set, part_set[0]),
+            functools.partial(middle_kernel, step, cap, late_highs, range(1, group)), "middle", tile_bytes // 2, [SM] * 3 + [VM] * 8,
+            (y_shape, hb_set, most_set[0]),
             (tile_of, row_of, land_of, held, turned, dual_step, dual_mask, part, dy, *far_moved[2:]), row_totals)
         rhs = call(settle_dual_kernel, "settle_dual", 1 << 20, [VM] * 3, y_shape, (dual_step, dy, rhs))
-        own, beside, aslant = call(rest_product_kernel, "rest_product", tile_bytes // 4, [SM] * 2 + [VM] * 2,
-                                   part_set[:3], (tile_of, row_of, held, hb))
+        own, beside, aslant = call(functools.partial(rest_product_kernel, cap, range(1, group)), "rest_product",
+                                   tile_bytes // 2, [SM] * 2 + [VM] * 2, most_set[:3], (tile_of, row_of, held, hb))
         far_parts = [own, beside, across, aslant]
-    y_state = call(last_kernel, "last", tile_bytes // 4, [SM] * 2 + [VM] * 5, y_shape,
+    y_state = call(functools.partial(last_kernel, cap, late_highs), "last", tile_bytes // 4, [SM] * 2 + [VM] * 5, y_shape,
                    (tile_of, land_of, turned, part, dy, *far_moved[2:]), row_totals)
     return spent, rhs, x_state, y_state
 

time: 122 us -> 130 us (1.066)
  waiting for transfers between devices: 28.1 us -> 35.9 us
    ppermute x72, waiting for transfers between devices: 28.1 us -> 35.9 us  [swap(): return lax.ppermute(array, 'rb', [(p, p ^ x) for p in range(peers)])]
  transfers between devices with their start and end apart: 72 -> 72, of which waited for: 29 -> 34; matrix products, arithmetic and copies ran while one was open for 0% -> 0% of each run, Pallas kernels for 16% -> 14%
where the time goes in v11:
time: 130 us
  starting transfers between devices  63.4 us (49%)
  waiting for transfers between devices  35.9 us (28%)
  Pallas kernels  28.9 us (22%)
  between operations  1.8 us (1%)
    ppermute x72, starting transfers between devices, swap(): return lax.ppermute(array, 'rb', [(p, p ^ x) for p in range(peers)])  63.4 us
    ppermute x72, waiting for transfers between devices, swap(): return lax.ppermute(array, 'rb', [(p, p ^ x) for p in range(peers)])  35.9 us
    pallas_call x47, Pallas kernels, call(): pl.pallas_call(kernel, out_shape=outs, in_specs=ins, out_specs=jax.tree.m...  22.1 us
    pallas_call x1, Pallas kernels, on_device(): pl.pallas_call(functools.partial(start_kernel, step, peers, cap, col_bloc...  6.21 us
  transfers between devices with their start and end apart: 72, of which 34 were waited for; matrix products, arithmetic and copies ran while one was open for 0% of the time, Pallas kernels for 14%

profile of v11, /device:TPU:0, one launch (start us, length us, event | category | flops | bytes accessed | tf_op | source)
XLA Modules:
  0.0 130.0 jit_solution(16410120272260116187)
XLA Ops:
  1.3 6.2 %start.1 = (bf16[88,256,256]{2,1,0:T(8,128)(2,1)S(1)}, f32[8,2048]{1,0:T(8,128)S(1)}, f32[8,2048]{1,0:T(8,128)S(1)}, bf16[8,8,256]{2,1,0:T(8,128)(2,1)S(1)}, s32...) custom-call(s32[1]{0:T(128)S(6)} %copy.14.count, ...), custom_call_target="tpu_custom_call" | custom-call | flops 184549376 | bytes 23068672 | tf_op jit(solution)/shard_map/start/pallas_call | solution.py:300
  8.0 2.6 %collective-permute-start.1 = (bf16[19,8,256]{2,1,0:T(8,128)(2,1)S(1)}, bf16[19,8,256]{2,1,0:T(8,128)(2,1)S(1)}, u32[]{:S(2)}, u32[]{:S(2)}) collective-permute-start(bf16[19,8,256]{2,1,0:T(8,128)(2,1)S(1)} %get-tuple-element.119), channel_id=1, source_target_pairs={{0,2},{1,3},{2,0},{3,1},{4,6},{5,7},{6,4},{7,5},{8,10},{9,11},{10,... | collective-permute-start | bytes 233480 | tf_op jit(solution)/shard_map/ppermute | solution.py:294
  11.3 2.2 %collective-permute-done.1.a2 = bf16[19,8,256]{2,1,0:T(8,128)(2,1)S(1)} collective-permute-done((bf16[19,8,256]{2,1,0:T(8,128)(2,1)S(1)}, bf16[19,8,256]{2,1,0:T(8,128)(2,1)S(1)}, u32[]{:S(2)}, u32[]{:S(2)}) %collective-permute-start.1) | collective-permute-done | bytes 77856 | tf_op jit(solution)/shard_map/ppermute | solution.py:294
  15.7 3.0 %collective-permute-start.6 = (bf16[12,8,256]{2,1,0:T(8,128)(2,1)S(1)}, bf16[12,8,256]{2,1,0:T(8,128)(2,1)S(1)}, u32[]{:S(2)}, u32[]{:S(2)}) collective-permute-start(bf16[12,8,256]{2,1,0:T(8,128)(2,1)S(1)} %get-tuple-element.128), channel_id=1, source_target_pairs={{0,8},{1,9},{2,10},{3,11},{4,12},{5,13},{6,14},{7,15},{8,0},{9,1},... | collective-permute-start | bytes 147464 | tf_op jit(solution)/shard_map/ppermute | solution.py:294
  21.6 3.7 %turn.1.turned = bf16[88,256,256]{2,1,0:T(8,128)(2,1)S(1)} custom-call(bf16[88,256,256]{2,1,0:T(8,128)(2,1)S(1)} %get-tuple-element.115.held), custom_call_target="tpu_custom_call" | custom-call | flops 92274688 | bytes 11534336 | tf_op jit(solution)/shard_map/turn/pallas_call | solution.py:282
  25.6 1.9 %collective-permute-start.9 = (bf16[12,8,256]{2,1,0:T(8,128)(2,1)S(1)}, bf16[12,8,256]{2,1,0:T(8,128)(2,1)S(1)}, u32[]{:S(2)}, u32[]{:S(2)}) collective-permute-start(bf16[12,8,256]{2,1,0:T(8,128)(2,1)S(1)} %get-tuple-element.136.refs_0_), channel_id=1, source_target_pairs={{0,4},{1,5},{2,6},{3,7},{4,0},{5,1},{6,2},{7,3},{8,12},{9,13},{10,... | collective-permute-start | bytes 147464 | tf_op jit(solution)/shard_map/ppermute | solution.py:294
  27.5 1.7 %collective-permute-start.14 = (bf16[12,8,256]{2,1,0:T(8,128)(2,1)S(1)}, bf16[12,8,256]{2,1,0:T(8,128)(2,1)S(1)}, u32[]{:S(2)}, u32[]{:S(2)}) collective-permute-start(bf16[12,8,256]{2,1,0:T(8,128)(2,1)S(1)} %get-tuple-element.136.refs_0_), channel_id=1, source_target_pairs={{0,8},{1,9},{2,10},{3,11},{4,12},{5,13},{6,14},{7,15},{8,0},{9,1},... | collective-permute-start | bytes 147464 | tf_op jit(solution)/shard_map/ppermute | solution.py:294
  45.5 1.9 %collective-permute-done.23.a3 = bf16[18,8,256]{2,1,0:T(8,128)(2,1)S(1)} collective-permute-done((bf16[18,8,256]{2,1,0:T(8,128)(2,1)S(1)}, bf16[18,8,256]{2,1,0:T(8,128)(2,1)S(1)}, u32[]{:S(2)}, u32[]{:S(2)}) %collective-permute-start.23) | collective-permute-done | bytes 73760 | tf_op jit(solution)/shard_map/ppermute | solution.py:294
  47.6 2.3 %collective-permute-start.24 = (bf16[12,8,256]{2,1,0:T(8,128)(2,1)S(1)}, bf16[12,8,256]{2,1,0:T(8,128)(2,1)S(1)}, u32[]{:S(2)}, u32[]{:S(2)}) collective-permute-start(bf16[12,8,256]{2,1,0:T(8,128)(2,1)S(1)} %get-tuple-element.155), channel_id=1, source_target_pairs={{0,8},{1,9},{2,10},{3,11},{4,12},{5,13},{6,14},{7,15},{8,0},{9,1},... | collective-permute-start | bytes 147464 | tf_op jit(solution)/shard_map/ppermute | solution.py:294
  52.5 2.6 %collective-permute-done.19.a2 = bf16[6,8,256]{2,1,0:T(8,128)(2,1)S(1)} collective-permute-done((bf16[6,8,256]{2,1,0:T(8,128)(2,1)S(1)}, bf16[6,8,256]{2,1,0:T(8,128)(2,1)S(1)}, u32[]{:S(2)}, u32[]{:S(2)}) %collective-permute-start.19) | collective-permute-done | bytes 24608 | tf_op jit(solution)/shard_map/ppermute | solution.py:294
  56.2 1.7 %collective-permute-start.27 = (bf16[12,8,256]{2,1,0:T(8,128)(2,1)S(1)}, bf16[12,8,256]{2,1,0:T(8,128)(2,1)S(1)}, u32[]{:S(2)}, u32[]{:S(2)}) collective-permute-start(bf16[12,8,256]{2,1,0:T(8,128)(2,1)S(1)} %get-tuple-element.162.refs_0_), channel_id=1, source_target_pairs={{0,4},{1,5},{2,6},{3,7},{4,0},{5,1},{6,2},{7,3},{8,12},{9,13},{10,... | collective-permute-start | bytes 147464 | tf_op jit(solution)/shard_map/ppermute | solution.py:294
  59.0 1.7 %collective-permute-start.31 = (bf16[12,8,256]{2,1,0:T(8,128)(2,1)S(1)}, bf16[12,8,256]{2,1,0:T(8,128)(2,1)S(1)}, u32[]{:S(2)}, u32[]{:S(2)}) collective-permute-start(bf16[12,8,256]{2,1,0:T(8,128)(2,1)S(1)} %get-tuple-element.162.refs_0_), channel_id=1, source_target_pairs={{0,12},{1,13},{2,14},{3,15},{4,8},{5,9},{6,10},{7,11},{8,4},{9,5},... | collective-permute-start | bytes 147464 | tf_op jit(solution)/shard_map/ppermute | solution.py:294
  62.6 2.3 %collective-permute-done.32.refs_1_ = bf16[12,8,256]{2,1,0:T(8,128)(2,1)S(1)} collective-permute-done((bf16[12,8,256]{2,1,0:T(8,128)(2,1)S(1)}, bf16[12,8,256]{2,1,0:T(8,128)(2,1)S(1)}, u32[]{:S(2)}, u32[]{:S(2)}) %collective-permute-start.32) | collective-permute-done | bytes 49184 | tf_op jit(solution)/shard_map/ppermute | solution.py:294
  75.4 1.8 %collective-permute-done.41.a3 = bf16[18,8,256]{2,1,0:T(8,128)(2,1)S(1)} collective-permute-done((bf16[18,8,256]{2,1,0:T(8,128)(2,1)S(1)}, bf16[18,8,256]{2,1,0:T(8,128)(2,1)S(1)}, u32[]{:S(2)}, u32[]{:S(2)}) %collective-permute-start.41) | collective-permute-done | bytes 73760 | tf_op jit(solution)/shard_map/ppermute | solution.py:294
  77.3 1.9 %collective-permute-start.42 = (bf16[12,8,256]{2,1,0:T(8,128)(2,1)S(1)}, bf16[12,8,256]{2,1,0:T(8,128)(2,1)S(1)}, u32[]{:S(2)}, u32[]{:S(2)}) collective-permute-start(bf16[12,8,256]{2,1,0:T(8,128)(2,1)S(1)} %get-tuple-element.181), channel_id=1, source_target_pairs={{0,8},{1,9},{2,10},{3,11},{4,12},{5,13},{6,14},{7,15},{8,0},{9,1},... | collective-permute-start | bytes 147464 | tf_op jit(solution)/shard_map/ppermute | solution.py:294
  82.1 2.6 %collective-permute-done.37.a2 = bf16[6,8,256]{2,1,0:T(8,128)(2,1)S(1)} collective-permute-done((bf16[6,8,256]{2,1,0:T(8,128)(2,1)S(1)}, bf16[6,8,256]{2,1,0:T(8,128)(2,1)S(1)}, u32[]{:S(2)}, u32[]{:S(2)}) %collective-permute-start.37) | collective-permute-done | bytes 24608 | tf_op jit(solution)/shard_map/ppermute | solution.py:294
  85.8 1.7 %collective-permute-start.45 = (bf16[12,8,256]{2,1,0:T(8,128)(2,1)S(1)}, bf16[12,8,256]{2,1,0:T(8,128)(2,1)S(1)}, u32[]{:S(2)}, u32[]{:S(2)}) collective-permute-start(bf16[12,8,256]{2,1,0:T(8,128)(2,1)S(1)} %get-tuple-element.188.refs_0_), channel_id=1, source_target_pairs={{0,4},{1,5},{2,6},{3,7},{4,0},{5,1},{6,2},{7,3},{8,12},{9,13},{10,... | collective-permute-start | bytes 147464 | tf_op jit(solution)/shard_map/ppermute | solution.py:294
  88.5 1.8 %collective-permute-start.49 = (bf16[12,8,256]{2,1,0:T(8,128)(2,1)S(1)}, bf16[12,8,256]{2,1,0:T(8,128)(2,1)S(1)}, u32[]{:S(2)}, u32[]{:S(2)}) collective-permute-start(bf16[12,8,256]{2,1,0:T(8,128)(2,1)S(1)} %get-tuple-element.188.refs_0_), channel_id=1, source_target_pairs={{0,12},{1,13},{2,14},{3,15},{4,8},{5,9},{6,10},{7,11},{8,4},{9,5},... | collective-permute-start | bytes 147464 | tf_op jit(solution)/shard_map/ppermute | solution.py:294
  92.2 1.7 %collective-permute-done.50.refs_1_ = bf16[12,8,256]{2,1,0:T(8,128)(2,1)S(1)} collective-permute-done((bf16[12,8,256]{2,1,0:T(8,128)(2,1)S(1)}, bf16[12,8,256]{2,1,0:T(8,128)(2,1)S(1)}, u32[]{:S(2)}, u32[]{:S(2)}) %collective-permute-start.50) | collective-permute-done | bytes 49184 | tf_op jit(solution)/shard_map/ppermute | solution.py:294
  104.9 1.7 %collective-permute-done.59.a3 = bf16[18,8,256]{2,1,0:T(8,128)(2,1)S(1)} collective-permute-done((bf16[18,8,256]{2,1,0:T(8,128)(2,1)S(1)}, bf16[18,8,256]{2,1,0:T(8,128)(2,1)S(1)}, u32[]{:S(2)}, u32[]{:S(2)}) %collective-permute-start.59) | collective-permute-done | bytes 73760 | tf_op jit(solution)/shard_map/ppermute | solution.py:294
  108.4 1.7 %collective-permute-start.61 = (bf16[12,8,256]{2,1,0:T(8,128)(2,1)S(1)}, bf16[12,8,256]{2,1,0:T(8,128)(2,1)S(1)}, u32[]{:S(2)}, u32[]{:S(2)}) collective-permute-start(bf16[12,8,256]{2,1,0:T(8,128)(2,1)S(1)} %get-tuple-element.208), channel_id=1, source_target_pairs={{0,12},{1,13},{2,14},{3,15},{4,8},{5,9},{6,10},{7,11},{8,4},{9,5},... | collective-permute-start | bytes 147464 | tf_op jit(solution)/shard_map/ppermute | solution.py:294
  111.4 2.8 %collective-permute-done.55.a2 = bf16[6,8,256]{2,1,0:T(8,128)(2,1)S(1)} collective-permute-done((bf16[6,8,256]{2,1,0:T(8,128)(2,1)S(1)}, bf16[6,8,256]{2,1,0:T(8,128)(2,1)S(1)}, u32[]{:S(2)}, u32[]{:S(2)}) %collective-permute-start.55) | collective-permute-done | bytes 24608 | tf_op jit(solution)/shard_map/ppermute | solution.py:294
  115.0 1.7 %collective-permute-start.63 = (bf16[12,8,256]{2,1,0:T(8,128)(2,1)S(1)}, bf16[12,8,256]{2,1,0:T(8,128)(2,1)S(1)}, u32[]{:S(2)}, u32[]{:S(2)}) collective-permute-start(bf16[12,8,256]{2,1,0:T(8,128)(2,1)S(1)} %get-tuple-element.217.refs_0_), channel_id=1, source_target_pairs={{0,4},{1,5},{2,6},{3,7},{4,0},{5,1},{6,2},{7,3},{8,12},{9,13},{10,... | collective-permute-start | bytes 147464 | tf_op jit(solution)/shard_map/ppermute | solution.py:294
  117.7 1.7 %collective-permute-start.67 = (bf16[12,8,256]{2,1,0:T(8,128)(2,1)S(1)}, bf16[12,8,256]{2,1,0:T(8,128)(2,1)S(1)}, u32[]{:S(2)}, u32[]{:S(2)}) collective-permute-start(bf16[12,8,256]{2,1,0:T(8,128)(2,1)S(1)} %get-tuple-element.217.refs_0_), channel_id=1, source_target_pairs={{0,12},{1,13},{2,14},{3,15},{4,8},{5,9},{6,10},{7,11},{8,4},{9,5},... | collective-permute-start | bytes 147464 | tf_op jit(solution)/shard_map/ppermute | solution.py:294
  (179 shorter events, 73.2 us)
Async XLA Ops:
  11.2 10.3 %collective-permute-start.3 = (bf16[6,8,256]{2,1,0:T(8,128)(2,1)S(1)}, bf16[6,8,256]{2,1,0:T(8,128)(2,1)S(1)}, u32[]{:S(2)}, u32[]{:S(2)}) collective-permute-start(bf16[6,8,256]{2,1,0:T(8,128)(2,1)S(1)} %get-tuple-element.125), channel_id=1, source_target_pairs={{0,1},{1,0},{2,3},{3,2},{4,5},{5,4},{6,7},{7,6},{8,9},{9,8},{10,11... | collective-permute-start | bytes 73736 | tf_op jit(solution)/shard_map/ppermute | solution.py:294
  15.7 9.8 %collective-permute-start.6 = (bf16[12,8,256]{2,1,0:T(8,128)(2,1)S(1)}, bf16[12,8,256]{2,1,0:T(8,128)(2,1)S(1)}, u32[]{:S(2)}, u32[]{:S(2)}) collective-permute-start(bf16[12,8,256]{2,1,0:T(8,128)(2,1)S(1)} %get-tuple-element.128), channel_id=1, source_target_pairs={{0,8},{1,9},{2,10},{3,11},{4,12},{5,13},{6,14},{7,15},{8,0},{9,1},... | collective-permute-start | bytes 147464 | tf_op jit(solution)/shard_map/ppermute | solution.py:294
  18.7 6.8 %collective-permute-start.7 = (bf16[12,8,256]{2,1,0:T(8,128)(2,1)S(1)}, bf16[12,8,256]{2,1,0:T(8,128)(2,1)S(1)}, u32[]{:S(2)}, u32[]{:S(2)}) collective-permute-start(bf16[12,8,256]{2,1,0:T(8,128)(2,1)S(1)} %get-tuple-element.129), channel_id=1, source_target_pairs={{0,12},{1,13},{2,14},{3,15},{4,8},{5,9},{6,10},{7,11},{8,4},{9,5},... | collective-permute-start | bytes 147464 | tf_op jit(solution)/shard_map/ppermute | solution.py:294
  27.5 6.2 %collective-permute-start.14 = (bf16[12,8,256]{2,1,0:T(8,128)(2,1)S(1)}, bf16[12,8,256]{2,1,0:T(8,128)(2,1)S(1)}, u32[]{:S(2)}, u32[]{:S(2)}) collective-permute-start(bf16[12,8,256]{2,1,0:T(8,128)(2,1)S(1)} %get-tuple-element.136.refs_0_), channel_id=1, source_target_pairs={{0,8},{1,9},{2,10},{3,11},{4,12},{5,13},{6,14},{7,15},{8,0},{9,1},... | collective-permute-start | bytes 147464 | tf_op jit(solution)/shard_map/ppermute | solution.py:294
  30.3 6.2 %collective-permute-start.10 = (bf16[12,8,256]{2,1,0:T(8,128)(2,1)S(1)}, bf16[12,8,256]{2,1,0:T(8,128)(2,1)S(1)}, u32[]{:S(2)}, u32[]{:S(2)}) collective-permute-start(bf16[12,8,256]{2,1,0:T(8,128)(2,1)S(1)} %get-tuple-element.138), channel_id=1, source_target_pairs={{0,1},{1,0},{2,3},{3,2},{4,5},{5,4},{6,7},{7,6},{8,9},{9,8},{10,11... | collective-permute-start | bytes 147464 | tf_op jit(solution)/shard_map/ppermute | solution.py:294
  30.4 6.7 %collective-permute-start.11 = (bf16[12,8,256]{2,1,0:T(8,128)(2,1)S(1)}, bf16[12,8,256]{2,1,0:T(8,128)(2,1)S(1)}, u32[]{:S(2)}, u32[]{:S(2)}) collective-permute-start(bf16[12,8,256]{2,1,0:T(8,128)(2,1)S(1)} %get-tuple-element.139), channel_id=1, source_target_pairs={{0,2},{1,3},{2,0},{3,1},{4,6},{5,7},{6,4},{7,5},{8,10},{9,11},{10,... | collective-permute-start | bytes 147464 | tf_op jit(solution)/shard_map/ppermute | solution.py:294
  44.9 7.4 %collective-permute-start.18 = (bf16[6,8,256]{2,1,0:T(8,128)(2,1)S(1)}, bf16[6,8,256]{2,1,0:T(8,128)(2,1)S(1)}, u32[]{:S(2)}, u32[]{:S(2)}) collective-permute-start(bf16[6,8,256]{2,1,0:T(8,128)(2,1)S(1)} %get-tuple-element.148), channel_id=1, source_target_pairs={{0,1},{1,0},{2,3},{3,2},{4,5},{5,4},{6,7},{7,6},{8,9},{9,8},{10,11... | collective-permute-start | bytes 73736 | tf_op jit(solution)/shard_map/ppermute | solution.py:294
  47.6 8.1 %collective-permute-start.24 = (bf16[12,8,256]{2,1,0:T(8,128)(2,1)S(1)}, bf16[12,8,256]{2,1,0:T(8,128)(2,1)S(1)}, u32[]{:S(2)}, u32[]{:S(2)}) collective-permute-start(bf16[12,8,256]{2,1,0:T(8,128)(2,1)S(1)} %get-tuple-element.155), channel_id=1, source_target_pairs={{0,8},{1,9},{2,10},{3,11},{4,12},{5,13},{6,14},{7,15},{8,0},{9,1},... | collective-permute-start | bytes 147464 | tf_op jit(solution)/shard_map/ppermute | solution.py:294
  49.9 6.1 %collective-permute-start.25 = (bf16[12,8,256]{2,1,0:T(8,128)(2,1)S(1)}, bf16[12,8,256]{2,1,0:T(8,128)(2,1)S(1)}, u32[]{:S(2)}, u32[]{:S(2)}) collective-permute-start(bf16[12,8,256]{2,1,0:T(8,128)(2,1)S(1)} %get-tuple-element.156), channel_id=1, source_target_pairs={{0,12},{1,13},{2,14},{3,15},{4,8},{5,9},{6,10},{7,11},{8,4},{9,5},... | collective-permute-start | bytes 147464 | tf_op jit(solution)/shard_map/ppermute | solution.py:294
  57.9 7.1 %collective-permute-start.32 = (bf16[12,8,256]{2,1,0:T(8,128)(2,1)S(1)}, bf16[12,8,256]{2,1,0:T(8,128)(2,1)S(1)}, u32[]{:S(2)}, u32[]{:S(2)}) collective-permute-start(bf16[12,8,256]{2,1,0:T(8,128)(2,1)S(1)} %get-tuple-element.162.refs_0_), channel_id=1, source_target_pairs={{0,8},{1,9},{2,10},{3,11},{4,12},{5,13},{6,14},{7,15},{8,0},{9,1},... | collective-permute-start | bytes 147464 | tf_op jit(solution)/shard_map/ppermute | solution.py:294
  59.0 6.0 %collective-permute-start.31 = (bf16[12,8,256]{2,1,0:T(8,128)(2,1)S(1)}, bf16[12,8,256]{2,1,0:T(8,128)(2,1)S(1)}, u32[]{:S(2)}, u32[]{:S(2)}) collective-permute-start(bf16[12,8,256]{2,1,0:T(8,128)(2,1)S(1)} %get-tuple-element.162.refs_0_), channel_id=1, source_target_pairs={{0,12},{1,13},{2,14},{3,15},{4,8},{5,9},{6,10},{7,11},{8,4},{9,5},... | collective-permute-start | bytes 147464 | tf_op jit(solution)/shard_map/ppermute | solution.py:294
  60.8 6.2 %collective-permute-start.29 = (bf16[12,8,256]{2,1,0:T(8,128)(2,1)S(1)}, bf16[12,8,256]{2,1,0:T(8,128)(2,1)S(1)}, u32[]{:S(2)}, u32[]{:S(2)}) collective-permute-start(bf16[12,8,256]{2,1,0:T(8,128)(2,1)S(1)} %get-tuple-element.165), channel_id=1, source_target_pairs={{0,2},{1,3},{2,0},{3,1},{4,6},{5,7},{6,4},{7,5},{8,10},{9,11},{10,... | collective-permute-start | bytes 147464 | tf_op jit(solution)/shard_map/ppermute | solution.py:294
  74.7 7.1 %collective-permute-start.36 = (bf16[6,8,256]{2,1,0:T(8,128)(2,1)S(1)}, bf16[6,8,256]{2,1,0:T(8,128)(2,1)S(1)}, u32[]{:S(2)}, u32[]{:S(2)}) collective-permute-start(bf16[6,8,256]{2,1,0:T(8,128)(2,1)S(1)} %get-tuple-element.174), channel_id=1, source_target_pairs={{0,1},{1,0},{2,3},{3,2},{4,5},{5,4},{6,7},{7,6},{8,9},{9,8},{10,11... | collective-permute-start | bytes 73736 | tf_op jit(solution)/shard_map/ppermute | solution.py:294
  77.3 8.0 %collective-permute-start.42 = (bf16[12,8,256]{2,1,0:T(8,128)(2,1)S(1)}, bf16[12,8,256]{2,1,0:T(8,128)(2,1)S(1)}, u32[]{:S(2)}, u32[]{:S(2)}) collective-permute-start(bf16[12,8,256]{2,1,0:T(8,128)(2,1)S(1)} %get-tuple-element.181), channel_id=1, source_target_pairs={{0,8},{1,9},{2,10},{3,11},{4,12},{5,13},{6,14},{7,15},{8,0},{9,1},... | collective-permute-start | bytes 147464 | tf_op jit(solution)/shard_map/ppermute | solution.py:294
  79.2 6.2 %collective-permute-start.43 = (bf16[12,8,256]{2,1,0:T(8,128)(2,1)S(1)}, bf16[12,8,256]{2,1,0:T(8,128)(2,1)S(1)}, u32[]{:S(2)}, u32[]{:S(2)}) collective-permute-start(bf16[12,8,256]{2,1,0:T(8,128)(2,1)S(1)} %get-tuple-element.182), channel_id=1, source_target_pairs={{0,12},{1,13},{2,14},{3,15},{4,8},{5,9},{6,10},{7,11},{8,4},{9,5},... | collective-permute-start | bytes 147464 | tf_op jit(solution)/shard_map/ppermute | solution.py:294
  87.4 6.5 %collective-permute-start.50 = (bf16[12,8,256]{2,1,0:T(8,128)(2,1)S(1)}, bf16[12,8,256]{2,1,0:T(8,128)(2,1)S(1)}, u32[]{:S(2)}, u32[]{:S(2)}) collective-permute-start(bf16[12,8,256]{2,1,0:T(8,128)(2,1)S(1)} %get-tuple-element.188.refs_0_), channel_id=1, source_target_pairs={{0,8},{1,9},{2,10},{3,11},{4,12},{5,13},{6,14},{7,15},{8,0},{9,1},... | collective-permute-start | bytes 147464 | tf_op jit(solution)/shard_map/ppermute | solution.py:294
  88.5 6.0 %collective-permute-start.49 = (bf16[12,8,256]{2,1,0:T(8,128)(2,1)S(1)}, bf16[12,8,256]{2,1,0:T(8,128)(2,1)S(1)}, u32[]{:S(2)}, u32[]{:S(2)}) collective-permute-start(bf16[12,8,256]{2,1,0:T(8,128)(2,1)S(1)} %get-tuple-element.188.refs_0_), channel_id=1, source_target_pairs={{0,12},{1,13},{2,14},{3,15},{4,8},{5,9},{6,10},{7,11},{8,4},{9,5},... | collective-permute-start | bytes 147464 | tf_op jit(solution)/shard_map/ppermute | solution.py:294
  90.4 6.1 %collective-permute-start.47 = (bf16[12,8,256]{2,1,0:T(8,128)(2,1)S(1)}, bf16[12,8,256]{2,1,0:T(8,128)(2,1)S(1)}, u32[]{:S(2)}, u32[]{:S(2)}) collective-permute-start(bf16[12,8,256]{2,1,0:T(8,128)(2,1)S(1)} %get-tuple-element.191), channel_id=1, source_target_pairs={{0,2},{1,3},{2,0},{3,1},{4,6},{5,7},{6,4},{7,5},{8,10},{9,11},{10,... | collective-permute-start | bytes 147464 | tf_op jit(solution)/shard_map/ppermute | solution.py:294
  104.2 7.1 %collective-permute-start.54 = (bf16[6,8,256]{2,1,0:T(8,128)(2,1)S(1)}, bf16[6,8,256]{2,1,0:T(8,128)(2,1)S(1)}, u32[]{:S(2)}, u32[]{:S(2)}) collective-permute-start(bf16[6,8,256]{2,1,0:T(8,128)(2,1)S(1)} %get-tuple-element.200), channel_id=1, source_target_pairs={{0,1},{1,0},{2,3},{3,2},{4,5},{5,4},{6,7},{7,6},{8,9},{9,8},{10,11... | collective-permute-start | bytes 73736 | tf_op jit(solution)/shard_map/ppermute | solution.py:294
  106.8 8.0 %collective-permute-start.60 = (bf16[12,8,256]{2,1,0:T(8,128)(2,1)S(1)}, bf16[12,8,256]{2,1,0:T(8,128)(2,1)S(1)}, u32[]{:S(2)}, u32[]{:S(2)}) collective-permute-start(bf16[12,8,256]{2,1,0:T(8,128)(2,1)S(1)} %get-tuple-element.207), channel_id=1, source_target_pairs={{0,8},{1,9},{2,10},{3,11},{4,12},{5,13},{6,14},{7,15},{8,0},{9,1},... | collective-permute-start | bytes 147464 | tf_op jit(solution)/shard_map/ppermute | solution.py:294
  108.4 6.4 %collective-permute-start.61 = (bf16[12,8,256]{2,1,0:T(8,128)(2,1)S(1)}, bf16[12,8,256]{2,1,0:T(8,128)(2,1)S(1)}, u32[]{:S(2)}, u32[]{:S(2)}) collective-permute-start(bf16[12,8,256]{2,1,0:T(8,128)(2,1)S(1)} %get-tuple-element.208), channel_id=1, source_target_pairs={{0,12},{1,13},{2,14},{3,15},{4,8},{5,9},{6,10},{7,11},{8,4},{9,5},... | collective-permute-start | bytes 147464 | tf_op jit(solution)/shard_map/ppermute | solution.py:294
  116.8 6.4 %collective-permute-start.68 = (bf16[12,8,256]{2,1,0:T(8,128)(2,1)S(1)}, bf16[12,8,256]{2,1,0:T(8,128)(2,1)S(1)}, u32[]{:S(2)}, u32[]{:S(2)}) collective-permute-start(bf16[12,8,256]{2,1,0:T(8,128)(2,1)S(1)} %get-tuple-element.217.refs_0_), channel_id=1, source_target_pairs={{0,8},{1,9},{2,10},{3,11},{4,12},{5,13},{6,14},{7,15},{8,0},{9,1},... | collective-permute-start | bytes 147464 | tf_op jit(solution)/shard_map/ppermute | solution.py:294
  119.6 7.5 %collective-permute-start.65 = (bf16[12,8,256]{2,1,0:T(8,128)(2,1)S(1)}, bf16[12,8,256]{2,1,0:T(8,128)(2,1)S(1)}, u32[]{:S(2)}, u32[]{:S(2)}) collective-permute-start(bf16[12,8,256]{2,1,0:T(8,128)(2,1)S(1)} %get-tuple-element.220), channel_id=1, source_target_pairs={{0,2},{1,3},{2,0},{3,1},{4,6},{5,7},{6,4},{7,5},{8,10},{9,11},{10,... | collective-permute-start | bytes 147464 | tf_op jit(solution)/shard_map/ppermute | solution.py:294
  120.8 6.3 %collective-permute-start.66 = (bf16[12,8,256]{2,1,0:T(8,128)(2,1)S(1)}, bf16[12,8,256]{2,1,0:T(8,128)(2,1)S(1)}, u32[]{:S(2)}, u32[]{:S(2)}) collective-permute-start(bf16[12,8,256]{2,1,0:T(8,128)(2,1)S(1)} %get-tuple-element.221), channel_id=1, source_target_pairs={{0,3},{1,2},{2,1},{3,0},{4,7},{5,6},{6,5},{7,4},{8,11},{9,10},{10,... | collective-permute-start | bytes 147464 | tf_op jit(solution)/shard_map/ppermute | solution.py:294
  (53 other events, 222.2 us)

commit v12 on v10

--- a/solution.py
+++ b/solution.py
@@ -142,8 +142,8 @@
     lax.fori_loop(0, held.shape[0] // CHUNK, one_chunk, 0)
 
 
-def near_product_kernel(tile_of, row_of, held, hb, o0, o1, o2, o3):
-    transpose_products(tile_of.shape[0] // 2, tile_of, row_of, held, hb, (o0, o1, o2, o3))
+def across_product_kernel(tile_of, row_of, held, hb, o2):
+    transpose_products(tile_of.shape[0] // 2, tile_of, row_of, held, hb, (o2,), (2,))
 
 
 def map_kernel(a0, a1, a2, a3, wants, whole, sem):
@@ -223,8 +223,8 @@
         out[r] = part[r] + gathered(totals, r)
 
 
-def rest_product_kernel(tile_of, row_of, held, hb, o0, o1, o3):
-    transpose_products(0, tile_of, row_of, held, hb, (o3, o1, o0), (3, 1, 0))
+def rest_product_kernel(base, tile_of, row_of, held, hb, o0, o1, o3):
+    transpose_products(base, tile_of, row_of, held, hb, (o3, o1, o0), (3, 1, 0))
 
 
 def middle_kernel(step, tile_of, row_of, land_of, held, turned, dual_step, dual_mask, part, dy, m2, m3,
@@ -316,8 +316,12 @@
     near_highs, far_highs = tuple(range(half)), tuple(reversed(range(half, group)))
     while True:
         far_got = near_swaps(far_parts)
-        near_parts = call(near_product_kernel, "near_product", tile_bytes // 2, [SM] * 2 + [VM] * 2, part_set,
-                          (tile_of, row_of, held, hb))
+        across = call(across_product_kernel, "near_across", tile_bytes // 8, [SM] * 2 + [VM] * 2, part_set[0],
+                      (tile_of, row_of, held, hb))
+        later_hb, across = lax.optimization_barrier((hb, across))
+        own, beside, aslant = call(functools.partial(rest_product_kernel, slots // 2), "near_rest", tile_bytes // 4,
+                                   [SM] * 2 + [VM] * 2, part_set[:3], (tile_of, row_of, held, later_hb))
+        near_parts = [own, beside, across, aslant]
         near_got = near_swaps(near_parts)
         if wants is None:
             wants = pl.pallas_call(
@@ -360,8 +364,9 @@
             (y_shape, hb_set, part_set[0]),
             (tile_of, row_of, land_of, held, turned, dual_step, dual_mask, part, dy, *far_moved[2:]), row_totals)
         rhs = call(settle_dual_kernel, "settle_dual", 1 << 20, [VM] * 3, y_shape, (dual_step, dy, rhs))
-        own, beside, aslant = call(rest_product_kernel, "rest_product", tile_bytes // 4, [SM] * 2 + [VM] * 2,
+        own, beside, aslant = call(functools.partial(rest_product_kernel, 0), "rest_product", tile_bytes // 4, [SM] * 2 + [VM] * 2,
                                    part_set[:3], (tile_of, row_of, held, hb))
+        hb, own = lax.optimization_barrier((hb, own))
         far_parts = [own, beside, across, aslant]
     y_state = call(last_kernel, "last", tile_bytes // 4, [SM] * 2 + [VM] * 5, y_shape,
                    (tile_of, land_of, turned, part, dy, *far_moved[2:]), row_totals)

time: 122 us -> 128 us (1.049)
  starting transfers between devices: 63.2 us -> 66.8 us
  waiting for transfers between devices: 28.1 us -> 29.5 us
    ppermute x72, starting transfers between devices: 63.2 us -> 66.8 us  [swap(): return lax.ppermute(array, 'rb', [(p, p ^ x) for p in range(peers)])]
    ppermute x72, waiting for transfers between devices: 28.1 us -> 29.5 us  [swap(): return lax.ppermute(array, 'rb', [(p, p ^ x) for p in range(peers)])]
    pallas_call x47 -> x51, Pallas kernels: 22.6 us -> 23.1 us  [call(): pl.pallas_call(kernel, out_shape=outs, in_specs=ins, out_specs=jax.tree.m...]
  transfers between devices with their start and end apart: 72 -> 72, of which waited for: 29 -> 30; matrix products, arithmetic and copies ran while one was open for 0% -> 0% of each run, Pallas kernels for 16% -> 14%
where the time goes in v12:
time: 128 us
  starting transfers between devices  66.8 us (52%)
  Pallas kernels  29.5 us (23%)
  waiting for transfers between devices  29.5 us (23%)
  between operations  1.77 us (1%)
    ppermute x72, starting transfers between devices, swap(): return lax.ppermute(array, 'rb', [(p, p ^ x) for p in range(peers)])  66.8 us
    ppermute x72, waiting for transfers between devices, swap(): return lax.ppermute(array, 'rb', [(p, p ^ x) for p in range(peers)])  29.5 us
    pallas_call x51, Pallas kernels, call(): pl.pallas_call(kernel, out_shape=outs, in_specs=ins, out_specs=jax.tree.m...  23.1 us
    pallas_call x1, Pallas kernels, on_device(): pl.pallas_call(functools.partial(start_kernel, step, peers, cap, col_bloc...  5.8 us
  transfers between devices with their start and end apart: 72, of which 30 were waited for; matrix products, arithmetic and copies ran while one was open for 0% of the time, Pallas kernels for 14%

profile of v12, /device:TPU:0, one launch (start us, length us, event | category | flops | bytes accessed | tf_op | source)
XLA Modules:
  0.0 127.6 jit_solution(15273936105099652944)
XLA Ops:
  1.3 5.8 %start.1 = (bf16[88,256,256]{2,1,0:T(8,128)(2,1)S(1)}, f32[8,2048]{1,0:T(8,128)S(1)}, f32[8,2048]{1,0:T(8,128)S(1)}, bf16[8,8,256]{2,1,0:T(8,128)(2,1)S(1)}, s32...) custom-call(s32[1]{0:T(128)S(6)} %copy.14.count, ...), custom_call_target="tpu_custom_call" | custom-call | flops 184549376 | bytes 23068672 | tf_op jit(solution)/shard_map/start/pallas_call | solution.py:294
  7.6 2.6 %collective-permute-start.1 = (bf16[13,8,256]{2,1,0:T(8,128)(2,1)S(1)}, bf16[13,8,256]{2,1,0:T(8,128)(2,1)S(1)}, u32[]{:S(2)}, u32[]{:S(2)}) collective-permute-start(bf16[13,8,256]{2,1,0:T(8,128)(2,1)S(1)} %get-tuple-element.133), channel_id=1, source_target_pairs={{0,2},{1,3},{2,0},{3,1},{4,6},{5,7},{6,4},{7,5},{8,10},{9,11},{10,... | collective-permute-start | bytes 159752 | tf_op jit(solution)/shard_map/ppermute | solution.py:288
  10.6 1.7 %collective-permute-start.4 = (bf16[12,8,256]{2,1,0:T(8,128)(2,1)S(1)}, bf16[12,8,256]{2,1,0:T(8,128)(2,1)S(1)}, u32[]{:S(2)}, u32[]{:S(2)}) collective-permute-start(bf16[12,8,256]{2,1,0:T(8,128)(2,1)S(1)} %near_across.4), channel_id=1, source_target_pairs={{0,2},{1,3},{2,0},{3,1},{4,6},{5,7},{6,4},{7,5},{8,10},{9,11},{10,... | collective-permute-start | bytes 147464 | tf_op jit(solution)/shard_map/ppermute | solution.py:288
  14.7 2.7 %collective-permute-start.6 = (bf16[12,8,256]{2,1,0:T(8,128)(2,1)S(1)}, bf16[12,8,256]{2,1,0:T(8,128)(2,1)S(1)}, u32[]{:S(2)}, u32[]{:S(2)}) collective-permute-start(bf16[12,8,256]{2,1,0:T(8,128)(2,1)S(1)} %get-tuple-element.144), channel_id=1, source_target_pairs={{0,8},{1,9},{2,10},{3,11},{4,12},{5,13},{6,14},{7,15},{8,0},{9,1},... | collective-permute-start | bytes 147464 | tf_op jit(solution)/shard_map/ppermute | solution.py:288
  19.2 3.7 %turn.1.turned = bf16[88,256,256]{2,1,0:T(8,128)(2,1)S(1)} custom-call(bf16[88,256,256]{2,1,0:T(8,128)(2,1)S(1)} %get-tuple-element.129.held), custom_call_target="tpu_custom_call" | custom-call | flops 92274688 | bytes 11534336 | tf_op jit(solution)/shard_map/turn/pallas_call | solution.py:276
  24.9 2.3 %collective-permute-start.14 = (bf16[12,8,256]{2,1,0:T(8,128)(2,1)S(1)}, bf16[12,8,256]{2,1,0:T(8,128)(2,1)S(1)}, u32[]{:S(2)}, u32[]{:S(2)}) collective-permute-start(bf16[12,8,256]{2,1,0:T(8,128)(2,1)S(1)} %get-tuple-element.152.refs_0_), channel_id=1, source_target_pairs={{0,8},{1,9},{2,10},{3,11},{4,12},{5,13},{6,14},{7,15},{8,0},{9,1},... | collective-permute-start | bytes 147464 | tf_op jit(solution)/shard_map/ppermute | solution.py:288
  30.9 2.2 %collective-permute-done.13.refs_0_ = bf16[12,8,256]{2,1,0:T(8,128)(2,1)S(1)} collective-permute-done((bf16[12,8,256]{2,1,0:T(8,128)(2,1)S(1)}, bf16[12,8,256]{2,1,0:T(8,128)(2,1)S(1)}, u32[]{:S(2)}, u32[]{:S(2)}) %collective-permute-start.13) | collective-permute-done | bytes 49184 | tf_op jit(solution)/shard_map/ppermute | solution.py:288
  46.6 1.6 %collective-permute-start.25 = (bf16[12,8,256]{2,1,0:T(8,128)(2,1)S(1)}, bf16[12,8,256]{2,1,0:T(8,128)(2,1)S(1)}, u32[]{:S(2)}, u32[]{:S(2)}) collective-permute-start(bf16[12,8,256]{2,1,0:T(8,128)(2,1)S(1)} %get-tuple-element.176), channel_id=1, source_target_pairs={{0,12},{1,13},{2,14},{3,15},{4,8},{5,9},{6,10},{7,11},{8,4},{9,5},... | collective-permute-start | bytes 147464 | tf_op jit(solution)/shard_map/ppermute | solution.py:288
  49.7 2.4 %collective-permute-done.24.refs_1_ = bf16[12,8,256]{2,1,0:T(8,128)(2,1)S(1)} collective-permute-done((bf16[12,8,256]{2,1,0:T(8,128)(2,1)S(1)}, bf16[12,8,256]{2,1,0:T(8,128)(2,1)S(1)}, u32[]{:S(2)}, u32[]{:S(2)}) %collective-permute-start.24) | collective-permute-done | bytes 49184 | tf_op jit(solution)/shard_map/ppermute | solution.py:288
  54.1 1.9 %collective-permute-start.32 = (bf16[12,8,256]{2,1,0:T(8,128)(2,1)S(1)}, bf16[12,8,256]{2,1,0:T(8,128)(2,1)S(1)}, u32[]{:S(2)}, u32[]{:S(2)}) collective-permute-start(bf16[12,8,256]{2,1,0:T(8,128)(2,1)S(1)} %get-tuple-element.182.refs_0_), channel_id=1, source_target_pairs={{0,8},{1,9},{2,10},{3,11},{4,12},{5,13},{6,14},{7,15},{8,0},{9,1},... | collective-permute-start | bytes 147464 | tf_op jit(solution)/shard_map/ppermute | solution.py:288
  56.0 1.9 %collective-permute-start.31 = (bf16[12,8,256]{2,1,0:T(8,128)(2,1)S(1)}, bf16[12,8,256]{2,1,0:T(8,128)(2,1)S(1)}, u32[]{:S(2)}, u32[]{:S(2)}) collective-permute-start(bf16[12,8,256]{2,1,0:T(8,128)(2,1)S(1)} %get-tuple-element.182.refs_0_), channel_id=1, source_target_pairs={{0,12},{1,13},{2,14},{3,15},{4,8},{5,9},{6,10},{7,11},{8,4},{9,5},... | collective-permute-start | bytes 147464 | tf_op jit(solution)/shard_map/ppermute | solution.py:288
  60.1 1.7 %collective-permute-done.31.refs_0_ = bf16[12,8,256]{2,1,0:T(8,128)(2,1)S(1)} collective-permute-done((bf16[12,8,256]{2,1,0:T(8,128)(2,1)S(1)}, bf16[12,8,256]{2,1,0:T(8,128)(2,1)S(1)}, u32[]{:S(2)}, u32[]{:S(2)}) %collective-permute-start.31) | collective-permute-done | bytes 49184 | tf_op jit(solution)/shard_map/ppermute | solution.py:288
  74.9 1.9 %collective-permute-start.43 = (bf16[12,8,256]{2,1,0:T(8,128)(2,1)S(1)}, bf16[12,8,256]{2,1,0:T(8,128)(2,1)S(1)}, u32[]{:S(2)}, u32[]{:S(2)}) collective-permute-start(bf16[12,8,256]{2,1,0:T(8,128)(2,1)S(1)} %get-tuple-element.206), channel_id=1, source_target_pairs={{0,12},{1,13},{2,14},{3,15},{4,8},{5,9},{6,10},{7,11},{8,4},{9,5},... | collective-permute-start | bytes 147464 | tf_op jit(solution)/shard_map/ppermute | solution.py:288
  76.9 1.7 %collective-permute-start.44 = (bf16[12,8,256]{2,1,0:T(8,128)(2,1)S(1)}, bf16[12,8,256]{2,1,0:T(8,128)(2,1)S(1)}, u32[]{:S(2)}, u32[]{:S(2)}) collective-permute-start(bf16[12,8,256]{2,1,0:T(8,128)(2,1)S(1)} %get-tuple-element.207), channel_id=1, source_target_pairs={{0,4},{1,5},{2,6},{3,7},{4,0},{5,1},{6,2},{7,3},{8,12},{9,13},{10,... | collective-permute-start | bytes 147464 | tf_op jit(solution)/shard_map/ppermute | solution.py:288
  78.6 2.8 %collective-permute-done.42.refs_1_ = bf16[12,8,256]{2,1,0:T(8,128)(2,1)S(1)} collective-permute-done((bf16[12,8,256]{2,1,0:T(8,128)(2,1)S(1)}, bf16[12,8,256]{2,1,0:T(8,128)(2,1)S(1)}, u32[]{:S(2)}, u32[]{:S(2)}) %collective-permute-start.42) | collective-permute-done | bytes 49184 | tf_op jit(solution)/shard_map/ppermute | solution.py:288
  82.8 1.9 %collective-permute-start.50 = (bf16[12,8,256]{2,1,0:T(8,128)(2,1)S(1)}, bf16[12,8,256]{2,1,0:T(8,128)(2,1)S(1)}, u32[]{:S(2)}, u32[]{:S(2)}) collective-permute-start(bf16[12,8,256]{2,1,0:T(8,128)(2,1)S(1)} %get-tuple-element.212.refs_0_), channel_id=1, source_target_pairs={{0,8},{1,9},{2,10},{3,11},{4,12},{5,13},{6,14},{7,15},{8,0},{9,1},... | collective-permute-start | bytes 147464 | tf_op jit(solution)/shard_map/ppermute | solution.py:288
  84.7 1.9 %collective-permute-start.49 = (bf16[12,8,256]{2,1,0:T(8,128)(2,1)S(1)}, bf16[12,8,256]{2,1,0:T(8,128)(2,1)S(1)}, u32[]{:S(2)}, u32[]{:S(2)}) collective-permute-start(bf16[12,8,256]{2,1,0:T(8,128)(2,1)S(1)} %get-tuple-element.212.refs_0_), channel_id=1, source_target_pairs={{0,12},{1,13},{2,14},{3,15},{4,8},{5,9},{6,10},{7,11},{8,4},{9,5},... | collective-permute-start | bytes 147464 | tf_op jit(solution)/shard_map/ppermute | solution.py:288
  102.5 1.5 %collective-permute-done.55.a2 = bf16[12,8,256]{2,1,0:T(8,128)(2,1)S(1)} collective-permute-done((bf16[12,8,256]{2,1,0:T(8,128)(2,1)S(1)}, bf16[12,8,256]{2,1,0:T(8,128)(2,1)S(1)}, u32[]{:S(2)}, u32[]{:S(2)}) %collective-permute-start.55) | collective-permute-done | bytes 49184 | tf_op jit(solution)/shard_map/ppermute | solution.py:288
  105.2 1.8 %collective-permute-start.60 = (bf16[12,8,256]{2,1,0:T(8,128)(2,1)S(1)}, bf16[12,8,256]{2,1,0:T(8,128)(2,1)S(1)}, u32[]{:S(2)}, u32[]{:S(2)}) collective-permute-start(bf16[12,8,256]{2,1,0:T(8,128)(2,1)S(1)} %get-tuple-element.235), channel_id=1, source_target_pairs={{0,8},{1,9},{2,10},{3,11},{4,12},{5,13},{6,14},{7,15},{8,0},{9,1},... | collective-permute-start | bytes 147464 | tf_op jit(solution)/shard_map/ppermute | solution.py:288
  107.0 1.8 %collective-permute-start.61 = (bf16[12,8,256]{2,1,0:T(8,128)(2,1)S(1)}, bf16[12,8,256]{2,1,0:T(8,128)(2,1)S(1)}, u32[]{:S(2)}, u32[]{:S(2)}) collective-permute-start(bf16[12,8,256]{2,1,0:T(8,128)(2,1)S(1)} %get-tuple-element.236), channel_id=1, source_target_pairs={{0,12},{1,13},{2,14},{3,15},{4,8},{5,9},{6,10},{7,11},{8,4},{9,5},... | collective-permute-start | bytes 147464 | tf_op jit(solution)/shard_map/ppermute | solution.py:288
  108.8 2.8 %collective-permute-done.60.refs_1_ = bf16[12,8,256]{2,1,0:T(8,128)(2,1)S(1)} collective-permute-done((bf16[12,8,256]{2,1,0:T(8,128)(2,1)S(1)}, bf16[12,8,256]{2,1,0:T(8,128)(2,1)S(1)}, u32[]{:S(2)}, u32[]{:S(2)}) %collective-permute-start.60) | collective-permute-done | bytes 49184 | tf_op jit(solution)/shard_map/ppermute | solution.py:288
  113.1 2.4 %collective-permute-start.68 = (bf16[12,8,256]{2,1,0:T(8,128)(2,1)S(1)}, bf16[12,8,256]{2,1,0:T(8,128)(2,1)S(1)}, u32[]{:S(2)}, u32[]{:S(2)}) collective-permute-start(bf16[12,8,256]{2,1,0:T(8,128)(2,1)S(1)} %get-tuple-element.245.refs_0_), channel_id=1, source_target_pairs={{0,8},{1,9},{2,10},{3,11},{4,12},{5,13},{6,14},{7,15},{8,0},{9,1},... | collective-permute-start | bytes 147464 | tf_op jit(solution)/shard_map/ppermute | solution.py:288
  115.5 2.0 %collective-permute-start.67 = (bf16[12,8,256]{2,1,0:T(8,128)(2,1)S(1)}, bf16[12,8,256]{2,1,0:T(8,128)(2,1)S(1)}, u32[]{:S(2)}, u32[]{:S(2)}) collective-permute-start(bf16[12,8,256]{2,1,0:T(8,128)(2,1)S(1)} %get-tuple-element.245.refs_0_), channel_id=1, source_target_pairs={{0,12},{1,13},{2,14},{3,15},{4,8},{5,9},{6,10},{7,11},{8,4},{9,5},... | collective-permute-start | bytes 147464 | tf_op jit(solution)/shard_map/ppermute | solution.py:288
  119.6 1.8 %collective-permute-done.67.refs_0_ = bf16[12,8,256]{2,1,0:T(8,128)(2,1)S(1)} collective-permute-done((bf16[12,8,256]{2,1,0:T(8,128)(2,1)S(1)}, bf16[12,8,256]{2,1,0:T(8,128)(2,1)S(1)}, u32[]{:S(2)}, u32[]{:S(2)}) %collective-permute-start.67) | collective-permute-done | bytes 49184 | tf_op jit(solution)/shard_map/ppermute | solution.py:288
  (183 shorter events, 71.0 us)
Async XLA Ops:
  7.1 6.0 %collective-permute-start = (bf16[13,8,256]{2,1,0:T(8,128)(2,1)S(1)}, bf16[13,8,256]{2,1,0:T(8,128)(2,1)S(1)}, u32[]{:S(2)}, u32[]{:S(2)}) collective-permute-start(bf16[13,8,256]{2,1,0:T(8,128)(2,1)S(1)} %get-tuple-element.132), channel_id=1, source_target_pairs={{0,1},{1,0},{2,3},{3,2},{4,5},{5,4},{6,7},{7,6},{8,9},{9,8},{10,11... | collective-permute-start | bytes 159752 | tf_op jit(solution)/shard_map/ppermute | solution.py:288
  10.6 8.2 %collective-permute-start.4 = (bf16[12,8,256]{2,1,0:T(8,128)(2,1)S(1)}, bf16[12,8,256]{2,1,0:T(8,128)(2,1)S(1)}, u32[]{:S(2)}, u32[]{:S(2)}) collective-permute-start(bf16[12,8,256]{2,1,0:T(8,128)(2,1)S(1)} %near_across.4), channel_id=1, source_target_pairs={{0,2},{1,3},{2,0},{3,1},{4,6},{5,7},{6,4},{7,5},{8,10},{9,11},{10,... | collective-permute-start | bytes 147464 | tf_op jit(solution)/shard_map/ppermute | solution.py:288
  14.7 8.2 %collective-permute-start.6 = (bf16[12,8,256]{2,1,0:T(8,128)(2,1)S(1)}, bf16[12,8,256]{2,1,0:T(8,128)(2,1)S(1)}, u32[]{:S(2)}, u32[]{:S(2)}) collective-permute-start(bf16[12,8,256]{2,1,0:T(8,128)(2,1)S(1)} %get-tuple-element.144), channel_id=1, source_target_pairs={{0,8},{1,9},{2,10},{3,11},{4,12},{5,13},{6,14},{7,15},{8,0},{9,1},... | collective-permute-start | bytes 147464 | tf_op jit(solution)/shard_map/ppermute | solution.py:288
  17.4 6.3 %collective-permute-start.7 = (bf16[12,8,256]{2,1,0:T(8,128)(2,1)S(1)}, bf16[12,8,256]{2,1,0:T(8,128)(2,1)S(1)}, u32[]{:S(2)}, u32[]{:S(2)}) collective-permute-start(bf16[12,8,256]{2,1,0:T(8,128)(2,1)S(1)} %get-tuple-element.145), channel_id=1, source_target_pairs={{0,12},{1,13},{2,14},{3,15},{4,8},{5,9},{6,10},{7,11},{8,4},{9,5},... | collective-permute-start | bytes 147464 | tf_op jit(solution)/shard_map/ppermute | solution.py:288
  24.9 5.9 %collective-permute-start.14 = (bf16[12,8,256]{2,1,0:T(8,128)(2,1)S(1)}, bf16[12,8,256]{2,1,0:T(8,128)(2,1)S(1)}, u32[]{:S(2)}, u32[]{:S(2)}) collective-permute-start(bf16[12,8,256]{2,1,0:T(8,128)(2,1)S(1)} %get-tuple-element.152.refs_0_), channel_id=1, source_target_pairs={{0,8},{1,9},{2,10},{3,11},{4,12},{5,13},{6,14},{7,15},{8,0},{9,1},... | collective-permute-start | bytes 147464 | tf_op jit(solution)/shard_map/ppermute | solution.py:288
  27.2 5.9 %collective-permute-start.13 = (bf16[12,8,256]{2,1,0:T(8,128)(2,1)S(1)}, bf16[12,8,256]{2,1,0:T(8,128)(2,1)S(1)}, u32[]{:S(2)}, u32[]{:S(2)}) collective-permute-start(bf16[12,8,256]{2,1,0:T(8,128)(2,1)S(1)} %get-tuple-element.152.refs_0_), channel_id=1, source_target_pairs={{0,12},{1,13},{2,14},{3,15},{4,8},{5,9},{6,10},{7,11},{8,4},{9,5},... | collective-permute-start | bytes 147464 | tf_op jit(solution)/shard_map/ppermute | solution.py:288
  28.3 6.0 %collective-permute-start.10 = (bf16[12,8,256]{2,1,0:T(8,128)(2,1)S(1)}, bf16[12,8,256]{2,1,0:T(8,128)(2,1)S(1)}, u32[]{:S(2)}, u32[]{:S(2)}) collective-permute-start(bf16[12,8,256]{2,1,0:T(8,128)(2,1)S(1)} %get-tuple-element.154), channel_id=1, source_target_pairs={{0,1},{1,0},{2,3},{3,2},{4,5},{5,4},{6,7},{7,6},{8,9},{9,8},{10,11... | collective-permute-start | bytes 147464 | tf_op jit(solution)/shard_map/ppermute | solution.py:288
  28.4 6.7 %collective-permute-start.11 = (bf16[12,8,256]{2,1,0:T(8,128)(2,1)S(1)}, bf16[12,8,256]{2,1,0:T(8,128)(2,1)S(1)}, u32[]{:S(2)}, u32[]{:S(2)}) collective-permute-start(bf16[12,8,256]{2,1,0:T(8,128)(2,1)S(1)} %get-tuple-element.155), channel_id=1, source_target_pairs={{0,2},{1,3},{2,0},{3,1},{4,6},{5,7},{6,4},{7,5},{8,10},{9,11},{10,... | collective-permute-start | bytes 147464 | tf_op jit(solution)/shard_map/ppermute | solution.py:288
  41.1 7.0 %collective-permute-start.19 = (bf16[12,8,256]{2,1,0:T(8,128)(2,1)S(1)}, bf16[12,8,256]{2,1,0:T(8,128)(2,1)S(1)}, u32[]{:S(2)}, u32[]{:S(2)}) collective-permute-start(bf16[12,8,256]{2,1,0:T(8,128)(2,1)S(1)} %near_across.5), channel_id=1, source_target_pairs={{0,2},{1,3},{2,0},{3,1},{4,6},{5,7},{6,4},{7,5},{8,10},{9,11},{10,... | collective-permute-start | bytes 147464 | tf_op jit(solution)/shard_map/ppermute | solution.py:288
  45.9 6.2 %collective-permute-start.24 = (bf16[12,8,256]{2,1,0:T(8,128)(2,1)S(1)}, bf16[12,8,256]{2,1,0:T(8,128)(2,1)S(1)}, u32[]{:S(2)}, u32[]{:S(2)}) collective-permute-start(bf16[12,8,256]{2,1,0:T(8,128)(2,1)S(1)} %get-tuple-element.175), channel_id=1, source_target_pairs={{0,8},{1,9},{2,10},{3,11},{4,12},{5,13},{6,14},{7,15},{8,0},{9,1},... | collective-permute-start | bytes 147464 | tf_op jit(solution)/shard_map/ppermute | solution.py:288
  46.6 6.2 %collective-permute-start.25 = (bf16[12,8,256]{2,1,0:T(8,128)(2,1)S(1)}, bf16[12,8,256]{2,1,0:T(8,128)(2,1)S(1)}, u32[]{:S(2)}, u32[]{:S(2)}) collective-permute-start(bf16[12,8,256]{2,1,0:T(8,128)(2,1)S(1)} %get-tuple-element.176), channel_id=1, source_target_pairs={{0,12},{1,13},{2,14},{3,15},{4,8},{5,9},{6,10},{7,11},{8,4},{9,5},... | collective-permute-start | bytes 147464 | tf_op jit(solution)/shard_map/ppermute | solution.py:288
  54.1 6.1 %collective-permute-start.32 = (bf16[12,8,256]{2,1,0:T(8,128)(2,1)S(1)}, bf16[12,8,256]{2,1,0:T(8,128)(2,1)S(1)}, u32[]{:S(2)}, u32[]{:S(2)}) collective-permute-start(bf16[12,8,256]{2,1,0:T(8,128)(2,1)S(1)} %get-tuple-element.182.refs_0_), channel_id=1, source_target_pairs={{0,8},{1,9},{2,10},{3,11},{4,12},{5,13},{6,14},{7,15},{8,0},{9,1},... | collective-permute-start | bytes 147464 | tf_op jit(solution)/shard_map/ppermute | solution.py:288
  56.0 5.9 %collective-permute-start.31 = (bf16[12,8,256]{2,1,0:T(8,128)(2,1)S(1)}, bf16[12,8,256]{2,1,0:T(8,128)(2,1)S(1)}, u32[]{:S(2)}, u32[]{:S(2)}) collective-permute-start(bf16[12,8,256]{2,1,0:T(8,128)(2,1)S(1)} %get-tuple-element.182.refs_0_), channel_id=1, source_target_pairs={{0,12},{1,13},{2,14},{3,15},{4,8},{5,9},{6,10},{7,11},{8,4},{9,5},... | collective-permute-start | bytes 147464 | tf_op jit(solution)/shard_map/ppermute | solution.py:288
  70.0 6.8 %collective-permute-start.37 = (bf16[12,8,256]{2,1,0:T(8,128)(2,1)S(1)}, bf16[12,8,256]{2,1,0:T(8,128)(2,1)S(1)}, u32[]{:S(2)}, u32[]{:S(2)}) collective-permute-start(bf16[12,8,256]{2,1,0:T(8,128)(2,1)S(1)} %near_across.6), channel_id=1, source_target_pairs={{0,2},{1,3},{2,0},{3,1},{4,6},{5,7},{6,4},{7,5},{8,10},{9,11},{10,... | collective-permute-start | bytes 147464 | tf_op jit(solution)/shard_map/ppermute | solution.py:288
  74.8 6.6 %collective-permute-start.42 = (bf16[12,8,256]{2,1,0:T(8,128)(2,1)S(1)}, bf16[12,8,256]{2,1,0:T(8,128)(2,1)S(1)}, u32[]{:S(2)}, u32[]{:S(2)}) collective-permute-start(bf16[12,8,256]{2,1,0:T(8,128)(2,1)S(1)} %get-tuple-element.205), channel_id=1, source_target_pairs={{0,8},{1,9},{2,10},{3,11},{4,12},{5,13},{6,14},{7,15},{8,0},{9,1},... | collective-permute-start | bytes 147464 | tf_op jit(solution)/shard_map/ppermute | solution.py:288
  74.9 6.5 %collective-permute-start.43 = (bf16[12,8,256]{2,1,0:T(8,128)(2,1)S(1)}, bf16[12,8,256]{2,1,0:T(8,128)(2,1)S(1)}, u32[]{:S(2)}, u32[]{:S(2)}) collective-permute-start(bf16[12,8,256]{2,1,0:T(8,128)(2,1)S(1)} %get-tuple-element.206), channel_id=1, source_target_pairs={{0,12},{1,13},{2,14},{3,15},{4,8},{5,9},{6,10},{7,11},{8,4},{9,5},... | collective-permute-start | bytes 147464 | tf_op jit(solution)/shard_map/ppermute | solution.py:288
  82.8 6.6 %collective-permute-start.50 = (bf16[12,8,256]{2,1,0:T(8,128)(2,1)S(1)}, bf16[12,8,256]{2,1,0:T(8,128)(2,1)S(1)}, u32[]{:S(2)}, u32[]{:S(2)}) collective-permute-start(bf16[12,8,256]{2,1,0:T(8,128)(2,1)S(1)} %get-tuple-element.212.refs_0_), channel_id=1, source_target_pairs={{0,8},{1,9},{2,10},{3,11},{4,12},{5,13},{6,14},{7,15},{8,0},{9,1},... | collective-permute-start | bytes 147464 | tf_op jit(solution)/shard_map/ppermute | solution.py:288
  84.7 5.9 %collective-permute-start.49 = (bf16[12,8,256]{2,1,0:T(8,128)(2,1)S(1)}, bf16[12,8,256]{2,1,0:T(8,128)(2,1)S(1)}, u32[]{:S(2)}, u32[]{:S(2)}) collective-permute-start(bf16[12,8,256]{2,1,0:T(8,128)(2,1)S(1)} %get-tuple-element.212.refs_0_), channel_id=1, source_target_pairs={{0,12},{1,13},{2,14},{3,15},{4,8},{5,9},{6,10},{7,11},{8,4},{9,5},... | collective-permute-start | bytes 147464 | tf_op jit(solution)/shard_map/ppermute | solution.py:288
  105.2 6.5 %collective-permute-start.60 = (bf16[12,8,256]{2,1,0:T(8,128)(2,1)S(1)}, bf16[12,8,256]{2,1,0:T(8,128)(2,1)S(1)}, u32[]{:S(2)}, u32[]{:S(2)}) collective-permute-start(bf16[12,8,256]{2,1,0:T(8,128)(2,1)S(1)} %get-tuple-element.235), channel_id=1, source_target_pairs={{0,8},{1,9},{2,10},{3,11},{4,12},{5,13},{6,14},{7,15},{8,0},{9,1},... | collective-permute-start | bytes 147464 | tf_op jit(solution)/shard_map/ppermute | solution.py:288
  107.0 5.9 %collective-permute-start.61 = (bf16[12,8,256]{2,1,0:T(8,128)(2,1)S(1)}, bf16[12,8,256]{2,1,0:T(8,128)(2,1)S(1)}, u32[]{:S(2)}, u32[]{:S(2)}) collective-permute-start(bf16[12,8,256]{2,1,0:T(8,128)(2,1)S(1)} %get-tuple-element.236), channel_id=1, source_target_pairs={{0,12},{1,13},{2,14},{3,15},{4,8},{5,9},{6,10},{7,11},{8,4},{9,5},... | collective-permute-start | bytes 147464 | tf_op jit(solution)/shard_map/ppermute | solution.py:288
  113.1 6.5 %collective-permute-start.68 = (bf16[12,8,256]{2,1,0:T(8,128)(2,1)S(1)}, bf16[12,8,256]{2,1,0:T(8,128)(2,1)S(1)}, u32[]{:S(2)}, u32[]{:S(2)}) collective-permute-start(bf16[12,8,256]{2,1,0:T(8,128)(2,1)S(1)} %get-tuple-element.245.refs_0_), channel_id=1, source_target_pairs={{0,8},{1,9},{2,10},{3,11},{4,12},{5,13},{6,14},{7,15},{8,0},{9,1},... | collective-permute-start | bytes 147464 | tf_op jit(solution)/shard_map/ppermute | solution.py:288
  115.5 5.9 %collective-permute-start.67 = (bf16[12,8,256]{2,1,0:T(8,128)(2,1)S(1)}, bf16[12,8,256]{2,1,0:T(8,128)(2,1)S(1)}, u32[]{:S(2)}, u32[]{:S(2)}) collective-permute-start(bf16[12,8,256]{2,1,0:T(8,128)(2,1)S(1)} %get-tuple-element.245.refs_0_), channel_id=1, source_target_pairs={{0,12},{1,13},{2,14},{3,15},{4,8},{5,9},{6,10},{7,11},{8,4},{9,5},... | collective-permute-start | bytes 147464 | tf_op jit(solution)/shard_map/ppermute | solution.py:288
  117.7 7.0 %collective-permute-start.65 = (bf16[12,8,256]{2,1,0:T(8,128)(2,1)S(1)}, bf16[12,8,256]{2,1,0:T(8,128)(2,1)S(1)}, u32[]{:S(2)}, u32[]{:S(2)}) collective-permute-start(bf16[12,8,256]{2,1,0:T(8,128)(2,1)S(1)} %get-tuple-element.248), channel_id=1, source_target_pairs={{0,2},{1,3},{2,0},{3,1},{4,6},{5,7},{6,4},{7,5},{8,10},{9,11},{10,... | collective-permute-start | bytes 147464 | tf_op jit(solution)/shard_map/ppermute | solution.py:288
  118.5 6.2 %collective-permute-start.66 = (bf16[12,8,256]{2,1,0:T(8,128)(2,1)S(1)}, bf16[12,8,256]{2,1,0:T(8,128)(2,1)S(1)}, u32[]{:S(2)}, u32[]{:S(2)}) collective-permute-start(bf16[12,8,256]{2,1,0:T(8,128)(2,1)S(1)} %get-tuple-element.249), channel_id=1, source_target_pairs={{0,3},{1,2},{2,1},{3,0},{4,7},{5,6},{6,5},{7,4},{8,11},{9,10},{10,... | collective-permute-start | bytes 147464 | tf_op jit(solution)/shard_map/ppermute | solution.py:288
  (53 other events, 228.5 us)

commit v13 on v10

--- a/solution.py
+++ b/solution.py
@@ -217,8 +217,9 @@
         out[r] = gathered(totals, r)
 
 
-def chip_forward_kernel(tile_of, land_of, turned, part, m0, m1, out, *totals):
-    forward_products(0, tile_of, land_of, turned, (m0, m1), totals, (0, 1))
+def far_forward_kernel(xs, tile_of, land_of, turned, part, *refs):
+    moved, out, totals = refs[:len(xs)], refs[len(xs)], refs[len(xs) + 1:]
+    forward_products(0, tile_of, land_of, turned, moved, totals, xs)
     for r in range(out.shape[0]):
         out[r] = part[r] + gathered(totals, r)
 
@@ -227,10 +228,10 @@
     transpose_products(0, tile_of, row_of, held, hb, (o3, o1, o0), (3, 1, 0))
 
 
-def middle_kernel(step, tile_of, row_of, land_of, held, turned, dual_step, dual_mask, part, dy, m2, m3,
+def middle_kernel(step, tile_of, row_of, land_of, held, turned, dual_step, dual_mask, part, dy, m3,
                   new_dy, hb, o2, *totals):
     side = held.shape[1]
-    forward_products(0, tile_of, land_of, turned, (m2, m3), totals, (2, 3))
+    forward_products(0, tile_of, land_of, turned, (m3,), totals, (3,))
     for r in range(hb.shape[0]):
         at = pl.ds(r * side, side)
         v = part[r] + gathered(totals, r)
@@ -240,9 +241,9 @@
     transpose_products(0, tile_of, row_of, held, hb, (o2,), (2,))
 
 
-def last_kernel(tile_of, land_of, turned, part, dy, m2, m3, new_y, *totals):
+def last_kernel(tile_of, land_of, turned, part, dy, m3, new_y, *totals):
     side = turned.shape[1]
-    forward_products(0, tile_of, land_of, turned, (m2, m3), totals, (2, 3))
+    forward_products(0, tile_of, land_of, turned, (m3,), totals, (3,))
     for r in range(part.shape[0]):
         at = pl.ds(r * side, side)
         new_y[:, at] = dy[:, at] - (part[r] + gathered(totals, r))
@@ -350,21 +351,23 @@
         )
         part = call(near_forward_kernel, "near_forward", tile_bytes // 2, [SM] * 2 + [VM] * (1 + QUAD),
                     shape(hb_set.shape, F32), (tile_of, land_of, turned, *near_moved), row_totals)
-        part = call(chip_forward_kernel, "chip_forward", tile_bytes // 4, [SM] * 2 + [VM] * 4,
-                    shape(hb_set.shape, F32), (tile_of, land_of, turned, part, *far_moved[:2]), row_totals)
+        for name, xs in (("chip_forward", (0, 1)), ("across_forward", (2,))):
+            part = call(functools.partial(far_forward_kernel, xs), name, tile_bytes // 8 * len(xs),
+                        [SM] * 2 + [VM] * (2 + len(xs)), shape(hb_set.shape, F32),
+                        (tile_of, land_of, turned, part, *(far_moved[x] for x in xs)), row_totals)
         if step == 0:
             break
         step -= 1
         dy, hb, across = call(
-            functools.partial(middle_kernel, step), "middle", tile_bytes // 2, [SM] * 3 + [VM] * 8,
+            functools.partial(middle_kernel, step), "middle", tile_bytes // 4, [SM] * 3 + [VM] * 7,
             (y_shape, hb_set, part_set[0]),
-            (tile_of, row_of, land_of, held, turned, dual_step, dual_mask, part, dy, *far_moved[2:]), row_totals)
+            (tile_of, row_of, land_of, held, turned, dual_step, dual_mask, part, dy, far_moved[3]), row_totals)
         rhs = call(settle_dual_kernel, "settle_dual", 1 << 20, [VM] * 3, y_shape, (dual_step, dy, rhs))
         own, beside, aslant = call(rest_product_kernel, "rest_product", tile_bytes // 4, [SM] * 2 + [VM] * 2,
                                    part_set[:3], (tile_of, row_of, held, hb))
         far_parts = [own, beside, across, aslant]
-    y_state = call(last_kernel, "last", tile_bytes // 4, [SM] * 2 + [VM] * 5, y_shape,
-                   (tile_of, land_of, turned, part, dy, *far_moved[2:]), row_totals)
+    y_state = call(last_kernel, "last", tile_bytes // 8, [SM] * 2 + [VM] * 4, y_shape,
+                   (tile_of, land_of, turned, part, dy, far_moved[3]), row_totals)
     return spent, rhs, x_state, y_state
 
 

time: 122 us -> 122 us (level)
    pallas_call x47 -> x51, Pallas kernels: 22.6 us -> 23 us  [call(): pl.pallas_call(kernel, out_shape=outs, in_specs=ins, out_specs=jax.tree.m...]
  transfers between devices with their start and end apart: 72 -> 72, of which waited for: 29 -> 28; matrix products, arithmetic and copies ran while one was open for 0% -> 0% of each run, Pallas kernels for 16% -> 17%
where the time goes in v13:
time: 122 us
  starting transfers between devices  63.2 us (52%)
  Pallas kernels  29.5 us (24%)
  waiting for transfers between devices  27.1 us (22%)
  between operations  1.78 us (1%)
    ppermute x72, starting transfers between devices, swap(): return lax.ppermute(array, 'rb', [(p, p ^ x) for p in range(peers)])  63.2 us
    ppermute x72, waiting for transfers between devices, swap(): return lax.ppermute(array, 'rb', [(p, p ^ x) for p in range(peers)])  27.1 us
    pallas_call x51, Pallas kernels, call(): pl.pallas_call(kernel, out_shape=outs, in_specs=ins, out_specs=jax.tree.m...  23 us
    pallas_call x1, Pallas kernels, on_device(): pl.pallas_call(functools.partial(start_kernel, step, peers, cap, col_bloc...  5.8 us
  transfers between devices with their start and end apart: 72, of which 28 were waited for; matrix products, arithmetic and copies ran while one was open for 0% of the time, Pallas kernels for 17%

profile of v13, /device:TPU:0, one launch (start us, length us, event | category | flops | bytes accessed | tf_op | source)
XLA Modules:
  0.0 121.6 jit_solution(1446896434449691057)
XLA Ops:
  1.3 5.8 %start.1 = (bf16[88,256,256]{2,1,0:T(8,128)(2,1)S(1)}, f32[8,2048]{1,0:T(8,128)S(1)}, f32[8,2048]{1,0:T(8,128)S(1)}, bf16[8,8,256]{2,1,0:T(8,128)(2,1)S(1)}, s32...) custom-call(s32[1]{0:T(128)S(6)} %copy.14.count, ...), custom_call_target="tpu_custom_call" | custom-call | flops 184549376 | bytes 23068672 | tf_op jit(solution)/shard_map/start/pallas_call | solution.py:295
  7.6 2.6 %collective-permute-start.1 = (bf16[13,8,256]{2,1,0:T(8,128)(2,1)S(1)}, bf16[13,8,256]{2,1,0:T(8,128)(2,1)S(1)}, u32[]{:S(2)}, u32[]{:S(2)}) collective-permute-start(bf16[13,8,256]{2,1,0:T(8,128)(2,1)S(1)} %get-tuple-element.123), channel_id=1, source_target_pairs={{0,2},{1,3},{2,0},{3,1},{4,6},{5,7},{6,4},{7,5},{8,10},{9,11},{10,... | collective-permute-start | bytes 159752 | tf_op jit(solution)/shard_map/ppermute | solution.py:289
  11.3 1.9 %collective-permute-start.4 = (bf16[12,8,256]{2,1,0:T(8,128)(2,1)S(1)}, bf16[12,8,256]{2,1,0:T(8,128)(2,1)S(1)}, u32[]{:S(2)}, u32[]{:S(2)}) collective-permute-start(bf16[12,8,256]{2,1,0:T(8,128)(2,1)S(1)} %get-tuple-element.130), channel_id=1, source_target_pairs={{0,2},{1,3},{2,0},{3,1},{4,6},{5,7},{6,4},{7,5},{8,10},{9,11},{10,... | collective-permute-start | bytes 147464 | tf_op jit(solution)/shard_map/ppermute | solution.py:289
  14.7 2.6 %collective-permute-start.6 = (bf16[12,8,256]{2,1,0:T(8,128)(2,1)S(1)}, bf16[12,8,256]{2,1,0:T(8,128)(2,1)S(1)}, u32[]{:S(2)}, u32[]{:S(2)}) collective-permute-start(bf16[12,8,256]{2,1,0:T(8,128)(2,1)S(1)} %get-tuple-element.133), channel_id=1, source_target_pairs={{0,8},{1,9},{2,10},{3,11},{4,12},{5,13},{6,14},{7,15},{8,0},{9,1},... | collective-permute-start | bytes 147464 | tf_op jit(solution)/shard_map/ppermute | solution.py:289
  17.4 1.3 %collective-permute-start.7 = (bf16[12,8,256]{2,1,0:T(8,128)(2,1)S(1)}, bf16[12,8,256]{2,1,0:T(8,128)(2,1)S(1)}, u32[]{:S(2)}, u32[]{:S(2)}) collective-permute-start(bf16[12,8,256]{2,1,0:T(8,128)(2,1)S(1)} %get-tuple-element.134), channel_id=1, source_target_pairs={{0,12},{1,13},{2,14},{3,15},{4,8},{5,9},{6,10},{7,11},{8,4},{9,5},... | collective-permute-start | bytes 147464 | tf_op jit(solution)/shard_map/ppermute | solution.py:289
  19.2 3.7 %turn.1.turned = bf16[88,256,256]{2,1,0:T(8,128)(2,1)S(1)} custom-call(bf16[88,256,256]{2,1,0:T(8,128)(2,1)S(1)} %get-tuple-element.119.held), custom_call_target="tpu_custom_call" | custom-call | flops 92274688 | bytes 11534336 | tf_op jit(solution)/shard_map/turn/pallas_call | solution.py:277
  24.9 1.9 %collective-permute-start.14 = (bf16[12,8,256]{2,1,0:T(8,128)(2,1)S(1)}, bf16[12,8,256]{2,1,0:T(8,128)(2,1)S(1)}, u32[]{:S(2)}, u32[]{:S(2)}) collective-permute-start(bf16[12,8,256]{2,1,0:T(8,128)(2,1)S(1)} %get-tuple-element.141.refs_0_), channel_id=1, source_target_pairs={{0,8},{1,9},{2,10},{3,11},{4,12},{5,13},{6,14},{7,15},{8,0},{9,1},... | collective-permute-start | bytes 147464 | tf_op jit(solution)/shard_map/ppermute | solution.py:289
  30.5 2.3 %collective-permute-done.13.refs_0_ = bf16[12,8,256]{2,1,0:T(8,128)(2,1)S(1)} collective-permute-done((bf16[12,8,256]{2,1,0:T(8,128)(2,1)S(1)}, bf16[12,8,256]{2,1,0:T(8,128)(2,1)S(1)}, u32[]{:S(2)}, u32[]{:S(2)}) %collective-permute-start.13) | collective-permute-done | bytes 49184 | tf_op jit(solution)/shard_map/ppermute | solution.py:289
  32.9 1.3 %collective-permute-start.16 = (bf16[12,8,256]{2,1,0:T(8,128)(2,1)S(1)}, bf16[12,8,256]{2,1,0:T(8,128)(2,1)S(1)}, u32[]{:S(2)}, u32[]{:S(2)}) collective-permute-start(bf16[12,8,256]{2,1,0:T(8,128)(2,1)S(1)} %get-tuple-element.148), channel_id=1, source_target_pairs={{0,2},{1,3},{2,0},{3,1},{4,6},{5,7},{6,4},{7,5},{8,10},{9,11},{10,... | collective-permute-start | bytes 147464 | tf_op jit(solution)/shard_map/ppermute | solution.py:289
  48.2 2.3 %collective-permute-done.24.refs_1_ = bf16[12,8,256]{2,1,0:T(8,128)(2,1)S(1)} collective-permute-done((bf16[12,8,256]{2,1,0:T(8,128)(2,1)S(1)}, bf16[12,8,256]{2,1,0:T(8,128)(2,1)S(1)}, u32[]{:S(2)}, u32[]{:S(2)}) %collective-permute-start.24) | collective-permute-done | bytes 49184 | tf_op jit(solution)/shard_map/ppermute | solution.py:289
  52.4 2.0 %collective-permute-start.32 = (bf16[12,8,256]{2,1,0:T(8,128)(2,1)S(1)}, bf16[12,8,256]{2,1,0:T(8,128)(2,1)S(1)}, u32[]{:S(2)}, u32[]{:S(2)}) collective-permute-start(bf16[12,8,256]{2,1,0:T(8,128)(2,1)S(1)} %get-tuple-element.168.refs_0_), channel_id=1, source_target_pairs={{0,8},{1,9},{2,10},{3,11},{4,12},{5,13},{6,14},{7,15},{8,0},{9,1},... | collective-permute-start | bytes 147464 | tf_op jit(solution)/shard_map/ppermute | solution.py:289
  54.4 2.1 %collective-permute-start.31 = (bf16[12,8,256]{2,1,0:T(8,128)(2,1)S(1)}, bf16[12,8,256]{2,1,0:T(8,128)(2,1)S(1)}, u32[]{:S(2)}, u32[]{:S(2)}) collective-permute-start(bf16[12,8,256]{2,1,0:T(8,128)(2,1)S(1)} %get-tuple-element.168.refs_0_), channel_id=1, source_target_pairs={{0,12},{1,13},{2,14},{3,15},{4,8},{5,9},{6,10},{7,11},{8,4},{9,5},... | collective-permute-start | bytes 147464 | tf_op jit(solution)/shard_map/ppermute | solution.py:289
  58.5 1.8 %collective-permute-done.31.refs_0_ = bf16[12,8,256]{2,1,0:T(8,128)(2,1)S(1)} collective-permute-done((bf16[12,8,256]{2,1,0:T(8,128)(2,1)S(1)}, bf16[12,8,256]{2,1,0:T(8,128)(2,1)S(1)}, u32[]{:S(2)}, u32[]{:S(2)}) %collective-permute-start.31) | collective-permute-done | bytes 49184 | tf_op jit(solution)/shard_map/ppermute | solution.py:289
  72.0 2.1 %collective-permute-start.43 = (bf16[12,8,256]{2,1,0:T(8,128)(2,1)S(1)}, bf16[12,8,256]{2,1,0:T(8,128)(2,1)S(1)}, u32[]{:S(2)}, u32[]{:S(2)}) collective-permute-start(bf16[12,8,256]{2,1,0:T(8,128)(2,1)S(1)} %get-tuple-element.189), channel_id=1, source_target_pairs={{0,12},{1,13},{2,14},{3,15},{4,8},{5,9},{6,10},{7,11},{8,4},{9,5},... | collective-permute-start | bytes 147464 | tf_op jit(solution)/shard_map/ppermute | solution.py:289
  75.6 2.9 %collective-permute-done.42.refs_1_ = bf16[12,8,256]{2,1,0:T(8,128)(2,1)S(1)} collective-permute-done((bf16[12,8,256]{2,1,0:T(8,128)(2,1)S(1)}, bf16[12,8,256]{2,1,0:T(8,128)(2,1)S(1)}, u32[]{:S(2)}, u32[]{:S(2)}) %collective-permute-start.42) | collective-permute-done | bytes 49184 | tf_op jit(solution)/shard_map/ppermute | solution.py:289
  80.0 1.9 %collective-permute-start.50 = (bf16[12,8,256]{2,1,0:T(8,128)(2,1)S(1)}, bf16[12,8,256]{2,1,0:T(8,128)(2,1)S(1)}, u32[]{:S(2)}, u32[]{:S(2)}) collective-permute-start(bf16[12,8,256]{2,1,0:T(8,128)(2,1)S(1)} %get-tuple-element.195.refs_0_), channel_id=1, source_target_pairs={{0,8},{1,9},{2,10},{3,11},{4,12},{5,13},{6,14},{7,15},{8,0},{9,1},... | collective-permute-start | bytes 147464 | tf_op jit(solution)/shard_map/ppermute | solution.py:289
  81.9 1.9 %collective-permute-start.49 = (bf16[12,8,256]{2,1,0:T(8,128)(2,1)S(1)}, bf16[12,8,256]{2,1,0:T(8,128)(2,1)S(1)}, u32[]{:S(2)}, u32[]{:S(2)}) collective-permute-start(bf16[12,8,256]{2,1,0:T(8,128)(2,1)S(1)} %get-tuple-element.195.refs_0_), channel_id=1, source_target_pairs={{0,12},{1,13},{2,14},{3,15},{4,8},{5,9},{6,10},{7,11},{8,4},{9,5},... | collective-permute-start | bytes 147464 | tf_op jit(solution)/shard_map/ppermute | solution.py:289
  84.2 1.3 %collective-permute-start.47 = (bf16[12,8,256]{2,1,0:T(8,128)(2,1)S(1)}, bf16[12,8,256]{2,1,0:T(8,128)(2,1)S(1)}, u32[]{:S(2)}, u32[]{:S(2)}) collective-permute-start(bf16[12,8,256]{2,1,0:T(8,128)(2,1)S(1)} %get-tuple-element.198), channel_id=1, source_target_pairs={{0,2},{1,3},{2,0},{3,1},{4,6},{5,7},{6,4},{7,5},{8,10},{9,11},{10,... | collective-permute-start | bytes 147464 | tf_op jit(solution)/shard_map/ppermute | solution.py:289
  86.1 1.7 %collective-permute-done.49.refs_0_ = bf16[12,8,256]{2,1,0:T(8,128)(2,1)S(1)} collective-permute-done((bf16[12,8,256]{2,1,0:T(8,128)(2,1)S(1)}, bf16[12,8,256]{2,1,0:T(8,128)(2,1)S(1)}, u32[]{:S(2)}, u32[]{:S(2)}) %collective-permute-start.49) | collective-permute-done | bytes 49184 | tf_op jit(solution)/shard_map/ppermute | solution.py:289
  99.7 1.8 %collective-permute-start.61 = (bf16[12,8,256]{2,1,0:T(8,128)(2,1)S(1)}, bf16[12,8,256]{2,1,0:T(8,128)(2,1)S(1)}, u32[]{:S(2)}, u32[]{:S(2)}) collective-permute-start(bf16[12,8,256]{2,1,0:T(8,128)(2,1)S(1)} %get-tuple-element.216), channel_id=1, source_target_pairs={{0,12},{1,13},{2,14},{3,15},{4,8},{5,9},{6,10},{7,11},{8,4},{9,5},... | collective-permute-start | bytes 147464 | tf_op jit(solution)/shard_map/ppermute | solution.py:289
  103.2 2.9 %collective-permute-done.60.refs_1_ = bf16[12,8,256]{2,1,0:T(8,128)(2,1)S(1)} collective-permute-done((bf16[12,8,256]{2,1,0:T(8,128)(2,1)S(1)}, bf16[12,8,256]{2,1,0:T(8,128)(2,1)S(1)}, u32[]{:S(2)}, u32[]{:S(2)}) %collective-permute-start.60) | collective-permute-done | bytes 49184 | tf_op jit(solution)/shard_map/ppermute | solution.py:289
  107.5 2.0 %collective-permute-start.68 = (bf16[12,8,256]{2,1,0:T(8,128)(2,1)S(1)}, bf16[12,8,256]{2,1,0:T(8,128)(2,1)S(1)}, u32[]{:S(2)}, u32[]{:S(2)}) collective-permute-start(bf16[12,8,256]{2,1,0:T(8,128)(2,1)S(1)} %get-tuple-element.225.refs_0_), channel_id=1, source_target_pairs={{0,8},{1,9},{2,10},{3,11},{4,12},{5,13},{6,14},{7,15},{8,0},{9,1},... | collective-permute-start | bytes 147464 | tf_op jit(solution)/shard_map/ppermute | solution.py:289
  109.5 1.9 %collective-permute-start.67 = (bf16[12,8,256]{2,1,0:T(8,128)(2,1)S(1)}, bf16[12,8,256]{2,1,0:T(8,128)(2,1)S(1)}, u32[]{:S(2)}, u32[]{:S(2)}) collective-permute-start(bf16[12,8,256]{2,1,0:T(8,128)(2,1)S(1)} %get-tuple-element.225.refs_0_), channel_id=1, source_target_pairs={{0,12},{1,13},{2,14},{3,15},{4,8},{5,9},{6,10},{7,11},{8,4},{9,5},... | collective-permute-start | bytes 147464 | tf_op jit(solution)/shard_map/ppermute | solution.py:289
  113.6 1.8 %collective-permute-done.67.refs_0_ = bf16[12,8,256]{2,1,0:T(8,128)(2,1)S(1)} collective-permute-done((bf16[12,8,256]{2,1,0:T(8,128)(2,1)S(1)}, bf16[12,8,256]{2,1,0:T(8,128)(2,1)S(1)}, u32[]{:S(2)}, u32[]{:S(2)}) %collective-permute-start.67) | collective-permute-done | bytes 49184 | tf_op jit(solution)/shard_map/ppermute | solution.py:289
  (183 shorter events, 65.9 us)
Async XLA Ops:
  7.1 6.2 %collective-permute-start = (bf16[13,8,256]{2,1,0:T(8,128)(2,1)S(1)}, bf16[13,8,256]{2,1,0:T(8,128)(2,1)S(1)}, u32[]{:S(2)}, u32[]{:S(2)}) collective-permute-start(bf16[13,8,256]{2,1,0:T(8,128)(2,1)S(1)} %get-tuple-element.122), channel_id=1, source_target_pairs={{0,1},{1,0},{2,3},{3,2},{4,5},{5,4},{6,7},{7,6},{8,9},{9,8},{10,11... | collective-permute-start | bytes 159752 | tf_op jit(solution)/shard_map/ppermute | solution.py:289
  7.6 5.7 %collective-permute-start.1 = (bf16[13,8,256]{2,1,0:T(8,128)(2,1)S(1)}, bf16[13,8,256]{2,1,0:T(8,128)(2,1)S(1)}, u32[]{:S(2)}, u32[]{:S(2)}) collective-permute-start(bf16[13,8,256]{2,1,0:T(8,128)(2,1)S(1)} %get-tuple-element.123), channel_id=1, source_target_pairs={{0,2},{1,3},{2,0},{3,1},{4,6},{5,7},{6,4},{7,5},{8,10},{9,11},{10,... | collective-permute-start | bytes 159752 | tf_op jit(solution)/shard_map/ppermute | solution.py:289
  11.2 7.5 %collective-permute-start.3 = (bf16[12,8,256]{2,1,0:T(8,128)(2,1)S(1)}, bf16[12,8,256]{2,1,0:T(8,128)(2,1)S(1)}, u32[]{:S(2)}, u32[]{:S(2)}) collective-permute-start(bf16[12,8,256]{2,1,0:T(8,128)(2,1)S(1)} %get-tuple-element.129), channel_id=1, source_target_pairs={{0,1},{1,0},{2,3},{3,2},{4,5},{5,4},{6,7},{7,6},{8,9},{9,8},{10,11... | collective-permute-start | bytes 147464 | tf_op jit(solution)/shard_map/ppermute | solution.py:289
  11.3 7.4 %collective-permute-start.4 = (bf16[12,8,256]{2,1,0:T(8,128)(2,1)S(1)}, bf16[12,8,256]{2,1,0:T(8,128)(2,1)S(1)}, u32[]{:S(2)}, u32[]{:S(2)}) collective-permute-start(bf16[12,8,256]{2,1,0:T(8,128)(2,1)S(1)} %get-tuple-element.130), channel_id=1, source_target_pairs={{0,2},{1,3},{2,0},{3,1},{4,6},{5,7},{6,4},{7,5},{8,10},{9,11},{10,... | collective-permute-start | bytes 147464 | tf_op jit(solution)/shard_map/ppermute | solution.py:289
  14.7 8.2 %collective-permute-start.6 = (bf16[12,8,256]{2,1,0:T(8,128)(2,1)S(1)}, bf16[12,8,256]{2,1,0:T(8,128)(2,1)S(1)}, u32[]{:S(2)}, u32[]{:S(2)}) collective-permute-start(bf16[12,8,256]{2,1,0:T(8,128)(2,1)S(1)} %get-tuple-element.133), channel_id=1, source_target_pairs={{0,8},{1,9},{2,10},{3,11},{4,12},{5,13},{6,14},{7,15},{8,0},{9,1},... | collective-permute-start | bytes 147464 | tf_op jit(solution)/shard_map/ppermute | solution.py:289
  17.4 6.0 %collective-permute-start.7 = (bf16[12,8,256]{2,1,0:T(8,128)(2,1)S(1)}, bf16[12,8,256]{2,1,0:T(8,128)(2,1)S(1)}, u32[]{:S(2)}, u32[]{:S(2)}) collective-permute-start(bf16[12,8,256]{2,1,0:T(8,128)(2,1)S(1)} %get-tuple-element.134), channel_id=1, source_target_pairs={{0,12},{1,13},{2,14},{3,15},{4,8},{5,9},{6,10},{7,11},{8,4},{9,5},... | collective-permute-start | bytes 147464 | tf_op jit(solution)/shard_map/ppermute | solution.py:289
  26.8 5.9 %collective-permute-start.13 = (bf16[12,8,256]{2,1,0:T(8,128)(2,1)S(1)}, bf16[12,8,256]{2,1,0:T(8,128)(2,1)S(1)}, u32[]{:S(2)}, u32[]{:S(2)}) collective-permute-start(bf16[12,8,256]{2,1,0:T(8,128)(2,1)S(1)} %get-tuple-element.141.refs_0_), channel_id=1, source_target_pairs={{0,12},{1,13},{2,14},{3,15},{4,8},{5,9},{6,10},{7,11},{8,4},{9,5},... | collective-permute-start | bytes 147464 | tf_op jit(solution)/shard_map/ppermute | solution.py:289
  28.4 5.8 %collective-permute-start.10 = (bf16[12,8,256]{2,1,0:T(8,128)(2,1)S(1)}, bf16[12,8,256]{2,1,0:T(8,128)(2,1)S(1)}, u32[]{:S(2)}, u32[]{:S(2)}) collective-permute-start(bf16[12,8,256]{2,1,0:T(8,128)(2,1)S(1)} %get-tuple-element.143), channel_id=1, source_target_pairs={{0,1},{1,0},{2,3},{3,2},{4,5},{5,4},{6,7},{7,6},{8,9},{9,8},{10,11... | collective-permute-start | bytes 147464 | tf_op jit(solution)/shard_map/ppermute | solution.py:289
  28.5 6.3 %collective-permute-start.11 = (bf16[12,8,256]{2,1,0:T(8,128)(2,1)S(1)}, bf16[12,8,256]{2,1,0:T(8,128)(2,1)S(1)}, u32[]{:S(2)}, u32[]{:S(2)}) collective-permute-start(bf16[12,8,256]{2,1,0:T(8,128)(2,1)S(1)} %get-tuple-element.144), channel_id=1, source_target_pairs={{0,2},{1,3},{2,0},{3,1},{4,6},{5,7},{6,4},{7,5},{8,10},{9,11},{10,... | collective-permute-start | bytes 147464 | tf_op jit(solution)/shard_map/ppermute | solution.py:289
  44.4 6.1 %collective-permute-start.24 = (bf16[12,8,256]{2,1,0:T(8,128)(2,1)S(1)}, bf16[12,8,256]{2,1,0:T(8,128)(2,1)S(1)}, u32[]{:S(2)}, u32[]{:S(2)}) collective-permute-start(bf16[12,8,256]{2,1,0:T(8,128)(2,1)S(1)} %get-tuple-element.161), channel_id=1, source_target_pairs={{0,8},{1,9},{2,10},{3,11},{4,12},{5,13},{6,14},{7,15},{8,0},{9,1},... | collective-permute-start | bytes 147464 | tf_op jit(solution)/shard_map/ppermute | solution.py:289
  45.1 6.4 %collective-permute-start.25 = (bf16[12,8,256]{2,1,0:T(8,128)(2,1)S(1)}, bf16[12,8,256]{2,1,0:T(8,128)(2,1)S(1)}, u32[]{:S(2)}, u32[]{:S(2)}) collective-permute-start(bf16[12,8,256]{2,1,0:T(8,128)(2,1)S(1)} %get-tuple-element.162), channel_id=1, source_target_pairs={{0,12},{1,13},{2,14},{3,15},{4,8},{5,9},{6,10},{7,11},{8,4},{9,5},... | collective-permute-start | bytes 147464 | tf_op jit(solution)/shard_map/ppermute | solution.py:289
  52.4 6.1 %collective-permute-start.32 = (bf16[12,8,256]{2,1,0:T(8,128)(2,1)S(1)}, bf16[12,8,256]{2,1,0:T(8,128)(2,1)S(1)}, u32[]{:S(2)}, u32[]{:S(2)}) collective-permute-start(bf16[12,8,256]{2,1,0:T(8,128)(2,1)S(1)} %get-tuple-element.168.refs_0_), channel_id=1, source_target_pairs={{0,8},{1,9},{2,10},{3,11},{4,12},{5,13},{6,14},{7,15},{8,0},{9,1},... | collective-permute-start | bytes 147464 | tf_op jit(solution)/shard_map/ppermute | solution.py:289
  54.4 5.9 %collective-permute-start.31 = (bf16[12,8,256]{2,1,0:T(8,128)(2,1)S(1)}, bf16[12,8,256]{2,1,0:T(8,128)(2,1)S(1)}, u32[]{:S(2)}, u32[]{:S(2)}) collective-permute-start(bf16[12,8,256]{2,1,0:T(8,128)(2,1)S(1)} %get-tuple-element.168.refs_0_), channel_id=1, source_target_pairs={{0,12},{1,13},{2,14},{3,15},{4,8},{5,9},{6,10},{7,11},{8,4},{9,5},... | collective-permute-start | bytes 147464 | tf_op jit(solution)/shard_map/ppermute | solution.py:289
  56.6 5.7 %collective-permute-start.29 = (bf16[12,8,256]{2,1,0:T(8,128)(2,1)S(1)}, bf16[12,8,256]{2,1,0:T(8,128)(2,1)S(1)}, u32[]{:S(2)}, u32[]{:S(2)}) collective-permute-start(bf16[12,8,256]{2,1,0:T(8,128)(2,1)S(1)} %get-tuple-element.171), channel_id=1, source_target_pairs={{0,2},{1,3},{2,0},{3,1},{4,6},{5,7},{6,4},{7,5},{8,10},{9,11},{10,... | collective-permute-start | bytes 147464 | tf_op jit(solution)/shard_map/ppermute | solution.py:289
  71.8 6.6 %collective-permute-start.42 = (bf16[12,8,256]{2,1,0:T(8,128)(2,1)S(1)}, bf16[12,8,256]{2,1,0:T(8,128)(2,1)S(1)}, u32[]{:S(2)}, u32[]{:S(2)}) collective-permute-start(bf16[12,8,256]{2,1,0:T(8,128)(2,1)S(1)} %get-tuple-element.188), channel_id=1, source_target_pairs={{0,8},{1,9},{2,10},{3,11},{4,12},{5,13},{6,14},{7,15},{8,0},{9,1},... | collective-permute-start | bytes 147464 | tf_op jit(solution)/shard_map/ppermute | solution.py:289
  72.0 6.5 %collective-permute-start.43 = (bf16[12,8,256]{2,1,0:T(8,128)(2,1)S(1)}, bf16[12,8,256]{2,1,0:T(8,128)(2,1)S(1)}, u32[]{:S(2)}, u32[]{:S(2)}) collective-permute-start(bf16[12,8,256]{2,1,0:T(8,128)(2,1)S(1)} %get-tuple-element.189), channel_id=1, source_target_pairs={{0,12},{1,13},{2,14},{3,15},{4,8},{5,9},{6,10},{7,11},{8,4},{9,5},... | collective-permute-start | bytes 147464 | tf_op jit(solution)/shard_map/ppermute | solution.py:289
  80.0 6.1 %collective-permute-start.50 = (bf16[12,8,256]{2,1,0:T(8,128)(2,1)S(1)}, bf16[12,8,256]{2,1,0:T(8,128)(2,1)S(1)}, u32[]{:S(2)}, u32[]{:S(2)}) collective-permute-start(bf16[12,8,256]{2,1,0:T(8,128)(2,1)S(1)} %get-tuple-element.195.refs_0_), channel_id=1, source_target_pairs={{0,8},{1,9},{2,10},{3,11},{4,12},{5,13},{6,14},{7,15},{8,0},{9,1},... | collective-permute-start | bytes 147464 | tf_op jit(solution)/shard_map/ppermute | solution.py:289
  81.9 5.9 %collective-permute-start.49 = (bf16[12,8,256]{2,1,0:T(8,128)(2,1)S(1)}, bf16[12,8,256]{2,1,0:T(8,128)(2,1)S(1)}, u32[]{:S(2)}, u32[]{:S(2)}) collective-permute-start(bf16[12,8,256]{2,1,0:T(8,128)(2,1)S(1)} %get-tuple-element.195.refs_0_), channel_id=1, source_target_pairs={{0,12},{1,13},{2,14},{3,15},{4,8},{5,9},{6,10},{7,11},{8,4},{9,5},... | collective-permute-start | bytes 147464 | tf_op jit(solution)/shard_map/ppermute | solution.py:289
  99.4 6.6 %collective-permute-start.60 = (bf16[12,8,256]{2,1,0:T(8,128)(2,1)S(1)}, bf16[12,8,256]{2,1,0:T(8,128)(2,1)S(1)}, u32[]{:S(2)}, u32[]{:S(2)}) collective-permute-start(bf16[12,8,256]{2,1,0:T(8,128)(2,1)S(1)} %get-tuple-element.215), channel_id=1, source_target_pairs={{0,8},{1,9},{2,10},{3,11},{4,12},{5,13},{6,14},{7,15},{8,0},{9,1},... | collective-permute-start | bytes 147464 | tf_op jit(solution)/shard_map/ppermute | solution.py:289
  99.7 6.3 %collective-permute-start.61 = (bf16[12,8,256]{2,1,0:T(8,128)(2,1)S(1)}, bf16[12,8,256]{2,1,0:T(8,128)(2,1)S(1)}, u32[]{:S(2)}, u32[]{:S(2)}) collective-permute-start(bf16[12,8,256]{2,1,0:T(8,128)(2,1)S(1)} %get-tuple-element.216), channel_id=1, source_target_pairs={{0,12},{1,13},{2,14},{3,15},{4,8},{5,9},{6,10},{7,11},{8,4},{9,5},... | collective-permute-start | bytes 147464 | tf_op jit(solution)/shard_map/ppermute | solution.py:289
  107.5 6.1 %collective-permute-start.68 = (bf16[12,8,256]{2,1,0:T(8,128)(2,1)S(1)}, bf16[12,8,256]{2,1,0:T(8,128)(2,1)S(1)}, u32[]{:S(2)}, u32[]{:S(2)}) collective-permute-start(bf16[12,8,256]{2,1,0:T(8,128)(2,1)S(1)} %get-tuple-element.225.refs_0_), channel_id=1, source_target_pairs={{0,8},{1,9},{2,10},{3,11},{4,12},{5,13},{6,14},{7,15},{8,0},{9,1},... | collective-permute-start | bytes 147464 | tf_op jit(solution)/shard_map/ppermute | solution.py:289
  109.5 5.9 %collective-permute-start.67 = (bf16[12,8,256]{2,1,0:T(8,128)(2,1)S(1)}, bf16[12,8,256]{2,1,0:T(8,128)(2,1)S(1)}, u32[]{:S(2)}, u32[]{:S(2)}) collective-permute-start(bf16[12,8,256]{2,1,0:T(8,128)(2,1)S(1)} %get-tuple-element.225.refs_0_), channel_id=1, source_target_pairs={{0,12},{1,13},{2,14},{3,15},{4,8},{5,9},{6,10},{7,11},{8,4},{9,5},... | collective-permute-start | bytes 147464 | tf_op jit(solution)/shard_map/ppermute | solution.py:289
  111.7 7.0 %collective-permute-start.65 = (bf16[12,8,256]{2,1,0:T(8,128)(2,1)S(1)}, bf16[12,8,256]{2,1,0:T(8,128)(2,1)S(1)}, u32[]{:S(2)}, u32[]{:S(2)}) collective-permute-start(bf16[12,8,256]{2,1,0:T(8,128)(2,1)S(1)} %get-tuple-element.228), channel_id=1, source_target_pairs={{0,2},{1,3},{2,0},{3,1},{4,6},{5,7},{6,4},{7,5},{8,10},{9,11},{10,... | collective-permute-start | bytes 147464 | tf_op jit(solution)/shard_map/ppermute | solution.py:289
  112.9 5.8 %collective-permute-start.66 = (bf16[12,8,256]{2,1,0:T(8,128)(2,1)S(1)}, bf16[12,8,256]{2,1,0:T(8,128)(2,1)S(1)}, u32[]{:S(2)}, u32[]{:S(2)}) collective-permute-start(bf16[12,8,256]{2,1,0:T(8,128)(2,1)S(1)} %get-tuple-element.229), channel_id=1, source_target_pairs={{0,3},{1,2},{2,1},{3,0},{4,7},{5,6},{6,5},{7,4},{8,11},{9,10},{10,... | collective-permute-start | bytes 147464 | tf_op jit(solution)/shard_map/ppermute | solution.py:289
  (53 other events, 223.8 us)

commit v14 on v13

--- a/solution.py
+++ b/solution.py
@@ -338,6 +338,8 @@
         got += [swap(near_sums[h], h * QUAD) for h in range(1, half)]
         if step == steps - 1:
             turned, x_state = lax.optimization_barrier((turned, x_state))
+        if step == 0:
+            rhs, x_state = lax.optimization_barrier((rhs, x_state))
         u, dx, moved = call(
             functools.partial(primal_kernel, step), "primal", 1 << 20, [VM] * (3 + group),
             (x_shape, x_shape, block_set), (primal_mask, primal_step, x_state, near_sums[0], *got))

time: 122 us -> 122 us (level)
  transfers between devices with their start and end apart: 72 -> 72, of which waited for: 28 -> 30; matrix products, arithmetic and copies ran while one was open for 0% -> 0% of each run, Pallas kernels for 17% -> 17%
where the time goes in v14:
time: 122 us; the launch traced here: 121 us
  starting transfers between devices  63.3 us (52%)
  Pallas kernels  29.4 us (24%)
  waiting for transfers between devices  26.8 us (22%)
  between operations  1.77 us (1%)
    ppermute x72, starting transfers between devices, swap(): return lax.ppermute(array, 'rb', [(p, p ^ x) for p in range(peers)])  63.3 us
    ppermute x72, waiting for transfers between devices, swap(): return lax.ppermute(array, 'rb', [(p, p ^ x) for p in range(peers)])  26.8 us
    pallas_call x51, Pallas kernels, call(): pl.pallas_call(kernel, out_shape=outs, in_specs=ins, out_specs=jax.tree.m...  23 us
    pallas_call x1, Pallas kernels, on_device(): pl.pallas_call(functools.partial(start_kernel, step, peers, cap, col_bloc...  5.8 us
  transfers between devices with their start and end apart: 72, of which 30 were waited for; matrix products, arithmetic and copies ran while one was open for 0% of the time, Pallas kernels for 17%

profile of v14, /device:TPU:0, one launch (start us, length us, event | category | flops | bytes accessed | tf_op | source)
XLA Modules:
  0.0 121.3 jit_solution(14812897070944188577)
XLA Ops:
  1.3 5.8 %start.1 = (bf16[88,256,256]{2,1,0:T(8,128)(2,1)S(1)}, f32[8,2048]{1,0:T(8,128)S(1)}, f32[8,2048]{1,0:T(8,128)S(1)}, bf16[8,8,256]{2,1,0:T(8,128)(2,1)S(1)}, s32...) custom-call(s32[1]{0:T(128)S(6)} %copy.14.count, ...), custom_call_target="tpu_custom_call" | custom-call | flops 184549376 | bytes 23068672 | tf_op jit(solution)/shard_map/start/pallas_call | solution.py:295
  7.6 2.6 %collective-permute-start.1 = (bf16[13,8,256]{2,1,0:T(8,128)(2,1)S(1)}, bf16[13,8,256]{2,1,0:T(8,128)(2,1)S(1)}, u32[]{:S(2)}, u32[]{:S(2)}) collective-permute-start(bf16[13,8,256]{2,1,0:T(8,128)(2,1)S(1)} %get-tuple-element.128), channel_id=1, source_target_pairs={{0,2},{1,3},{2,0},{3,1},{4,6},{5,7},{6,4},{7,5},{8,10},{9,11},{10,... | collective-permute-start | bytes 159752 | tf_op jit(solution)/shard_map/ppermute | solution.py:289
  11.3 1.9 %collective-permute-start.4 = (bf16[12,8,256]{2,1,0:T(8,128)(2,1)S(1)}, bf16[12,8,256]{2,1,0:T(8,128)(2,1)S(1)}, u32[]{:S(2)}, u32[]{:S(2)}) collective-permute-start(bf16[12,8,256]{2,1,0:T(8,128)(2,1)S(1)} %get-tuple-element.134), channel_id=1, source_target_pairs={{0,2},{1,3},{2,0},{3,1},{4,6},{5,7},{6,4},{7,5},{8,10},{9,11},{10,... | collective-permute-start | bytes 147464 | tf_op jit(solution)/shard_map/ppermute | solution.py:289
  14.7 2.7 %collective-permute-start.6 = (bf16[12,8,256]{2,1,0:T(8,128)(2,1)S(1)}, bf16[12,8,256]{2,1,0:T(8,128)(2,1)S(1)}, u32[]{:S(2)}, u32[]{:S(2)}) collective-permute-start(bf16[12,8,256]{2,1,0:T(8,128)(2,1)S(1)} %get-tuple-element.137), channel_id=1, source_target_pairs={{0,8},{1,9},{2,10},{3,11},{4,12},{5,13},{6,14},{7,15},{8,0},{9,1},... | collective-permute-start | bytes 147464 | tf_op jit(solution)/shard_map/ppermute | solution.py:289
  17.4 1.3 %collective-permute-start.7 = (bf16[12,8,256]{2,1,0:T(8,128)(2,1)S(1)}, bf16[12,8,256]{2,1,0:T(8,128)(2,1)S(1)}, u32[]{:S(2)}, u32[]{:S(2)}) collective-permute-start(bf16[12,8,256]{2,1,0:T(8,128)(2,1)S(1)} %get-tuple-element.138), channel_id=1, source_target_pairs={{0,12},{1,13},{2,14},{3,15},{4,8},{5,9},{6,10},{7,11},{8,4},{9,5},... | collective-permute-start | bytes 147464 | tf_op jit(solution)/shard_map/ppermute | solution.py:289
  19.2 3.7 %turn.1.turned = bf16[88,256,256]{2,1,0:T(8,128)(2,1)S(1)} custom-call(bf16[88,256,256]{2,1,0:T(8,128)(2,1)S(1)} %get-tuple-element.124.held), custom_call_target="tpu_custom_call" | custom-call | flops 92274688 | bytes 11534336 | tf_op jit(solution)/shard_map/turn/pallas_call | solution.py:277
  24.9 1.9 %collective-permute-start.14 = (bf16[12,8,256]{2,1,0:T(8,128)(2,1)S(1)}, bf16[12,8,256]{2,1,0:T(8,128)(2,1)S(1)}, u32[]{:S(2)}, u32[]{:S(2)}) collective-permute-start(bf16[12,8,256]{2,1,0:T(8,128)(2,1)S(1)} %get-tuple-element.143.refs_0_), channel_id=1, source_target_pairs={{0,8},{1,9},{2,10},{3,11},{4,12},{5,13},{6,14},{7,15},{8,0},{9,1},... | collective-permute-start | bytes 147464 | tf_op jit(solution)/shard_map/ppermute | solution.py:289
  30.5 2.3 %collective-permute-done.13.refs_0_ = bf16[12,8,256]{2,1,0:T(8,128)(2,1)S(1)} collective-permute-done((bf16[12,8,256]{2,1,0:T(8,128)(2,1)S(1)}, bf16[12,8,256]{2,1,0:T(8,128)(2,1)S(1)}, u32[]{:S(2)}, u32[]{:S(2)}) %collective-permute-start.13) | collective-permute-done | bytes 49184 | tf_op jit(solution)/shard_map/ppermute | solution.py:289
  32.9 1.3 %collective-permute-start.16 = (bf16[12,8,256]{2,1,0:T(8,128)(2,1)S(1)}, bf16[12,8,256]{2,1,0:T(8,128)(2,1)S(1)}, u32[]{:S(2)}, u32[]{:S(2)}) collective-permute-start(bf16[12,8,256]{2,1,0:T(8,128)(2,1)S(1)} %get-tuple-element.150), channel_id=1, source_target_pairs={{0,2},{1,3},{2,0},{3,1},{4,6},{5,7},{6,4},{7,5},{8,10},{9,11},{10,... | collective-permute-start | bytes 147464 | tf_op jit(solution)/shard_map/ppermute | solution.py:289
  48.2 2.3 %collective-permute-done.24.refs_1_ = bf16[12,8,256]{2,1,0:T(8,128)(2,1)S(1)} collective-permute-done((bf16[12,8,256]{2,1,0:T(8,128)(2,1)S(1)}, bf16[12,8,256]{2,1,0:T(8,128)(2,1)S(1)}, u32[]{:S(2)}, u32[]{:S(2)}) %collective-permute-start.24) | collective-permute-done | bytes 49184 | tf_op jit(solution)/shard_map/ppermute | solution.py:289
  52.4 2.0 %collective-permute-start.32 = (bf16[12,8,256]{2,1,0:T(8,128)(2,1)S(1)}, bf16[12,8,256]{2,1,0:T(8,128)(2,1)S(1)}, u32[]{:S(2)}, u32[]{:S(2)}) collective-permute-start(bf16[12,8,256]{2,1,0:T(8,128)(2,1)S(1)} %get-tuple-element.170.refs_0_), channel_id=1, source_target_pairs={{0,8},{1,9},{2,10},{3,11},{4,12},{5,13},{6,14},{7,15},{8,0},{9,1},... | collective-permute-start | bytes 147464 | tf_op jit(solution)/shard_map/ppermute | solution.py:289
  54.4 2.0 %collective-permute-start.31 = (bf16[12,8,256]{2,1,0:T(8,128)(2,1)S(1)}, bf16[12,8,256]{2,1,0:T(8,128)(2,1)S(1)}, u32[]{:S(2)}, u32[]{:S(2)}) collective-permute-start(bf16[12,8,256]{2,1,0:T(8,128)(2,1)S(1)} %get-tuple-element.170.refs_0_), channel_id=1, source_target_pairs={{0,12},{1,13},{2,14},{3,15},{4,8},{5,9},{6,10},{7,11},{8,4},{9,5},... | collective-permute-start | bytes 147464 | tf_op jit(solution)/shard_map/ppermute | solution.py:289
  58.5 1.8 %collective-permute-done.31.refs_0_ = bf16[12,8,256]{2,1,0:T(8,128)(2,1)S(1)} collective-permute-done((bf16[12,8,256]{2,1,0:T(8,128)(2,1)S(1)}, bf16[12,8,256]{2,1,0:T(8,128)(2,1)S(1)}, u32[]{:S(2)}, u32[]{:S(2)}) %collective-permute-start.31) | collective-permute-done | bytes 49184 | tf_op jit(solution)/shard_map/ppermute | solution.py:289
  72.0 2.1 %collective-permute-start.43 = (bf16[12,8,256]{2,1,0:T(8,128)(2,1)S(1)}, bf16[12,8,256]{2,1,0:T(8,128)(2,1)S(1)}, u32[]{:S(2)}, u32[]{:S(2)}) collective-permute-start(bf16[12,8,256]{2,1,0:T(8,128)(2,1)S(1)} %get-tuple-element.191), channel_id=1, source_target_pairs={{0,12},{1,13},{2,14},{3,15},{4,8},{5,9},{6,10},{7,11},{8,4},{9,5},... | collective-permute-start | bytes 147464 | tf_op jit(solution)/shard_map/ppermute | solution.py:289
  75.6 2.8 %collective-permute-done.42.refs_1_ = bf16[12,8,256]{2,1,0:T(8,128)(2,1)S(1)} collective-permute-done((bf16[12,8,256]{2,1,0:T(8,128)(2,1)S(1)}, bf16[12,8,256]{2,1,0:T(8,128)(2,1)S(1)}, u32[]{:S(2)}, u32[]{:S(2)}) %collective-permute-start.42) | collective-permute-done | bytes 49184 | tf_op jit(solution)/shard_map/ppermute | solution.py:289
  80.0 1.9 %collective-permute-start.50 = (bf16[12,8,256]{2,1,0:T(8,128)(2,1)S(1)}, bf16[12,8,256]{2,1,0:T(8,128)(2,1)S(1)}, u32[]{:S(2)}, u32[]{:S(2)}) collective-permute-start(bf16[12,8,256]{2,1,0:T(8,128)(2,1)S(1)} %get-tuple-element.193.refs_0_), channel_id=1, source_target_pairs={{0,8},{1,9},{2,10},{3,11},{4,12},{5,13},{6,14},{7,15},{8,0},{9,1},... | collective-permute-start | bytes 147464 | tf_op jit(solution)/shard_map/ppermute | solution.py:289
  81.9 1.9 %collective-permute-start.49 = (bf16[12,8,256]{2,1,0:T(8,128)(2,1)S(1)}, bf16[12,8,256]{2,1,0:T(8,128)(2,1)S(1)}, u32[]{:S(2)}, u32[]{:S(2)}) collective-permute-start(bf16[12,8,256]{2,1,0:T(8,128)(2,1)S(1)} %get-tuple-element.193.refs_0_), channel_id=1, source_target_pairs={{0,12},{1,13},{2,14},{3,15},{4,8},{5,9},{6,10},{7,11},{8,4},{9,5},... | collective-permute-start | bytes 147464 | tf_op jit(solution)/shard_map/ppermute | solution.py:289
  84.2 1.3 %collective-permute-start.47 = (bf16[12,8,256]{2,1,0:T(8,128)(2,1)S(1)}, bf16[12,8,256]{2,1,0:T(8,128)(2,1)S(1)}, u32[]{:S(2)}, u32[]{:S(2)}) collective-permute-start(bf16[12,8,256]{2,1,0:T(8,128)(2,1)S(1)} %get-tuple-element.196), channel_id=1, source_target_pairs={{0,2},{1,3},{2,0},{3,1},{4,6},{5,7},{6,4},{7,5},{8,10},{9,11},{10,... | collective-permute-start | bytes 147464 | tf_op jit(solution)/shard_map/ppermute | solution.py:289
  86.1 1.7 %collective-permute-done.49.refs_0_ = bf16[12,8,256]{2,1,0:T(8,128)(2,1)S(1)} collective-permute-done((bf16[12,8,256]{2,1,0:T(8,128)(2,1)S(1)}, bf16[12,8,256]{2,1,0:T(8,128)(2,1)S(1)}, u32[]{:S(2)}, u32[]{:S(2)}) %collective-permute-start.49) | collective-permute-done | bytes 49184 | tf_op jit(solution)/shard_map/ppermute | solution.py:289
  99.7 1.8 %collective-permute-start.61 = (bf16[12,8,256]{2,1,0:T(8,128)(2,1)S(1)}, bf16[12,8,256]{2,1,0:T(8,128)(2,1)S(1)}, u32[]{:S(2)}, u32[]{:S(2)}) collective-permute-start(bf16[12,8,256]{2,1,0:T(8,128)(2,1)S(1)} %get-tuple-element.221), channel_id=1, source_target_pairs={{0,12},{1,13},{2,14},{3,15},{4,8},{5,9},{6,10},{7,11},{8,4},{9,5},... | collective-permute-start | bytes 147464 | tf_op jit(solution)/shard_map/ppermute | solution.py:289
  103.9 2.2 %collective-permute-done.60.refs_1_ = bf16[12,8,256]{2,1,0:T(8,128)(2,1)S(1)} collective-permute-done((bf16[12,8,256]{2,1,0:T(8,128)(2,1)S(1)}, bf16[12,8,256]{2,1,0:T(8,128)(2,1)S(1)}, u32[]{:S(2)}, u32[]{:S(2)}) %collective-permute-start.60) | collective-permute-done | bytes 49184 | tf_op jit(solution)/shard_map/ppermute | solution.py:289
  107.5 2.0 %collective-permute-start.68 = (bf16[12,8,256]{2,1,0:T(8,128)(2,1)S(1)}, bf16[12,8,256]{2,1,0:T(8,128)(2,1)S(1)}, u32[]{:S(2)}, u32[]{:S(2)}) collective-permute-start(bf16[12,8,256]{2,1,0:T(8,128)(2,1)S(1)} %get-tuple-element.229.refs_0_), channel_id=1, source_target_pairs={{0,8},{1,9},{2,10},{3,11},{4,12},{5,13},{6,14},{7,15},{8,0},{9,1},... | collective-permute-start | bytes 147464 | tf_op jit(solution)/shard_map/ppermute | solution.py:289
  109.5 1.9 %collective-permute-start.67 = (bf16[12,8,256]{2,1,0:T(8,128)(2,1)S(1)}, bf16[12,8,256]{2,1,0:T(8,128)(2,1)S(1)}, u32[]{:S(2)}, u32[]{:S(2)}) collective-permute-start(bf16[12,8,256]{2,1,0:T(8,128)(2,1)S(1)} %get-tuple-element.229.refs_0_), channel_id=1, source_target_pairs={{0,12},{1,13},{2,14},{3,15},{4,8},{5,9},{6,10},{7,11},{8,4},{9,5},... | collective-permute-start | bytes 147464 | tf_op jit(solution)/shard_map/ppermute | solution.py:289
  113.6 1.8 %collective-permute-done.67.refs_0_ = bf16[12,8,256]{2,1,0:T(8,128)(2,1)S(1)} collective-permute-done((bf16[12,8,256]{2,1,0:T(8,128)(2,1)S(1)}, bf16[12,8,256]{2,1,0:T(8,128)(2,1)S(1)}, u32[]{:S(2)}, u32[]{:S(2)}) %collective-permute-start.67) | collective-permute-done | bytes 49184 | tf_op jit(solution)/shard_map/ppermute | solution.py:289
  (183 shorter events, 66.4 us)
Async XLA Ops:
  7.1 6.2 %collective-permute-start = (bf16[13,8,256]{2,1,0:T(8,128)(2,1)S(1)}, bf16[13,8,256]{2,1,0:T(8,128)(2,1)S(1)}, u32[]{:S(2)}, u32[]{:S(2)}) collective-permute-start(bf16[13,8,256]{2,1,0:T(8,128)(2,1)S(1)} %get-tuple-element.127), channel_id=1, source_target_pairs={{0,1},{1,0},{2,3},{3,2},{4,5},{5,4},{6,7},{7,6},{8,9},{9,8},{10,11... | collective-permute-start | bytes 159752 | tf_op jit(solution)/shard_map/ppermute | solution.py:289
  7.6 5.7 %collective-permute-start.1 = (bf16[13,8,256]{2,1,0:T(8,128)(2,1)S(1)}, bf16[13,8,256]{2,1,0:T(8,128)(2,1)S(1)}, u32[]{:S(2)}, u32[]{:S(2)}) collective-permute-start(bf16[13,8,256]{2,1,0:T(8,128)(2,1)S(1)} %get-tuple-element.128), channel_id=1, source_target_pairs={{0,2},{1,3},{2,0},{3,1},{4,6},{5,7},{6,4},{7,5},{8,10},{9,11},{10,... | collective-permute-start | bytes 159752 | tf_op jit(solution)/shard_map/ppermute | solution.py:289
  11.2 7.5 %collective-permute-start.3 = (bf16[12,8,256]{2,1,0:T(8,128)(2,1)S(1)}, bf16[12,8,256]{2,1,0:T(8,128)(2,1)S(1)}, u32[]{:S(2)}, u32[]{:S(2)}) collective-permute-start(bf16[12,8,256]{2,1,0:T(8,128)(2,1)S(1)} %get-tuple-element.133), channel_id=1, source_target_pairs={{0,1},{1,0},{2,3},{3,2},{4,5},{5,4},{6,7},{7,6},{8,9},{9,8},{10,11... | collective-permute-start | bytes 147464 | tf_op jit(solution)/shard_map/ppermute | solution.py:289
  11.3 7.4 %collective-permute-start.4 = (bf16[12,8,256]{2,1,0:T(8,128)(2,1)S(1)}, bf16[12,8,256]{2,1,0:T(8,128)(2,1)S(1)}, u32[]{:S(2)}, u32[]{:S(2)}) collective-permute-start(bf16[12,8,256]{2,1,0:T(8,128)(2,1)S(1)} %get-tuple-element.134), channel_id=1, source_target_pairs={{0,2},{1,3},{2,0},{3,1},{4,6},{5,7},{6,4},{7,5},{8,10},{9,11},{10,... | collective-permute-start | bytes 147464 | tf_op jit(solution)/shard_map/ppermute | solution.py:289
  14.7 8.2 %collective-permute-start.6 = (bf16[12,8,256]{2,1,0:T(8,128)(2,1)S(1)}, bf16[12,8,256]{2,1,0:T(8,128)(2,1)S(1)}, u32[]{:S(2)}, u32[]{:S(2)}) collective-permute-start(bf16[12,8,256]{2,1,0:T(8,128)(2,1)S(1)} %get-tuple-element.137), channel_id=1, source_target_pairs={{0,8},{1,9},{2,10},{3,11},{4,12},{5,13},{6,14},{7,15},{8,0},{9,1},... | collective-permute-start | bytes 147464 | tf_op jit(solution)/shard_map/ppermute | solution.py:289
  17.4 6.0 %collective-permute-start.7 = (bf16[12,8,256]{2,1,0:T(8,128)(2,1)S(1)}, bf16[12,8,256]{2,1,0:T(8,128)(2,1)S(1)}, u32[]{:S(2)}, u32[]{:S(2)}) collective-permute-start(bf16[12,8,256]{2,1,0:T(8,128)(2,1)S(1)} %get-tuple-element.138), channel_id=1, source_target_pairs={{0,12},{1,13},{2,14},{3,15},{4,8},{5,9},{6,10},{7,11},{8,4},{9,5},... | collective-permute-start | bytes 147464 | tf_op jit(solution)/shard_map/ppermute | solution.py:289
  26.9 5.9 %collective-permute-start.13 = (bf16[12,8,256]{2,1,0:T(8,128)(2,1)S(1)}, bf16[12,8,256]{2,1,0:T(8,128)(2,1)S(1)}, u32[]{:S(2)}, u32[]{:S(2)}) collective-permute-start(bf16[12,8,256]{2,1,0:T(8,128)(2,1)S(1)} %get-tuple-element.143.refs_0_), channel_id=1, source_target_pairs={{0,12},{1,13},{2,14},{3,15},{4,8},{5,9},{6,10},{7,11},{8,4},{9,5},... | collective-permute-start | bytes 147464 | tf_op jit(solution)/shard_map/ppermute | solution.py:289
  28.4 5.8 %collective-permute-start.10 = (bf16[12,8,256]{2,1,0:T(8,128)(2,1)S(1)}, bf16[12,8,256]{2,1,0:T(8,128)(2,1)S(1)}, u32[]{:S(2)}, u32[]{:S(2)}) collective-permute-start(bf16[12,8,256]{2,1,0:T(8,128)(2,1)S(1)} %get-tuple-element.145), channel_id=1, source_target_pairs={{0,1},{1,0},{2,3},{3,2},{4,5},{5,4},{6,7},{7,6},{8,9},{9,8},{10,11... | collective-permute-start | bytes 147464 | tf_op jit(solution)/shard_map/ppermute | solution.py:289
  28.5 6.3 %collective-permute-start.11 = (bf16[12,8,256]{2,1,0:T(8,128)(2,1)S(1)}, bf16[12,8,256]{2,1,0:T(8,128)(2,1)S(1)}, u32[]{:S(2)}, u32[]{:S(2)}) collective-permute-start(bf16[12,8,256]{2,1,0:T(8,128)(2,1)S(1)} %get-tuple-element.146), channel_id=1, source_target_pairs={{0,2},{1,3},{2,0},{3,1},{4,6},{5,7},{6,4},{7,5},{8,10},{9,11},{10,... | collective-permute-start | bytes 147464 | tf_op jit(solution)/shard_map/ppermute | solution.py:289
  44.4 6.1 %collective-permute-start.24 = (bf16[12,8,256]{2,1,0:T(8,128)(2,1)S(1)}, bf16[12,8,256]{2,1,0:T(8,128)(2,1)S(1)}, u32[]{:S(2)}, u32[]{:S(2)}) collective-permute-start(bf16[12,8,256]{2,1,0:T(8,128)(2,1)S(1)} %get-tuple-element.163), channel_id=1, source_target_pairs={{0,8},{1,9},{2,10},{3,11},{4,12},{5,13},{6,14},{7,15},{8,0},{9,1},... | collective-permute-start | bytes 147464 | tf_op jit(solution)/shard_map/ppermute | solution.py:289
  45.1 6.4 %collective-permute-start.25 = (bf16[12,8,256]{2,1,0:T(8,128)(2,1)S(1)}, bf16[12,8,256]{2,1,0:T(8,128)(2,1)S(1)}, u32[]{:S(2)}, u32[]{:S(2)}) collective-permute-start(bf16[12,8,256]{2,1,0:T(8,128)(2,1)S(1)} %get-tuple-element.164), channel_id=1, source_target_pairs={{0,12},{1,13},{2,14},{3,15},{4,8},{5,9},{6,10},{7,11},{8,4},{9,5},... | collective-permute-start | bytes 147464 | tf_op jit(solution)/shard_map/ppermute | solution.py:289
  52.4 6.1 %collective-permute-start.32 = (bf16[12,8,256]{2,1,0:T(8,128)(2,1)S(1)}, bf16[12,8,256]{2,1,0:T(8,128)(2,1)S(1)}, u32[]{:S(2)}, u32[]{:S(2)}) collective-permute-start(bf16[12,8,256]{2,1,0:T(8,128)(2,1)S(1)} %get-tuple-element.170.refs_0_), channel_id=1, source_target_pairs={{0,8},{1,9},{2,10},{3,11},{4,12},{5,13},{6,14},{7,15},{8,0},{9,1},... | collective-permute-start | bytes 147464 | tf_op jit(solution)/shard_map/ppermute | solution.py:289
  54.4 5.9 %collective-permute-start.31 = (bf16[12,8,256]{2,1,0:T(8,128)(2,1)S(1)}, bf16[12,8,256]{2,1,0:T(8,128)(2,1)S(1)}, u32[]{:S(2)}, u32[]{:S(2)}) collective-permute-start(bf16[12,8,256]{2,1,0:T(8,128)(2,1)S(1)} %get-tuple-element.170.refs_0_), channel_id=1, source_target_pairs={{0,12},{1,13},{2,14},{3,15},{4,8},{5,9},{6,10},{7,11},{8,4},{9,5},... | collective-permute-start | bytes 147464 | tf_op jit(solution)/shard_map/ppermute | solution.py:289
  56.6 5.7 %collective-permute-start.29 = (bf16[12,8,256]{2,1,0:T(8,128)(2,1)S(1)}, bf16[12,8,256]{2,1,0:T(8,128)(2,1)S(1)}, u32[]{:S(2)}, u32[]{:S(2)}) collective-permute-start(bf16[12,8,256]{2,1,0:T(8,128)(2,1)S(1)} %get-tuple-element.173), channel_id=1, source_target_pairs={{0,2},{1,3},{2,0},{3,1},{4,6},{5,7},{6,4},{7,5},{8,10},{9,11},{10,... | collective-permute-start | bytes 147464 | tf_op jit(solution)/shard_map/ppermute | solution.py:289
  71.8 6.6 %collective-permute-start.42 = (bf16[12,8,256]{2,1,0:T(8,128)(2,1)S(1)}, bf16[12,8,256]{2,1,0:T(8,128)(2,1)S(1)}, u32[]{:S(2)}, u32[]{:S(2)}) collective-permute-start(bf16[12,8,256]{2,1,0:T(8,128)(2,1)S(1)} %get-tuple-element.190), channel_id=1, source_target_pairs={{0,8},{1,9},{2,10},{3,11},{4,12},{5,13},{6,14},{7,15},{8,0},{9,1},... | collective-permute-start | bytes 147464 | tf_op jit(solution)/shard_map/ppermute | solution.py:289
  72.0 6.5 %collective-permute-start.43 = (bf16[12,8,256]{2,1,0:T(8,128)(2,1)S(1)}, bf16[12,8,256]{2,1,0:T(8,128)(2,1)S(1)}, u32[]{:S(2)}, u32[]{:S(2)}) collective-permute-start(bf16[12,8,256]{2,1,0:T(8,128)(2,1)S(1)} %get-tuple-element.191), channel_id=1, source_target_pairs={{0,12},{1,13},{2,14},{3,15},{4,8},{5,9},{6,10},{7,11},{8,4},{9,5},... | collective-permute-start | bytes 147464 | tf_op jit(solution)/shard_map/ppermute | solution.py:289
  80.0 6.1 %collective-permute-start.50 = (bf16[12,8,256]{2,1,0:T(8,128)(2,1)S(1)}, bf16[12,8,256]{2,1,0:T(8,128)(2,1)S(1)}, u32[]{:S(2)}, u32[]{:S(2)}) collective-permute-start(bf16[12,8,256]{2,1,0:T(8,128)(2,1)S(1)} %get-tuple-element.193.refs_0_), channel_id=1, source_target_pairs={{0,8},{1,9},{2,10},{3,11},{4,12},{5,13},{6,14},{7,15},{8,0},{9,1},... | collective-permute-start | bytes 147464 | tf_op jit(solution)/shard_map/ppermute | solution.py:289
  81.9 5.9 %collective-permute-start.49 = (bf16[12,8,256]{2,1,0:T(8,128)(2,1)S(1)}, bf16[12,8,256]{2,1,0:T(8,128)(2,1)S(1)}, u32[]{:S(2)}, u32[]{:S(2)}) collective-permute-start(bf16[12,8,256]{2,1,0:T(8,128)(2,1)S(1)} %get-tuple-element.193.refs_0_), channel_id=1, source_target_pairs={{0,12},{1,13},{2,14},{3,15},{4,8},{5,9},{6,10},{7,11},{8,4},{9,5},... | collective-permute-start | bytes 147464 | tf_op jit(solution)/shard_map/ppermute | solution.py:289
  84.2 5.6 %collective-permute-start.47 = (bf16[12,8,256]{2,1,0:T(8,128)(2,1)S(1)}, bf16[12,8,256]{2,1,0:T(8,128)(2,1)S(1)}, u32[]{:S(2)}, u32[]{:S(2)}) collective-permute-start(bf16[12,8,256]{2,1,0:T(8,128)(2,1)S(1)} %get-tuple-element.196), channel_id=1, source_target_pairs={{0,2},{1,3},{2,0},{3,1},{4,6},{5,7},{6,4},{7,5},{8,10},{9,11},{10,... | collective-permute-start | bytes 147464 | tf_op jit(solution)/shard_map/ppermute | solution.py:289
  99.4 6.6 %collective-permute-start.60 = (bf16[12,8,256]{2,1,0:T(8,128)(2,1)S(1)}, bf16[12,8,256]{2,1,0:T(8,128)(2,1)S(1)}, u32[]{:S(2)}, u32[]{:S(2)}) collective-permute-start(bf16[12,8,256]{2,1,0:T(8,128)(2,1)S(1)} %get-tuple-element.220), channel_id=1, source_target_pairs={{0,8},{1,9},{2,10},{3,11},{4,12},{5,13},{6,14},{7,15},{8,0},{9,1},... | collective-permute-start | bytes 147464 | tf_op jit(solution)/shard_map/ppermute | solution.py:289
  99.7 6.3 %collective-permute-start.61 = (bf16[12,8,256]{2,1,0:T(8,128)(2,1)S(1)}, bf16[12,8,256]{2,1,0:T(8,128)(2,1)S(1)}, u32[]{:S(2)}, u32[]{:S(2)}) collective-permute-start(bf16[12,8,256]{2,1,0:T(8,128)(2,1)S(1)} %get-tuple-element.221), channel_id=1, source_target_pairs={{0,12},{1,13},{2,14},{3,15},{4,8},{5,9},{6,10},{7,11},{8,4},{9,5},... | collective-permute-start | bytes 147464 | tf_op jit(solution)/shard_map/ppermute | solution.py:289
  107.5 6.1 %collective-permute-start.68 = (bf16[12,8,256]{2,1,0:T(8,128)(2,1)S(1)}, bf16[12,8,256]{2,1,0:T(8,128)(2,1)S(1)}, u32[]{:S(2)}, u32[]{:S(2)}) collective-permute-start(bf16[12,8,256]{2,1,0:T(8,128)(2,1)S(1)} %get-tuple-element.229.refs_0_), channel_id=1, source_target_pairs={{0,8},{1,9},{2,10},{3,11},{4,12},{5,13},{6,14},{7,15},{8,0},{9,1},... | collective-permute-start | bytes 147464 | tf_op jit(solution)/shard_map/ppermute | solution.py:289
  109.5 5.9 %collective-permute-start.67 = (bf16[12,8,256]{2,1,0:T(8,128)(2,1)S(1)}, bf16[12,8,256]{2,1,0:T(8,128)(2,1)S(1)}, u32[]{:S(2)}, u32[]{:S(2)}) collective-permute-start(bf16[12,8,256]{2,1,0:T(8,128)(2,1)S(1)} %get-tuple-element.229.refs_0_), channel_id=1, source_target_pairs={{0,12},{1,13},{2,14},{3,15},{4,8},{5,9},{6,10},{7,11},{8,4},{9,5},... | collective-permute-start | bytes 147464 | tf_op jit(solution)/shard_map/ppermute | solution.py:289
  111.7 6.3 %collective-permute-start.65 = (bf16[12,8,256]{2,1,0:T(8,128)(2,1)S(1)}, bf16[12,8,256]{2,1,0:T(8,128)(2,1)S(1)}, u32[]{:S(2)}, u32[]{:S(2)}) collective-permute-start(bf16[12,8,256]{2,1,0:T(8,128)(2,1)S(1)} %get-tuple-element.232), channel_id=1, source_target_pairs={{0,2},{1,3},{2,0},{3,1},{4,6},{5,7},{6,4},{7,5},{8,10},{9,11},{10,... | collective-permute-start | bytes 147464 | tf_op jit(solution)/shard_map/ppermute | solution.py:289
  (53 other events, 221.9 us)
